TPU v7x, 512 devices: a whole 4x4x16 slice. The times are simulated.
512 devices in a mesh: row: 8 (over y, core), col: 16 (over z), layer: 4 (over x).
Axes of the slice: x: 4, y: 4, z: 16, core: 2. Of those that a mesh axis runs over, the one named last changes fastest.
Arguments:
- a_panel: bfloat16 [4, 8192, 4096], P('layer', 'row', 'col'), may hold values from -6 to 6
- b_panel: bfloat16 [4, 4096, 8192], P('layer', 'row', 'col'), may hold values from -0.375 to 0.375
- mask_a: int32 [4, 32, 16], P('layer', 'row', 'col'), may hold values from 0 to 1, as said below
- mask_b: int32 [4, 16, 32], P('layer', 'row', 'col'), may hold values from 0 to 1, as said below
- row_sizes: int32 [32], P('row'), may hold values from 128 to 256
- inner_sizes: int32 [4, 16], P('layer'), may hold values from 128 to 256
- col_sizes: int32 [32], P('col'), may hold values from 128 to 256
Outputs:
- product: float32 [8192, 8192], P(('row', 'layer'), 'col')
Inputs may be any that keep to these rules, and one draw needn't show every extreme that they name: `mask_a`: 0 or 1; the share of ones differs from block row to block row; every block row of every group has at least one 1; in every draw at least one group is all ones, and some block rows of other groups may be all ones. `mask_b`: 0 or 1; the share of ones differs from block column to block column; every block column of every group has at least one 1; in every draw at least one group is all ones, and some block columns of other groups may be all ones.
All inputs are finite; a program needn't handle non-finite values.
Results may differ from a plain program's by a relative error of at most 0.0003.
Values may be sent and summed in bfloat16 or wider, within the bound.
No kernel may reach another device: no remote copies, remote signals or barrier semaphores. Data moves between devices by JAX's collectives and lax.ppermute only.
A program may use at most 64 MiB of HBM per device.

v0:
```python
import jax
import jax.numpy as jnp
from jax import lax
from jax.sharding import PartitionSpec as P

BS = 256


def keep(mask, rsize, csize, bsize):
    offs = jnp.arange(bsize, dtype=jnp.int32)
    rows = (offs[None, :] < rsize[:, None]).astype(jnp.float32)
    cols = (offs[None, :] < csize[:, None]).astype(jnp.float32)
    mult = (
        mask.astype(jnp.float32)[:, None, :, None] * rows[:, :, None, None] * cols[None, None, :, :]
    )
    return mult.reshape(mask.shape[0] * bsize, mask.shape[1] * bsize).astype(jnp.bfloat16)


def on_device(a_panel, b_panel, mask_a, mask_b, row_sizes, inner_sizes, col_sizes):
    a_local = a_panel[0]
    b_local = b_panel[0]
    a_blocks = a_local.shape[1] // BS
    b_blocks = b_local.shape[0] // BS
    group_sizes = inner_sizes[0]
    a_inner = lax.dynamic_slice_in_dim(group_sizes, lax.axis_index("col") * a_blocks, a_blocks)
    b_inner = lax.dynamic_slice_in_dim(group_sizes, lax.axis_index("row") * b_blocks, b_blocks)
    a_eff = a_local * keep(mask_a[0], row_sizes, a_inner, BS)
    b_eff = b_local * keep(mask_b[0], b_inner, col_sizes, BS)
    a_full = lax.all_gather(a_eff, "col", axis=1, tiled=True)
    partial_sum = jnp.dot(
        a_full, lax.all_gather(b_eff, "row", axis=0, tiled=True), preferred_element_type=jnp.float32
    )
    return lax.psum_scatter(partial_sum, "layer", scatter_dimension=0, tiled=True)


def solution(mesh):
    return jax.shard_map(
        on_device,
        mesh=mesh,
        in_specs=(
            P("layer", "row", "col"),
            P("layer", "row", "col"),
            P("layer", "row", "col"),
            P("layer", "row", "col"),
            P("row"),
            P("layer", None),
            P("col"),
        ),
        out_specs=P(("row", "layer"), "col"),
        check_vma=False,
    )
```

profile of v0, /device:TPU:1, one launch (start us, length us, event | category | flops | bytes accessed | tf_op | source)
XLA Modules:
  0.0 238.5 jit_solution(17061032546859427623)
XLA Ops:
  6.5 0.0 copy-start
  6.5 0.0 copy-start.3
  6.5 0.0 copy-start.2
  6.5 0.0 copy-start.1
  6.5 0.0 all-gather.5.cloned.1.call-start
  6.6 0.8 convert_bitcast_fusion
  7.4 0.0 copy-done
  7.4 0.1 dynamic-slice_bitcast_fusion
  7.4 0.1 compare_convert_fusion
  7.5 0.1 broadcast_multiply_fusion
  7.7 0.6 mul.82
  8.3 0.1 copy.9
  8.3 0.7 lt.94
  9.1 2.0 fusion.1
  11.1 0.0 all-gather.5.cloned.1.call-update
  11.1 0.0 all-gather.3.cloned.1.call-start
  11.2 0.6 constant_dynamic-slice_fusion
  11.8 0.0 copy-done.3
  11.8 0.0 copy-done.2
  11.8 0.1 select_bitcast_fusion
  11.9 0.6 compare_convert_fusion.2
  12.5 0.0 copy-done.1
  12.5 1.0 fusion
  13.5 0.0 all-gather.3.cloned.1.call-update
  13.5 0.0 reduce-scatter.2.cloned.1.call-start
  13.6 43.2 %all-gather.5.cloned.1.call-done = bf16[4096,512]{1,0:T(8,128)(2,1)} async-done(((bf16[512,512]{1,0:T(8,128)(2,1)}), bf16[4096,512]{1,0:T(8,128)(2,1)}) %all-gather.5.cloned.1.call-update) | async-done | bytes 4194320 | tf_op jit(solution)/shard_map/all_gather | solution.py:31
  56.8 122.9 %all-gather.3.cloned.1.call-done = bf16[1024,4096]{1,0:T(8,128)(2,1)} async-done(((bf16[1024,256]{1,0:T(8,128)(2,1)}), bf16[1024,4096]{1,0:T(8,128)(2,1)}) %all-gather.3.cloned.1.call-update) | async-done | bytes 8388624 | tf_op jit(solution)/shard_map/all_gather | solution.py:29
  179.8 10.4 %fusion.2 = f32[1024,512]{1,0:T(8,128)} fusion(bf16[1024,4096]{1,0:T(8,128)(2,1)} %all-gather.3.cloned.1.call-done, bf16[4096,512]{1,0:T(8,128)(2,1)} %all-gather.5.cloned.1.call-done), kind=kOutput, calls=%fused_computation.15 | convolution fusion | flops 4294967296 | bytes 14680064 | tf_op jit(solution)/shard_map/dot_general | solution.py:30
  190.2 0.0 reduce-scatter.2.cloned.1.call-update
  190.2 41.8 %reduce-scatter.2.cloned.1.call-done = f32[256,512]{1,0:T(8,128)} async-done(((f32[1024,512]{1,0:T(8,128)}), f32[256,512]{1,0:T(8,128)}) %reduce-scatter.2.cloned.1.call-update) | async-done | bytes 524304 | tf_op jit(solution)/shard_map/reduce_scatter | solution.py:33
  (5 shorter events, 0.0 us)
Async XLA Ops:
  6.5 0.8 copy-start
  6.5 5.2 %copy-start.3 = (s32[1,4,1]{1,2,0:T(1,128)S(1)}, s32[1,4,1]{1,2,0:T(1,128)}, u32[]{:S(2)}) copy-start(s32[1,4,1]{1,2,0:T(1,128)} %param.9) | copy-start | bytes 52
  6.5 5.2 %copy-start.2 = (s32[4]{0:T(128)S(1)}, s32[4]{0:T(128)}, u32[]{:S(2)}) copy-start(s32[4]{0:T(128)} %param.11) | copy-start | bytes 52
  6.5 6.0 %copy-start.1 = (bf16[1,1024,256]{2,1,0:T(8,128)(2,1)S(1)}, bf16[1,1024,256]{2,1,0:T(8,128)(2,1)}, u32[]{:S(2)}) copy-start(bf16[1,1024,256]{2,1,0:T(8,128)(2,1)} %param.7) | copy-start | bytes 1572868
  6.5 50.3 %all-gather.5.cloned.1.call-start = ((), (), s32[]{:S(2)}) async-start(), calls=%async_computation.2 | async-start | bytes 4718592 | tf_op jit(solution)/shard_map/all_gather | solution.py:31
  11.1 168.6 %all-gather.3.cloned.1.call-start = ((), (), s32[]{:S(2)}) async-start(), calls=%async_computation.1 | async-start | bytes 8912896 | tf_op jit(solution)/shard_map/all_gather | solution.py:29
  13.5 218.4 %reduce-scatter.2.cloned.1.call-start = ((), (), s32[]{:S(2)}) async-start(), calls=%async_computation.3 | async-start | bytes 2621440 | tf_op jit(solution)/shard_map/reduce_scatter | solution.py:33
Sparse Core Ops, SparseCore 0:
  11.2 45.5 all-gather.4
  58.8 120.8 all-gather.2
  190.3 41.6 reduce-scatter.1
where the time goes:
time: 239 us; the launch traced here: 238 us
  waiting for transfers between devices  208 us (87%)
  between operations  13.2 us (6%)
  matrix products  10.4 us (4%)
  other arithmetic  4.72 us (2%)
    all_gather x1, waiting for transfers between devices, on_device(): a_full = lax.all_gather(a_eff, 'col', axis=1, tiled=True)  123 us
    all_gather x1, waiting for transfers between devices, on_device(): lax.all_gather(b_eff, 'row', axis=0, tiled=True)  43.2 us
    reduce_scatter x1, waiting for transfers between devices, on_device(): lax.psum_scatter(partial_sum, 'layer', scatter_dimension=0, tiled=True)  41.8 us
    dot_general x1, matrix products, on_device(): jnp.dot(a_full, lax.all_gather(b_eff, 'row', axis=0, tiled=True), preferr...  10.4 us
  transfers between devices with their start and end apart: 3, of which 3 were waited for; matrix products, arithmetic and copies ran while one was open for 1% of the time, Pallas kernels for 0%

commit v1 on v0

v1 whole, which is shorter than its diff:
```python
import functools

import jax
import jax.numpy as jnp
from jax import lax
from jax.experimental import pallas as pl
from jax.experimental.pallas import tpu as pltpu
from jax.sharding import PartitionSpec as P

BS = 256
HALF = BS // 2
VMEM = pl.BlockSpec(memory_space=pltpu.VMEM)
SMEM = pl.BlockSpec(memory_space=pltpu.SMEM)
PARAMS = pltpu.CompilerParams(vmem_limit_bytes=40 * 1024 * 1024)


def below(shape, axis, size):
    return lax.broadcasted_iota(jnp.int32, shape, axis) < size


def mask_a_kernel(at_ref, mask_ref, rows_ref, inner_ref, a_ref, first_ref, second_ref):
    inner = inner_ref[0, at_ref[0]]
    for i in range(mask_ref.shape[1]):
        shape = (BS, BS)
        on = below(shape, 0, rows_ref[i] * mask_ref[0, i, 0]) & below(shape, 1, inner)
        block = jnp.where(on, a_ref[0, i * BS : (i + 1) * BS, :].astype(jnp.float32), 0.0)
        block = block.astype(jnp.bfloat16)
        first_ref[i * HALF : (i + 1) * HALF, :] = block[:HALF]
        second_ref[i * HALF : (i + 1) * HALF, :] = block[HALF:]


def mask_b_kernel(at_ref, mask_ref, inner_ref, cols_ref, b_ref, out_ref):
    blocks_k, blocks_n = mask_ref.shape[1], mask_ref.shape[2]
    for k in range(blocks_k):
        inner = inner_ref[0, at_ref[0] * blocks_k + k]
        for n in range(blocks_n):
            shape = (BS, BS)
            on = below(shape, 0, inner * mask_ref[0, k, n]) & below(shape, 1, cols_ref[n])
            place = (slice(k * BS, (k + 1) * BS), slice(n * BS, (n + 1) * BS))
            block = jnp.where(on, b_ref[(0,) + place].astype(jnp.float32), 0.0)
            out_ref[place] = block.astype(jnp.bfloat16)


def sum_kernel(first, count, blocks, place_ref, b_ref, *refs):
    a_refs, out_ref = refs[:count], refs[count]
    for step in range(count):
        k = lax.rem(place_ref[0] + place_ref[1] * (first + step) + 2 * blocks, blocks)
        term = jnp.dot(a_refs[step][...], b_ref[k], preferred_element_type=jnp.float32)
        if step == 0:
            out_ref[...] = term
        else:
            out_ref[...] += term


def last_kernel(last, blocks, place_ref, b_ref, a0_ref, a1_ref, p0_ref, p1_ref, q0_ref, q1_ref, out_ref):
    k = lax.rem(place_ref[0] + place_ref[1] * last + 2 * blocks, blocks)
    b = b_ref[k]
    for h, (a, p, q) in enumerate(((a0_ref, p0_ref, q0_ref), (a1_ref, p1_ref, q1_ref))):
        total = p[...] + q[...] + jnp.dot(a[...], b, preferred_element_type=jnp.float32)
        for owner in range(out_ref.shape[0]):
            out_ref[owner, h * HALF : (h + 1) * HALF, :] = total[owner * HALF : (owner + 1) * HALF]


def owners_kernel(in_ref, out_ref):
    out_ref[...] = jnp.sum(in_ref[...], axis=0)


def on_device(rows, cols, a_panel, b_panel, mask_a, mask_b, row_sizes, inner_sizes, col_sizes):
    z = lax.axis_index("col")
    row = lax.axis_index("row")
    way = 2 * lax.rem(row, 2) - 1
    swap = [(r, r ^ 1) for r in range(rows)]
    ring = [
        (r * cols + c, r * cols + (c + (1 if r % 2 == 0 else -1)) % cols)
        for r in range(rows)
        for c in range(cols)
    ]
    half = a_panel.shape[1] // 2
    width = b_panel.shape[2]
    stream = jax.ShapeDtypeStruct((half, BS), jnp.bfloat16)
    own = pl.pallas_call(
        mask_a_kernel,
        out_shape=(stream, stream),
        in_specs=[SMEM, SMEM, SMEM, SMEM, VMEM],
        out_specs=(VMEM, VMEM),
        compiler_params=PARAMS,
    )(z.reshape(1), mask_a, row_sizes, inner_sizes, a_panel)
    b_eff = pl.pallas_call(
        mask_b_kernel,
        out_shape=jax.ShapeDtypeStruct(b_panel.shape[1:], jnp.bfloat16),
        in_specs=[SMEM, SMEM, SMEM, SMEM, VMEM],
        out_specs=VMEM,
        compiler_params=PARAMS,
    )(row.reshape(1), mask_b, inner_sizes, col_sizes, b_panel)
    b_full = lax.all_gather(b_eff, "row", axis=0, tiled=True).reshape(cols, BS, width)

    other = [lax.ppermute(a, "row", swap) for a in own]
    held = [[a] for a in (*own, *other)]
    last = cols // 2
    for step in range(1, last + 1):
        for j in (2, 3, 0, 1):
            if step < last or j < 2:
                held[j].append(lax.ppermute(held[j][-1], ("row", "col"), ring))

    place = jnp.stack([z, way]).astype(jnp.int32)
    part = jax.ShapeDtypeStruct((half, width), jnp.float32)

    def total(first, shards):
        return pl.pallas_call(
            functools.partial(sum_kernel, first, len(shards), cols),
            out_shape=part,
            in_specs=[SMEM, VMEM] + [VMEM] * len(shards),
            out_specs=VMEM,
            compiler_params=PARAMS,
        )(place, b_full, *shards)

    theirs = [lax.ppermute(total(1, held[j][1:]), "row", swap) for j in (2, 3)]
    mine = [total(0, held[j][:last]) for j in (0, 1)]
    owners = a_panel.shape[1] // BS
    parts = pl.pallas_call(
        functools.partial(last_kernel, last, cols),
        out_shape=jax.ShapeDtypeStruct((owners, BS, width), jnp.float32),
        in_specs=[SMEM] + [VMEM] * 7,
        out_specs=VMEM,
        compiler_params=PARAMS,
    )(place, b_full, held[0][last], held[1][last], *mine, *theirs)
    parts = lax.all_to_all(parts, "layer", 0, 0)
    return pl.pallas_call(
        owners_kernel,
        out_shape=jax.ShapeDtypeStruct((BS, width), jnp.float32),
        in_specs=[VMEM],
        out_specs=VMEM,
        compiler_params=PARAMS,
    )(parts)


def solution(mesh):
    return jax.shard_map(
        functools.partial(on_device, mesh.shape["row"], mesh.shape["col"]),
        mesh=mesh,
        in_specs=(
            P("layer", "row", "col"),
            P("layer", "row", "col"),
            P("layer", "row", "col"),
            P("layer", "row", "col"),
            P("row"),
            P("layer", None),
            P("col"),
        ),
        out_specs=P(("row", "layer"), "col"),
        check_vma=False,
    )
```

time: 239 us -> 188 us (0.79)
  the two profiles are of different devices: /device:TPU:1 before, /device:TPU:8 now
where the time goes in v1:
time: 188 us; the launch traced here: 187 us
  starting transfers between devices  96.2 us (51%)
  blocking collectives  26.7 us (14%)
  waiting for transfers between devices  25 us (13%)
  between operations  14 us (7%)
  Pallas kernels  12.6 us (7%)
  local copies, waits for them, and re-layouts  12.5 us (7%)
    ppermute x30, starting transfers between devices, on_device(): held[j].append(lax.ppermute(held[j][-1], ('row', 'col'), ring))  87.2 us
    all_to_all x1, blocking collectives, on_device(): parts = lax.all_to_all(parts, 'layer', 0, 0)  26.7 us
    ppermute x30, waiting for transfers between devices, on_device(): held[j].append(lax.ppermute(held[j][-1], ('row', 'col'), ring))  25 us
    unnamed x43, local copies, waits for them, and re-layouts  12.5 us
    pallas_call x4, Pallas kernels, total(): pl.pallas_call(functools.partial(sum_kernel, first, len(shards), cols), o...  8.47 us
    ppermute x2, starting transfers between devices, on_device(): theirs = [lax.ppermute(total(1, held[j][1:]), 'row', swap) for j in (2, 3)]  4.72 us
    ppermute x2, starting transfers between devices, on_device(): other = [lax.ppermute(a, 'row', swap) for a in own]  4.33 us
  transfers between devices with their start and end apart: 35, of which 10 were waited for; matrix products, arithmetic and copies ran while one was open for 0% of the time, Pallas kernels for 5%

profile of v1, /device:TPU:8, one launch (start us, length us, event | category | flops | bytes accessed | tf_op | source)
XLA Modules:
  0.0 187.1 jit_solution(12651918765600572530)
XLA Ops:
  6.5 1.0 copy-done.3
  8.2 0.7 copy-done.18
  8.9 0.7 copy-done.19
  9.6 1.5 shard_map.73
  11.1 0.7 copy.8.mask_ref
  11.8 1.0 copy-done.2
  14.2 0.7 shard_map.74
  14.9 1.9 %collective-permute-start.25 = (bf16[512,256]{1,0:T(8,128)(2,1)S(1)}, bf16[512,256]{1,0:T(8,128)(2,1)S(1)}, u32[]{:S(2)}, u32[]{:S(2)}) collective-permute-start(bf16[512,256]{1,0:T(8,128)(2,1)S(1)} %get-tuple-element.8.refs_0_), channel_id=1, source_target_pairs={{0,64},{64,0},{128,192},{192,128},{256,320},{320,256},{384,448},{4... | collective-permute-start | bytes 786440 | tf_op jit(solution)/shard_map/ppermute | solution.py:97
  16.8 2.4 %collective-permute-start.16 = (bf16[512,256]{1,0:T(8,128)(2,1)S(1)}, bf16[512,256]{1,0:T(8,128)(2,1)S(1)}, u32[]{:S(2)}, u32[]{:S(2)}) collective-permute-start(bf16[512,256]{1,0:T(8,128)(2,1)S(1)} %get-tuple-element.7.refs_0_), channel_id=1, source_target_pairs={{0,64},{64,0},{128,192},{192,128},{256,320},{320,256},{384,448},{4... | collective-permute-start | bytes 786440 | tf_op jit(solution)/shard_map/ppermute | solution.py:97
  19.3 3.8 %collective-permute-start.26 = (bf16[512,256]{1,0:T(8,128)(2,1)S(1)}, bf16[512,256]{1,0:T(8,128)(2,1)S(1)}, u32[]{:S(2)}, u32[]{:S(2)}) collective-permute-start(bf16[512,256]{1,0:T(8,128)(2,1)S(1)} %collective-permute-done.25), channel_id=1, source_target_pairs={{0,4},{4,8},{8,12},{12,16},{16,20},{20,24},{24,28},{28,32},{32,36}... | collective-permute-start | bytes 786440 | tf_op jit(solution)/shard_map/ppermute | solution.py:103
  23.1 3.8 %collective-permute-start.17 = (bf16[512,256]{1,0:T(8,128)(2,1)S(1)}, bf16[512,256]{1,0:T(8,128)(2,1)S(1)}, u32[]{:S(2)}, u32[]{:S(2)}) collective-permute-start(bf16[512,256]{1,0:T(8,128)(2,1)S(1)} %collective-permute-done.16), channel_id=1, source_target_pairs={{0,4},{4,8},{8,12},{12,16},{16,20},{20,24},{24,28},{28,32},{32,36}... | collective-permute-start | bytes 786440 | tf_op jit(solution)/shard_map/ppermute | solution.py:103
  26.9 8.1 %collective-permute-done.26.refs_0_ = bf16[512,256]{1,0:T(8,128)(2,1)S(1)} collective-permute-done((bf16[512,256]{1,0:T(8,128)(2,1)S(1)}, bf16[512,256]{1,0:T(8,128)(2,1)S(1)}, u32[]{:S(2)}, u32[]{:S(2)}) %collective-permute-start.26) | collective-permute-done | bytes 262176 | tf_op jit(solution)/shard_map/ppermute | solution.py:103
  35.0 1.9 %collective-permute-start.27 = (bf16[512,256]{1,0:T(8,128)(2,1)S(1)}, bf16[512,256]{1,0:T(8,128)(2,1)S(1)}, u32[]{:S(2)}, u32[]{:S(2)}) collective-permute-start(bf16[512,256]{1,0:T(8,128)(2,1)S(1)} %collective-permute-done.26.refs_0_), channel_id=1, source_target_pairs={{0,4},{4,8},{8,12},{12,16},{16,20},{20,24},{24,28},{28,32},{32,36}... | collective-permute-start | bytes 786440 | tf_op jit(solution)/shard_map/ppermute | solution.py:103
  36.9 0.9 collective-permute-done.17.refs_0_
  37.8 1.9 %collective-permute-start.18 = (bf16[512,256]{1,0:T(8,128)(2,1)S(1)}, bf16[512,256]{1,0:T(8,128)(2,1)S(1)}, u32[]{:S(2)}, u32[]{:S(2)}) collective-permute-start(bf16[512,256]{1,0:T(8,128)(2,1)S(1)} %collective-permute-done.17.refs_0_), channel_id=1, source_target_pairs={{0,4},{4,8},{8,12},{12,16},{16,20},{20,24},{24,28},{28,32},{32,36}... | collective-permute-start | bytes 786440 | tf_op jit(solution)/shard_map/ppermute | solution.py:103
  39.7 4.7 %collective-permute-done.27.refs_1_ = bf16[512,256]{1,0:T(8,128)(2,1)S(1)} collective-permute-done((bf16[512,256]{1,0:T(8,128)(2,1)S(1)}, bf16[512,256]{1,0:T(8,128)(2,1)S(1)}, u32[]{:S(2)}, u32[]{:S(2)}) %collective-permute-start.27) | collective-permute-done | bytes 262176 | tf_op jit(solution)/shard_map/ppermute | solution.py:103
  44.5 1.9 %collective-permute-start.28 = (bf16[512,256]{1,0:T(8,128)(2,1)S(1)}, bf16[512,256]{1,0:T(8,128)(2,1)S(1)}, u32[]{:S(2)}, u32[]{:S(2)}) collective-permute-start(bf16[512,256]{1,0:T(8,128)(2,1)S(1)} %collective-permute-done.27.refs_1_), channel_id=1, source_target_pairs={{0,4},{4,8},{8,12},{12,16},{16,20},{20,24},{24,28},{28,32},{32,36}... | collective-permute-start | bytes 786440 | tf_op jit(solution)/shard_map/ppermute | solution.py:103
  46.4 0.9 collective-permute-done.18.refs_1_
  47.3 1.9 %collective-permute-start.19 = (bf16[512,256]{1,0:T(8,128)(2,1)S(1)}, bf16[512,256]{1,0:T(8,128)(2,1)S(1)}, u32[]{:S(2)}, u32[]{:S(2)}) collective-permute-start(bf16[512,256]{1,0:T(8,128)(2,1)S(1)} %collective-permute-done.18.refs_1_), channel_id=1, source_target_pairs={{0,4},{4,8},{8,12},{12,16},{16,20},{20,24},{24,28},{28,32},{32,36}... | collective-permute-start | bytes 786440 | tf_op jit(solution)/shard_map/ppermute | solution.py:103
  49.2 1.9 %collective-permute-start.8 = (bf16[512,256]{1,0:T(8,128)(2,1)S(1)}, bf16[512,256]{1,0:T(8,128)(2,1)S(1)}, u32[]{:S(2)}, u32[]{:S(2)}) collective-permute-start(bf16[512,256]{1,0:T(8,128)(2,1)S(1)} %get-tuple-element.8.refs_0_), channel_id=1, source_target_pairs={{0,4},{4,8},{8,12},{12,16},{16,20},{20,24},{24,28},{28,32},{32,36}... | collective-permute-start | bytes 786440 | tf_op jit(solution)/shard_map/ppermute | solution.py:103
  51.1 0.7 copy-done.6
  51.8 3.6 %collective-permute-start = (bf16[512,256]{1,0:T(8,128)(2,1)S(1)}, bf16[512,256]{1,0:T(8,128)(2,1)S(1)}, u32[]{:S(2)}, u32[]{:S(2)}) collective-permute-start(bf16[512,256]{1,0:T(8,128)(2,1)S(1)} %get-tuple-element.7.refs_0_), channel_id=1, source_target_pairs={{0,4},{4,8},{8,12},{12,16},{16,20},{20,24},{24,28},{28,32},{32,36}... | collective-permute-start | bytes 786440 | tf_op jit(solution)/shard_map/ppermute | solution.py:103
  55.5 0.7 copy-done.4
  56.2 3.8 %collective-permute-start.29 = (bf16[512,256]{1,0:T(8,128)(2,1)S(1)}, bf16[512,256]{1,0:T(8,128)(2,1)S(1)}, u32[]{:S(2)}, u32[]{:S(2)}) collective-permute-start(bf16[512,256]{1,0:T(8,128)(2,1)S(1)} %collective-permute-done.28.refs_2_), channel_id=1, source_target_pairs={{0,4},{4,8},{8,12},{12,16},{16,20},{20,24},{24,28},{28,32},{32,36}... | collective-permute-start | bytes 786440 | tf_op jit(solution)/shard_map/ppermute | solution.py:103
  60.0 3.3 %collective-permute-start.20 = (bf16[512,256]{1,0:T(8,128)(2,1)S(1)}, bf16[512,256]{1,0:T(8,128)(2,1)S(1)}, u32[]{:S(2)}, u32[]{:S(2)}) collective-permute-start(bf16[512,256]{1,0:T(8,128)(2,1)S(1)} %collective-permute-done.19.refs_2_), channel_id=1, source_target_pairs={{0,4},{4,8},{8,12},{12,16},{16,20},{20,24},{24,28},{28,32},{32,36}... | collective-permute-start | bytes 786440 | tf_op jit(solution)/shard_map/ppermute | solution.py:103
  63.3 3.8 %collective-permute-start.9 = (bf16[512,256]{1,0:T(8,128)(2,1)S(1)}, bf16[512,256]{1,0:T(8,128)(2,1)S(1)}, u32[]{:S(2)}, u32[]{:S(2)}) collective-permute-start(bf16[512,256]{1,0:T(8,128)(2,1)S(1)} %collective-permute-done.8.refs_1_), channel_id=1, source_target_pairs={{0,4},{4,8},{8,12},{12,16},{16,20},{20,24},{24,28},{28,32},{32,36}... | collective-permute-start | bytes 786440 | tf_op jit(solution)/shard_map/ppermute | solution.py:103
  67.1 0.7 copy-done.10
  67.8 5.6 %collective-permute-start.1 = (bf16[512,256]{1,0:T(8,128)(2,1)S(1)}, bf16[512,256]{1,0:T(8,128)(2,1)S(1)}, u32[]{:S(2)}, u32[]{:S(2)}) collective-permute-start(bf16[512,256]{1,0:T(8,128)(2,1)S(1)} %collective-permute-done.refs_1_), channel_id=1, source_target_pairs={{0,4},{4,8},{8,12},{12,16},{16,20},{20,24},{24,28},{28,32},{32,36}... | collective-permute-start | bytes 786440 | tf_op jit(solution)/shard_map/ppermute | solution.py:103
  73.4 0.7 copy-done.8
  74.1 2.9 %collective-permute-start.30 = (bf16[512,256]{1,0:T(8,128)(2,1)S(1)}, bf16[512,256]{1,0:T(8,128)(2,1)S(1)}, u32[]{:S(2)}, u32[]{:S(2)}) collective-permute-start(bf16[512,256]{1,0:T(8,128)(2,1)S(1)} %collective-permute-done.29.refs_3_), channel_id=1, source_target_pairs={{0,4},{4,8},{8,12},{12,16},{16,20},{20,24},{24,28},{28,32},{32,36}... | collective-permute-start | bytes 786440 | tf_op jit(solution)/shard_map/ppermute | solution.py:103
  77.1 1.9 %collective-permute-start.21 = (bf16[512,256]{1,0:T(8,128)(2,1)S(1)}, bf16[512,256]{1,0:T(8,128)(2,1)S(1)}, u32[]{:S(2)}, u32[]{:S(2)}) collective-permute-start(bf16[512,256]{1,0:T(8,128)(2,1)S(1)} %collective-permute-done.20.refs_3_), channel_id=1, source_target_pairs={{0,4},{4,8},{8,12},{12,16},{16,20},{20,24},{24,28},{28,32},{32,36}... | collective-permute-start | bytes 786440 | tf_op jit(solution)/shard_map/ppermute | solution.py:103
  79.0 1.9 %collective-permute-start.10 = (bf16[512,256]{1,0:T(8,128)(2,1)S(1)}, bf16[512,256]{1,0:T(8,128)(2,1)}, u32[]{:S(2)}, u32[]{:S(2)}) collective-permute-start(bf16[512,256]{1,0:T(8,128)(2,1)S(1)} %collective-permute-done.9.refs_2_), channel_id=1, source_target_pairs={{0,4},{4,8},{8,12},{12,16},{16,20},{20,24},{24,28},{28,32},{32,36}... | collective-permute-start | bytes 786440 | tf_op jit(solution)/shard_map/ppermute | solution.py:103
  80.9 0.7 copy-done.14
  81.6 4.9 %collective-permute-start.2 = (bf16[512,256]{1,0:T(8,128)(2,1)S(1)}, bf16[512,256]{1,0:T(8,128)(2,1)}, u32[]{:S(2)}, u32[]{:S(2)}) collective-permute-start(bf16[512,256]{1,0:T(8,128)(2,1)S(1)} %collective-permute-done.1.refs_2_), channel_id=1, source_target_pairs={{0,4},{4,8},{8,12},{12,16},{16,20},{20,24},{24,28},{28,32},{32,36}... | collective-permute-start | bytes 786440 | tf_op jit(solution)/shard_map/ppermute | solution.py:103
  86.6 0.7 copy-done.12
  87.3 2.9 %collective-permute-start.31 = (bf16[512,256]{1,0:T(8,128)(2,1)S(1)}, bf16[512,256]{1,0:T(8,128)(2,1)S(1)}, u32[]{:S(2)}, u32[]{:S(2)}) collective-permute-start(bf16[512,256]{1,0:T(8,128)(2,1)S(1)} %collective-permute-done.30.refs_4_), channel_id=1, source_target_pairs={{0,4},{4,8},{8,12},{12,16},{16,20},{20,24},{24,28},{28,32},{32,36}... | collective-permute-start | bytes 786440 | tf_op jit(solution)/shard_map/ppermute | solution.py:103
  90.2 1.9 %collective-permute-start.22 = (bf16[512,256]{1,0:T(8,128)(2,1)S(1)}, bf16[512,256]{1,0:T(8,128)(2,1)S(1)}, u32[]{:S(2)}, u32[]{:S(2)}) collective-permute-start(bf16[512,256]{1,0:T(8,128)(2,1)S(1)} %collective-permute-done.21.refs_4_), channel_id=1, source_target_pairs={{0,4},{4,8},{8,12},{12,16},{16,20},{20,24},{24,28},{28,32},{32,36}... | collective-permute-start | bytes 786440 | tf_op jit(solution)/shard_map/ppermute | solution.py:103
  92.2 1.9 %collective-permute-start.11 = (bf16[512,256]{1,0:T(8,128)(2,1)}, bf16[512,256]{1,0:T(8,128)(2,1)}, u32[]{:S(2)}, u32[]{:S(2)}) collective-permute-start(bf16[512,256]{1,0:T(8,128)(2,1)} %collective-permute-done.10.refs_3_), channel_id=1, source_target_pairs={{0,4},{4,8},{8,12},{12,16},{16,20},{20,24},{24,28},{28,32},{32,36}... | collective-permute-start | bytes 786440 | tf_op jit(solution)/shard_map/ppermute | solution.py:103
  94.1 3.9 %collective-permute-start.3 = (bf16[512,256]{1,0:T(8,128)(2,1)}, bf16[512,256]{1,0:T(8,128)(2,1)}, u32[]{:S(2)}, u32[]{:S(2)}) collective-permute-start(bf16[512,256]{1,0:T(8,128)(2,1)} %collective-permute-done.2.refs_3_), channel_id=1, source_target_pairs={{0,4},{4,8},{8,12},{12,16},{16,20},{20,24},{24,28},{28,32},{32,36}... | collective-permute-start | bytes 786440 | tf_op jit(solution)/shard_map/ppermute | solution.py:103
  98.0 2.8 %collective-permute-start.32 = (bf16[512,256]{1,0:T(8,128)(2,1)S(1)}, bf16[512,256]{1,0:T(8,128)(2,1)}, u32[]{:S(2)}, u32[]{:S(2)}) collective-permute-start(bf16[512,256]{1,0:T(8,128)(2,1)S(1)} %collective-permute-done.31.refs_5_), channel_id=1, source_target_pairs={{0,4},{4,8},{8,12},{12,16},{16,20},{20,24},{24,28},{28,32},{32,36}... | collective-permute-start | bytes 786440 | tf_op jit(solution)/shard_map/ppermute | solution.py:103
  100.9 1.9 %collective-permute-start.23 = (bf16[512,256]{1,0:T(8,128)(2,1)S(1)}, bf16[512,256]{1,0:T(8,128)(2,1)S(1)}, u32[]{:S(2)}, u32[]{:S(2)}) collective-permute-start(bf16[512,256]{1,0:T(8,128)(2,1)S(1)} %collective-permute-done.22.refs_5_), channel_id=1, source_target_pairs={{0,4},{4,8},{8,12},{12,16},{16,20},{20,24},{24,28},{28,32},{32,36}... | collective-permute-start | bytes 786440 | tf_op jit(solution)/shard_map/ppermute | solution.py:103
  102.9 1.9 %collective-permute-start.12 = (bf16[512,256]{1,0:T(8,128)(2,1)}, bf16[512,256]{1,0:T(8,128)(2,1)}, u32[]{:S(2)}, u32[]{:S(2)}) collective-permute-start(bf16[512,256]{1,0:T(8,128)(2,1)} %collective-permute-done.11.refs_4_), channel_id=1, source_target_pairs={{0,4},{4,8},{8,12},{12,16},{16,20},{20,24},{24,28},{28,32},{32,36}... | collective-permute-start | bytes 786440 | tf_op jit(solution)/shard_map/ppermute | solution.py:103
  105.4 3.0 %collective-permute-start.4 = (bf16[512,256]{1,0:T(8,128)(2,1)}, bf16[512,256]{1,0:T(8,128)(2,1)}, u32[]{:S(2)}, u32[]{:S(2)}) collective-permute-start(bf16[512,256]{1,0:T(8,128)(2,1)} %collective-permute-done.3.refs_4_), channel_id=1, source_target_pairs={{0,4},{4,8},{8,12},{12,16},{16,20},{20,24},{24,28},{28,32},{32,36}... | collective-permute-start | bytes 786440 | tf_op jit(solution)/shard_map/ppermute | solution.py:103
  108.5 2.2 %copy-done = bf16[4096,512]{1,0:T(8,128)(2,1)S(1)} copy-done((bf16[4096,512]{1,0:T(8,128)(2,1)S(1)}, bf16[4096,512]{1,0:T(8,128)(2,1)}, u32[]{:S(2)}) %copy-start) | copy-done | bytes 4194328
  110.6 2.1 %shard_map.78 = f32[512,512]{1,0:T(8,128)S(1)} custom-call(s32[2]{0:T(128)S(1)} %pad_add_fusion.place_ref, bf16[16,256,512]{2,1,0:T(8,128)(2,1)S(1)} %bitcast.4, bf16[512,256]{1,0:T(8,128)(2,1)S(1)} %collective-permute-done.26.refs_0_, bf16[512,256]{1,0:T(8,128)(2,1)S(1)} %collective-permute-done.27.refs_1_, ...), custom_call_target="tpu_custom_call" | custom-call | tf_op jit(solution)/shard_map/pallas_call | solution.py:109
  112.8 2.2 %collective-permute-start.33 = (f32[512,512]{1,0:T(8,128)S(1)}, f32[512,512]{1,0:T(8,128)S(1)}, u32[]{:S(2)}, u32[]{:S(2)}) collective-permute-start(f32[512,512]{1,0:T(8,128)S(1)} %shard_map.78), channel_id=1, source_target_pairs={{0,64},{64,0},{128,192},{192,128},{256,320},{320,256},{384,448},{4... | collective-permute-start | bytes 3145736 | tf_op jit(solution)/shard_map/ppermute | solution.py:117
  115.0 1.7 shard_map.77
  116.7 2.5 %collective-permute-start.24 = (f32[512,512]{1,0:T(8,128)S(1)}, f32[512,512]{1,0:T(8,128)S(1)}, u32[]{:S(2)}, u32[]{:S(2)}) collective-permute-start(f32[512,512]{1,0:T(8,128)S(1)} %shard_map.77), channel_id=1, source_target_pairs={{0,64},{64,0},{128,192},{192,128},{256,320},{320,256},{384,448},{4... | collective-permute-start | bytes 3145736 | tf_op jit(solution)/shard_map/ppermute | solution.py:117
  119.2 3.8 %collective-permute-start.13 = (bf16[512,256]{1,0:T(8,128)(2,1)}, bf16[512,256]{1,0:T(8,128)(2,1)S(1)}, u32[]{:S(2)}, u32[]{:S(2)}) collective-permute-start(bf16[512,256]{1,0:T(8,128)(2,1)} %collective-permute-done.12.refs_5_), channel_id=1, source_target_pairs={{0,4},{4,8},{8,12},{12,16},{16,20},{20,24},{24,28},{28,32},{32,36}... | collective-permute-start | bytes 786440 | tf_op jit(solution)/shard_map/ppermute | solution.py:103
  123.1 3.3 %collective-permute-start.5 = (bf16[512,256]{1,0:T(8,128)(2,1)}, bf16[512,256]{1,0:T(8,128)(2,1)S(1)}, u32[]{:S(2)}, u32[]{:S(2)}) collective-permute-start(bf16[512,256]{1,0:T(8,128)(2,1)} %collective-permute-done.4.refs_5_), channel_id=1, source_target_pairs={{0,4},{4,8},{8,12},{12,16},{16,20},{20,24},{24,28},{28,32},{32,36}... | collective-permute-start | bytes 786440 | tf_op jit(solution)/shard_map/ppermute | solution.py:103
  126.3 2.6 %collective-permute-done.13.refs_6_ = bf16[512,256]{1,0:T(8,128)(2,1)S(1)} collective-permute-done((bf16[512,256]{1,0:T(8,128)(2,1)}, bf16[512,256]{1,0:T(8,128)(2,1)S(1)}, u32[]{:S(2)}, u32[]{:S(2)}) %collective-permute-start.13) | collective-permute-done | bytes 262176 | tf_op jit(solution)/shard_map/ppermute | solution.py:103
  128.9 2.6 %collective-permute-start.14 = (bf16[512,256]{1,0:T(8,128)(2,1)S(1)}, bf16[512,256]{1,0:T(8,128)(2,1)S(1)}, u32[]{:S(2)}, u32[]{:S(2)}) collective-permute-start(bf16[512,256]{1,0:T(8,128)(2,1)S(1)} %collective-permute-done.13.refs_6_), channel_id=1, source_target_pairs={{0,4},{4,8},{8,12},{12,16},{16,20},{20,24},{24,28},{28,32},{32,36}... | collective-permute-start | bytes 786440 | tf_op jit(solution)/shard_map/ppermute | solution.py:103
  131.5 1.2 collective-permute-done.5.refs_6_
  132.7 3.0 %collective-permute-start.6 = (bf16[512,256]{1,0:T(8,128)(2,1)S(1)}, bf16[512,256]{1,0:T(8,128)(2,1)S(1)}, u32[]{:S(2)}, u32[]{:S(2)}) collective-permute-start(bf16[512,256]{1,0:T(8,128)(2,1)S(1)} %collective-permute-done.5.refs_6_), channel_id=1, source_target_pairs={{0,4},{4,8},{8,12},{12,16},{16,20},{20,24},{24,28},{28,32},{32,36}... | collective-permute-start | bytes 786440 | tf_op jit(solution)/shard_map/ppermute | solution.py:103
  135.8 2.6 %collective-permute-done.14.refs_7_ = bf16[512,256]{1,0:T(8,128)(2,1)S(1)} collective-permute-done((bf16[512,256]{1,0:T(8,128)(2,1)S(1)}, bf16[512,256]{1,0:T(8,128)(2,1)S(1)}, u32[]{:S(2)}, u32[]{:S(2)}) %collective-permute-start.14) | collective-permute-done | bytes 262176 | tf_op jit(solution)/shard_map/ppermute | solution.py:103
  138.4 1.9 %collective-permute-start.15 = (bf16[512,256]{1,0:T(8,128)(2,1)S(1)}, bf16[512,256]{1,0:T(8,128)(2,1)S(1)}, u32[]{:S(2)}, u32[]{:S(2)}) collective-permute-start(bf16[512,256]{1,0:T(8,128)(2,1)S(1)} %collective-permute-done.14.refs_7_), channel_id=1, source_target_pairs={{0,4},{4,8},{8,12},{12,16},{16,20},{20,24},{24,28},{28,32},{32,36}... | collective-permute-start | bytes 786440 | tf_op jit(solution)/shard_map/ppermute | solution.py:103
  140.3 1.9 %collective-permute-done.6.refs_7_ = bf16[512,256]{1,0:T(8,128)(2,1)S(1)} collective-permute-done((bf16[512,256]{1,0:T(8,128)(2,1)S(1)}, bf16[512,256]{1,0:T(8,128)(2,1)S(1)}, u32[]{:S(2)}, u32[]{:S(2)}) %collective-permute-start.6) | collective-permute-done | bytes 262176 | tf_op jit(solution)/shard_map/ppermute | solution.py:103
  142.2 3.2 %collective-permute-start.7 = (bf16[512,256]{1,0:T(8,128)(2,1)S(1)}, bf16[512,256]{1,0:T(8,128)(2,1)S(1)}, u32[]{:S(2)}, u32[]{:S(2)}) collective-permute-start(bf16[512,256]{1,0:T(8,128)(2,1)S(1)} %collective-permute-done.6.refs_7_), channel_id=1, source_target_pairs={{0,4},{4,8},{8,12},{12,16},{16,20},{20,24},{24,28},{28,32},{32,36}... | collective-permute-start | bytes 786440 | tf_op jit(solution)/shard_map/ppermute | solution.py:103
  145.5 2.4 %shard_map.76.p1_ref = f32[512,512]{1,0:T(8,128)S(1)} custom-call(s32[2]{0:T(128)S(1)} %pad_add_fusion.place_ref, bf16[16,256,512]{2,1,0:T(8,128)(2,1)S(1)} %bitcast.6, bf16[512,256]{1,0:T(8,128)(2,1)S(1)} %copy-done.7, bf16[512,256]{1,0:T(8,128)(2,1)S(1)} %copy-done.11, bf16[512,256]{1,0:T(8,128)(2,1)S(1)} %copy-done.15, ...), custom_call_target="tpu_custom_call" | custom-call | tf_op jit(solution)/shard_map/pallas_call | solution.py:109
  147.9 2.4 %shard_map.75.p0_ref = f32[512,512]{1,0:T(8,128)S(1)} custom-call(s32[2]{0:T(128)S(1)} %pad_add_fusion.place_ref, bf16[16,256,512]{2,1,0:T(8,128)(2,1)S(1)} %bitcast.7, bf16[512,256]{1,0:T(8,128)(2,1)S(1)} %copy-done.5, bf16[512,256]{1,0:T(8,128)(2,1)S(1)} %copy-done.9, bf16[512,256]{1,0:T(8,128)(2,1)S(1)} %copy-done.13, ...), custom_call_target="tpu_custom_call" | custom-call | tf_op jit(solution)/shard_map/pallas_call | solution.py:109
  150.3 1.4 collective-permute-done.7.a0_ref
  151.7 1.0 shard_map.79
  152.7 26.7 %all_to_all.5.in_ref = f32[4,256,512]{2,1,0:T(8,128)S(1)} all-to-all(f32[4,256,512]{2,1,0:T(8,128)S(1)} %shard_map.79), channel_id=1, replica_groups=mesh['row'=8,'col'=16,'layer'=4] {'layer'}, dimensions={0} | all-to-all | bytes 4194304 | tf_op jit(solution)/shard_map/all_to_all | solution.py:127
  179.3 0.9 shard_map.80
  (60 shorter events, 2.8 us)
Async XLA Ops:
  6.5 101.9 %all-gather.2.cloned.1.call-start = ((), (), s32[]{:S(2)}) async-start(), calls=%async_computation.1 | async-start | bytes 4718592 | tf_op jit(solution)/shard_map/all_gather | solution.py:95
  6.5 1.0 copy-start.3
  7.6 0.7 copy-start.16
  8.2 0.7 copy-start.18
  8.9 0.7 copy-start.19
  11.8 1.0 copy-start.2
  12.9 0.7 copy-start.17
  13.5 0.7 copy-start.20
  14.9 4.3 %collective-permute-start.25 = (bf16[512,256]{1,0:T(8,128)(2,1)S(1)}, bf16[512,256]{1,0:T(8,128)(2,1)S(1)}, u32[]{:S(2)}, u32[]{:S(2)}) collective-permute-start(bf16[512,256]{1,0:T(8,128)(2,1)S(1)} %get-tuple-element.8.refs_0_), channel_id=1, source_target_pairs={{0,64},{64,0},{128,192},{192,128},{256,320},{320,256},{384,448},{4... | collective-permute-start | bytes 786440 | tf_op jit(solution)/shard_map/ppermute | solution.py:97
  16.8 6.3 %collective-permute-start.16 = (bf16[512,256]{1,0:T(8,128)(2,1)S(1)}, bf16[512,256]{1,0:T(8,128)(2,1)S(1)}, u32[]{:S(2)}, u32[]{:S(2)}) collective-permute-start(bf16[512,256]{1,0:T(8,128)(2,1)S(1)} %get-tuple-element.7.refs_0_), channel_id=1, source_target_pairs={{0,64},{64,0},{128,192},{192,128},{256,320},{320,256},{384,448},{4... | collective-permute-start | bytes 786440 | tf_op jit(solution)/shard_map/ppermute | solution.py:97
  19.3 15.7 %collective-permute-start.26 = (bf16[512,256]{1,0:T(8,128)(2,1)S(1)}, bf16[512,256]{1,0:T(8,128)(2,1)S(1)}, u32[]{:S(2)}, u32[]{:S(2)}) collective-permute-start(bf16[512,256]{1,0:T(8,128)(2,1)S(1)} %collective-permute-done.25), channel_id=1, source_target_pairs={{0,4},{4,8},{8,12},{12,16},{16,20},{20,24},{24,28},{28,32},{32,36}... | collective-permute-start | bytes 786440 | tf_op jit(solution)/shard_map/ppermute | solution.py:103
  23.1 14.7 %collective-permute-start.17 = (bf16[512,256]{1,0:T(8,128)(2,1)S(1)}, bf16[512,256]{1,0:T(8,128)(2,1)S(1)}, u32[]{:S(2)}, u32[]{:S(2)}) collective-permute-start(bf16[512,256]{1,0:T(8,128)(2,1)S(1)} %collective-permute-done.16), channel_id=1, source_target_pairs={{0,4},{4,8},{8,12},{12,16},{16,20},{20,24},{24,28},{28,32},{32,36}... | collective-permute-start | bytes 786440 | tf_op jit(solution)/shard_map/ppermute | solution.py:103
  35.0 9.5 %collective-permute-start.27 = (bf16[512,256]{1,0:T(8,128)(2,1)S(1)}, bf16[512,256]{1,0:T(8,128)(2,1)S(1)}, u32[]{:S(2)}, u32[]{:S(2)}) collective-permute-start(bf16[512,256]{1,0:T(8,128)(2,1)S(1)} %collective-permute-done.26.refs_0_), channel_id=1, source_target_pairs={{0,4},{4,8},{8,12},{12,16},{16,20},{20,24},{24,28},{28,32},{32,36}... | collective-permute-start | bytes 786440 | tf_op jit(solution)/shard_map/ppermute | solution.py:103
  37.8 9.5 %collective-permute-start.18 = (bf16[512,256]{1,0:T(8,128)(2,1)S(1)}, bf16[512,256]{1,0:T(8,128)(2,1)S(1)}, u32[]{:S(2)}, u32[]{:S(2)}) collective-permute-start(bf16[512,256]{1,0:T(8,128)(2,1)S(1)} %collective-permute-done.17.refs_0_), channel_id=1, source_target_pairs={{0,4},{4,8},{8,12},{12,16},{16,20},{20,24},{24,28},{28,32},{32,36}... | collective-permute-start | bytes 786440 | tf_op jit(solution)/shard_map/ppermute | solution.py:103
  44.5 11.7 %collective-permute-start.28 = (bf16[512,256]{1,0:T(8,128)(2,1)S(1)}, bf16[512,256]{1,0:T(8,128)(2,1)S(1)}, u32[]{:S(2)}, u32[]{:S(2)}) collective-permute-start(bf16[512,256]{1,0:T(8,128)(2,1)S(1)} %collective-permute-done.27.refs_1_), channel_id=1, source_target_pairs={{0,4},{4,8},{8,12},{12,16},{16,20},{20,24},{24,28},{28,32},{32,36}... | collective-permute-start | bytes 786440 | tf_op jit(solution)/shard_map/ppermute | solution.py:103
  47.3 12.7 %collective-permute-start.19 = (bf16[512,256]{1,0:T(8,128)(2,1)S(1)}, bf16[512,256]{1,0:T(8,128)(2,1)S(1)}, u32[]{:S(2)}, u32[]{:S(2)}) collective-permute-start(bf16[512,256]{1,0:T(8,128)(2,1)S(1)} %collective-permute-done.18.refs_1_), channel_id=1, source_target_pairs={{0,4},{4,8},{8,12},{12,16},{16,20},{20,24},{24,28},{28,32},{32,36}... | collective-permute-start | bytes 786440 | tf_op jit(solution)/shard_map/ppermute | solution.py:103
  49.2 14.1 %collective-permute-start.8 = (bf16[512,256]{1,0:T(8,128)(2,1)S(1)}, bf16[512,256]{1,0:T(8,128)(2,1)S(1)}, u32[]{:S(2)}, u32[]{:S(2)}) collective-permute-start(bf16[512,256]{1,0:T(8,128)(2,1)S(1)} %get-tuple-element.8.refs_0_), channel_id=1, source_target_pairs={{0,4},{4,8},{8,12},{12,16},{16,20},{20,24},{24,28},{28,32},{32,36}... | collective-permute-start | bytes 786440 | tf_op jit(solution)/shard_map/ppermute | solution.py:103
  51.1 0.7 copy-start.6
  51.8 16.0 %collective-permute-start = (bf16[512,256]{1,0:T(8,128)(2,1)S(1)}, bf16[512,256]{1,0:T(8,128)(2,1)S(1)}, u32[]{:S(2)}, u32[]{:S(2)}) collective-permute-start(bf16[512,256]{1,0:T(8,128)(2,1)S(1)} %get-tuple-element.7.refs_0_), channel_id=1, source_target_pairs={{0,4},{4,8},{8,12},{12,16},{16,20},{20,24},{24,28},{28,32},{32,36}... | collective-permute-start | bytes 786440 | tf_op jit(solution)/shard_map/ppermute | solution.py:103
  55.5 0.7 copy-start.4
  56.2 18.0 %collective-permute-start.29 = (bf16[512,256]{1,0:T(8,128)(2,1)S(1)}, bf16[512,256]{1,0:T(8,128)(2,1)S(1)}, u32[]{:S(2)}, u32[]{:S(2)}) collective-permute-start(bf16[512,256]{1,0:T(8,128)(2,1)S(1)} %collective-permute-done.28.refs_2_), channel_id=1, source_target_pairs={{0,4},{4,8},{8,12},{12,16},{16,20},{20,24},{24,28},{28,32},{32,36}... | collective-permute-start | bytes 786440 | tf_op jit(solution)/shard_map/ppermute | solution.py:103
  60.0 17.1 %collective-permute-start.20 = (bf16[512,256]{1,0:T(8,128)(2,1)S(1)}, bf16[512,256]{1,0:T(8,128)(2,1)S(1)}, u32[]{:S(2)}, u32[]{:S(2)}) collective-permute-start(bf16[512,256]{1,0:T(8,128)(2,1)S(1)} %collective-permute-done.19.refs_2_), channel_id=1, source_target_pairs={{0,4},{4,8},{8,12},{12,16},{16,20},{20,24},{24,28},{28,32},{32,36}... | collective-permute-start | bytes 786440 | tf_op jit(solution)/shard_map/ppermute | solution.py:103
  63.3 15.7 %collective-permute-start.9 = (bf16[512,256]{1,0:T(8,128)(2,1)S(1)}, bf16[512,256]{1,0:T(8,128)(2,1)S(1)}, u32[]{:S(2)}, u32[]{:S(2)}) collective-permute-start(bf16[512,256]{1,0:T(8,128)(2,1)S(1)} %collective-permute-done.8.refs_1_), channel_id=1, source_target_pairs={{0,4},{4,8},{8,12},{12,16},{16,20},{20,24},{24,28},{28,32},{32,36}... | collective-permute-start | bytes 786440 | tf_op jit(solution)/shard_map/ppermute | solution.py:103
  67.1 0.7 copy-start.10
  67.8 13.8 %collective-permute-start.1 = (bf16[512,256]{1,0:T(8,128)(2,1)S(1)}, bf16[512,256]{1,0:T(8,128)(2,1)S(1)}, u32[]{:S(2)}, u32[]{:S(2)}) collective-permute-start(bf16[512,256]{1,0:T(8,128)(2,1)S(1)} %collective-permute-done.refs_1_), channel_id=1, source_target_pairs={{0,4},{4,8},{8,12},{12,16},{16,20},{20,24},{24,28},{28,32},{32,36}... | collective-permute-start | bytes 786440 | tf_op jit(solution)/shard_map/ppermute | solution.py:103
  73.4 0.7 copy-start.8
  74.1 13.1 %collective-permute-start.30 = (bf16[512,256]{1,0:T(8,128)(2,1)S(1)}, bf16[512,256]{1,0:T(8,128)(2,1)S(1)}, u32[]{:S(2)}, u32[]{:S(2)}) collective-permute-start(bf16[512,256]{1,0:T(8,128)(2,1)S(1)} %collective-permute-done.29.refs_3_), channel_id=1, source_target_pairs={{0,4},{4,8},{8,12},{12,16},{16,20},{20,24},{24,28},{28,32},{32,36}... | collective-permute-start | bytes 786440 | tf_op jit(solution)/shard_map/ppermute | solution.py:103
  77.1 13.1 %collective-permute-start.21 = (bf16[512,256]{1,0:T(8,128)(2,1)S(1)}, bf16[512,256]{1,0:T(8,128)(2,1)S(1)}, u32[]{:S(2)}, u32[]{:S(2)}) collective-permute-start(bf16[512,256]{1,0:T(8,128)(2,1)S(1)} %collective-permute-done.20.refs_3_), channel_id=1, source_target_pairs={{0,4},{4,8},{8,12},{12,16},{16,20},{20,24},{24,28},{28,32},{32,36}... | collective-permute-start | bytes 786440 | tf_op jit(solution)/shard_map/ppermute | solution.py:103
  79.0 13.1 %collective-permute-start.10 = (bf16[512,256]{1,0:T(8,128)(2,1)S(1)}, bf16[512,256]{1,0:T(8,128)(2,1)}, u32[]{:S(2)}, u32[]{:S(2)}) collective-permute-start(bf16[512,256]{1,0:T(8,128)(2,1)S(1)} %collective-permute-done.9.refs_2_), channel_id=1, source_target_pairs={{0,4},{4,8},{8,12},{12,16},{16,20},{20,24},{24,28},{28,32},{32,36}... | collective-permute-start | bytes 786440 | tf_op jit(solution)/shard_map/ppermute | solution.py:103
  80.9 0.7 copy-start.14
  81.6 12.4 %collective-permute-start.2 = (bf16[512,256]{1,0:T(8,128)(2,1)S(1)}, bf16[512,256]{1,0:T(8,128)(2,1)}, u32[]{:S(2)}, u32[]{:S(2)}) collective-permute-start(bf16[512,256]{1,0:T(8,128)(2,1)S(1)} %collective-permute-done.1.refs_2_), channel_id=1, source_target_pairs={{0,4},{4,8},{8,12},{12,16},{16,20},{20,24},{24,28},{28,32},{32,36}... | collective-permute-start | bytes 786440 | tf_op jit(solution)/shard_map/ppermute | solution.py:103
  86.6 0.7 copy-start.12
  87.3 10.8 %collective-permute-start.31 = (bf16[512,256]{1,0:T(8,128)(2,1)S(1)}, bf16[512,256]{1,0:T(8,128)(2,1)S(1)}, u32[]{:S(2)}, u32[]{:S(2)}) collective-permute-start(bf16[512,256]{1,0:T(8,128)(2,1)S(1)} %collective-permute-done.30.refs_4_), channel_id=1, source_target_pairs={{0,4},{4,8},{8,12},{12,16},{16,20},{20,24},{24,28},{28,32},{32,36}... | collective-permute-start | bytes 786440 | tf_op jit(solution)/shard_map/ppermute | solution.py:103
  90.2 10.6 %collective-permute-start.22 = (bf16[512,256]{1,0:T(8,128)(2,1)S(1)}, bf16[512,256]{1,0:T(8,128)(2,1)S(1)}, u32[]{:S(2)}, u32[]{:S(2)}) collective-permute-start(bf16[512,256]{1,0:T(8,128)(2,1)S(1)} %collective-permute-done.21.refs_4_), channel_id=1, source_target_pairs={{0,4},{4,8},{8,12},{12,16},{16,20},{20,24},{24,28},{28,32},{32,36}... | collective-permute-start | bytes 786440 | tf_op jit(solution)/shard_map/ppermute | solution.py:103
  92.2 10.7 %collective-permute-start.11 = (bf16[512,256]{1,0:T(8,128)(2,1)}, bf16[512,256]{1,0:T(8,128)(2,1)}, u32[]{:S(2)}, u32[]{:S(2)}) collective-permute-start(bf16[512,256]{1,0:T(8,128)(2,1)} %collective-permute-done.10.refs_3_), channel_id=1, source_target_pairs={{0,4},{4,8},{8,12},{12,16},{16,20},{20,24},{24,28},{28,32},{32,36}... | collective-permute-start | bytes 786440 | tf_op jit(solution)/shard_map/ppermute | solution.py:103
  94.1 11.3 %collective-permute-start.3 = (bf16[512,256]{1,0:T(8,128)(2,1)}, bf16[512,256]{1,0:T(8,128)(2,1)}, u32[]{:S(2)}, u32[]{:S(2)}) collective-permute-start(bf16[512,256]{1,0:T(8,128)(2,1)} %collective-permute-done.2.refs_3_), channel_id=1, source_target_pairs={{0,4},{4,8},{8,12},{12,16},{16,20},{20,24},{24,28},{28,32},{32,36}... | collective-permute-start | bytes 786440 | tf_op jit(solution)/shard_map/ppermute | solution.py:103
  98.0 10.4 %collective-permute-start.32 = (bf16[512,256]{1,0:T(8,128)(2,1)S(1)}, bf16[512,256]{1,0:T(8,128)(2,1)}, u32[]{:S(2)}, u32[]{:S(2)}) collective-permute-start(bf16[512,256]{1,0:T(8,128)(2,1)S(1)} %collective-permute-done.31.refs_5_), channel_id=1, source_target_pairs={{0,4},{4,8},{8,12},{12,16},{16,20},{20,24},{24,28},{28,32},{32,36}... | collective-permute-start | bytes 786440 | tf_op jit(solution)/shard_map/ppermute | solution.py:103
  100.9 14.1 %collective-permute-start.23 = (bf16[512,256]{1,0:T(8,128)(2,1)S(1)}, bf16[512,256]{1,0:T(8,128)(2,1)S(1)}, u32[]{:S(2)}, u32[]{:S(2)}) collective-permute-start(bf16[512,256]{1,0:T(8,128)(2,1)S(1)} %collective-permute-done.22.refs_5_), channel_id=1, source_target_pairs={{0,4},{4,8},{8,12},{12,16},{16,20},{20,24},{24,28},{28,32},{32,36}... | collective-permute-start | bytes 786440 | tf_op jit(solution)/shard_map/ppermute | solution.py:103
  102.9 16.3 %collective-permute-start.12 = (bf16[512,256]{1,0:T(8,128)(2,1)}, bf16[512,256]{1,0:T(8,128)(2,1)}, u32[]{:S(2)}, u32[]{:S(2)}) collective-permute-start(bf16[512,256]{1,0:T(8,128)(2,1)} %collective-permute-done.11.refs_4_), channel_id=1, source_target_pairs={{0,4},{4,8},{8,12},{12,16},{16,20},{20,24},{24,28},{28,32},{32,36}... | collective-permute-start | bytes 786440 | tf_op jit(solution)/shard_map/ppermute | solution.py:103
  105.4 17.6 %collective-permute-start.4 = (bf16[512,256]{1,0:T(8,128)(2,1)}, bf16[512,256]{1,0:T(8,128)(2,1)}, u32[]{:S(2)}, u32[]{:S(2)}) collective-permute-start(bf16[512,256]{1,0:T(8,128)(2,1)} %collective-permute-done.3.refs_4_), channel_id=1, source_target_pairs={{0,4},{4,8},{8,12},{12,16},{16,20},{20,24},{24,28},{28,32},{32,36}... | collective-permute-start | bytes 786440 | tf_op jit(solution)/shard_map/ppermute | solution.py:103
  108.5 2.2 %copy-start = (bf16[4096,512]{1,0:T(8,128)(2,1)S(1)}, bf16[4096,512]{1,0:T(8,128)(2,1)}, u32[]{:S(2)}) copy-start(bf16[4096,512]{1,0:T(8,128)(2,1)} %all-gather.2.cloned.1.call-done) | copy-start | bytes 12582916
  112.7 32.7 %copy-start.1 = (bf16[4096,512]{1,0:T(8,128)(2,1)S(1)}, bf16[4096,512]{1,0:T(8,128)(2,1)}, u32[]{:S(2)}) copy-start(bf16[4096,512]{1,0:T(8,128)(2,1)} %all-gather.2.cloned.1.call-done) | copy-start | bytes 12582916
  112.7 32.7 %copy-start.7 = (bf16[512,256]{1,0:T(8,128)(2,1)S(1)}, bf16[512,256]{1,0:T(8,128)(2,1)}, u32[]{:S(2)}) copy-start(bf16[512,256]{1,0:T(8,128)(2,1)} %copy-done.6) | copy-start | bytes 786436
  112.7 32.7 %copy-start.11 = (bf16[512,256]{1,0:T(8,128)(2,1)S(1)}, bf16[512,256]{1,0:T(8,128)(2,1)}, u32[]{:S(2)}) copy-start(bf16[512,256]{1,0:T(8,128)(2,1)} %copy-done.10) | copy-start | bytes 786436
  112.8 32.7 %copy-start.15 = (bf16[512,256]{1,0:T(8,128)(2,1)S(1)}, bf16[512,256]{1,0:T(8,128)(2,1)}, u32[]{:S(2)}) copy-start(bf16[512,256]{1,0:T(8,128)(2,1)} %copy-done.14) | copy-start | bytes 786436
  112.8 38.9 %collective-permute-start.33 = (f32[512,512]{1,0:T(8,128)S(1)}, f32[512,512]{1,0:T(8,128)S(1)}, u32[]{:S(2)}, u32[]{:S(2)}) collective-permute-start(f32[512,512]{1,0:T(8,128)S(1)} %shard_map.78), channel_id=1, source_target_pairs={{0,64},{64,0},{128,192},{192,128},{256,320},{320,256},{384,448},{4... | collective-permute-start | bytes 3145736 | tf_op jit(solution)/shard_map/ppermute | solution.py:117
  116.6 31.3 %copy-start.5 = (bf16[512,256]{1,0:T(8,128)(2,1)S(1)}, bf16[512,256]{1,0:T(8,128)(2,1)}, u32[]{:S(2)}) copy-start(bf16[512,256]{1,0:T(8,128)(2,1)} %copy-done.4) | copy-start | bytes 786436
  116.6 31.3 %copy-start.9 = (bf16[512,256]{1,0:T(8,128)(2,1)S(1)}, bf16[512,256]{1,0:T(8,128)(2,1)}, u32[]{:S(2)}) copy-start(bf16[512,256]{1,0:T(8,128)(2,1)} %copy-done.8) | copy-start | bytes 786436
  116.6 31.3 %copy-start.13 = (bf16[512,256]{1,0:T(8,128)(2,1)S(1)}, bf16[512,256]{1,0:T(8,128)(2,1)}, u32[]{:S(2)}) copy-start(bf16[512,256]{1,0:T(8,128)(2,1)} %copy-done.12) | copy-start | bytes 786436
  116.7 35.0 %collective-permute-start.24 = (f32[512,512]{1,0:T(8,128)S(1)}, f32[512,512]{1,0:T(8,128)S(1)}, u32[]{:S(2)}, u32[]{:S(2)}) collective-permute-start(f32[512,512]{1,0:T(8,128)S(1)} %shard_map.77), channel_id=1, source_target_pairs={{0,64},{64,0},{128,192},{192,128},{256,320},{320,256},{384,448},{4... | collective-permute-start | bytes 3145736 | tf_op jit(solution)/shard_map/ppermute | solution.py:117
  119.2 9.7 %collective-permute-start.13 = (bf16[512,256]{1,0:T(8,128)(2,1)}, bf16[512,256]{1,0:T(8,128)(2,1)S(1)}, u32[]{:S(2)}, u32[]{:S(2)}) collective-permute-start(bf16[512,256]{1,0:T(8,128)(2,1)} %collective-permute-done.12.refs_5_), channel_id=1, source_target_pairs={{0,4},{4,8},{8,12},{12,16},{16,20},{20,24},{24,28},{28,32},{32,36}... | collective-permute-start | bytes 786440 | tf_op jit(solution)/shard_map/ppermute | solution.py:103
  123.1 9.7 %collective-permute-start.5 = (bf16[512,256]{1,0:T(8,128)(2,1)}, bf16[512,256]{1,0:T(8,128)(2,1)S(1)}, u32[]{:S(2)}, u32[]{:S(2)}) collective-permute-start(bf16[512,256]{1,0:T(8,128)(2,1)} %collective-permute-done.4.refs_5_), channel_id=1, source_target_pairs={{0,4},{4,8},{8,12},{12,16},{16,20},{20,24},{24,28},{28,32},{32,36}... | collective-permute-start | bytes 786440 | tf_op jit(solution)/shard_map/ppermute | solution.py:103
  128.9 9.5 %collective-permute-start.14 = (bf16[512,256]{1,0:T(8,128)(2,1)S(1)}, bf16[512,256]{1,0:T(8,128)(2,1)S(1)}, u32[]{:S(2)}, u32[]{:S(2)}) collective-permute-start(bf16[512,256]{1,0:T(8,128)(2,1)S(1)} %collective-permute-done.13.refs_6_), channel_id=1, source_target_pairs={{0,4},{4,8},{8,12},{12,16},{16,20},{20,24},{24,28},{28,32},{32,36}... | collective-permute-start | bytes 786440 | tf_op jit(solution)/shard_map/ppermute | solution.py:103
  132.7 9.5 %collective-permute-start.6 = (bf16[512,256]{1,0:T(8,128)(2,1)S(1)}, bf16[512,256]{1,0:T(8,128)(2,1)S(1)}, u32[]{:S(2)}, u32[]{:S(2)}) collective-permute-start(bf16[512,256]{1,0:T(8,128)(2,1)S(1)} %collective-permute-done.5.refs_6_), channel_id=1, source_target_pairs={{0,4},{4,8},{8,12},{12,16},{16,20},{20,24},{24,28},{28,32},{32,36}... | collective-permute-start | bytes 786440 | tf_op jit(solution)/shard_map/ppermute | solution.py:103
  138.4 11.9 %collective-permute-start.15 = (bf16[512,256]{1,0:T(8,128)(2,1)S(1)}, bf16[512,256]{1,0:T(8,128)(2,1)S(1)}, u32[]{:S(2)}, u32[]{:S(2)}) collective-permute-start(bf16[512,256]{1,0:T(8,128)(2,1)S(1)} %collective-permute-done.14.refs_7_), channel_id=1, source_target_pairs={{0,4},{4,8},{8,12},{12,16},{16,20},{20,24},{24,28},{28,32},{32,36}... | collective-permute-start | bytes 786440 | tf_op jit(solution)/shard_map/ppermute | solution.py:103
  142.2 9.5 %collective-permute-start.7 = (bf16[512,256]{1,0:T(8,128)(2,1)S(1)}, bf16[512,256]{1,0:T(8,128)(2,1)S(1)}, u32[]{:S(2)}, u32[]{:S(2)}) collective-permute-start(bf16[512,256]{1,0:T(8,128)(2,1)S(1)} %collective-permute-done.6.refs_7_), channel_id=1, source_target_pairs={{0,4},{4,8},{8,12},{12,16},{16,20},{20,24},{24,28},{28,32},{32,36}... | collective-permute-start | bytes 786440 | tf_op jit(solution)/shard_map/ppermute | solution.py:103
Sparse Core Ops, SparseCore 0:
  11.2 43.1 all-gather.1

commit v2 on v0

v2 whole, which is shorter than its diff:
```python
import functools

import jax
import jax.numpy as jnp
from jax import lax
from jax.experimental import pallas as pl
from jax.experimental.pallas import tpu as pltpu
from jax.sharding import Mesh, PartitionSpec as P

BS = 256
CORES = 2
SLOTS = 4
HBM = pl.BlockSpec(memory_space=pl.ANY)
VMEM = pl.BlockSpec(memory_space=pltpu.VMEM)
SMEM = pl.BlockSpec(memory_space=pltpu.SMEM)
PARAMS = pltpu.CompilerParams(vmem_limit_bytes=40 * 1024 * 1024)


def below(axis, size):
    return lax.broadcasted_iota(jnp.int32, (BS, BS), axis) < size


def masked(block, rows, columns):
    kept = jnp.where(below(0, rows) & below(1, columns), block.astype(jnp.float32), 0.0)
    return kept.astype(jnp.bfloat16)


def mask_kernel(at, mask_a, mask_b, row_sizes, inner_sizes, col_sizes, a_ref, b_ref, a_out, b_out):
    for k in range(mask_b.shape[1]):
        inner = inner_sizes[0, at[1] * mask_b.shape[1] + k]
        for n in range(mask_b.shape[2]):
            place = (slice(k * BS, (k + 1) * BS), slice(n * BS, (n + 1) * BS))
            b_out[place] = masked(b_ref[(0,) + place], inner * mask_b[0, k, n], col_sizes[n])
    inner = inner_sizes[0, at[0]]
    for i in range(mask_a.shape[1]):
        block = a_ref[0, i * BS : (i + 1) * BS, :]
        a_out[i] = masked(block, row_sizes[i] * mask_a[0, i, 0], inner)


def product_kernel(jobs, blocks, groups, adds, place, mine_ref, others_ref, *refs):
    sums = 1 + max(s for _, _, uses in jobs for s, _, _ in uses)
    count = 1 + max(i for _, _, uses in jobs for _, i, _ in uses)
    a_refs, starts = refs[:count], refs[count : count + adds]
    outs = refs[count + adds : count + adds + sums]
    slots, sems = refs[-2:]
    per_core = blocks // CORES

    def wanted(step):
        return lax.rem(place[0] + place[1] * step + blocks, blocks)

    def fetch(n):
        step, group, _ = jobs[n]
        k = wanted(step)
        index = group * per_core + (k // 4) * 2 + lax.rem(k, 2)
        here = lax.rem(k // 2, 2) == place[2]

        @pl.when(here)
        def _():
            pltpu.make_async_copy(mine_ref.at[index], slots.at[n % SLOTS], sems.at[n % SLOTS]).start()

        @pl.when(jnp.logical_not(here))
        def _():
            pltpu.make_async_copy(others_ref.at[index], slots.at[n % SLOTS], sems.at[n % SLOTS]).start()

    for n in range(min(SLOTS - 1, len(jobs))):
        fetch(n)
    for s in range(sums):
        mine = starts[s::sums]
        if mine:
            outs[s][...] = functools.reduce(lambda p, q: p + q, [r[...] for r in mine])
        else:
            outs[s][...] = jnp.zeros_like(outs[s])
    for n, (_, _, uses) in enumerate(jobs):
        if n + SLOTS - 1 < len(jobs):
            fetch(n + SLOTS - 1)
        slot = n % SLOTS
        pltpu.make_async_copy(mine_ref.at[0], slots.at[slot], sems.at[slot]).wait()
        for s, i, index in uses:
            outs[s][...] += jnp.dot(
                a_refs[i][index], slots[slot], preferred_element_type=jnp.float32
            )


def on_device(sizes, a_panel, b_panel, mask_a, mask_b, row_sizes, inner_sizes, col_sizes):
    cols, groups = sizes["col"], sizes["layer"]
    z, y, core = lax.axis_index("col"), lax.axis_index("y"), lax.axis_index("core")
    way = 2 * core - 1
    swap = [(0, 1), (1, 0)]
    ring = [
        (c * cols + i, c * cols + (i + (1, -1)[c]) % cols) for c in range(CORES) for i in range(cols)
    ]
    width = b_panel.shape[2]
    a_eff, b_eff = pl.pallas_call(
        mask_kernel,
        out_shape=(
            jax.ShapeDtypeStruct((groups, BS, BS), jnp.bfloat16),
            jax.ShapeDtypeStruct(b_panel.shape[1:], jnp.bfloat16),
        ),
        in_specs=[SMEM] * 6 + [VMEM] * 2,
        out_specs=(VMEM, VMEM),
        compiler_params=PARAMS,
    )(
        jnp.stack([z, y * CORES + core]),
        mask_a, mask_b, row_sizes, inner_sizes, col_sizes, a_panel, b_panel,
    )
    b_mine = lax.all_gather(b_eff, ("layer", "y"), axis=0, tiled=True).reshape(-1, BS, width)
    own = lax.all_to_all(a_eff, "layer", 0, 0)

    def after(value, earlier):
        return lax.optimization_barrier((value, earlier))[0]

    early = lax.ppermute(own[:2], "core", swap)
    late = lax.ppermute(own[2:], "core", swap)
    held = [[own[:3]], [jnp.concatenate([own[3:], early])], [late]]
    last = cols // 2
    sent = None
    b_others = None
    for step in range(1, last + 1):
        for j in range(3):
            value = held[j][-1]
            if step == last:
                if j == 2:
                    continue
                value = value[:1] if j == 1 else value
            if step > 1:
                value = after(value, sent)
            sent = value
            held[j].append(lax.ppermute(value, ("core", "col"), ring))
        if step == 6:
            b_others = lax.ppermute(after(b_mine, sent), "core", swap)

    def uses(step, which, first):
        spots = {
            "own": [(0, 0), (0, 1), (0, 2), (1, 0)],
            "other": [(1, 1), (1, 2), (2, 0), (2, 1)],
        }
        return [[(s, first + spots[w][g][0], spots[w][g][1]) for s, w in which] for g in range(groups)]

    place = jnp.stack([z, way, core]).astype(jnp.int32)
    part = jax.ShapeDtypeStruct((BS, width), jnp.float32)

    def products(steps, which, extra=()):
        arrays, jobs = [], []
        for step in steps:
            found = uses(step, which, len(arrays))
            if step == 0:
                found = [[u for u, (_, w) in zip(f, which) if w == "own"] for f in found]
            jobs += [(step, g, found[g]) for g in range(groups)]
            arrays += [h[step] for h in held if len(h) > step]
        sums = len(which)
        used = 1 + max(i for _, _, u in jobs for _, i, _ in u)
        return pl.pallas_call(
            functools.partial(product_kernel, jobs, cols, groups, len(extra)),
            out_shape=(part,) * sums,
            in_specs=[SMEM, HBM, HBM] + [VMEM] * (used + len(extra)),
            out_specs=(VMEM,) * sums,
            scratch_shapes=[
                pltpu.VMEM((SLOTS, BS, width), jnp.bfloat16),
                pltpu.SemaphoreType.DMA((SLOTS,)),
            ],
            compiler_params=PARAMS,
        )(place, b_mine, b_others, *arrays[:used], *extra)

    mine, others = products(range(0, 7), [(0, "own"), (1, "other")])
    (others,) = products([7], [(0, "other")], (others,))
    others = lax.ppermute(others, "core", swap)
    (mine,) = products([7, 8], [(0, "own")], (mine, others))
    return mine


def solution(mesh):
    rows, cols, layers = (mesh.shape[name] for name in ("row", "col", "layer"))
    devices = mesh.devices.reshape(rows // CORES, CORES, cols, layers)
    cores = Mesh(devices, ("y", "core", "col", "layer"))
    row = ("y", "core")
    return jax.shard_map(
        functools.partial(on_device, dict(cores.shape)),
        mesh=cores,
        in_specs=(
            P("layer", row, "col"),
            P("layer", row, "col"),
            P("layer", row, "col"),
            P("layer", row, "col"),
            P(row),
            P("layer", None),
            P("col"),
        ),
        out_specs=P((*row, "layer"), "col"),
        check_vma=False,
    )
```

time: 239 us -> 187 us (0.78)
  waiting for transfers between devices: 208 us -> 25.7 us
  starting transfers between devices: 0.12 us -> 95 us
  local copies, waits for them, and re-layouts: 2.08 us -> 23.2 us
  Pallas kernels: 0 us -> 15.8 us
  blocking collectives: 0 us -> 11.6 us
  matrix products: 10.4 us -> 0 us
  other arithmetic: 4.72 us -> 0.19 us
    all_gather x2 -> x1, waiting for transfers between devices: 166 us -> 0.01 us  [on_device(): lax.all_gather(b_eff, ('layer', 'y'), axis=0, tiled=True)]
    ppermute x0 -> x27, starting transfers between devices: none -> 95 us  [the longest x23 78 us: on_device(): held[j].append(lax.ppermute(value, ('core', 'col'), ring))]
    reduce_scatter x1 -> x0, waiting for transfers between devices: 41.8 us -> none  [on_device(): lax.psum_scatter(partial_sum, 'layer', scatter_dimension=0, tiled=True)]
    ppermute x0 -> x27, waiting for transfers between devices: none -> 25.6 us  [the longest x23 24.1 us: on_device(): held[j].append(lax.ppermute(value, ('core', 'col'), ring))]
    unnamed x12 -> x57, local copies, waits for them, and re-layouts: 0.1 us -> 23.1 us
    pallas_call x0 -> x4, Pallas kernels: none -> 15.8 us  [the longest x3 14.2 us: products(): pl.pallas_call(functools.partial(product_kernel, jobs, cols, groups, len(...]
    all_to_all x0 -> x1, blocking collectives: none -> 11.6 us  [on_device(): own = lax.all_to_all(a_eff, 'layer', 0, 0)]
    dot_general x1 -> x0, matrix products: 10.4 us -> none  [on_device(): jnp.dot(a_full, lax.all_gather(b_eff, 'row', axis=0, tiled=True), preferr...]
  transfers between devices with their start and end apart: 3 -> 28, of which waited for: 3 -> 8; matrix products, arithmetic and copies ran while one was open for 1% -> 0% of each run, Pallas kernels for 0% -> 5%
where the time goes in v2:
time: 187 us; the launch traced here: 185 us
  starting transfers between devices  95 us (51%)
  waiting for transfers between devices  25.7 us (14%)
  local copies, waits for them, and re-layouts  23.2 us (12%)
  Pallas kernels  15.8 us (8%)
  between operations  13.9 us (7%)
  blocking collectives  11.6 us (6%)
    ppermute x23, starting transfers between devices, on_device(): held[j].append(lax.ppermute(value, ('core', 'col'), ring))  78 us
    ppermute x23, waiting for transfers between devices, on_device(): held[j].append(lax.ppermute(value, ('core', 'col'), ring))  24.1 us
    unnamed x57, local copies, waits for them, and re-layouts  23.1 us
    pallas_call x3, Pallas kernels, products(): pl.pallas_call(functools.partial(product_kernel, jobs, cols, groups, len(...  14.2 us
    all_to_all x1, blocking collectives, on_device(): own = lax.all_to_all(a_eff, 'layer', 0, 0)  11.6 us
    ppermute x1, starting transfers between devices, on_device(): early = lax.ppermute(own[:2], 'core', swap)  7.69 us
    ppermute x1, starting transfers between devices, on_device(): b_others = lax.ppermute(after(b_mine, sent), 'core', swap)  4.13 us
  transfers between devices with their start and end apart: 28, of which 8 were waited for; matrix products, arithmetic and copies ran while one was open for 0% of the time, Pallas kernels for 5%

profile of v2, /device:TPU:1, one launch (start us, length us, event | category | flops | bytes accessed | tf_op | source)
XLA Modules:
  0.0 185.3 jit_solution(2264798323486750196)
XLA Ops:
  6.5 0.7 copy.8.mask_a
  7.4 1.0 copy-done
  8.4 1.0 copy-done.1
  9.4 0.7 copy-done.22
  10.1 0.7 copy-done.23
  10.8 0.7 copy-done.24
  12.1 1.5 shard_map.73
  13.7 11.6 %all_to_all.5 = bf16[4,256,256]{2,1,0:T(8,128)(2,1)S(1)} all-to-all(bf16[4,256,256]{2,1,0:T(8,128)(2,1)S(1)} %get-tuple-element.31), channel_id=1, replica_groups=mesh['y'=4,'core'=2,'col'=16,'layer'=4] {'layer'}, dimensions={0} | all-to-all | bytes 1048576 | tf_op jit(solution)/shard_map/all_to_all | solution.py:107
  25.3 7.7 %collective-permute-start.2 = (bf16[2,256,256]{2,1,0:T(8,128)(2,1)S(1)}, bf16[2,256,256]{2,1,0:T(8,128)(2,1)S(1)}, u32[]{:S(2)}, u32[]{:S(2)}) collective-permute-start(bf16[2,256,256]{2,1,0:T(8,128)(2,1)S(1)} %get-tuple-element.55), channel_id=1, source_target_pairs={{0,64},{64,0},{1,65},{65,1},{2,66},{66,2},{3,67},{67,3},{4,68},{68... | collective-permute-start | bytes 786440 | tf_op jit(solution)/shard_map/ppermute | solution.py:112
  33.0 8.8 %collective-permute-start.4 = (bf16[3,256,256]{2,1,0:T(8,128)(2,1)S(1)}, bf16[3,256,256]{2,1,0:T(8,128)(2,1)S(1)}, u32[]{:S(2)}, u32[]{:S(2)}) collective-permute-start(bf16[3,256,256]{2,1,0:T(8,128)(2,1)S(1)} %slice.23.refs_0_), channel_id=1, source_target_pairs={{0,4},{4,8},{8,12},{12,16},{16,20},{20,24},{24,28},{28,32},{32,36}... | collective-permute-start | bytes 1179656 | tf_op jit(solution)/shard_map/ppermute | solution.py:128
  41.9 2.6 %collective-permute-start.3 = (bf16[3,256,256]{2,1,0:T(8,128)(2,1)S(1)}, bf16[3,256,256]{2,1,0:T(8,128)(2,1)S(1)}, u32[]{:S(2)}, u32[]{:S(2)}) collective-permute-start(bf16[3,256,256]{2,1,0:T(8,128)(2,1)S(1)} %pad_maximum_fusion.refs_1_), channel_id=1, source_target_pairs={{0,4},{4,8},{8,12},{12,16},{16,20},{20,24},{24,28},{28,32},{32,36}... | collective-permute-start | bytes 1179656 | tf_op jit(solution)/shard_map/ppermute | solution.py:128
  44.6 1.9 %collective-permute-start = (bf16[2,256,256]{2,1,0:T(8,128)(2,1)S(1)}, bf16[2,256,256]{2,1,0:T(8,128)(2,1)S(1)}, u32[]{:S(2)}, u32[]{:S(2)}) collective-permute-start(bf16[2,256,256]{2,1,0:T(8,128)(2,1)S(1)} %get-tuple-element.56), channel_id=1, source_target_pairs={{0,64},{64,0},{1,65},{65,1},{2,66},{66,2},{3,67},{67,3},{4,68},{68... | collective-permute-start | bytes 786440 | tf_op jit(solution)/shard_map/ppermute | solution.py:113
  46.5 1.5 collective-permute-done.refs_2_
  48.0 3.6 %collective-permute-start.7 = (bf16[3,256,256]{2,1,0:T(8,128)(2,1)S(1)}, bf16[3,256,256]{2,1,0:T(8,128)(2,1)S(1)}, u32[]{:S(2)}, u32[]{:S(2)}) collective-permute-start(bf16[3,256,256]{2,1,0:T(8,128)(2,1)S(1)} %collective-permute-done.4.refs_3_), channel_id=1, source_target_pairs={{0,4},{4,8},{8,12},{12,16},{16,20},{20,24},{24,28},{28,32},{32,36}... | collective-permute-start | bytes 1179656 | tf_op jit(solution)/shard_map/ppermute | solution.py:128
  51.6 4.6 %collective-permute-start.6 = (bf16[3,256,256]{2,1,0:T(8,128)(2,1)S(1)}, bf16[3,256,256]{2,1,0:T(8,128)(2,1)S(1)}, u32[]{:S(2)}, u32[]{:S(2)}) collective-permute-start(bf16[3,256,256]{2,1,0:T(8,128)(2,1)S(1)} %collective-permute-done.3.refs_4_), channel_id=1, source_target_pairs={{0,4},{4,8},{8,12},{12,16},{16,20},{20,24},{24,28},{28,32},{32,36}... | collective-permute-start | bytes 1179656 | tf_op jit(solution)/shard_map/ppermute | solution.py:128
  56.2 1.9 %collective-permute-start.1 = (bf16[2,256,256]{2,1,0:T(8,128)(2,1)S(1)}, bf16[2,256,256]{2,1,0:T(8,128)(2,1)S(1)}, u32[]{:S(2)}, u32[]{:S(2)}) collective-permute-start(bf16[2,256,256]{2,1,0:T(8,128)(2,1)S(1)} %collective-permute-done.refs_2_), channel_id=1, source_target_pairs={{0,4},{4,8},{8,12},{12,16},{16,20},{20,24},{24,28},{28,32},{32,36}... | collective-permute-start | bytes 786440 | tf_op jit(solution)/shard_map/ppermute | solution.py:128
  58.1 0.7 copy-done.12
  58.8 5.0 %collective-permute-done.1.refs_5_ = bf16[2,256,256]{2,1,0:T(8,128)(2,1)S(1)} collective-permute-done((bf16[2,256,256]{2,1,0:T(8,128)(2,1)S(1)}, bf16[2,256,256]{2,1,0:T(8,128)(2,1)S(1)}, u32[]{:S(2)}, u32[]{:S(2)}) %collective-permute-start.1) | collective-permute-done | bytes 262176 | tf_op jit(solution)/shard_map/ppermute | solution.py:128
  63.8 4.9 %collective-permute-start.10 = (bf16[3,256,256]{2,1,0:T(8,128)(2,1)S(1)}, bf16[3,256,256]{2,1,0:T(8,128)(2,1)S(1)}, u32[]{:S(2)}, u32[]{:S(2)}) collective-permute-start(bf16[3,256,256]{2,1,0:T(8,128)(2,1)S(1)} %collective-permute-done.7.refs_6_), channel_id=1, source_target_pairs={{0,4},{4,8},{8,12},{12,16},{16,20},{20,24},{24,28},{28,32},{32,36}... | collective-permute-start | bytes 1179656 | tf_op jit(solution)/shard_map/ppermute | solution.py:128
  68.7 1.9 %collective-permute-start.9 = (bf16[3,256,256]{2,1,0:T(8,128)(2,1)S(1)}, bf16[3,256,256]{2,1,0:T(8,128)(2,1)S(1)}, u32[]{:S(2)}, u32[]{:S(2)}) collective-permute-start(bf16[3,256,256]{2,1,0:T(8,128)(2,1)S(1)} %collective-permute-done.6.refs_7_), channel_id=1, source_target_pairs={{0,4},{4,8},{8,12},{12,16},{16,20},{20,24},{24,28},{28,32},{32,36}... | collective-permute-start | bytes 1179656 | tf_op jit(solution)/shard_map/ppermute | solution.py:128
  70.7 2.3 %collective-permute-start.5 = (bf16[2,256,256]{2,1,0:T(8,128)(2,1)S(1)}, bf16[2,256,256]{2,1,0:T(8,128)(2,1)S(1)}, u32[]{:S(2)}, u32[]{:S(2)}) collective-permute-start(bf16[2,256,256]{2,1,0:T(8,128)(2,1)S(1)} %collective-permute-done.1.refs_5_), channel_id=1, source_target_pairs={{0,4},{4,8},{8,12},{12,16},{16,20},{20,24},{24,28},{28,32},{32,36}... | collective-permute-start | bytes 786440 | tf_op jit(solution)/shard_map/ppermute | solution.py:128
  73.0 0.7 copy-done.14
  73.7 6.8 %collective-permute-done.5.refs_8_ = bf16[2,256,256]{2,1,0:T(8,128)(2,1)S(1)} collective-permute-done((bf16[2,256,256]{2,1,0:T(8,128)(2,1)S(1)}, bf16[2,256,256]{2,1,0:T(8,128)(2,1)S(1)}, u32[]{:S(2)}, u32[]{:S(2)}) %collective-permute-start.5) | collective-permute-done | bytes 262176 | tf_op jit(solution)/shard_map/ppermute | solution.py:128
  80.5 5.4 %collective-permute-start.8 = (bf16[2,256,256]{2,1,0:T(8,128)(2,1)S(1)}, bf16[2,256,256]{2,1,0:T(8,128)(2,1)S(1)}, u32[]{:S(2)}, u32[]{:S(2)}) collective-permute-start(bf16[2,256,256]{2,1,0:T(8,128)(2,1)S(1)} %collective-permute-done.5.refs_8_), channel_id=1, source_target_pairs={{0,4},{4,8},{8,12},{12,16},{16,20},{20,24},{24,28},{28,32},{32,36}... | collective-permute-start | bytes 786440 | tf_op jit(solution)/shard_map/ppermute | solution.py:128
  85.9 0.7 copy-done.16
  86.6 1.9 %collective-permute-start.13 = (bf16[3,256,256]{2,1,0:T(8,128)(2,1)S(1)}, bf16[3,256,256]{2,1,0:T(8,128)(2,1)S(1)}, u32[]{:S(2)}, u32[]{:S(2)}) collective-permute-start(bf16[3,256,256]{2,1,0:T(8,128)(2,1)S(1)} %collective-permute-done.10.refs_9_), channel_id=1, source_target_pairs={{0,4},{4,8},{8,12},{12,16},{16,20},{20,24},{24,28},{28,32},{32,36}... | collective-permute-start | bytes 1179656 | tf_op jit(solution)/shard_map/ppermute | solution.py:128
  88.5 0.7 copy-done.2
  89.3 1.9 %collective-permute-start.12 = (bf16[3,256,256]{2,1,0:T(8,128)(2,1)S(1)}, bf16[3,256,256]{2,1,0:T(8,128)(2,1)S(1)}, u32[]{:S(2)}, u32[]{:S(2)}) collective-permute-start(bf16[3,256,256]{2,1,0:T(8,128)(2,1)S(1)} %collective-permute-done.9.refs_10_), channel_id=1, source_target_pairs={{0,4},{4,8},{8,12},{12,16},{16,20},{20,24},{24,28},{28,32},{32,36}... | collective-permute-start | bytes 1179656 | tf_op jit(solution)/shard_map/ppermute | solution.py:128
  91.2 0.7 copy-done.4
  91.9 2.6 %collective-permute-start.11 = (bf16[2,256,256]{2,1,0:T(8,128)(2,1)S(1)}, bf16[2,256,256]{2,1,0:T(8,128)(2,1)S(1)}, u32[]{:S(2)}, u32[]{:S(2)}) collective-permute-start(bf16[2,256,256]{2,1,0:T(8,128)(2,1)S(1)} %collective-permute-done.8.refs_11_), channel_id=1, source_target_pairs={{0,4},{4,8},{8,12},{12,16},{16,20},{20,24},{24,28},{28,32},{32,36}... | collective-permute-start | bytes 786440 | tf_op jit(solution)/shard_map/ppermute | solution.py:128
  94.6 0.7 copy-done.18
  95.5 5.0 %collective-permute-start.16 = (bf16[3,256,256]{2,1,0:T(8,128)(2,1)S(1)}, bf16[3,256,256]{2,1,0:T(8,128)(2,1)S(1)}, u32[]{:S(2)}, u32[]{:S(2)}) collective-permute-start(bf16[3,256,256]{2,1,0:T(8,128)(2,1)S(1)} %collective-permute-done.13.refs_12_), channel_id=1, source_target_pairs={{0,4},{4,8},{8,12},{12,16},{16,20},{20,24},{24,28},{28,32},{32,36}... | collective-permute-start | bytes 1179656 | tf_op jit(solution)/shard_map/ppermute | solution.py:128
  100.6 0.8 copy-done.6
  101.3 1.9 %collective-permute-start.15 = (bf16[3,256,256]{2,1,0:T(8,128)(2,1)S(1)}, bf16[3,256,256]{2,1,0:T(8,128)(2,1)}, u32[]{:S(2)}, u32[]{:S(2)}) collective-permute-start(bf16[3,256,256]{2,1,0:T(8,128)(2,1)S(1)} %collective-permute-done.12.refs_13_), channel_id=1, source_target_pairs={{0,4},{4,8},{8,12},{12,16},{16,20},{20,24},{24,28},{28,32},{32,36}... | collective-permute-start | bytes 1179656 | tf_op jit(solution)/shard_map/ppermute | solution.py:128
  103.2 0.7 copy-done.8
  104.0 1.9 %collective-permute-start.14 = (bf16[2,256,256]{2,1,0:T(8,128)(2,1)S(1)}, bf16[2,256,256]{2,1,0:T(8,128)(2,1)}, u32[]{:S(2)}, u32[]{:S(2)}) collective-permute-start(bf16[2,256,256]{2,1,0:T(8,128)(2,1)S(1)} %collective-permute-done.11.refs_14_), channel_id=1, source_target_pairs={{0,4},{4,8},{8,12},{12,16},{16,20},{20,24},{24,28},{28,32},{32,36}... | collective-permute-start | bytes 786440 | tf_op jit(solution)/shard_map/ppermute | solution.py:128
  105.9 0.7 copy-done.20
  106.6 4.3 %collective-permute-done.15.refs_16_ = bf16[3,256,256]{2,1,0:T(8,128)(2,1)} collective-permute-done((bf16[3,256,256]{2,1,0:T(8,128)(2,1)S(1)}, bf16[3,256,256]{2,1,0:T(8,128)(2,1)}, u32[]{:S(2)}, u32[]{:S(2)}) %collective-permute-start.15) | collective-permute-done | bytes 393248 | tf_op jit(solution)/shard_map/ppermute | solution.py:128
  110.9 2.8 %collective-permute-done.14.refs_17_ = bf16[2,256,256]{2,1,0:T(8,128)(2,1)} collective-permute-done((bf16[2,256,256]{2,1,0:T(8,128)(2,1)S(1)}, bf16[2,256,256]{2,1,0:T(8,128)(2,1)}, u32[]{:S(2)}, u32[]{:S(2)}) %collective-permute-start.14) | collective-permute-done | bytes 262176 | tf_op jit(solution)/shard_map/ppermute | solution.py:128
  113.7 4.1 %collective-permute-start.17 = (bf16[32,256,512]{2,1,0:T(8,128)(2,1)}, bf16[32,256,512]{2,1,0:T(8,128)(2,1)}, u32[]{:S(2)}, u32[]{:S(2)}) collective-permute-start(bf16[32,256,512]{2,1,0:T(8,128)(2,1)} %bitcast.5), channel_id=1, source_target_pairs={{0,64},{64,0},{1,65},{65,1},{2,66},{66,2},{3,67},{67,3},{4,68},{68... | collective-permute-start | bytes 25165832 | tf_op jit(solution)/shard_map/ppermute | solution.py:130
  117.9 3.5 %collective-permute-start.18 = (bf16[3,256,256]{2,1,0:T(8,128)(2,1)S(1)}, bf16[3,256,256]{2,1,0:T(8,128)(2,1)}, u32[]{:S(2)}, u32[]{:S(2)}) collective-permute-start(bf16[3,256,256]{2,1,0:T(8,128)(2,1)S(1)} %collective-permute-done.16.refs_15_), channel_id=1, source_target_pairs={{0,4},{4,8},{8,12},{12,16},{16,20},{20,24},{24,28},{28,32},{32,36}... | collective-permute-start | bytes 1179656 | tf_op jit(solution)/shard_map/ppermute | solution.py:128
  121.4 0.7 copy-done.10
  122.1 2.1 %collective-permute-start.20 = (bf16[3,256,256]{2,1,0:T(8,128)(2,1)}, bf16[3,256,256]{2,1,0:T(8,128)(2,1)}, u32[]{:S(2)}, u32[]{:S(2)}) collective-permute-start(bf16[3,256,256]{2,1,0:T(8,128)(2,1)} %collective-permute-done.15.refs_16_), channel_id=1, source_target_pairs={{0,4},{4,8},{8,12},{12,16},{16,20},{20,24},{24,28},{28,32},{32,36}... | collective-permute-start | bytes 1179656 | tf_op jit(solution)/shard_map/ppermute | solution.py:128
  124.2 2.1 %collective-permute-start.22 = (bf16[2,256,256]{2,1,0:T(8,128)(2,1)}, bf16[2,256,256]{2,1,0:T(8,128)(2,1)}, u32[]{:S(2)}, u32[]{:S(2)}) collective-permute-start(bf16[2,256,256]{2,1,0:T(8,128)(2,1)} %collective-permute-done.14.refs_17_), channel_id=1, source_target_pairs={{0,4},{4,8},{8,12},{12,16},{16,20},{20,24},{24,28},{28,32},{32,36}... | collective-permute-start | bytes 786440 | tf_op jit(solution)/shard_map/ppermute | solution.py:128
  126.8 4.4 %collective-permute-start.19 = (bf16[3,256,256]{2,1,0:T(8,128)(2,1)}, bf16[3,256,256]{2,1,0:T(8,128)(2,1)S(1)}, u32[]{:S(2)}, u32[]{:S(2)}) collective-permute-start(bf16[3,256,256]{2,1,0:T(8,128)(2,1)} %collective-permute-done.18.refs_18_), channel_id=1, source_target_pairs={{0,4},{4,8},{8,12},{12,16},{16,20},{20,24},{24,28},{28,32},{32,36}... | collective-permute-start | bytes 1179656 | tf_op jit(solution)/shard_map/ppermute | solution.py:128
  131.2 4.2 %collective-permute-start.21 = (bf16[3,256,256]{2,1,0:T(8,128)(2,1)}, bf16[3,256,256]{2,1,0:T(8,128)(2,1)S(1)}, u32[]{:S(2)}, u32[]{:S(2)}) collective-permute-start(bf16[3,256,256]{2,1,0:T(8,128)(2,1)} %collective-permute-done.20.refs_19_), channel_id=1, source_target_pairs={{0,4},{4,8},{8,12},{12,16},{16,20},{20,24},{24,28},{28,32},{32,36}... | collective-permute-start | bytes 1179656 | tf_op jit(solution)/shard_map/ppermute | solution.py:128
  135.4 2.8 %collective-permute-start.23 = (bf16[2,256,256]{2,1,0:T(8,128)(2,1)}, bf16[2,256,256]{2,1,0:T(8,128)(2,1)S(1)}, u32[]{:S(2)}, u32[]{:S(2)}) collective-permute-start(bf16[2,256,256]{2,1,0:T(8,128)(2,1)} %collective-permute-done.22.refs_20_), channel_id=1, source_target_pairs={{0,4},{4,8},{8,12},{12,16},{16,20},{20,24},{24,28},{28,32},{32,36}... | collective-permute-start | bytes 786440 | tf_op jit(solution)/shard_map/ppermute | solution.py:128
  138.3 1.1 copy-done.3
  139.5 1.6 copy-done.5
  141.0 1.0 copy-done.7
  142.0 1.0 copy-done.9
  143.0 1.0 copy-done.11
  144.0 0.9 copy-done.13
  145.0 0.9 copy-done.15
  145.9 0.9 copy-done.17
  146.9 0.9 copy-done.19
  147.8 0.9 copy-done.21
  148.8 9.6 %shard_map.74 = (f32[256,512]{1,0:T(8,128)S(1)}, f32[256,512]{1,0:T(8,128)S(1)}) custom-call(s32[3]{0:T(128)S(1)} %pad_add_fusion.place, bf16[32,256,512]{2,1,0:T(8,128)(2,1)} %bitcast.6, bf16[32,256,512]{2,1,0:T(8,128)(2,1)} %collective-permute-done.17.others_ref, bf16[3,256,256]{2,1,0:T(8,128)(2,1)S(1)} %slice.23.refs_0_, ...), custom_call_target="tpu_custom_call" | custom-call | tf_op jit(solution)/shard_map/pallas_call | solution.py:152
  158.4 1.3 shard_map.75
  159.8 3.3 %collective-permute-start.26 = (f32[256,512]{1,0:T(8,128)S(1)}, f32[256,512]{1,0:T(8,128)S(1)}, u32[]{:S(2)}, u32[]{:S(2)}) collective-permute-start(f32[256,512]{1,0:T(8,128)S(1)} %shard_map.75), channel_id=1, source_target_pairs={{0,64},{64,0},{1,65},{65,1},{2,66},{66,2},{3,67},{67,3},{4,68},{68... | collective-permute-start | bytes 1572872 | tf_op jit(solution)/shard_map/ppermute | solution.py:166
  163.1 3.2 %collective-permute-start.24 = (bf16[3,256,256]{2,1,0:T(8,128)(2,1)S(1)}, bf16[3,256,256]{2,1,0:T(8,128)(2,1)S(1)}, u32[]{:S(2)}, u32[]{:S(2)}) collective-permute-start(bf16[3,256,256]{2,1,0:T(8,128)(2,1)S(1)} %collective-permute-done.19.refs_0_), channel_id=1, source_target_pairs={{0,4},{4,8},{8,12},{12,16},{16,20},{20,24},{24,28},{28,32},{32,36}... | collective-permute-start | bytes 1179656 | tf_op jit(solution)/shard_map/ppermute | solution.py:128
  166.3 4.4 %collective-permute-start.25 = (bf16[1,256,256]{2,1,0:T(8,128)(2,1)S(1)}, bf16[1,256,256]{2,1,0:T(8,128)(2,1)S(1)}, u32[]{:S(2)}, u32[]{:S(2)}) collective-permute-start(bf16[1,256,256]{2,1,0:T(8,128)(2,1)S(1)} %slice.24), channel_id=1, source_target_pairs={{0,4},{4,8},{8,12},{12,16},{16,20},{20,24},{24,28},{28,32},{32,36}... | collective-permute-start | bytes 393224 | tf_op jit(solution)/shard_map/ppermute | solution.py:128
  170.8 4.4 %collective-permute-done.25.refs_4_ = bf16[1,256,256]{2,1,0:T(8,128)(2,1)S(1)} collective-permute-done((bf16[1,256,256]{2,1,0:T(8,128)(2,1)S(1)}, bf16[1,256,256]{2,1,0:T(8,128)(2,1)S(1)}, u32[]{:S(2)}, u32[]{:S(2)}) %collective-permute-start.25) | collective-permute-done | bytes 131104 | tf_op jit(solution)/shard_map/ppermute | solution.py:128
  175.2 3.3 %shard_map.76 = f32[256,512]{1,0:T(8,128)} custom-call(s32[3]{0:T(128)S(1)} %pad_add_fusion.place, bf16[32,256,512]{2,1,0:T(8,128)(2,1)S(1)} %bitcast.10, bf16[32,256,512]{2,1,0:T(8,128)(2,1)} %collective-permute-done.17.others_ref, bf16[3,256,256]{2,1,0:T(8,128)(2,1)S(1)} %collective-permute-done.19.refs_0_, ...), custom_call_target="tpu_custom_call" | custom-call | tf_op jit(solution)/shard_map/pallas_call | solution.py:152
  (63 shorter events, 1.8 us)
Async XLA Ops:
  6.5 107.2 %all-gather.2.cloned.1.call-start = ((), (), s32[]{:S(2)}) async-start(), calls=%async_computation.1 | async-start | bytes 8912896 | tf_op jit(solution)/shard_map/all_gather | solution.py:106
  7.4 1.0 copy-start
  8.4 1.0 copy-start.1
  9.4 0.7 copy-start.22
  10.1 0.7 copy-start.23
  10.8 0.7 copy-start.24
  11.4 0.7 copy-start.25
  25.3 16.6 %collective-permute-start.2 = (bf16[2,256,256]{2,1,0:T(8,128)(2,1)S(1)}, bf16[2,256,256]{2,1,0:T(8,128)(2,1)S(1)}, u32[]{:S(2)}, u32[]{:S(2)}) collective-permute-start(bf16[2,256,256]{2,1,0:T(8,128)(2,1)S(1)} %get-tuple-element.55), channel_id=1, source_target_pairs={{0,64},{64,0},{1,65},{65,1},{2,66},{66,2},{3,67},{67,3},{4,68},{68... | collective-permute-start | bytes 786440 | tf_op jit(solution)/shard_map/ppermute | solution.py:112
  33.0 15.0 %collective-permute-start.4 = (bf16[3,256,256]{2,1,0:T(8,128)(2,1)S(1)}, bf16[3,256,256]{2,1,0:T(8,128)(2,1)S(1)}, u32[]{:S(2)}, u32[]{:S(2)}) collective-permute-start(bf16[3,256,256]{2,1,0:T(8,128)(2,1)S(1)} %slice.23.refs_0_), channel_id=1, source_target_pairs={{0,4},{4,8},{8,12},{12,16},{16,20},{20,24},{24,28},{28,32},{32,36}... | collective-permute-start | bytes 1179656 | tf_op jit(solution)/shard_map/ppermute | solution.py:128
  41.9 9.6 %collective-permute-start.3 = (bf16[3,256,256]{2,1,0:T(8,128)(2,1)S(1)}, bf16[3,256,256]{2,1,0:T(8,128)(2,1)S(1)}, u32[]{:S(2)}, u32[]{:S(2)}) collective-permute-start(bf16[3,256,256]{2,1,0:T(8,128)(2,1)S(1)} %pad_maximum_fusion.refs_1_), channel_id=1, source_target_pairs={{0,4},{4,8},{8,12},{12,16},{16,20},{20,24},{24,28},{28,32},{32,36}... | collective-permute-start | bytes 1179656 | tf_op jit(solution)/shard_map/ppermute | solution.py:128
  44.6 3.4 %collective-permute-start = (bf16[2,256,256]{2,1,0:T(8,128)(2,1)S(1)}, bf16[2,256,256]{2,1,0:T(8,128)(2,1)S(1)}, u32[]{:S(2)}, u32[]{:S(2)}) collective-permute-start(bf16[2,256,256]{2,1,0:T(8,128)(2,1)S(1)} %get-tuple-element.56), channel_id=1, source_target_pairs={{0,64},{64,0},{1,65},{65,1},{2,66},{66,2},{3,67},{67,3},{4,68},{68... | collective-permute-start | bytes 786440 | tf_op jit(solution)/shard_map/ppermute | solution.py:113
  48.0 15.8 %collective-permute-start.7 = (bf16[3,256,256]{2,1,0:T(8,128)(2,1)S(1)}, bf16[3,256,256]{2,1,0:T(8,128)(2,1)S(1)}, u32[]{:S(2)}, u32[]{:S(2)}) collective-permute-start(bf16[3,256,256]{2,1,0:T(8,128)(2,1)S(1)} %collective-permute-done.4.refs_3_), channel_id=1, source_target_pairs={{0,4},{4,8},{8,12},{12,16},{16,20},{20,24},{24,28},{28,32},{32,36}... | collective-permute-start | bytes 1179656 | tf_op jit(solution)/shard_map/ppermute | solution.py:128
  51.6 17.1 %collective-permute-start.6 = (bf16[3,256,256]{2,1,0:T(8,128)(2,1)S(1)}, bf16[3,256,256]{2,1,0:T(8,128)(2,1)S(1)}, u32[]{:S(2)}, u32[]{:S(2)}) collective-permute-start(bf16[3,256,256]{2,1,0:T(8,128)(2,1)S(1)} %collective-permute-done.3.refs_4_), channel_id=1, source_target_pairs={{0,4},{4,8},{8,12},{12,16},{16,20},{20,24},{24,28},{28,32},{32,36}... | collective-permute-start | bytes 1179656 | tf_op jit(solution)/shard_map/ppermute | solution.py:128
  56.2 7.6 %collective-permute-start.1 = (bf16[2,256,256]{2,1,0:T(8,128)(2,1)S(1)}, bf16[2,256,256]{2,1,0:T(8,128)(2,1)S(1)}, u32[]{:S(2)}, u32[]{:S(2)}) collective-permute-start(bf16[2,256,256]{2,1,0:T(8,128)(2,1)S(1)} %collective-permute-done.refs_2_), channel_id=1, source_target_pairs={{0,4},{4,8},{8,12},{12,16},{16,20},{20,24},{24,28},{28,32},{32,36}... | collective-permute-start | bytes 786440 | tf_op jit(solution)/shard_map/ppermute | solution.py:128
  58.1 0.7 copy-start.12
  63.8 22.7 %collective-permute-start.10 = (bf16[3,256,256]{2,1,0:T(8,128)(2,1)S(1)}, bf16[3,256,256]{2,1,0:T(8,128)(2,1)S(1)}, u32[]{:S(2)}, u32[]{:S(2)}) collective-permute-start(bf16[3,256,256]{2,1,0:T(8,128)(2,1)S(1)} %collective-permute-done.7.refs_6_), channel_id=1, source_target_pairs={{0,4},{4,8},{8,12},{12,16},{16,20},{20,24},{24,28},{28,32},{32,36}... | collective-permute-start | bytes 1179656 | tf_op jit(solution)/shard_map/ppermute | solution.py:128
  68.7 20.5 %collective-permute-start.9 = (bf16[3,256,256]{2,1,0:T(8,128)(2,1)S(1)}, bf16[3,256,256]{2,1,0:T(8,128)(2,1)S(1)}, u32[]{:S(2)}, u32[]{:S(2)}) collective-permute-start(bf16[3,256,256]{2,1,0:T(8,128)(2,1)S(1)} %collective-permute-done.6.refs_7_), channel_id=1, source_target_pairs={{0,4},{4,8},{8,12},{12,16},{16,20},{20,24},{24,28},{28,32},{32,36}... | collective-permute-start | bytes 1179656 | tf_op jit(solution)/shard_map/ppermute | solution.py:128
  70.7 9.8 %collective-permute-start.5 = (bf16[2,256,256]{2,1,0:T(8,128)(2,1)S(1)}, bf16[2,256,256]{2,1,0:T(8,128)(2,1)S(1)}, u32[]{:S(2)}, u32[]{:S(2)}) collective-permute-start(bf16[2,256,256]{2,1,0:T(8,128)(2,1)S(1)} %collective-permute-done.1.refs_5_), channel_id=1, source_target_pairs={{0,4},{4,8},{8,12},{12,16},{16,20},{20,24},{24,28},{28,32},{32,36}... | collective-permute-start | bytes 786440 | tf_op jit(solution)/shard_map/ppermute | solution.py:128
  73.0 0.7 copy-start.14
  80.5 11.5 %collective-permute-start.8 = (bf16[2,256,256]{2,1,0:T(8,128)(2,1)S(1)}, bf16[2,256,256]{2,1,0:T(8,128)(2,1)S(1)}, u32[]{:S(2)}, u32[]{:S(2)}) collective-permute-start(bf16[2,256,256]{2,1,0:T(8,128)(2,1)S(1)} %collective-permute-done.5.refs_8_), channel_id=1, source_target_pairs={{0,4},{4,8},{8,12},{12,16},{16,20},{20,24},{24,28},{28,32},{32,36}... | collective-permute-start | bytes 786440 | tf_op jit(solution)/shard_map/ppermute | solution.py:128
  85.9 0.7 copy-start.16
  86.6 8.9 %collective-permute-start.13 = (bf16[3,256,256]{2,1,0:T(8,128)(2,1)S(1)}, bf16[3,256,256]{2,1,0:T(8,128)(2,1)S(1)}, u32[]{:S(2)}, u32[]{:S(2)}) collective-permute-start(bf16[3,256,256]{2,1,0:T(8,128)(2,1)S(1)} %collective-permute-done.10.refs_9_), channel_id=1, source_target_pairs={{0,4},{4,8},{8,12},{12,16},{16,20},{20,24},{24,28},{28,32},{32,36}... | collective-permute-start | bytes 1179656 | tf_op jit(solution)/shard_map/ppermute | solution.py:128
  88.5 0.8 copy-start.2
  89.3 12.1 %collective-permute-start.12 = (bf16[3,256,256]{2,1,0:T(8,128)(2,1)S(1)}, bf16[3,256,256]{2,1,0:T(8,128)(2,1)S(1)}, u32[]{:S(2)}, u32[]{:S(2)}) collective-permute-start(bf16[3,256,256]{2,1,0:T(8,128)(2,1)S(1)} %collective-permute-done.9.refs_10_), channel_id=1, source_target_pairs={{0,4},{4,8},{8,12},{12,16},{16,20},{20,24},{24,28},{28,32},{32,36}... | collective-permute-start | bytes 1179656 | tf_op jit(solution)/shard_map/ppermute | solution.py:128
  91.2 0.8 copy-start.4
  91.9 12.0 %collective-permute-start.11 = (bf16[2,256,256]{2,1,0:T(8,128)(2,1)S(1)}, bf16[2,256,256]{2,1,0:T(8,128)(2,1)S(1)}, u32[]{:S(2)}, u32[]{:S(2)}) collective-permute-start(bf16[2,256,256]{2,1,0:T(8,128)(2,1)S(1)} %collective-permute-done.8.refs_11_), channel_id=1, source_target_pairs={{0,4},{4,8},{8,12},{12,16},{16,20},{20,24},{24,28},{28,32},{32,36}... | collective-permute-start | bytes 786440 | tf_op jit(solution)/shard_map/ppermute | solution.py:128
  94.6 0.7 copy-start.18
  95.5 11.1 %collective-permute-start.16 = (bf16[3,256,256]{2,1,0:T(8,128)(2,1)S(1)}, bf16[3,256,256]{2,1,0:T(8,128)(2,1)S(1)}, u32[]{:S(2)}, u32[]{:S(2)}) collective-permute-start(bf16[3,256,256]{2,1,0:T(8,128)(2,1)S(1)} %collective-permute-done.13.refs_12_), channel_id=1, source_target_pairs={{0,4},{4,8},{8,12},{12,16},{16,20},{20,24},{24,28},{28,32},{32,36}... | collective-permute-start | bytes 1179656 | tf_op jit(solution)/shard_map/ppermute | solution.py:128
  100.5 0.8 copy-start.6
  101.3 9.6 %collective-permute-start.15 = (bf16[3,256,256]{2,1,0:T(8,128)(2,1)S(1)}, bf16[3,256,256]{2,1,0:T(8,128)(2,1)}, u32[]{:S(2)}, u32[]{:S(2)}) collective-permute-start(bf16[3,256,256]{2,1,0:T(8,128)(2,1)S(1)} %collective-permute-done.12.refs_13_), channel_id=1, source_target_pairs={{0,4},{4,8},{8,12},{12,16},{16,20},{20,24},{24,28},{28,32},{32,36}... | collective-permute-start | bytes 1179656 | tf_op jit(solution)/shard_map/ppermute | solution.py:128
  103.2 0.7 copy-start.8
  104.0 9.8 %collective-permute-start.14 = (bf16[2,256,256]{2,1,0:T(8,128)(2,1)S(1)}, bf16[2,256,256]{2,1,0:T(8,128)(2,1)}, u32[]{:S(2)}, u32[]{:S(2)}) collective-permute-start(bf16[2,256,256]{2,1,0:T(8,128)(2,1)S(1)} %collective-permute-done.11.refs_14_), channel_id=1, source_target_pairs={{0,4},{4,8},{8,12},{12,16},{16,20},{20,24},{24,28},{28,32},{32,36}... | collective-permute-start | bytes 786440 | tf_op jit(solution)/shard_map/ppermute | solution.py:128
  105.9 0.7 copy-start.20
  113.7 24.6 %collective-permute-start.17 = (bf16[32,256,512]{2,1,0:T(8,128)(2,1)}, bf16[32,256,512]{2,1,0:T(8,128)(2,1)}, u32[]{:S(2)}, u32[]{:S(2)}) collective-permute-start(bf16[32,256,512]{2,1,0:T(8,128)(2,1)} %bitcast.5), channel_id=1, source_target_pairs={{0,64},{64,0},{1,65},{65,1},{2,66},{66,2},{3,67},{67,3},{4,68},{68... | collective-permute-start | bytes 25165832 | tf_op jit(solution)/shard_map/ppermute | solution.py:130
  117.9 8.9 %collective-permute-start.18 = (bf16[3,256,256]{2,1,0:T(8,128)(2,1)S(1)}, bf16[3,256,256]{2,1,0:T(8,128)(2,1)}, u32[]{:S(2)}, u32[]{:S(2)}) collective-permute-start(bf16[3,256,256]{2,1,0:T(8,128)(2,1)S(1)} %collective-permute-done.16.refs_15_), channel_id=1, source_target_pairs={{0,4},{4,8},{8,12},{12,16},{16,20},{20,24},{24,28},{28,32},{32,36}... | collective-permute-start | bytes 1179656 | tf_op jit(solution)/shard_map/ppermute | solution.py:128
  121.4 0.7 copy-start.10
  122.1 9.1 %collective-permute-start.20 = (bf16[3,256,256]{2,1,0:T(8,128)(2,1)}, bf16[3,256,256]{2,1,0:T(8,128)(2,1)}, u32[]{:S(2)}, u32[]{:S(2)}) collective-permute-start(bf16[3,256,256]{2,1,0:T(8,128)(2,1)} %collective-permute-done.15.refs_16_), channel_id=1, source_target_pairs={{0,4},{4,8},{8,12},{12,16},{16,20},{20,24},{24,28},{28,32},{32,36}... | collective-permute-start | bytes 1179656 | tf_op jit(solution)/shard_map/ppermute | solution.py:128
  124.2 11.2 %collective-permute-start.22 = (bf16[2,256,256]{2,1,0:T(8,128)(2,1)}, bf16[2,256,256]{2,1,0:T(8,128)(2,1)}, u32[]{:S(2)}, u32[]{:S(2)}) collective-permute-start(bf16[2,256,256]{2,1,0:T(8,128)(2,1)} %collective-permute-done.14.refs_17_), channel_id=1, source_target_pairs={{0,4},{4,8},{8,12},{12,16},{16,20},{20,24},{24,28},{28,32},{32,36}... | collective-permute-start | bytes 786440 | tf_op jit(solution)/shard_map/ppermute | solution.py:128
  126.8 31.6 %collective-permute-start.19 = (bf16[3,256,256]{2,1,0:T(8,128)(2,1)}, bf16[3,256,256]{2,1,0:T(8,128)(2,1)S(1)}, u32[]{:S(2)}, u32[]{:S(2)}) collective-permute-start(bf16[3,256,256]{2,1,0:T(8,128)(2,1)} %collective-permute-done.18.refs_18_), channel_id=1, source_target_pairs={{0,4},{4,8},{8,12},{12,16},{16,20},{20,24},{24,28},{28,32},{32,36}... | collective-permute-start | bytes 1179656 | tf_op jit(solution)/shard_map/ppermute | solution.py:128
  131.2 27.2 %collective-permute-start.21 = (bf16[3,256,256]{2,1,0:T(8,128)(2,1)}, bf16[3,256,256]{2,1,0:T(8,128)(2,1)S(1)}, u32[]{:S(2)}, u32[]{:S(2)}) collective-permute-start(bf16[3,256,256]{2,1,0:T(8,128)(2,1)} %collective-permute-done.20.refs_19_), channel_id=1, source_target_pairs={{0,4},{4,8},{8,12},{12,16},{16,20},{20,24},{24,28},{28,32},{32,36}... | collective-permute-start | bytes 1179656 | tf_op jit(solution)/shard_map/ppermute | solution.py:128
  135.4 23.0 %collective-permute-start.23 = (bf16[2,256,256]{2,1,0:T(8,128)(2,1)}, bf16[2,256,256]{2,1,0:T(8,128)(2,1)S(1)}, u32[]{:S(2)}, u32[]{:S(2)}) collective-permute-start(bf16[2,256,256]{2,1,0:T(8,128)(2,1)} %collective-permute-done.22.refs_20_), channel_id=1, source_target_pairs={{0,4},{4,8},{8,12},{12,16},{16,20},{20,24},{24,28},{28,32},{32,36}... | collective-permute-start | bytes 786440 | tf_op jit(solution)/shard_map/ppermute | solution.py:128
  138.2 20.2 %slice-start = ((s8[8388608]{0:T(1024)(128)(4,1)}), s8[4194304]{0:T(1024)(128)(4,1)S(1)}, s32[]{:S(2)}) async-start(s8[8388608]{0:T(1024)(128)(4,1)} %bitcast.7), calls=%async_computation.2 | async-start | bytes 8388608
  138.3 20.1 %slice-start.1 = ((s8[8388608]{0:T(1024)(128)(4,1)}), s8[4194304]{0:T(1024)(128)(4,1)S(1)}, s32[]{:S(2)}) async-start(s8[8388608]{0:T(1024)(128)(4,1)} %bitcast.7), calls=%async_computation.3 | async-start | bytes 8388608
  138.3 1.1 copy-start.3
  139.5 1.6 copy-start.5
  141.0 1.0 copy-start.7
  142.0 1.0 copy-start.9
  143.0 1.0 copy-start.11
  144.0 0.9 copy-start.13
  145.0 0.9 copy-start.15
  145.9 0.9 copy-start.17
  146.9 0.9 copy-start.19
  147.8 0.9 copy-start.21
  159.8 15.4 %collective-permute-start.26 = (f32[256,512]{1,0:T(8,128)S(1)}, f32[256,512]{1,0:T(8,128)S(1)}, u32[]{:S(2)}, u32[]{:S(2)}) collective-permute-start(f32[256,512]{1,0:T(8,128)S(1)} %shard_map.75), channel_id=1, source_target_pairs={{0,64},{64,0},{1,65},{65,1},{2,66},{66,2},{3,67},{67,3},{4,68},{68... | collective-permute-start | bytes 1572872 | tf_op jit(solution)/shard_map/ppermute | solution.py:166
  163.1 12.0 %collective-permute-start.24 = (bf16[3,256,256]{2,1,0:T(8,128)(2,1)S(1)}, bf16[3,256,256]{2,1,0:T(8,128)(2,1)S(1)}, u32[]{:S(2)}, u32[]{:S(2)}) collective-permute-start(bf16[3,256,256]{2,1,0:T(8,128)(2,1)S(1)} %collective-permute-done.19.refs_0_), channel_id=1, source_target_pairs={{0,4},{4,8},{8,12},{12,16},{16,20},{20,24},{24,28},{28,32},{32,36}... | collective-permute-start | bytes 1179656 | tf_op jit(solution)/shard_map/ppermute | solution.py:128
  166.3 8.9 %collective-permute-start.25 = (bf16[1,256,256]{2,1,0:T(8,128)(2,1)S(1)}, bf16[1,256,256]{2,1,0:T(8,128)(2,1)S(1)}, u32[]{:S(2)}, u32[]{:S(2)}) collective-permute-start(bf16[1,256,256]{2,1,0:T(8,128)(2,1)S(1)} %slice.24), channel_id=1, source_target_pairs={{0,4},{4,8},{8,12},{12,16},{16,20},{20,24},{24,28},{28,32},{32,36}... | collective-permute-start | bytes 393224 | tf_op jit(solution)/shard_map/ppermute | solution.py:128
Sparse Core Ops, SparseCore 0:
  13.8 91.3 all-gather.1

commit v3 on v0

v3 whole, which is shorter than its diff:
```python
import functools

import jax
import jax.numpy as jnp
from jax import lax
from jax.experimental import pallas as pl
from jax.experimental.pallas import tpu as pltpu
from jax.sharding import Mesh, PartitionSpec as P

BS = 256
CORES = 2
ROWS = 1024
CUT = 688
SPARE = 3 * CUT - 2 * ROWS
HBM = pl.BlockSpec(memory_space=pl.ANY)
VMEM = pl.BlockSpec(memory_space=pltpu.VMEM)
PARAMS = pltpu.CompilerParams(vmem_limit_bytes=40 * 1024 * 1024)
SWAP = [(0, 1), (1, 0)]


def below(axis, size):
    return lax.broadcasted_iota(jnp.int32, (BS, BS), axis) < size


def masked(block, rows, columns):
    kept = jnp.where(below(0, rows) & below(1, columns), block.astype(jnp.float32), 0.0)
    return kept.astype(jnp.bfloat16)


def mask_kernel(*refs):
    count = 7
    a_out, b_out = refs[count : count + 2]
    slots, sems = refs[count + 2 : -1], refs[-1]
    copies = [pltpu.make_async_copy(refs[i], slots[i], sems.at[i]) for i in range(count)]
    for copy in copies:
        copy.start()
    for copy in copies:
        copy.wait()
    mask_a, mask_b, rows, inner, cols, a, b = slots
    columns = inner[0, lax.axis_index("col")]
    for i in range(ROWS // BS):
        place = slice(i * BS, (i + 1) * BS)
        a_out[place, :] = masked(a[0, place, :], rows[i] * mask_a[i], columns)
    first = (lax.axis_index("y") * CORES + lax.axis_index("core")) * mask_b.shape[1]
    for k in range(mask_b.shape[1]):
        for n in range(mask_b.shape[2]):
            place = (slice(k * BS, (k + 1) * BS), slice(n * BS, (n + 1) * BS))
            size = inner[0, first + k] * mask_b[0, k, n]
            b_out[place] = masked(b[(0,) + place], size, cols[n])


def product_kernel(steps, own, blocks, added, *refs):
    b_refs, refs = refs[:5], refs[5:]
    a_refs, refs = refs[: 2 * len(steps)], refs[2 * len(steps) :]
    adds, (out_ref, a_all, b_all, extra, sems) = refs[:added], refs[added:]
    z, y, core = lax.axis_index("col"), lax.axis_index("y"), lax.axis_index("core")
    way = 2 * core - 1
    first, count = steps[0], len(steps)

    chips, mine, theirs = 4, core, 1 - core
    parts = (
        (0, 0, y, mine), (0, 1, y, theirs),
        (1, 0, y + way, mine), (1, 1, y + way, theirs),
        (2, 0, y - way, theirs), (2, 1, y - way, mine),
        (3, 0, y + 2, mine), (4, 0, y + 2, theirs),
    )
    for i, at, chip, owner in parts:
        for half in range(2):
            k = (lax.rem(chip + chips, chips) * CORES + owner) * 2 + half
            step = lax.rem(way * (k - z) + blocks, blocks)

            @pl.when((step >= first) & (step < first + count))
            def _(ref=b_refs[i], start=(at * 2 + half) * BS, step=step):
                pltpu.make_async_copy(
                    ref.at[pl.ds(start, BS)], b_all.at[step - first], sems.at[0]
                ).start()

    for i in range(count):
        upper, lower = a_refs[2 * i], a_refs[2 * i + 1]
        lanes = pl.ds(i * BS, BS)
        if own:
            pieces = ((upper, 0, 0, CUT), (lower, 0, CUT, ROWS - CUT))
        else:
            done = 2 * CUT - ROWS
            pieces = ((upper, ROWS - CUT, 0, done), (lower, SPARE, done, ROWS - done))
        for ref, start, to, size in pieces:
            pltpu.make_async_copy(
                ref.at[pl.ds(start, size)], a_all.at[pl.ds(to, size), lanes], sems.at[1]
            ).start()
    for i, ref in enumerate(adds):
        pltpu.make_async_copy(ref, extra.at[i], sems.at[2 + i]).start()
    pltpu.make_async_copy(b_all, b_all, sems.at[0]).wait()
    pltpu.make_async_copy(a_all, a_all, sems.at[1]).wait()
    for i, ref in enumerate(adds):
        pltpu.make_async_copy(ref, extra.at[i], sems.at[2 + i]).wait()

    b = b_all[...].reshape(count * BS, b_all.shape[2])
    for tile in range(ROWS // BS):
        rows = pl.ds(tile * BS, BS)
        total = jnp.dot(a_all[rows, :], b, preferred_element_type=jnp.float32)
        for i in range(added):
            total = total + extra[i, rows, :]
        out_ref[rows, :] = total


def layers_kernel(in_hbm, out_ref, parts, sem):
    copy = pltpu.make_async_copy(in_hbm, parts, sem)
    copy.start()
    copy.wait()
    out_ref[...] = (parts[0] + parts[1]) + (parts[2] + parts[3])


def after(value, earlier):
    return lax.optimization_barrier((value, earlier))[0]


def on_device(sizes, a_panel, b_panel, mask_a, mask_b, row_sizes, inner_sizes, col_sizes):
    cols, chips = sizes["col"], sizes["y"]
    width = b_panel.shape[2]
    ring = [
        (c * cols + i, c * cols + (i + (1, -1)[c]) % cols) for c in range(CORES) for i in range(cols)
    ]
    args = (mask_a.reshape(-1), mask_b, row_sizes, inner_sizes, col_sizes, a_panel, b_panel)
    own, b_eff = pl.pallas_call(
        mask_kernel,
        out_shape=tuple(
            jax.ShapeDtypeStruct(p.shape[1:], jnp.bfloat16) for p in (a_panel, b_panel)
        ),
        in_specs=[pl.BlockSpec(memory_space=pltpu.HBM)] * len(args),
        out_specs=(VMEM, VMEM),
        scratch_shapes=[pltpu.SMEM(x.shape, x.dtype) for x in args[:5]]
        + [pltpu.VMEM(x.shape, x.dtype) for x in args[5:]]
        + [pltpu.SemaphoreType.DMA((len(args),))],
        compiler_params=pltpu.CompilerParams(vmem_limit_bytes=60 * 1024 * 1024),
    )(*args)

    last = cols // 2
    held = [[own[:CUT]], [], []]
    sent = held[0][0]
    with jax.named_scope("stream_0_step_1"):
        held[0].append(lax.ppermute(sent, ("core", "col"), ring))
    other = lax.ppermute(own, "core", SWAP)
    held[1] = [jnp.concatenate([own[CUT:], other[: 2 * CUT - ROWS]])]
    held[2] = [other[ROWS - CUT :]]
    def product(steps, own, pairs, adds=()):
        n = len(steps)
        arrays = [a for pair in pairs for a in pair]
        return pl.pallas_call(
            functools.partial(product_kernel, steps, own, cols, len(adds)),
            out_shape=jax.ShapeDtypeStruct((ROWS, width), jnp.float32),
            in_specs=[HBM] * (5 + len(arrays) + len(adds)),
            out_specs=VMEM,
            scratch_shapes=[
                pltpu.VMEM((ROWS, n * BS), jnp.bfloat16),
                pltpu.VMEM((n, BS, width), jnp.bfloat16),
                pltpu.VMEM((max(1, len(adds)), ROWS, width), jnp.float32),
                pltpu.SemaphoreType.DMA((2 + max(1, len(adds)),)),
            ],
            compiler_params=PARAMS,
            cost_estimate=pl.CostEstimate(
                flops=2 * ROWS * n * BS * width, bytes_accessed=2 * 2**20, transcendentals=0
            ),
        )(*b_all, *arrays, *adds)

    near_by = [
        (i * CORES + c, (i + (1, -1)[c]) % chips * CORES + c) for i in range(chips) for c in range(CORES)
    ]
    far_away = [(i, (i + 2) % chips) for i in range(chips)]
    b_all = [None] * 5
    b_other = None
    for step in range(1, last + 1):
        for j in range(3):
            if (step, j) == (1, 0) or (step, j) == (last, 2):
                continue
            value = held[j][-1]
            if (step, j) == (last, 1):
                value = value[: ROWS - CUT]
            sent = after(value, sent)
            with jax.named_scope(f"stream_{j}_step_{step}"):
                held[j].append(lax.ppermute(sent, ("core", "col"), ring))
            if (step, j) == (1, 2):
                b_other = lax.ppermute(after(b_eff, sent), "core", SWAP)
            if (step, j) == (2, 0):
                b_all[3] = lax.ppermute(after(b_eff, sent), "y", far_away)
            if (step, j) == (3, 2):
                b_all[0] = jnp.concatenate([b_eff, after(b_other, sent)])
                b_all[1] = lax.ppermute(b_all[0], ("y", "core"), near_by)
            if (step, j) == (6, 0):
                b_all[4] = lax.ppermute(after(b_all[3], sent), "core", SWAP)
            if (step, j) == (6, 1):
                b_all[2] = lax.ppermute(after(b_all[1], sent), "core", SWAP)

    steps = range(1, last)
    pairs = [(held[1][s], held[2][s]) for s in steps]
    pairs[-1] = after(pairs[-1], held[0][last - 1])
    others = lax.ppermute(product(steps, False, pairs), "core", SWAP)
    steps = range(last)
    mine = product(steps, True, [(held[0][s], held[1][s]) for s in steps])
    parts = product((last,), True, [(held[0][last], held[1][last])], (mine, others))
    parts = parts.reshape(-1, BS, width)
    parts = lax.all_to_all(parts, "layer", 0, 0)
    return pl.pallas_call(
        layers_kernel,
        out_shape=jax.ShapeDtypeStruct((BS, width), jnp.float32),
        in_specs=[HBM],
        out_specs=VMEM,
        scratch_shapes=[pltpu.VMEM(parts.shape, jnp.float32), pltpu.SemaphoreType.DMA],
        compiler_params=PARAMS,
    )(parts)


def solution(mesh):
    rows, cols, layers = (mesh.shape[name] for name in ("row", "col", "layer"))
    devices = mesh.devices.reshape(rows // CORES, CORES, cols, layers)
    cores = Mesh(devices, ("y", "core", "col", "layer"))
    row = ("y", "core")
    return jax.shard_map(
        functools.partial(on_device, dict(cores.shape)),
        mesh=cores,
        in_specs=(
            P("layer", row, "col"),
            P("layer", row, "col"),
            P("layer", row, "col"),
            P("layer", row, "col"),
            P(row),
            P("layer", None),
            P("col"),
        ),
        out_specs=P((*row, "layer"), "col"),
        check_vma=False,
    )
```

time: 239 us -> 159 us (0.67)
  waiting for transfers between devices: 208 us -> 12.3 us
  starting transfers between devices: 0.12 us -> 103 us
  blocking collectives: 0 us -> 27.8 us
  between operations: 13.2 us -> 0.47 us
  Pallas kernels: 0 us -> 10.6 us
  matrix products: 10.4 us -> 0 us
  other arithmetic: 4.72 us -> 0.03 us
    all_gather x2 -> x0, waiting for transfers between devices: 166 us -> none  [the longest x1 123 us: on_device(): a_full = lax.all_gather(a_eff, 'col', axis=1, tiled=True)]
    ppermute x0 -> x30, starting transfers between devices: none -> 103 us  [the longest x22 66.7 us: on_device(): held[j].append(lax.ppermute(sent, ('core', 'col'), ring))]
    reduce_scatter x1 -> x0, waiting for transfers between devices: 41.8 us -> none  [on_device(): lax.psum_scatter(partial_sum, 'layer', scatter_dimension=0, tiled=True)]
    all_to_all x0 -> x1, blocking collectives: none -> 27.8 us  [on_device(): parts = lax.all_to_all(parts, 'layer', 0, 0)]
    ppermute x0 -> x30, waiting for transfers between devices: none -> 12.3 us  [the longest x22 11.9 us: on_device(): held[j].append(lax.ppermute(sent, ('core', 'col'), ring))]
    pallas_call x0 -> x5, Pallas kernels: none -> 10.6 us  [the longest x3 7.11 us: product(): pl.pallas_call(functools.partial(product_kernel, steps, own, cols, len(ad...]
    dot_general x1 -> x0, matrix products: 10.4 us -> none  [on_device(): jnp.dot(a_full, lax.all_gather(b_eff, 'row', axis=0, tiled=True), preferr...]
    mul x3 -> x0, other arithmetic: 3.15 us -> none  [the longest x1 2.03 us: on_device(): b_eff = b_local * keep(mask_b[0], b_inner, col_sizes, BS)]
  transfers between devices with their start and end apart: 3 -> 30, of which waited for: 3 -> 9; matrix products, arithmetic and copies ran while one was open for 1% -> 1% of each run, Pallas kernels for 0% -> 2%
where the time goes in v3:
time: 159 us; the launch traced here: 157 us
  starting transfers between devices  103 us (65%)
  blocking collectives  27.8 us (17%)
  waiting for transfers between devices  12.3 us (8%)
  Pallas kernels  10.6 us (7%)
  local copies, waits for them, and re-layouts  2.07 us (1%)
    ppermute x22, starting transfers between devices, on_device(): held[j].append(lax.ppermute(sent, ('core', 'col'), ring))  66.7 us
    all_to_all x1, blocking collectives, on_device(): parts = lax.all_to_all(parts, 'layer', 0, 0)  27.8 us
    ppermute x22, waiting for transfers between devices, on_device(): held[j].append(lax.ppermute(sent, ('core', 'col'), ring))  11.9 us
    ppermute x1, starting transfers between devices, on_device(): other = lax.ppermute(own, 'core', SWAP)  8.92 us
    pallas_call x3, Pallas kernels, product(): pl.pallas_call(functools.partial(product_kernel, steps, own, cols, len(ad...  7.11 us
    ppermute x1, starting transfers between devices, on_device(): held[0].append(lax.ppermute(sent, ('core', 'col'), ring))  5.75 us
    ppermute x1, starting transfers between devices, on_device(): b_all[2] = lax.ppermute(after(b_all[1], sent), 'core', SWAP)  5.09 us
    ppermute x1, starting transfers between devices, on_device(): others = lax.ppermute(product(steps, False, pairs), 'core', SWAP)  4.78 us
  transfers between devices with their start and end apart: 30, of which 9 were waited for; matrix products, arithmetic and copies ran while one was open for 1% of the time, Pallas kernels for 2%

profile of v3, /device:TPU:1, one launch (start us, length us, event | category | flops | bytes accessed | tf_op | source)
XLA Modules:
  0.0 156.6 jit_solution(13886029004301245383)
XLA Ops:
  0.0 2.4 %shard_map.73 = (bf16[1024,256]{1,0:T(8,128)(2,1)}, bf16[512,512]{1,0:T(8,128)(2,1)}) custom-call(s32[4]{0:T(128)} %bitcast.3, s32[1,2,2]{2,1,0:T(2,128)} %refs_1_.1, s32[4]{0:T(128)} %refs_2_.1, s32[1,16]{1,0:T(1,128)} %refs_3_.1, s32[2]{0:T(128)} %refs_4_.1, bf16[1,1024,256]{2,1,0:T(8,128)(2,1)} %refs_5_.1, bf16[1,512,512]{2,1,0:T(8,128)(2,1)} %refs_6_.1), custom_call_target="tpu_custom_call" | custom-call | tf_op jit(solution)/shard_map/pallas_call | solution.py:124
  2.4 8.9 %collective-permute-start = (bf16[1024,256]{1,0:T(8,128)(2,1)}, bf16[1024,256]{1,0:T(8,128)(2,1)S(1)}, u32[]{:S(2)}, u32[]{:S(2)}) collective-permute-start(bf16[1024,256]{1,0:T(8,128)(2,1)} %get-tuple-element.37), channel_id=1, source_target_pairs={{0,64},{64,0},{1,65},{65,1},{2,66},{66,2},{3,67},{67,3},{4,68},{68... | collective-permute-start | bytes 1572872 | tf_op jit(solution)/shard_map/ppermute | solution.py:142
  11.3 1.0 slice.18.refs_5_
  12.4 5.7 %collective-permute-start.4 = (bf16[688,256]{1,0:T(8,128)(2,1)S(1)}, bf16[688,256]{1,0:T(8,128)(2,1)S(1)}, u32[]{:S(2)}, u32[]{:S(2)}) collective-permute-start(bf16[688,256]{1,0:T(8,128)(2,1)S(1)} %slice.18.refs_5_), channel_id=1, source_target_pairs={{0,4},{4,8},{8,12},{12,16},{16,20},{20,24},{24,28},{28,32},{32,36}... | collective-permute-start | bytes 1056776 | tf_op jit(solution)/shard_map/stream_0_step_1/ppermute | solution.py:141
  18.1 0.9 slice.16
  19.0 0.0 collective-permute-done
  19.1 2.6 %collective-permute-start.3 = (bf16[688,256]{1,0:T(8,128)(2,1)S(1)}, bf16[688,256]{1,0:T(8,128)(2,1)S(1)}, u32[]{:S(2)}, u32[]{:S(2)}) collective-permute-start(bf16[688,256]{1,0:T(8,128)(2,1)S(1)} %pad_maximum_fusion.refs_6_), channel_id=1, source_target_pairs={{0,4},{4,8},{8,12},{12,16},{16,20},{20,24},{24,28},{28,32},{32,36}... | collective-permute-start | bytes 1056776 | tf_op jit(solution)/shard_map/stream_1_step_1/ppermute | solution.py:180
  21.8 2.6 %collective-permute-start.2 = (bf16[688,256]{1,0:T(8,128)(2,1)S(1)}, bf16[688,256]{1,0:T(8,128)(2,1)S(1)}, u32[]{:S(2)}, u32[]{:S(2)}) collective-permute-start(bf16[688,256]{1,0:T(8,128)(2,1)S(1)} %slice.20), channel_id=1, source_target_pairs={{0,4},{4,8},{8,12},{12,16},{16,20},{20,24},{24,28},{28,32},{32,36}... | collective-permute-start | bytes 1056776 | tf_op jit(solution)/shard_map/stream_2_step_1/ppermute | solution.py:180
  24.4 1.9 %collective-permute-start.1 = (bf16[512,512]{1,0:T(8,128)(2,1)S(1)}, bf16[512,512]{1,0:T(8,128)(2,1)S(1)}, u32[]{:S(2)}, u32[]{:S(2)}) collective-permute-start(bf16[512,512]{1,0:T(8,128)(2,1)S(1)} %copy-done), channel_id=1, source_target_pairs={{0,64},{64,0},{1,65},{65,1},{2,66},{66,2},{3,67},{67,3},{4,68},{68... | collective-permute-start | bytes 1572872 | tf_op jit(solution)/shard_map/ppermute | solution.py:182
  26.4 0.0 collective-permute-done.4.refs_7_
  26.4 2.6 %collective-permute-start.7 = (bf16[688,256]{1,0:T(8,128)(2,1)S(1)}, bf16[688,256]{1,0:T(8,128)(2,1)S(1)}, u32[]{:S(2)}, u32[]{:S(2)}) collective-permute-start(bf16[688,256]{1,0:T(8,128)(2,1)S(1)} %collective-permute-done.4.refs_7_), channel_id=1, source_target_pairs={{0,4},{4,8},{8,12},{12,16},{16,20},{20,24},{24,28},{28,32},{32,36}... | collective-permute-start | bytes 1056776 | tf_op jit(solution)/shard_map/stream_0_step_2/ppermute | solution.py:180
  29.0 0.0 collective-permute-done.3.refs_8_.refs_5_
  29.0 3.8 %collective-permute-start.6 = (bf16[688,256]{1,0:T(8,128)(2,1)S(1)}, bf16[688,256]{1,0:T(8,128)(2,1)S(1)}, u32[]{:S(2)}, u32[]{:S(2)}) collective-permute-start(bf16[688,256]{1,0:T(8,128)(2,1)S(1)} %collective-permute-done.3.refs_8_.refs_5_), channel_id=1, source_target_pairs={{0,4},{4,8},{8,12},{12,16},{16,20},{20,24},{24,28},{28,32},{32,36}... | collective-permute-start | bytes 1056776 | tf_op jit(solution)/shard_map/stream_1_step_2/ppermute | solution.py:180
  32.9 0.0 collective-permute-done.2.refs_6_
  32.9 2.6 %collective-permute-start.5 = (bf16[688,256]{1,0:T(8,128)(2,1)S(1)}, bf16[688,256]{1,0:T(8,128)(2,1)S(1)}, u32[]{:S(2)}, u32[]{:S(2)}) collective-permute-start(bf16[688,256]{1,0:T(8,128)(2,1)S(1)} %collective-permute-done.2.refs_6_), channel_id=1, source_target_pairs={{0,4},{4,8},{8,12},{12,16},{16,20},{20,24},{24,28},{28,32},{32,36}... | collective-permute-start | bytes 1056776 | tf_op jit(solution)/shard_map/stream_2_step_2/ppermute | solution.py:180
  35.6 0.0 collective-permute-done.7.refs_9_
  35.6 3.1 %collective-permute-start.10 = (bf16[688,256]{1,0:T(8,128)(2,1)S(1)}, bf16[688,256]{1,0:T(8,128)(2,1)S(1)}, u32[]{:S(2)}, u32[]{:S(2)}) collective-permute-start(bf16[688,256]{1,0:T(8,128)(2,1)S(1)} %collective-permute-done.7.refs_9_), channel_id=1, source_target_pairs={{0,4},{4,8},{8,12},{12,16},{16,20},{20,24},{24,28},{28,32},{32,36}... | collective-permute-start | bytes 1056776 | tf_op jit(solution)/shard_map/stream_0_step_3/ppermute | solution.py:180
  38.7 0.1 collective-permute-done.6.refs_10_.refs_7_
  38.8 3.7 %collective-permute-start.9 = (bf16[688,256]{1,0:T(8,128)(2,1)S(1)}, bf16[688,256]{1,0:T(8,128)(2,1)S(1)}, u32[]{:S(2)}, u32[]{:S(2)}) collective-permute-start(bf16[688,256]{1,0:T(8,128)(2,1)S(1)} %collective-permute-done.6.refs_10_.refs_7_), channel_id=1, source_target_pairs={{0,4},{4,8},{8,12},{12,16},{16,20},{20,24},{24,28},{28,32},{32,36}... | collective-permute-start | bytes 1056776 | tf_op jit(solution)/shard_map/stream_1_step_3/ppermute | solution.py:180
  42.5 0.1 collective-permute-done.5.refs_8_
  42.6 0.0 collective-permute-done.1
  42.6 4.6 %collective-permute-start.8 = (bf16[1024,512]{1,0:T(8,128)(2,1)S(1)}, bf16[1024,512]{1,0:T(8,128)(2,1)S(1)}, u32[]{:S(2)}, u32[]{:S(2)}) collective-permute-start(bf16[1024,512]{1,0:T(8,128)(2,1)S(1)} %constant_dynamic-update-slice_fusion.refs_0_), channel_id=1, source_target_pairs={{0,128},{64,448},{128,256},{192,64},{256,384},{320,192},{384,0},{4... | collective-permute-start | bytes 3145736 | tf_op jit(solution)/shard_map/ppermute | solution.py:187
  47.3 3.7 %collective-permute-start.13 = (bf16[688,256]{1,0:T(8,128)(2,1)S(1)}, bf16[688,256]{1,0:T(8,128)(2,1)S(1)}, u32[]{:S(2)}, u32[]{:S(2)}) collective-permute-start(bf16[688,256]{1,0:T(8,128)(2,1)S(1)} %collective-permute-done.5.refs_8_), channel_id=1, source_target_pairs={{0,4},{4,8},{8,12},{12,16},{16,20},{20,24},{24,28},{28,32},{32,36}... | collective-permute-start | bytes 1056776 | tf_op jit(solution)/shard_map/stream_2_step_3/ppermute | solution.py:180
  51.0 0.0 collective-permute-done.10.refs_11_
  51.0 2.5 %collective-permute-start.12 = (bf16[688,256]{1,0:T(8,128)(2,1)S(1)}, bf16[688,256]{1,0:T(8,128)(2,1)S(1)}, u32[]{:S(2)}, u32[]{:S(2)}) collective-permute-start(bf16[688,256]{1,0:T(8,128)(2,1)S(1)} %collective-permute-done.10.refs_11_), channel_id=1, source_target_pairs={{0,4},{4,8},{8,12},{12,16},{16,20},{20,24},{24,28},{28,32},{32,36}... | collective-permute-start | bytes 1056776 | tf_op jit(solution)/shard_map/stream_0_step_4/ppermute | solution.py:180
  53.5 0.0 collective-permute-done.9.refs_12_.refs_9_
  53.5 2.6 %collective-permute-start.11 = (bf16[688,256]{1,0:T(8,128)(2,1)S(1)}, bf16[688,256]{1,0:T(8,128)(2,1)S(1)}, u32[]{:S(2)}, u32[]{:S(2)}) collective-permute-start(bf16[688,256]{1,0:T(8,128)(2,1)S(1)} %collective-permute-done.9.refs_12_.refs_9_), channel_id=1, source_target_pairs={{0,4},{4,8},{8,12},{12,16},{16,20},{20,24},{24,28},{28,32},{32,36}... | collective-permute-start | bytes 1056776 | tf_op jit(solution)/shard_map/stream_1_step_4/ppermute | solution.py:180
  56.2 0.0 collective-permute-done.13.refs_10_
  56.2 4.4 %collective-permute-start.16 = (bf16[688,256]{1,0:T(8,128)(2,1)S(1)}, bf16[688,256]{1,0:T(8,128)(2,1)S(1)}, u32[]{:S(2)}, u32[]{:S(2)}) collective-permute-start(bf16[688,256]{1,0:T(8,128)(2,1)S(1)} %collective-permute-done.13.refs_10_), channel_id=1, source_target_pairs={{0,4},{4,8},{8,12},{12,16},{16,20},{20,24},{24,28},{28,32},{32,36}... | collective-permute-start | bytes 1056776 | tf_op jit(solution)/shard_map/stream_2_step_4/ppermute | solution.py:180
  60.5 0.0 collective-permute-done.12.refs_13_
  60.6 3.8 %collective-permute-start.15 = (bf16[688,256]{1,0:T(8,128)(2,1)S(1)}, bf16[688,256]{1,0:T(8,128)(2,1)S(1)}, u32[]{:S(2)}, u32[]{:S(2)}) collective-permute-start(bf16[688,256]{1,0:T(8,128)(2,1)S(1)} %collective-permute-done.12.refs_13_), channel_id=1, source_target_pairs={{0,4},{4,8},{8,12},{12,16},{16,20},{20,24},{24,28},{28,32},{32,36}... | collective-permute-start | bytes 1056776 | tf_op jit(solution)/shard_map/stream_0_step_5/ppermute | solution.py:180
  64.3 0.0 collective-permute-done.11.refs_14_.refs_11_
  64.3 3.5 %collective-permute-start.14 = (bf16[688,256]{1,0:T(8,128)(2,1)S(1)}, bf16[688,256]{1,0:T(8,128)(2,1)S(1)}, u32[]{:S(2)}, u32[]{:S(2)}) collective-permute-start(bf16[688,256]{1,0:T(8,128)(2,1)S(1)} %collective-permute-done.11.refs_14_.refs_11_), channel_id=1, source_target_pairs={{0,4},{4,8},{8,12},{12,16},{16,20},{20,24},{24,28},{28,32},{32,36}... | collective-permute-start | bytes 1056776 | tf_op jit(solution)/shard_map/stream_1_step_5/ppermute | solution.py:180
  67.8 0.0 collective-permute-done.16.refs_12_
  67.8 3.8 %collective-permute-start.21 = (bf16[688,256]{1,0:T(8,128)(2,1)S(1)}, bf16[688,256]{1,0:T(8,128)(2,1)S(1)}, u32[]{:S(2)}, u32[]{:S(2)}) collective-permute-start(bf16[688,256]{1,0:T(8,128)(2,1)S(1)} %collective-permute-done.16.refs_12_), channel_id=1, source_target_pairs={{0,4},{4,8},{8,12},{12,16},{16,20},{20,24},{24,28},{28,32},{32,36}... | collective-permute-start | bytes 1056776 | tf_op jit(solution)/shard_map/stream_2_step_5/ppermute | solution.py:180
  71.6 2.3 %collective-permute-start.18 = (bf16[512,512]{1,0:T(8,128)(2,1)S(1)}, bf16[512,512]{1,0:T(8,128)(2,1)S(1)}, u32[]{:S(2)}, u32[]{:S(2)}) collective-permute-start(bf16[512,512]{1,0:T(8,128)(2,1)S(1)} %copy-done), channel_id=1, source_target_pairs={{0,256},{128,384},{256,0},{384,128},{1,257},{129,385},{257,1},{385... | collective-permute-start | bytes 1572872 | tf_op jit(solution)/shard_map/ppermute | solution.py:184
  73.8 0.0 collective-permute-done.15.refs_15_
  73.9 0.7 collective-permute-done.14.refs_16_.refs_13_
  74.5 0.0 collective-permute-done.8.refs_1_
  74.5 5.1 %collective-permute-start.17 = (bf16[1024,512]{1,0:T(8,128)(2,1)S(1)}, bf16[1024,512]{1,0:T(8,128)(2,1)S(1)}, u32[]{:S(2)}, u32[]{:S(2)}) collective-permute-start(bf16[1024,512]{1,0:T(8,128)(2,1)S(1)} %collective-permute-done.8.refs_1_), channel_id=1, source_target_pairs={{0,64},{64,0},{1,65},{65,1},{2,66},{66,2},{3,67},{67,3},{4,68},{68... | collective-permute-start | bytes 3145736 | tf_op jit(solution)/shard_map/ppermute | solution.py:191
  79.6 4.1 %collective-permute-start.20 = (bf16[688,256]{1,0:T(8,128)(2,1)S(1)}, bf16[688,256]{1,0:T(8,128)(2,1)S(1)}, u32[]{:S(2)}, u32[]{:S(2)}) collective-permute-start(bf16[688,256]{1,0:T(8,128)(2,1)S(1)} %collective-permute-done.15.refs_15_), channel_id=1, source_target_pairs={{0,4},{4,8},{8,12},{12,16},{16,20},{20,24},{24,28},{28,32},{32,36}... | collective-permute-start | bytes 1056776 | tf_op jit(solution)/shard_map/stream_0_step_6/ppermute | solution.py:180
  83.7 1.9 %collective-permute-start.24 = (bf16[688,256]{1,0:T(8,128)(2,1)S(1)}, bf16[688,256]{1,0:T(8,128)(2,1)S(1)}, u32[]{:S(2)}, u32[]{:S(2)}) collective-permute-start(bf16[688,256]{1,0:T(8,128)(2,1)S(1)} %collective-permute-done.14.refs_16_.refs_13_), channel_id=1, source_target_pairs={{0,4},{4,8},{8,12},{12,16},{16,20},{20,24},{24,28},{28,32},{32,36}... | collective-permute-start | bytes 1056776 | tf_op jit(solution)/shard_map/stream_1_step_6/ppermute | solution.py:180
  85.6 0.0 collective-permute-done.21.refs_14_
  85.7 1.9 %collective-permute-start.23 = (bf16[688,256]{1,0:T(8,128)(2,1)S(1)}, bf16[688,256]{1,0:T(8,128)(2,1)S(1)}, u32[]{:S(2)}, u32[]{:S(2)}) collective-permute-start(bf16[688,256]{1,0:T(8,128)(2,1)S(1)} %collective-permute-done.21.refs_14_), channel_id=1, source_target_pairs={{0,4},{4,8},{8,12},{12,16},{16,20},{20,24},{24,28},{28,32},{32,36}... | collective-permute-start | bytes 1056776 | tf_op jit(solution)/shard_map/stream_2_step_6/ppermute | solution.py:180
  87.6 0.4 collective-permute-done.18.refs_3_
  87.9 3.3 %collective-permute-start.19 = (bf16[512,512]{1,0:T(8,128)(2,1)S(1)}, bf16[512,512]{1,0:T(8,128)(2,1)S(1)}, u32[]{:S(2)}, u32[]{:S(2)}) collective-permute-start(bf16[512,512]{1,0:T(8,128)(2,1)S(1)} %collective-permute-done.18.refs_3_), channel_id=1, source_target_pairs={{0,64},{64,0},{1,65},{65,1},{2,66},{66,2},{3,67},{67,3},{4,68},{68... | collective-permute-start | bytes 1572872 | tf_op jit(solution)/shard_map/ppermute | solution.py:189
  91.3 0.0 collective-permute-done.20.refs_17_
  91.3 3.0 %collective-permute-start.22 = (bf16[688,256]{1,0:T(8,128)(2,1)S(1)}, bf16[688,256]{1,0:T(8,128)(2,1)S(1)}, u32[]{:S(2)}, u32[]{:S(2)}) collective-permute-start(bf16[688,256]{1,0:T(8,128)(2,1)S(1)} %collective-permute-done.20.refs_17_), channel_id=1, source_target_pairs={{0,4},{4,8},{8,12},{12,16},{16,20},{20,24},{24,28},{28,32},{32,36}... | collective-permute-start | bytes 1056776 | tf_op jit(solution)/shard_map/stream_0_step_7/ppermute | solution.py:180
  94.3 1.5 collective-permute-done.23.refs_16_
  95.9 4.7 %collective-permute-start.28 = (bf16[688,256]{1,0:T(8,128)(2,1)S(1)}, bf16[688,256]{1,0:T(8,128)(2,1)S(1)}, u32[]{:S(2)}, u32[]{:S(2)}) collective-permute-start(bf16[688,256]{1,0:T(8,128)(2,1)S(1)} %collective-permute-done.23.refs_16_), channel_id=1, source_target_pairs={{0,4},{4,8},{8,12},{12,16},{16,20},{20,24},{24,28},{28,32},{32,36}... | collective-permute-start | bytes 1056776 | tf_op jit(solution)/shard_map/stream_2_step_7/ppermute | solution.py:180
  100.5 1.9 %collective-permute-start.26 = (bf16[688,256]{1,0:T(8,128)(2,1)S(1)}, bf16[688,256]{1,0:T(8,128)(2,1)S(1)}, u32[]{:S(2)}, u32[]{:S(2)}) collective-permute-start(bf16[688,256]{1,0:T(8,128)(2,1)S(1)} %collective-permute-done.24.refs_18_.refs_15_), channel_id=1, source_target_pairs={{0,4},{4,8},{8,12},{12,16},{16,20},{20,24},{24,28},{28,32},{32,36}... | collective-permute-start | bytes 1056776 | tf_op jit(solution)/shard_map/stream_1_step_7/ppermute | solution.py:180
  102.5 2.3 %collective-permute-done.28.refs_18_ = bf16[688,256]{1,0:T(8,128)(2,1)S(1)} collective-permute-done((bf16[688,256]{1,0:T(8,128)(2,1)S(1)}, bf16[688,256]{1,0:T(8,128)(2,1)S(1)}, u32[]{:S(2)}, u32[]{:S(2)}) %collective-permute-start.28) | collective-permute-done | bytes 352288 | tf_op jit(solution)/shard_map/stream_2_step_7/ppermute | solution.py:180
  104.8 4.1 %collective-permute-done.26.refs_20_.refs_17_ = bf16[688,256]{1,0:T(8,128)(2,1)S(1)} collective-permute-done((bf16[688,256]{1,0:T(8,128)(2,1)S(1)}, bf16[688,256]{1,0:T(8,128)(2,1)S(1)}, u32[]{:S(2)}, u32[]{:S(2)}) %collective-permute-start.26) | collective-permute-done | bytes 352288 | tf_op jit(solution)/shard_map/stream_1_step_7/ppermute | solution.py:180
  108.9 2.7 %shard_map.75 = f32[1024,512]{1,0:T(8,128)S(1)} custom-call(bf16[1024,512]{1,0:T(8,128)(2,1)S(1)} %constant_dynamic-update-slice_fusion.refs_0_, bf16[1024,512]{1,0:T(8,128)(2,1)S(1)} %collective-permute-done.8.refs_1_, bf16[1024,512]{1,0:T(8,128)(2,1)S(1)} %collective-permute-done.17.refs_2_, bf16[512,512]{1,0:T(8,128)(2,1)S(1)} %collective-permute-done.18.refs_3_, ...), custom_call_target="tpu_custom_call" | custom-call | flops 1879048192 | bytes 2097152 | tf_op jit(solution)/shard_map/pallas_call | solution.py:148
  111.6 4.8 %collective-permute-start.29 = (f32[1024,512]{1,0:T(8,128)S(1)}, f32[1024,512]{1,0:T(8,128)S(1)}, u32[]{:S(2)}, u32[]{:S(2)}) collective-permute-start(f32[1024,512]{1,0:T(8,128)S(1)} %shard_map.75), channel_id=1, source_target_pairs={{0,64},{64,0},{1,65},{65,1},{2,66},{66,2},{3,67},{67,3},{4,68},{68... | collective-permute-start | bytes 6291464 | tf_op jit(solution)/shard_map/ppermute | solution.py:196
  116.4 1.9 %collective-permute-start.25 = (bf16[688,256]{1,0:T(8,128)(2,1)S(1)}, bf16[688,256]{1,0:T(8,128)(2,1)S(1)}, u32[]{:S(2)}, u32[]{:S(2)}) collective-permute-start(bf16[688,256]{1,0:T(8,128)(2,1)S(1)} %collective-permute-done.22.refs_19_), channel_id=1, source_target_pairs={{0,4},{4,8},{8,12},{12,16},{16,20},{20,24},{24,28},{28,32},{32,36}... | collective-permute-start | bytes 1056776 | tf_op jit(solution)/shard_map/stream_0_step_8/ppermute | solution.py:180
  118.3 1.9 %collective-permute-start.27 = (bf16[336,256]{1,0:T(8,128)(2,1)S(1)}, bf16[336,256]{1,0:T(8,128)(2,1)S(1)}, u32[]{:S(2)}, u32[]{:S(2)}) collective-permute-start(bf16[336,256]{1,0:T(8,128)(2,1)S(1)} %slice.22), channel_id=1, source_target_pairs={{0,4},{4,8},{8,12},{12,16},{16,20},{20,24},{24,28},{28,32},{32,36}... | collective-permute-start | bytes 516104 | tf_op jit(solution)/shard_map/stream_1_step_8/ppermute | solution.py:180
  120.3 3.3 %shard_map.74.refs_7_ = f32[1024,512]{1,0:T(8,128)S(1)} custom-call(bf16[1024,512]{1,0:T(8,128)(2,1)S(1)} %constant_dynamic-update-slice_fusion.refs_0_, bf16[1024,512]{1,0:T(8,128)(2,1)S(1)} %collective-permute-done.8.refs_1_, bf16[1024,512]{1,0:T(8,128)(2,1)S(1)} %collective-permute-done.17.refs_2_, bf16[512,512]{1,0:T(8,128)(2,1)S(1)} %collective-permute-done.18.refs_3_, ...), custom_call_target="tpu_custom_call" | custom-call | flops 2147483648 | bytes 2097152 | tf_op jit(solution)/shard_map/pallas_call | solution.py:148
  123.6 1.2 collective-permute-done.25.refs_5_
  124.8 1.8 %collective-permute-done.27.refs_6_ = bf16[336,256]{1,0:T(8,128)(2,1)S(1)} collective-permute-done((bf16[336,256]{1,0:T(8,128)(2,1)S(1)}, bf16[336,256]{1,0:T(8,128)(2,1)S(1)}, u32[]{:S(2)}, u32[]{:S(2)}) %collective-permute-start.27) | collective-permute-done | bytes 172064 | tf_op jit(solution)/shard_map/stream_1_step_8/ppermute | solution.py:180
  126.6 0.0 collective-permute-done.29.refs_8_
  126.6 1.1 shard_map.76
  127.8 27.8 %all_to_all.5.in_hbm = f32[4,256,512]{2,1,0:T(8,128)S(1)} all-to-all(f32[4,256,512]{2,1,0:T(8,128)S(1)} %bitcast.2), channel_id=1, replica_groups=mesh['y'=4,'core'=2,'col'=16,'layer'=4] {'layer'}, dimensions={0} | all-to-all | bytes 4194304 | tf_op jit(solution)/shard_map/all_to_all | solution.py:201
  155.6 1.0 shard_map.77
  (12 shorter events, 0.2 us)
Async XLA Ops:
  2.4 22.0 %copy-start = (bf16[512,512]{1,0:T(8,128)(2,1)S(1)}, bf16[512,512]{1,0:T(8,128)(2,1)}, u32[]{:S(2)}) copy-start(bf16[512,512]{1,0:T(8,128)(2,1)} %get-tuple-element.57) | copy-start | bytes 1572868
  2.4 16.6 %collective-permute-start = (bf16[1024,256]{1,0:T(8,128)(2,1)}, bf16[1024,256]{1,0:T(8,128)(2,1)S(1)}, u32[]{:S(2)}, u32[]{:S(2)}) collective-permute-start(bf16[1024,256]{1,0:T(8,128)(2,1)} %get-tuple-element.37), channel_id=1, source_target_pairs={{0,64},{64,0},{1,65},{65,1},{2,66},{66,2},{3,67},{67,3},{4,68},{68... | collective-permute-start | bytes 1572872 | tf_op jit(solution)/shard_map/ppermute | solution.py:142
  12.4 14.0 %collective-permute-start.4 = (bf16[688,256]{1,0:T(8,128)(2,1)S(1)}, bf16[688,256]{1,0:T(8,128)(2,1)S(1)}, u32[]{:S(2)}, u32[]{:S(2)}) collective-permute-start(bf16[688,256]{1,0:T(8,128)(2,1)S(1)} %slice.18.refs_5_), channel_id=1, source_target_pairs={{0,4},{4,8},{8,12},{12,16},{16,20},{20,24},{24,28},{28,32},{32,36}... | collective-permute-start | bytes 1056776 | tf_op jit(solution)/shard_map/stream_0_step_1/ppermute | solution.py:141
  19.1 9.9 %collective-permute-start.3 = (bf16[688,256]{1,0:T(8,128)(2,1)S(1)}, bf16[688,256]{1,0:T(8,128)(2,1)S(1)}, u32[]{:S(2)}, u32[]{:S(2)}) collective-permute-start(bf16[688,256]{1,0:T(8,128)(2,1)S(1)} %pad_maximum_fusion.refs_6_), channel_id=1, source_target_pairs={{0,4},{4,8},{8,12},{12,16},{16,20},{20,24},{24,28},{28,32},{32,36}... | collective-permute-start | bytes 1056776 | tf_op jit(solution)/shard_map/stream_1_step_1/ppermute | solution.py:180
  21.8 11.1 %collective-permute-start.2 = (bf16[688,256]{1,0:T(8,128)(2,1)S(1)}, bf16[688,256]{1,0:T(8,128)(2,1)S(1)}, u32[]{:S(2)}, u32[]{:S(2)}) collective-permute-start(bf16[688,256]{1,0:T(8,128)(2,1)S(1)} %slice.20), channel_id=1, source_target_pairs={{0,4},{4,8},{8,12},{12,16},{16,20},{20,24},{24,28},{28,32},{32,36}... | collective-permute-start | bytes 1056776 | tf_op jit(solution)/shard_map/stream_2_step_1/ppermute | solution.py:180
  24.4 18.1 %collective-permute-start.1 = (bf16[512,512]{1,0:T(8,128)(2,1)S(1)}, bf16[512,512]{1,0:T(8,128)(2,1)S(1)}, u32[]{:S(2)}, u32[]{:S(2)}) collective-permute-start(bf16[512,512]{1,0:T(8,128)(2,1)S(1)} %copy-done), channel_id=1, source_target_pairs={{0,64},{64,0},{1,65},{65,1},{2,66},{66,2},{3,67},{67,3},{4,68},{68... | collective-permute-start | bytes 1572872 | tf_op jit(solution)/shard_map/ppermute | solution.py:182
  26.4 9.2 %collective-permute-start.7 = (bf16[688,256]{1,0:T(8,128)(2,1)S(1)}, bf16[688,256]{1,0:T(8,128)(2,1)S(1)}, u32[]{:S(2)}, u32[]{:S(2)}) collective-permute-start(bf16[688,256]{1,0:T(8,128)(2,1)S(1)} %collective-permute-done.4.refs_7_), channel_id=1, source_target_pairs={{0,4},{4,8},{8,12},{12,16},{16,20},{20,24},{24,28},{28,32},{32,36}... | collective-permute-start | bytes 1056776 | tf_op jit(solution)/shard_map/stream_0_step_2/ppermute | solution.py:180
  29.0 9.8 %collective-permute-start.6 = (bf16[688,256]{1,0:T(8,128)(2,1)S(1)}, bf16[688,256]{1,0:T(8,128)(2,1)S(1)}, u32[]{:S(2)}, u32[]{:S(2)}) collective-permute-start(bf16[688,256]{1,0:T(8,128)(2,1)S(1)} %collective-permute-done.3.refs_8_.refs_5_), channel_id=1, source_target_pairs={{0,4},{4,8},{8,12},{12,16},{16,20},{20,24},{24,28},{28,32},{32,36}... | collective-permute-start | bytes 1056776 | tf_op jit(solution)/shard_map/stream_1_step_2/ppermute | solution.py:180
  32.9 9.7 %collective-permute-start.5 = (bf16[688,256]{1,0:T(8,128)(2,1)S(1)}, bf16[688,256]{1,0:T(8,128)(2,1)S(1)}, u32[]{:S(2)}, u32[]{:S(2)}) collective-permute-start(bf16[688,256]{1,0:T(8,128)(2,1)S(1)} %collective-permute-done.2.refs_6_), channel_id=1, source_target_pairs={{0,4},{4,8},{8,12},{12,16},{16,20},{20,24},{24,28},{28,32},{32,36}... | collective-permute-start | bytes 1056776 | tf_op jit(solution)/shard_map/stream_2_step_2/ppermute | solution.py:180
  35.6 15.4 %collective-permute-start.10 = (bf16[688,256]{1,0:T(8,128)(2,1)S(1)}, bf16[688,256]{1,0:T(8,128)(2,1)S(1)}, u32[]{:S(2)}, u32[]{:S(2)}) collective-permute-start(bf16[688,256]{1,0:T(8,128)(2,1)S(1)} %collective-permute-done.7.refs_9_), channel_id=1, source_target_pairs={{0,4},{4,8},{8,12},{12,16},{16,20},{20,24},{24,28},{28,32},{32,36}... | collective-permute-start | bytes 1056776 | tf_op jit(solution)/shard_map/stream_0_step_3/ppermute | solution.py:180
  38.8 14.7 %collective-permute-start.9 = (bf16[688,256]{1,0:T(8,128)(2,1)S(1)}, bf16[688,256]{1,0:T(8,128)(2,1)S(1)}, u32[]{:S(2)}, u32[]{:S(2)}) collective-permute-start(bf16[688,256]{1,0:T(8,128)(2,1)S(1)} %collective-permute-done.6.refs_10_.refs_7_), channel_id=1, source_target_pairs={{0,4},{4,8},{8,12},{12,16},{16,20},{20,24},{24,28},{28,32},{32,36}... | collective-permute-start | bytes 1056776 | tf_op jit(solution)/shard_map/stream_1_step_3/ppermute | solution.py:180
  42.6 31.9 %collective-permute-start.8 = (bf16[1024,512]{1,0:T(8,128)(2,1)S(1)}, bf16[1024,512]{1,0:T(8,128)(2,1)S(1)}, u32[]{:S(2)}, u32[]{:S(2)}) collective-permute-start(bf16[1024,512]{1,0:T(8,128)(2,1)S(1)} %constant_dynamic-update-slice_fusion.refs_0_), channel_id=1, source_target_pairs={{0,128},{64,448},{128,256},{192,64},{256,384},{320,192},{384,0},{4... | collective-permute-start | bytes 3145736 | tf_op jit(solution)/shard_map/ppermute | solution.py:187
  47.3 8.9 %collective-permute-start.13 = (bf16[688,256]{1,0:T(8,128)(2,1)S(1)}, bf16[688,256]{1,0:T(8,128)(2,1)S(1)}, u32[]{:S(2)}, u32[]{:S(2)}) collective-permute-start(bf16[688,256]{1,0:T(8,128)(2,1)S(1)} %collective-permute-done.5.refs_8_), channel_id=1, source_target_pairs={{0,4},{4,8},{8,12},{12,16},{16,20},{20,24},{24,28},{28,32},{32,36}... | collective-permute-start | bytes 1056776 | tf_op jit(solution)/shard_map/stream_2_step_3/ppermute | solution.py:180
  51.0 9.6 %collective-permute-start.12 = (bf16[688,256]{1,0:T(8,128)(2,1)S(1)}, bf16[688,256]{1,0:T(8,128)(2,1)S(1)}, u32[]{:S(2)}, u32[]{:S(2)}) collective-permute-start(bf16[688,256]{1,0:T(8,128)(2,1)S(1)} %collective-permute-done.10.refs_11_), channel_id=1, source_target_pairs={{0,4},{4,8},{8,12},{12,16},{16,20},{20,24},{24,28},{28,32},{32,36}... | collective-permute-start | bytes 1056776 | tf_op jit(solution)/shard_map/stream_0_step_4/ppermute | solution.py:180
  53.5 10.8 %collective-permute-start.11 = (bf16[688,256]{1,0:T(8,128)(2,1)S(1)}, bf16[688,256]{1,0:T(8,128)(2,1)S(1)}, u32[]{:S(2)}, u32[]{:S(2)}) collective-permute-start(bf16[688,256]{1,0:T(8,128)(2,1)S(1)} %collective-permute-done.9.refs_12_.refs_9_), channel_id=1, source_target_pairs={{0,4},{4,8},{8,12},{12,16},{16,20},{20,24},{24,28},{28,32},{32,36}... | collective-permute-start | bytes 1056776 | tf_op jit(solution)/shard_map/stream_1_step_4/ppermute | solution.py:180
  56.2 11.6 %collective-permute-start.16 = (bf16[688,256]{1,0:T(8,128)(2,1)S(1)}, bf16[688,256]{1,0:T(8,128)(2,1)S(1)}, u32[]{:S(2)}, u32[]{:S(2)}) collective-permute-start(bf16[688,256]{1,0:T(8,128)(2,1)S(1)} %collective-permute-done.13.refs_10_), channel_id=1, source_target_pairs={{0,4},{4,8},{8,12},{12,16},{16,20},{20,24},{24,28},{28,32},{32,36}... | collective-permute-start | bytes 1056776 | tf_op jit(solution)/shard_map/stream_2_step_4/ppermute | solution.py:180
  60.6 13.3 %collective-permute-start.15 = (bf16[688,256]{1,0:T(8,128)(2,1)S(1)}, bf16[688,256]{1,0:T(8,128)(2,1)S(1)}, u32[]{:S(2)}, u32[]{:S(2)}) collective-permute-start(bf16[688,256]{1,0:T(8,128)(2,1)S(1)} %collective-permute-done.12.refs_13_), channel_id=1, source_target_pairs={{0,4},{4,8},{8,12},{12,16},{16,20},{20,24},{24,28},{28,32},{32,36}... | collective-permute-start | bytes 1056776 | tf_op jit(solution)/shard_map/stream_0_step_5/ppermute | solution.py:180
  64.3 10.2 %collective-permute-start.14 = (bf16[688,256]{1,0:T(8,128)(2,1)S(1)}, bf16[688,256]{1,0:T(8,128)(2,1)S(1)}, u32[]{:S(2)}, u32[]{:S(2)}) collective-permute-start(bf16[688,256]{1,0:T(8,128)(2,1)S(1)} %collective-permute-done.11.refs_14_.refs_11_), channel_id=1, source_target_pairs={{0,4},{4,8},{8,12},{12,16},{16,20},{20,24},{24,28},{28,32},{32,36}... | collective-permute-start | bytes 1056776 | tf_op jit(solution)/shard_map/stream_1_step_5/ppermute | solution.py:180
  67.8 17.8 %collective-permute-start.21 = (bf16[688,256]{1,0:T(8,128)(2,1)S(1)}, bf16[688,256]{1,0:T(8,128)(2,1)S(1)}, u32[]{:S(2)}, u32[]{:S(2)}) collective-permute-start(bf16[688,256]{1,0:T(8,128)(2,1)S(1)} %collective-permute-done.16.refs_12_), channel_id=1, source_target_pairs={{0,4},{4,8},{8,12},{12,16},{16,20},{20,24},{24,28},{28,32},{32,36}... | collective-permute-start | bytes 1056776 | tf_op jit(solution)/shard_map/stream_2_step_5/ppermute | solution.py:180
  71.6 16.4 %collective-permute-start.18 = (bf16[512,512]{1,0:T(8,128)(2,1)S(1)}, bf16[512,512]{1,0:T(8,128)(2,1)S(1)}, u32[]{:S(2)}, u32[]{:S(2)}) collective-permute-start(bf16[512,512]{1,0:T(8,128)(2,1)S(1)} %copy-done), channel_id=1, source_target_pairs={{0,256},{128,384},{256,0},{384,128},{1,257},{129,385},{257,1},{385... | collective-permute-start | bytes 1572872 | tf_op jit(solution)/shard_map/ppermute | solution.py:184
  74.5 34.4 %collective-permute-start.17 = (bf16[1024,512]{1,0:T(8,128)(2,1)S(1)}, bf16[1024,512]{1,0:T(8,128)(2,1)S(1)}, u32[]{:S(2)}, u32[]{:S(2)}) collective-permute-start(bf16[1024,512]{1,0:T(8,128)(2,1)S(1)} %collective-permute-done.8.refs_1_), channel_id=1, source_target_pairs={{0,64},{64,0},{1,65},{65,1},{2,66},{66,2},{3,67},{67,3},{4,68},{68... | collective-permute-start | bytes 3145736 | tf_op jit(solution)/shard_map/ppermute | solution.py:191
  79.6 11.7 %collective-permute-start.20 = (bf16[688,256]{1,0:T(8,128)(2,1)S(1)}, bf16[688,256]{1,0:T(8,128)(2,1)S(1)}, u32[]{:S(2)}, u32[]{:S(2)}) collective-permute-start(bf16[688,256]{1,0:T(8,128)(2,1)S(1)} %collective-permute-done.15.refs_15_), channel_id=1, source_target_pairs={{0,4},{4,8},{8,12},{12,16},{16,20},{20,24},{24,28},{28,32},{32,36}... | collective-permute-start | bytes 1056776 | tf_op jit(solution)/shard_map/stream_0_step_6/ppermute | solution.py:180
  83.7 10.6 %collective-permute-start.24 = (bf16[688,256]{1,0:T(8,128)(2,1)S(1)}, bf16[688,256]{1,0:T(8,128)(2,1)S(1)}, u32[]{:S(2)}, u32[]{:S(2)}) collective-permute-start(bf16[688,256]{1,0:T(8,128)(2,1)S(1)} %collective-permute-done.14.refs_16_.refs_13_), channel_id=1, source_target_pairs={{0,4},{4,8},{8,12},{12,16},{16,20},{20,24},{24,28},{28,32},{32,36}... | collective-permute-start | bytes 1056776 | tf_op jit(solution)/shard_map/stream_1_step_6/ppermute | solution.py:180
  85.7 10.2 %collective-permute-start.23 = (bf16[688,256]{1,0:T(8,128)(2,1)S(1)}, bf16[688,256]{1,0:T(8,128)(2,1)S(1)}, u32[]{:S(2)}, u32[]{:S(2)}) collective-permute-start(bf16[688,256]{1,0:T(8,128)(2,1)S(1)} %collective-permute-done.21.refs_14_), channel_id=1, source_target_pairs={{0,4},{4,8},{8,12},{12,16},{16,20},{20,24},{24,28},{28,32},{32,36}... | collective-permute-start | bytes 1056776 | tf_op jit(solution)/shard_map/stream_2_step_6/ppermute | solution.py:180
  87.9 21.0 %collective-permute-start.19 = (bf16[512,512]{1,0:T(8,128)(2,1)S(1)}, bf16[512,512]{1,0:T(8,128)(2,1)S(1)}, u32[]{:S(2)}, u32[]{:S(2)}) collective-permute-start(bf16[512,512]{1,0:T(8,128)(2,1)S(1)} %collective-permute-done.18.refs_3_), channel_id=1, source_target_pairs={{0,64},{64,0},{1,65},{65,1},{2,66},{66,2},{3,67},{67,3},{4,68},{68... | collective-permute-start | bytes 1572872 | tf_op jit(solution)/shard_map/ppermute | solution.py:189
  91.3 11.2 %collective-permute-start.22 = (bf16[688,256]{1,0:T(8,128)(2,1)S(1)}, bf16[688,256]{1,0:T(8,128)(2,1)S(1)}, u32[]{:S(2)}, u32[]{:S(2)}) collective-permute-start(bf16[688,256]{1,0:T(8,128)(2,1)S(1)} %collective-permute-done.20.refs_17_), channel_id=1, source_target_pairs={{0,4},{4,8},{8,12},{12,16},{16,20},{20,24},{24,28},{28,32},{32,36}... | collective-permute-start | bytes 1056776 | tf_op jit(solution)/shard_map/stream_0_step_7/ppermute | solution.py:180
  95.9 8.9 %collective-permute-start.28 = (bf16[688,256]{1,0:T(8,128)(2,1)S(1)}, bf16[688,256]{1,0:T(8,128)(2,1)S(1)}, u32[]{:S(2)}, u32[]{:S(2)}) collective-permute-start(bf16[688,256]{1,0:T(8,128)(2,1)S(1)} %collective-permute-done.23.refs_16_), channel_id=1, source_target_pairs={{0,4},{4,8},{8,12},{12,16},{16,20},{20,24},{24,28},{28,32},{32,36}... | collective-permute-start | bytes 1056776 | tf_op jit(solution)/shard_map/stream_2_step_7/ppermute | solution.py:180
  100.5 8.4 %collective-permute-start.26 = (bf16[688,256]{1,0:T(8,128)(2,1)S(1)}, bf16[688,256]{1,0:T(8,128)(2,1)S(1)}, u32[]{:S(2)}, u32[]{:S(2)}) collective-permute-start(bf16[688,256]{1,0:T(8,128)(2,1)S(1)} %collective-permute-done.24.refs_18_.refs_15_), channel_id=1, source_target_pairs={{0,4},{4,8},{8,12},{12,16},{16,20},{20,24},{24,28},{28,32},{32,36}... | collective-permute-start | bytes 1056776 | tf_op jit(solution)/shard_map/stream_1_step_7/ppermute | solution.py:180
  111.6 15.0 %collective-permute-start.29 = (f32[1024,512]{1,0:T(8,128)S(1)}, f32[1024,512]{1,0:T(8,128)S(1)}, u32[]{:S(2)}, u32[]{:S(2)}) collective-permute-start(f32[1024,512]{1,0:T(8,128)S(1)} %shard_map.75), channel_id=1, source_target_pairs={{0,64},{64,0},{1,65},{65,1},{2,66},{66,2},{3,67},{67,3},{4,68},{68... | collective-permute-start | bytes 6291464 | tf_op jit(solution)/shard_map/ppermute | solution.py:196
  116.4 8.4 %collective-permute-start.25 = (bf16[688,256]{1,0:T(8,128)(2,1)S(1)}, bf16[688,256]{1,0:T(8,128)(2,1)S(1)}, u32[]{:S(2)}, u32[]{:S(2)}) collective-permute-start(bf16[688,256]{1,0:T(8,128)(2,1)S(1)} %collective-permute-done.22.refs_19_), channel_id=1, source_target_pairs={{0,4},{4,8},{8,12},{12,16},{16,20},{20,24},{24,28},{28,32},{32,36}... | collective-permute-start | bytes 1056776 | tf_op jit(solution)/shard_map/stream_0_step_8/ppermute | solution.py:180
  118.3 8.3 %collective-permute-start.27 = (bf16[336,256]{1,0:T(8,128)(2,1)S(1)}, bf16[336,256]{1,0:T(8,128)(2,1)S(1)}, u32[]{:S(2)}, u32[]{:S(2)}) collective-permute-start(bf16[336,256]{1,0:T(8,128)(2,1)S(1)} %slice.22), channel_id=1, source_target_pairs={{0,4},{4,8},{8,12},{12,16},{16,20},{20,24},{24,28},{28,32},{32,36}... | collective-permute-start | bytes 516104 | tf_op jit(solution)/shard_map/stream_1_step_8/ppermute | solution.py:180

commit v4 on v3

--- a/solution.py
+++ b/solution.py
@@ -10,8 +10,6 @@
 BS = 256
 CORES = 2
 ROWS = 1024
-CUT = 688
-SPARE = 3 * CUT - 2 * ROWS
 HBM = pl.BlockSpec(memory_space=pl.ANY)
 VMEM = pl.BlockSpec(memory_space=pltpu.VMEM)
 PARAMS = pltpu.CompilerParams(vmem_limit_bytes=40 * 1024 * 1024)
@@ -49,9 +47,9 @@
             b_out[place] = masked(b[(0,) + place], size, cols[n])
 
 
-def product_kernel(steps, own, blocks, added, *refs):
+def product_kernel(steps, blocks, added, *refs):
     b_refs, refs = refs[:5], refs[5:]
-    a_refs, refs = refs[: 2 * len(steps)], refs[2 * len(steps) :]
+    a_refs, refs = refs[: len(steps)], refs[len(steps) :]
     adds, (out_ref, a_all, b_all, extra, sems) = refs[:added], refs[added:]
     z, y, core = lax.axis_index("col"), lax.axis_index("y"), lax.axis_index("core")
     way = 2 * core - 1
@@ -75,18 +73,8 @@
                     ref.at[pl.ds(start, BS)], b_all.at[step - first], sems.at[0]
                 ).start()
 
-    for i in range(count):
-        upper, lower = a_refs[2 * i], a_refs[2 * i + 1]
-        lanes = pl.ds(i * BS, BS)
-        if own:
-            pieces = ((upper, 0, 0, CUT), (lower, 0, CUT, ROWS - CUT))
-        else:
-            done = 2 * CUT - ROWS
-            pieces = ((upper, ROWS - CUT, 0, done), (lower, SPARE, done, ROWS - done))
-        for ref, start, to, size in pieces:
-            pltpu.make_async_copy(
-                ref.at[pl.ds(start, size)], a_all.at[pl.ds(to, size), lanes], sems.at[1]
-            ).start()
+    for i, ref in enumerate(a_refs):
+        pltpu.make_async_copy(ref, a_all.at[:, pl.ds(i * BS, BS)], sems.at[1]).start()
     for i, ref in enumerate(adds):
         pltpu.make_async_copy(ref, extra.at[i], sems.at[2 + i]).start()
     pltpu.make_async_copy(b_all, b_all, sems.at[0]).wait()
@@ -135,18 +123,12 @@
     )(*args)
 
     last = cols // 2
-    held = [[own[:CUT]], [], []]
-    sent = held[0][0]
-    with jax.named_scope("stream_0_step_1"):
-        held[0].append(lax.ppermute(sent, ("core", "col"), ring))
-    other = lax.ppermute(own, "core", SWAP)
-    held[1] = [jnp.concatenate([own[CUT:], other[: 2 * CUT - ROWS]])]
-    held[2] = [other[ROWS - CUT :]]
-    def product(steps, own, pairs, adds=()):
+    held = [[own], [lax.ppermute(own, "core", SWAP)]]
+
+    def product(steps, arrays, adds=()):
         n = len(steps)
-        arrays = [a for pair in pairs for a in pair]
         return pl.pallas_call(
-            functools.partial(product_kernel, steps, own, cols, len(adds)),
+            functools.partial(product_kernel, steps, cols, len(adds)),
             out_shape=jax.ShapeDtypeStruct((ROWS, width), jnp.float32),
             in_specs=[HBM] * (5 + len(arrays) + len(adds)),
             out_specs=VMEM,
@@ -167,36 +149,36 @@
     ]
     far_away = [(i, (i + 2) % chips) for i in range(chips)]
     b_all = [None] * 5
-    b_other = None
+    b_other = others = None
     for step in range(1, last + 1):
-        for j in range(3):
-            if (step, j) == (1, 0) or (step, j) == (last, 2):
+        for j in range(2):
+            if (step, j) == (last, 1):
                 continue
-            value = held[j][-1]
-            if (step, j) == (last, 1):
-                value = value[: ROWS - CUT]
-            sent = after(value, sent)
+            sent = held[j][-1]
+            if step == last:
+                shards = held[1][1 : last - 1]
+                shards[-1] = after(shards[-1], sent)
+                others = product(range(1, last - 1), shards)
+                sent = after(sent, others)
             with jax.named_scope(f"stream_{j}_step_{step}"):
                 held[j].append(lax.ppermute(sent, ("core", "col"), ring))
-            if (step, j) == (1, 2):
-                b_other = lax.ppermute(after(b_eff, sent), "core", SWAP)
-            if (step, j) == (2, 0):
-                b_all[3] = lax.ppermute(after(b_eff, sent), "y", far_away)
-            if (step, j) == (3, 2):
+            if (step, j) == (1, 1):
+                b_other = lax.ppermute(after(b_eff, own), "core", SWAP)
+            if (step, j) == (2, 1):
                 b_all[0] = jnp.concatenate([b_eff, after(b_other, sent)])
                 b_all[1] = lax.ppermute(b_all[0], ("y", "core"), near_by)
-            if (step, j) == (6, 0):
+            if (step, j) == (3, 1):
+                b_all[3] = lax.ppermute(after(b_eff, sent), "y", far_away)
+            if (step, j) == (5, 1):
+                b_all[2] = lax.ppermute(after(b_all[1], sent), "core", SWAP)
+            if (step, j) == (6, 1):
                 b_all[4] = lax.ppermute(after(b_all[3], sent), "core", SWAP)
-            if (step, j) == (6, 1):
-                b_all[2] = lax.ppermute(after(b_all[1], sent), "core", SWAP)
-
-    steps = range(1, last)
-    pairs = [(held[1][s], held[2][s]) for s in steps]
-    pairs[-1] = after(pairs[-1], held[0][last - 1])
-    others = lax.ppermute(product(steps, False, pairs), "core", SWAP)
-    steps = range(last)
-    mine = product(steps, True, [(held[0][s], held[1][s]) for s in steps])
-    parts = product((last,), True, [(held[0][last], held[1][last])], (mine, others))
+
+    others = product((last - 1,), held[1][last - 1 :], (others,))
+    others = lax.ppermute(others, "core", SWAP)
+    mine = product(range(last - 1), held[0][: last - 1])
+    mine = product((last - 1,), held[0][last - 1 : last], (mine,))
+    parts = product((last,), held[0][last:], (mine, others))
     parts = parts.reshape(-1, BS, width)
     parts = lax.all_to_all(parts, "layer", 0, 0)
     return pl.pallas_call(

time: 159 us -> 149 us (0.937)
  starting transfers between devices: 103 us -> 90.5 us
  waiting for transfers between devices: 12.3 us -> 16.1 us
    ppermute x22 -> x15, starting transfers between devices: 66.7 us -> 59.3 us  [on_device(): held[j].append(lax.ppermute(sent, ('core', 'col'), ring))]
    ppermute x4 -> x3, starting transfers between devices: 21.4 us -> 15.7 us  [the longest x1 8.92 us: on_device(): held = [[own], [lax.ppermute(own, 'core', SWAP)]]]
    ppermute x22 -> x15, waiting for transfers between devices: 11.9 us -> 16.1 us  [on_device(): held[j].append(lax.ppermute(sent, ('core', 'col'), ring))]
    slice x5 -> x0, local copies, waits for them, and re-layouts: 1.99 us -> none  [the longest x1 1.01 us: on_device(): held = [[own[:CUT]], [], []]]
    pallas_call x3 -> x5, Pallas kernels: 7.11 us -> 7.51 us  [product(): pl.pallas_call(functools.partial(product_kernel, steps, cols, len(adds)),...]
  transfers between devices with their start and end apart: 30 -> 22, of which waited for: 9 -> 6; matrix products, arithmetic and copies ran while one was open for 1% -> 1% of each run, Pallas kernels for 2% -> 4%
where the time goes in v4:
time: 149 us; the launch traced here: 147 us
  starting transfers between devices  90.5 us (61%)
  blocking collectives  27.8 us (19%)
  waiting for transfers between devices  16.1 us (11%)
  Pallas kernels  11 us (7%)
    ppermute x15, starting transfers between devices, on_device(): held[j].append(lax.ppermute(sent, ('core', 'col'), ring))  59.3 us
    all_to_all x1, blocking collectives, on_device(): parts = lax.all_to_all(parts, 'layer', 0, 0)  27.8 us
    ppermute x15, waiting for transfers between devices, on_device(): held[j].append(lax.ppermute(sent, ('core', 'col'), ring))  16.1 us
    ppermute x1, starting transfers between devices, on_device(): held = [[own], [lax.ppermute(own, 'core', SWAP)]]  8.92 us
    pallas_call x5, Pallas kernels, product(): pl.pallas_call(functools.partial(product_kernel, steps, cols, len(adds)),...  7.51 us
    ppermute x1, starting transfers between devices, on_device(): others = lax.ppermute(others, 'core', SWAP)  4.89 us
    ppermute x1, starting transfers between devices, on_device(): b_all[1] = lax.ppermute(b_all[0], ('y', 'core'), near_by)  4.64 us
    ppermute x1, starting transfers between devices, on_device(): b_all[4] = lax.ppermute(after(b_all[3], sent), 'core', SWAP)  3.72 us
  transfers between devices with their start and end apart: 22, of which 6 were waited for; matrix products, arithmetic and copies ran while one was open for 1% of the time, Pallas kernels for 4%

profile of v4, /device:TPU:1, one launch (start us, length us, event | category | flops | bytes accessed | tf_op | source)
XLA Modules:
  0.0 146.9 jit_solution(11201753149954534521)
XLA Ops:
  0.0 2.4 %shard_map.73 = (bf16[1024,256]{1,0:T(8,128)(2,1)}, bf16[512,512]{1,0:T(8,128)(2,1)}) custom-call(s32[4]{0:T(128)} %bitcast.3, s32[1,2,2]{2,1,0:T(2,128)} %refs_1_.1, s32[4]{0:T(128)} %refs_2_.1, s32[1,16]{1,0:T(1,128)} %refs_3_.1, s32[2]{0:T(128)} %refs_4_.1, bf16[1,1024,256]{2,1,0:T(8,128)(2,1)} %refs_5_.1, bf16[1,512,512]{2,1,0:T(8,128)(2,1)} %refs_6_.1), custom_call_target="tpu_custom_call" | custom-call | tf_op jit(solution)/shard_map/pallas_call | solution.py:112
  2.4 0.0 copy-start.1
  2.4 8.9 %collective-permute-start.1 = (bf16[1024,256]{1,0:T(8,128)(2,1)}, bf16[1024,256]{1,0:T(8,128)(2,1)S(1)}, u32[]{:S(2)}, u32[]{:S(2)}) collective-permute-start(bf16[1024,256]{1,0:T(8,128)(2,1)} %get-tuple-element.15.refs_5_), channel_id=1, source_target_pairs={{0,64},{64,0},{1,65},{65,1},{2,66},{66,2},{3,67},{67,3},{4,68},{68... | collective-permute-start | bytes 1572872 | tf_op jit(solution)/shard_map/ppermute | solution.py:126
  11.3 5.7 %collective-permute-start.11 = (bf16[1024,256]{1,0:T(8,128)(2,1)}, bf16[1024,256]{1,0:T(8,128)(2,1)S(1)}, u32[]{:S(2)}, u32[]{:S(2)}) collective-permute-start(bf16[1024,256]{1,0:T(8,128)(2,1)} %get-tuple-element.15.refs_5_), channel_id=1, source_target_pairs={{0,4},{4,8},{8,12},{12,16},{16,20},{20,24},{24,28},{28,32},{32,36}... | collective-permute-start | bytes 1572872 | tf_op jit(solution)/shard_map/stream_0_step_1/ppermute | solution.py:164
  17.1 0.0 collective-permute-done.1
  17.1 2.6 %collective-permute-start.2 = (bf16[1024,256]{1,0:T(8,128)(2,1)S(1)}, bf16[1024,256]{1,0:T(8,128)(2,1)S(1)}, u32[]{:S(2)}, u32[]{:S(2)}) collective-permute-start(bf16[1024,256]{1,0:T(8,128)(2,1)S(1)} %collective-permute-done.1), channel_id=1, source_target_pairs={{0,4},{4,8},{8,12},{12,16},{16,20},{20,24},{24,28},{28,32},{32,36}... | collective-permute-start | bytes 1572872 | tf_op jit(solution)/shard_map/stream_1_step_1/ppermute | solution.py:164
  19.8 3.8 %collective-permute-done.11.refs_6_ = bf16[1024,256]{1,0:T(8,128)(2,1)S(1)} collective-permute-done((bf16[1024,256]{1,0:T(8,128)(2,1)}, bf16[1024,256]{1,0:T(8,128)(2,1)S(1)}, u32[]{:S(2)}, u32[]{:S(2)}) %collective-permute-start.11) | collective-permute-done | bytes 524320 | tf_op jit(solution)/shard_map/stream_0_step_1/ppermute | solution.py:164
  23.5 4.9 %collective-permute-start.12 = (bf16[1024,256]{1,0:T(8,128)(2,1)S(1)}, bf16[1024,256]{1,0:T(8,128)(2,1)S(1)}, u32[]{:S(2)}, u32[]{:S(2)}) collective-permute-start(bf16[1024,256]{1,0:T(8,128)(2,1)S(1)} %collective-permute-done.11.refs_6_), channel_id=1, source_target_pairs={{0,4},{4,8},{8,12},{12,16},{16,20},{20,24},{24,28},{28,32},{32,36}... | collective-permute-start | bytes 1572872 | tf_op jit(solution)/shard_map/stream_0_step_2/ppermute | solution.py:164
  28.4 0.6 collective-permute-done.2.refs_5_
  29.0 5.0 %collective-permute-start.4 = (bf16[1024,256]{1,0:T(8,128)(2,1)S(1)}, bf16[1024,256]{1,0:T(8,128)(2,1)S(1)}, u32[]{:S(2)}, u32[]{:S(2)}) collective-permute-start(bf16[1024,256]{1,0:T(8,128)(2,1)S(1)} %collective-permute-done.2.refs_5_), channel_id=1, source_target_pairs={{0,4},{4,8},{8,12},{12,16},{16,20},{20,24},{24,28},{28,32},{32,36}... | collective-permute-start | bytes 1572872 | tf_op jit(solution)/shard_map/stream_1_step_2/ppermute | solution.py:164
  34.1 1.9 %collective-permute-start = (bf16[512,512]{1,0:T(8,128)(2,1)}, bf16[512,512]{1,0:T(8,128)(2,1)S(1)}, u32[]{:S(2)}, u32[]{:S(2)}) collective-permute-start(bf16[512,512]{1,0:T(8,128)(2,1)} %get-tuple-element.19), channel_id=1, source_target_pairs={{0,64},{64,0},{1,65},{65,1},{2,66},{66,2},{3,67},{67,3},{4,68},{68... | collective-permute-start | bytes 1572872 | tf_op jit(solution)/shard_map/ppermute | solution.py:166
  36.0 0.0 collective-permute-done.12.refs_7_
  36.0 3.7 %collective-permute-start.13 = (bf16[1024,256]{1,0:T(8,128)(2,1)S(1)}, bf16[1024,256]{1,0:T(8,128)(2,1)S(1)}, u32[]{:S(2)}, u32[]{:S(2)}) collective-permute-start(bf16[1024,256]{1,0:T(8,128)(2,1)S(1)} %collective-permute-done.12.refs_7_), channel_id=1, source_target_pairs={{0,4},{4,8},{8,12},{12,16},{16,20},{20,24},{24,28},{28,32},{32,36}... | collective-permute-start | bytes 1572872 | tf_op jit(solution)/shard_map/stream_0_step_3/ppermute | solution.py:164
  39.7 0.6 collective-permute-done.4.refs_6_
  40.3 5.0 %collective-permute-start.5 = (bf16[1024,256]{1,0:T(8,128)(2,1)S(1)}, bf16[1024,256]{1,0:T(8,128)(2,1)S(1)}, u32[]{:S(2)}, u32[]{:S(2)}) collective-permute-start(bf16[1024,256]{1,0:T(8,128)(2,1)S(1)} %collective-permute-done.4.refs_6_), channel_id=1, source_target_pairs={{0,4},{4,8},{8,12},{12,16},{16,20},{20,24},{24,28},{28,32},{32,36}... | collective-permute-start | bytes 1572872 | tf_op jit(solution)/shard_map/stream_1_step_3/ppermute | solution.py:164
  45.3 1.1 constant_dynamic-update-slice_fusion.1
  46.4 0.0 collective-permute-done
  46.4 0.0 collective-permute-done.13.refs_8_
  46.4 4.5 %collective-permute-start.14 = (bf16[1024,256]{1,0:T(8,128)(2,1)S(1)}, bf16[1024,256]{1,0:T(8,128)(2,1)S(1)}, u32[]{:S(2)}, u32[]{:S(2)}) collective-permute-start(bf16[1024,256]{1,0:T(8,128)(2,1)S(1)} %collective-permute-done.13.refs_8_), channel_id=1, source_target_pairs={{0,4},{4,8},{8,12},{12,16},{16,20},{20,24},{24,28},{28,32},{32,36}... | collective-permute-start | bytes 1572872 | tf_op jit(solution)/shard_map/stream_0_step_4/ppermute | solution.py:164
  50.9 4.6 %collective-permute-start.3 = (bf16[1024,512]{1,0:T(8,128)(2,1)S(1)}, bf16[1024,512]{1,0:T(8,128)(2,1)S(1)}, u32[]{:S(2)}, u32[]{:S(2)}) collective-permute-start(bf16[1024,512]{1,0:T(8,128)(2,1)S(1)} %constant_dynamic-update-slice_fusion.refs_0_), channel_id=1, source_target_pairs={{0,128},{64,448},{128,256},{192,64},{256,384},{320,192},{384,0},{4... | collective-permute-start | bytes 3145736 | tf_op jit(solution)/shard_map/ppermute | solution.py:169
  55.6 0.0 collective-permute-done.5.refs_7_
  55.6 1.9 %collective-permute-start.6 = (bf16[1024,256]{1,0:T(8,128)(2,1)S(1)}, bf16[1024,256]{1,0:T(8,128)(2,1)S(1)}, u32[]{:S(2)}, u32[]{:S(2)}) collective-permute-start(bf16[1024,256]{1,0:T(8,128)(2,1)S(1)} %collective-permute-done.5.refs_7_), channel_id=1, source_target_pairs={{0,4},{4,8},{8,12},{12,16},{16,20},{20,24},{24,28},{28,32},{32,36}... | collective-permute-start | bytes 1572872 | tf_op jit(solution)/shard_map/stream_1_step_4/ppermute | solution.py:164
  57.5 0.0 collective-permute-done.14.refs_9_
  57.5 4.9 %collective-permute-start.15 = (bf16[1024,256]{1,0:T(8,128)(2,1)S(1)}, bf16[1024,256]{1,0:T(8,128)(2,1)S(1)}, u32[]{:S(2)}, u32[]{:S(2)}) collective-permute-start(bf16[1024,256]{1,0:T(8,128)(2,1)S(1)} %collective-permute-done.14.refs_9_), channel_id=1, source_target_pairs={{0,4},{4,8},{8,12},{12,16},{16,20},{20,24},{24,28},{28,32},{32,36}... | collective-permute-start | bytes 1572872 | tf_op jit(solution)/shard_map/stream_0_step_5/ppermute | solution.py:164
  62.4 3.4 %collective-permute-done.6.refs_8_ = bf16[1024,256]{1,0:T(8,128)(2,1)S(1)} collective-permute-done((bf16[1024,256]{1,0:T(8,128)(2,1)S(1)}, bf16[1024,256]{1,0:T(8,128)(2,1)S(1)}, u32[]{:S(2)}, u32[]{:S(2)}) %collective-permute-start.6) | collective-permute-done | bytes 524320 | tf_op jit(solution)/shard_map/stream_1_step_4/ppermute | solution.py:164
  65.8 3.1 %collective-permute-start.9 = (bf16[1024,256]{1,0:T(8,128)(2,1)S(1)}, bf16[1024,256]{1,0:T(8,128)(2,1)S(1)}, u32[]{:S(2)}, u32[]{:S(2)}) collective-permute-start(bf16[1024,256]{1,0:T(8,128)(2,1)S(1)} %collective-permute-done.6.refs_8_), channel_id=1, source_target_pairs={{0,4},{4,8},{8,12},{12,16},{16,20},{20,24},{24,28},{28,32},{32,36}... | collective-permute-start | bytes 1572872 | tf_op jit(solution)/shard_map/stream_1_step_5/ppermute | solution.py:164
  69.0 0.0 copy-done.1
  69.0 3.6 %collective-permute-start.8 = (bf16[512,512]{1,0:T(8,128)(2,1)S(1)}, bf16[512,512]{1,0:T(8,128)(2,1)S(1)}, u32[]{:S(2)}, u32[]{:S(2)}) collective-permute-start(bf16[512,512]{1,0:T(8,128)(2,1)S(1)} %copy-done.1), channel_id=1, source_target_pairs={{0,256},{128,384},{256,0},{384,128},{1,257},{129,385},{257,1},{385... | collective-permute-start | bytes 1572872 | tf_op jit(solution)/shard_map/ppermute | solution.py:171
  72.6 0.0 collective-permute-done.15.refs_10_
  72.6 1.9 %collective-permute-start.16 = (bf16[1024,256]{1,0:T(8,128)(2,1)S(1)}, bf16[1024,256]{1,0:T(8,128)(2,1)S(1)}, u32[]{:S(2)}, u32[]{:S(2)}) collective-permute-start(bf16[1024,256]{1,0:T(8,128)(2,1)S(1)} %collective-permute-done.15.refs_10_), channel_id=1, source_target_pairs={{0,4},{4,8},{8,12},{12,16},{16,20},{20,24},{24,28},{28,32},{32,36}... | collective-permute-start | bytes 1572872 | tf_op jit(solution)/shard_map/stream_0_step_6/ppermute | solution.py:164
  74.5 0.0 collective-permute-done.3.refs_1_
  74.5 3.5 %collective-permute-start.7 = (bf16[1024,512]{1,0:T(8,128)(2,1)S(1)}, bf16[1024,512]{1,0:T(8,128)(2,1)S(1)}, u32[]{:S(2)}, u32[]{:S(2)}) collective-permute-start(bf16[1024,512]{1,0:T(8,128)(2,1)S(1)} %collective-permute-done.3.refs_1_), channel_id=1, source_target_pairs={{0,64},{64,0},{1,65},{65,1},{2,66},{66,2},{3,67},{67,3},{4,68},{68... | collective-permute-start | bytes 3145736 | tf_op jit(solution)/shard_map/ppermute | solution.py:173
  78.1 0.0 collective-permute-done.9.refs_9_
  78.1 4.9 %collective-permute-start.18 = (bf16[1024,256]{1,0:T(8,128)(2,1)S(1)}, bf16[1024,256]{1,0:T(8,128)(2,1)S(1)}, u32[]{:S(2)}, u32[]{:S(2)}) collective-permute-start(bf16[1024,256]{1,0:T(8,128)(2,1)S(1)} %collective-permute-done.9.refs_9_), channel_id=1, source_target_pairs={{0,4},{4,8},{8,12},{12,16},{16,20},{20,24},{24,28},{28,32},{32,36}... | collective-permute-start | bytes 1572872 | tf_op jit(solution)/shard_map/stream_1_step_6/ppermute | solution.py:164
  83.0 0.0 collective-permute-done.16.refs_11_
  83.0 3.6 %collective-permute-start.17 = (bf16[1024,256]{1,0:T(8,128)(2,1)S(1)}, bf16[1024,256]{1,0:T(8,128)(2,1)S(1)}, u32[]{:S(2)}, u32[]{:S(2)}) collective-permute-start(bf16[1024,256]{1,0:T(8,128)(2,1)S(1)} %collective-permute-done.16.refs_11_), channel_id=1, source_target_pairs={{0,4},{4,8},{8,12},{12,16},{16,20},{20,24},{24,28},{28,32},{32,36}... | collective-permute-start | bytes 1572872 | tf_op jit(solution)/shard_map/stream_0_step_7/ppermute | solution.py:164
  86.6 0.0 collective-permute-done.8.refs_3_
  86.6 3.7 %collective-permute-start.10 = (bf16[512,512]{1,0:T(8,128)(2,1)S(1)}, bf16[512,512]{1,0:T(8,128)(2,1)S(1)}, u32[]{:S(2)}, u32[]{:S(2)}) collective-permute-start(bf16[512,512]{1,0:T(8,128)(2,1)S(1)} %collective-permute-done.8.refs_3_), channel_id=1, source_target_pairs={{0,64},{64,0},{1,65},{65,1},{2,66},{66,2},{3,67},{67,3},{4,68},{68... | collective-permute-start | bytes 1572872 | tf_op jit(solution)/shard_map/ppermute | solution.py:175
  90.4 0.0 collective-permute-done.18.refs_10_
  90.4 4.9 %collective-permute-start.20 = (bf16[1024,256]{1,0:T(8,128)(2,1)S(1)}, bf16[1024,256]{1,0:T(8,128)(2,1)S(1)}, u32[]{:S(2)}, u32[]{:S(2)}) collective-permute-start(bf16[1024,256]{1,0:T(8,128)(2,1)S(1)} %collective-permute-done.18.refs_10_), channel_id=1, source_target_pairs={{0,4},{4,8},{8,12},{12,16},{16,20},{20,24},{24,28},{28,32},{32,36}... | collective-permute-start | bytes 1572872 | tf_op jit(solution)/shard_map/stream_1_step_7/ppermute | solution.py:164
  95.2 0.0 collective-permute-done.17.refs_5_
  95.2 0.0 collective-permute-done.7.refs_2_
  95.3 0.0 collective-permute-done.10.refs_4_
  95.3 2.4 %shard_map.74.refs_6_ = f32[1024,512]{1,0:T(8,128)S(1)} custom-call(bf16[1024,512]{1,0:T(8,128)(2,1)S(1)} %constant_dynamic-update-slice_fusion.refs_0_, bf16[1024,512]{1,0:T(8,128)(2,1)S(1)} %collective-permute-done.3.refs_1_, bf16[1024,512]{1,0:T(8,128)(2,1)S(1)} %collective-permute-done.7.refs_2_, bf16[512,512]{1,0:T(8,128)(2,1)S(1)} %collective-permute-done.8.refs_3_, ...), custom_call_target="tpu_custom_call" | custom-call | flops 1610612736 | bytes 2097152 | tf_op jit(solution)/shard_map/pallas_call | solution.py:130
  97.6 0.0 copy-start
  97.7 3.7 %collective-permute-done.20.refs_5_ = bf16[1024,256]{1,0:T(8,128)(2,1)S(1)} collective-permute-done((bf16[1024,256]{1,0:T(8,128)(2,1)S(1)}, bf16[1024,256]{1,0:T(8,128)(2,1)S(1)}, u32[]{:S(2)}, u32[]{:S(2)}) %collective-permute-start.20) | collective-permute-done | bytes 524320 | tf_op jit(solution)/shard_map/stream_1_step_7/ppermute | solution.py:164
  101.3 0.8 shard_map.77
  102.1 4.9 %collective-permute-start.21 = (f32[1024,512]{1,0:T(8,128)S(1)}, f32[1024,512]{1,0:T(8,128)S(1)}, u32[]{:S(2)}, u32[]{:S(2)}) collective-permute-start(f32[1024,512]{1,0:T(8,128)S(1)} %shard_map.77), channel_id=1, source_target_pairs={{0,64},{64,0},{1,65},{65,1},{2,66},{66,2},{3,67},{67,3},{4,68},{68... | collective-permute-start | bytes 6291464 | tf_op jit(solution)/shard_map/ppermute | solution.py:178
  107.0 2.6 %collective-permute-start.19 = (bf16[1024,256]{1,0:T(8,128)(2,1)S(1)}, bf16[1024,256]{1,0:T(8,128)(2,1)S(1)}, u32[]{:S(2)}, u32[]{:S(2)}) collective-permute-start(bf16[1024,256]{1,0:T(8,128)(2,1)S(1)} %collective-permute-done.17.refs_5_), channel_id=1, source_target_pairs={{0,4},{4,8},{8,12},{12,16},{16,20},{20,24},{24,28},{28,32},{32,36}... | collective-permute-start | bytes 1572872 | tf_op jit(solution)/shard_map/stream_0_step_8/ppermute | solution.py:164
  109.6 0.0 copy-done
  109.7 2.7 %shard_map.75.refs_6_ = f32[1024,512]{1,0:T(8,128)S(1)} custom-call(bf16[1024,512]{1,0:T(8,128)(2,1)S(1)} %constant_dynamic-update-slice_fusion.refs_0_, bf16[1024,512]{1,0:T(8,128)(2,1)S(1)} %collective-permute-done.3.refs_1_, bf16[1024,512]{1,0:T(8,128)(2,1)S(1)} %collective-permute-done.7.refs_2_, bf16[512,512]{1,0:T(8,128)(2,1)S(1)} %collective-permute-done.8.refs_3_, ...), custom_call_target="tpu_custom_call" | custom-call | flops 1879048192 | bytes 2097152 | tf_op jit(solution)/shard_map/pallas_call | solution.py:130
  112.3 0.9 shard_map.76.refs_6_
  113.2 4.0 %collective-permute-done.19.refs_5_ = bf16[1024,256]{1,0:T(8,128)(2,1)S(1)} collective-permute-done((bf16[1024,256]{1,0:T(8,128)(2,1)S(1)}, bf16[1024,256]{1,0:T(8,128)(2,1)S(1)}, u32[]{:S(2)}, u32[]{:S(2)}) %collective-permute-start.19) | collective-permute-done | bytes 524320 | tf_op jit(solution)/shard_map/stream_0_step_8/ppermute | solution.py:164
  117.2 0.0 collective-permute-done.21.refs_7_
  117.2 0.8 shard_map.78
  118.1 27.8 %all_to_all.5.in_hbm = f32[4,256,512]{2,1,0:T(8,128)S(1)} all-to-all(f32[4,256,512]{2,1,0:T(8,128)S(1)} %bitcast.2), channel_id=1, replica_groups=mesh['y'=4,'core'=2,'col'=16,'layer'=4] {'layer'}, dimensions={0} | all-to-all | bytes 4194304 | tf_op jit(solution)/shard_map/all_to_all | solution.py:183
  145.9 1.0 shard_map.79
  (1 shorter events, 0.0 us)
Async XLA Ops:
  2.4 66.6 %copy-start.1 = (bf16[512,512]{1,0:T(8,128)(2,1)S(1)}, bf16[512,512]{1,0:T(8,128)(2,1)}, u32[]{:S(2)}) copy-start(bf16[512,512]{1,0:T(8,128)(2,1)} %get-tuple-element.19) | copy-start | bytes 1572868
  2.4 14.7 %collective-permute-start.1 = (bf16[1024,256]{1,0:T(8,128)(2,1)}, bf16[1024,256]{1,0:T(8,128)(2,1)S(1)}, u32[]{:S(2)}, u32[]{:S(2)}) collective-permute-start(bf16[1024,256]{1,0:T(8,128)(2,1)} %get-tuple-element.15.refs_5_), channel_id=1, source_target_pairs={{0,64},{64,0},{1,65},{65,1},{2,66},{66,2},{3,67},{67,3},{4,68},{68... | collective-permute-start | bytes 1572872 | tf_op jit(solution)/shard_map/ppermute | solution.py:126
  11.3 12.2 %collective-permute-start.11 = (bf16[1024,256]{1,0:T(8,128)(2,1)}, bf16[1024,256]{1,0:T(8,128)(2,1)S(1)}, u32[]{:S(2)}, u32[]{:S(2)}) collective-permute-start(bf16[1024,256]{1,0:T(8,128)(2,1)} %get-tuple-element.15.refs_5_), channel_id=1, source_target_pairs={{0,4},{4,8},{8,12},{12,16},{16,20},{20,24},{24,28},{28,32},{32,36}... | collective-permute-start | bytes 1572872 | tf_op jit(solution)/shard_map/stream_0_step_1/ppermute | solution.py:164
  17.1 11.9 %collective-permute-start.2 = (bf16[1024,256]{1,0:T(8,128)(2,1)S(1)}, bf16[1024,256]{1,0:T(8,128)(2,1)S(1)}, u32[]{:S(2)}, u32[]{:S(2)}) collective-permute-start(bf16[1024,256]{1,0:T(8,128)(2,1)S(1)} %collective-permute-done.1), channel_id=1, source_target_pairs={{0,4},{4,8},{8,12},{12,16},{16,20},{20,24},{24,28},{28,32},{32,36}... | collective-permute-start | bytes 1572872 | tf_op jit(solution)/shard_map/stream_1_step_1/ppermute | solution.py:164
  23.5 12.5 %collective-permute-start.12 = (bf16[1024,256]{1,0:T(8,128)(2,1)S(1)}, bf16[1024,256]{1,0:T(8,128)(2,1)S(1)}, u32[]{:S(2)}, u32[]{:S(2)}) collective-permute-start(bf16[1024,256]{1,0:T(8,128)(2,1)S(1)} %collective-permute-done.11.refs_6_), channel_id=1, source_target_pairs={{0,4},{4,8},{8,12},{12,16},{16,20},{20,24},{24,28},{28,32},{32,36}... | collective-permute-start | bytes 1572872 | tf_op jit(solution)/shard_map/stream_0_step_2/ppermute | solution.py:164
  29.0 11.2 %collective-permute-start.4 = (bf16[1024,256]{1,0:T(8,128)(2,1)S(1)}, bf16[1024,256]{1,0:T(8,128)(2,1)S(1)}, u32[]{:S(2)}, u32[]{:S(2)}) collective-permute-start(bf16[1024,256]{1,0:T(8,128)(2,1)S(1)} %collective-permute-done.2.refs_5_), channel_id=1, source_target_pairs={{0,4},{4,8},{8,12},{12,16},{16,20},{20,24},{24,28},{28,32},{32,36}... | collective-permute-start | bytes 1572872 | tf_op jit(solution)/shard_map/stream_1_step_2/ppermute | solution.py:164
  34.1 12.3 %collective-permute-start = (bf16[512,512]{1,0:T(8,128)(2,1)}, bf16[512,512]{1,0:T(8,128)(2,1)S(1)}, u32[]{:S(2)}, u32[]{:S(2)}) collective-permute-start(bf16[512,512]{1,0:T(8,128)(2,1)} %get-tuple-element.19), channel_id=1, source_target_pairs={{0,64},{64,0},{1,65},{65,1},{2,66},{66,2},{3,67},{67,3},{4,68},{68... | collective-permute-start | bytes 1572872 | tf_op jit(solution)/shard_map/ppermute | solution.py:166
  36.0 10.4 %collective-permute-start.13 = (bf16[1024,256]{1,0:T(8,128)(2,1)S(1)}, bf16[1024,256]{1,0:T(8,128)(2,1)S(1)}, u32[]{:S(2)}, u32[]{:S(2)}) collective-permute-start(bf16[1024,256]{1,0:T(8,128)(2,1)S(1)} %collective-permute-done.12.refs_7_), channel_id=1, source_target_pairs={{0,4},{4,8},{8,12},{12,16},{16,20},{20,24},{24,28},{28,32},{32,36}... | collective-permute-start | bytes 1572872 | tf_op jit(solution)/shard_map/stream_0_step_3/ppermute | solution.py:164
  40.3 15.3 %collective-permute-start.5 = (bf16[1024,256]{1,0:T(8,128)(2,1)S(1)}, bf16[1024,256]{1,0:T(8,128)(2,1)S(1)}, u32[]{:S(2)}, u32[]{:S(2)}) collective-permute-start(bf16[1024,256]{1,0:T(8,128)(2,1)S(1)} %collective-permute-done.4.refs_6_), channel_id=1, source_target_pairs={{0,4},{4,8},{8,12},{12,16},{16,20},{20,24},{24,28},{28,32},{32,36}... | collective-permute-start | bytes 1572872 | tf_op jit(solution)/shard_map/stream_1_step_3/ppermute | solution.py:164
  46.4 11.2 %collective-permute-start.14 = (bf16[1024,256]{1,0:T(8,128)(2,1)S(1)}, bf16[1024,256]{1,0:T(8,128)(2,1)S(1)}, u32[]{:S(2)}, u32[]{:S(2)}) collective-permute-start(bf16[1024,256]{1,0:T(8,128)(2,1)S(1)} %collective-permute-done.13.refs_8_), channel_id=1, source_target_pairs={{0,4},{4,8},{8,12},{12,16},{16,20},{20,24},{24,28},{28,32},{32,36}... | collective-permute-start | bytes 1572872 | tf_op jit(solution)/shard_map/stream_0_step_4/ppermute | solution.py:164
  50.9 23.6 %collective-permute-start.3 = (bf16[1024,512]{1,0:T(8,128)(2,1)S(1)}, bf16[1024,512]{1,0:T(8,128)(2,1)S(1)}, u32[]{:S(2)}, u32[]{:S(2)}) collective-permute-start(bf16[1024,512]{1,0:T(8,128)(2,1)S(1)} %constant_dynamic-update-slice_fusion.refs_0_), channel_id=1, source_target_pairs={{0,128},{64,448},{128,256},{192,64},{256,384},{320,192},{384,0},{4... | collective-permute-start | bytes 3145736 | tf_op jit(solution)/shard_map/ppermute | solution.py:169
  55.6 10.2 %collective-permute-start.6 = (bf16[1024,256]{1,0:T(8,128)(2,1)S(1)}, bf16[1024,256]{1,0:T(8,128)(2,1)S(1)}, u32[]{:S(2)}, u32[]{:S(2)}) collective-permute-start(bf16[1024,256]{1,0:T(8,128)(2,1)S(1)} %collective-permute-done.5.refs_7_), channel_id=1, source_target_pairs={{0,4},{4,8},{8,12},{12,16},{16,20},{20,24},{24,28},{28,32},{32,36}... | collective-permute-start | bytes 1572872 | tf_op jit(solution)/shard_map/stream_1_step_4/ppermute | solution.py:164
  57.5 15.1 %collective-permute-start.15 = (bf16[1024,256]{1,0:T(8,128)(2,1)S(1)}, bf16[1024,256]{1,0:T(8,128)(2,1)S(1)}, u32[]{:S(2)}, u32[]{:S(2)}) collective-permute-start(bf16[1024,256]{1,0:T(8,128)(2,1)S(1)} %collective-permute-done.14.refs_9_), channel_id=1, source_target_pairs={{0,4},{4,8},{8,12},{12,16},{16,20},{20,24},{24,28},{28,32},{32,36}... | collective-permute-start | bytes 1572872 | tf_op jit(solution)/shard_map/stream_0_step_5/ppermute | solution.py:164
  65.8 12.3 %collective-permute-start.9 = (bf16[1024,256]{1,0:T(8,128)(2,1)S(1)}, bf16[1024,256]{1,0:T(8,128)(2,1)S(1)}, u32[]{:S(2)}, u32[]{:S(2)}) collective-permute-start(bf16[1024,256]{1,0:T(8,128)(2,1)S(1)} %collective-permute-done.6.refs_8_), channel_id=1, source_target_pairs={{0,4},{4,8},{8,12},{12,16},{16,20},{20,24},{24,28},{28,32},{32,36}... | collective-permute-start | bytes 1572872 | tf_op jit(solution)/shard_map/stream_1_step_5/ppermute | solution.py:164
  69.0 17.7 %collective-permute-start.8 = (bf16[512,512]{1,0:T(8,128)(2,1)S(1)}, bf16[512,512]{1,0:T(8,128)(2,1)S(1)}, u32[]{:S(2)}, u32[]{:S(2)}) collective-permute-start(bf16[512,512]{1,0:T(8,128)(2,1)S(1)} %copy-done.1), channel_id=1, source_target_pairs={{0,256},{128,384},{256,0},{384,128},{1,257},{129,385},{257,1},{385... | collective-permute-start | bytes 1572872 | tf_op jit(solution)/shard_map/ppermute | solution.py:171
  72.6 10.4 %collective-permute-start.16 = (bf16[1024,256]{1,0:T(8,128)(2,1)S(1)}, bf16[1024,256]{1,0:T(8,128)(2,1)S(1)}, u32[]{:S(2)}, u32[]{:S(2)}) collective-permute-start(bf16[1024,256]{1,0:T(8,128)(2,1)S(1)} %collective-permute-done.15.refs_10_), channel_id=1, source_target_pairs={{0,4},{4,8},{8,12},{12,16},{16,20},{20,24},{24,28},{28,32},{32,36}... | collective-permute-start | bytes 1572872 | tf_op jit(solution)/shard_map/stream_0_step_6/ppermute | solution.py:164
  74.5 20.7 %collective-permute-start.7 = (bf16[1024,512]{1,0:T(8,128)(2,1)S(1)}, bf16[1024,512]{1,0:T(8,128)(2,1)S(1)}, u32[]{:S(2)}, u32[]{:S(2)}) collective-permute-start(bf16[1024,512]{1,0:T(8,128)(2,1)S(1)} %collective-permute-done.3.refs_1_), channel_id=1, source_target_pairs={{0,64},{64,0},{1,65},{65,1},{2,66},{66,2},{3,67},{67,3},{4,68},{68... | collective-permute-start | bytes 3145736 | tf_op jit(solution)/shard_map/ppermute | solution.py:173
  78.1 12.3 %collective-permute-start.18 = (bf16[1024,256]{1,0:T(8,128)(2,1)S(1)}, bf16[1024,256]{1,0:T(8,128)(2,1)S(1)}, u32[]{:S(2)}, u32[]{:S(2)}) collective-permute-start(bf16[1024,256]{1,0:T(8,128)(2,1)S(1)} %collective-permute-done.9.refs_9_), channel_id=1, source_target_pairs={{0,4},{4,8},{8,12},{12,16},{16,20},{20,24},{24,28},{28,32},{32,36}... | collective-permute-start | bytes 1572872 | tf_op jit(solution)/shard_map/stream_1_step_6/ppermute | solution.py:164
  83.0 12.3 %collective-permute-start.17 = (bf16[1024,256]{1,0:T(8,128)(2,1)S(1)}, bf16[1024,256]{1,0:T(8,128)(2,1)S(1)}, u32[]{:S(2)}, u32[]{:S(2)}) collective-permute-start(bf16[1024,256]{1,0:T(8,128)(2,1)S(1)} %collective-permute-done.16.refs_11_), channel_id=1, source_target_pairs={{0,4},{4,8},{8,12},{12,16},{16,20},{20,24},{24,28},{28,32},{32,36}... | collective-permute-start | bytes 1572872 | tf_op jit(solution)/shard_map/stream_0_step_7/ppermute | solution.py:164
  86.6 8.6 %collective-permute-start.10 = (bf16[512,512]{1,0:T(8,128)(2,1)S(1)}, bf16[512,512]{1,0:T(8,128)(2,1)S(1)}, u32[]{:S(2)}, u32[]{:S(2)}) collective-permute-start(bf16[512,512]{1,0:T(8,128)(2,1)S(1)} %collective-permute-done.8.refs_3_), channel_id=1, source_target_pairs={{0,64},{64,0},{1,65},{65,1},{2,66},{66,2},{3,67},{67,3},{4,68},{68... | collective-permute-start | bytes 1572872 | tf_op jit(solution)/shard_map/ppermute | solution.py:175
  90.4 11.0 %collective-permute-start.20 = (bf16[1024,256]{1,0:T(8,128)(2,1)S(1)}, bf16[1024,256]{1,0:T(8,128)(2,1)S(1)}, u32[]{:S(2)}, u32[]{:S(2)}) collective-permute-start(bf16[1024,256]{1,0:T(8,128)(2,1)S(1)} %collective-permute-done.18.refs_10_), channel_id=1, source_target_pairs={{0,4},{4,8},{8,12},{12,16},{16,20},{20,24},{24,28},{28,32},{32,36}... | collective-permute-start | bytes 1572872 | tf_op jit(solution)/shard_map/stream_1_step_7/ppermute | solution.py:164
  97.6 12.0 %copy-start = (bf16[1024,256]{1,0:T(8,128)(2,1)S(1)}, bf16[1024,256]{1,0:T(8,128)(2,1)}, u32[]{:S(2)}) copy-start(bf16[1024,256]{1,0:T(8,128)(2,1)} %get-tuple-element.15.refs_5_) | copy-start | bytes 1572868
  102.1 15.1 %collective-permute-start.21 = (f32[1024,512]{1,0:T(8,128)S(1)}, f32[1024,512]{1,0:T(8,128)S(1)}, u32[]{:S(2)}, u32[]{:S(2)}) collective-permute-start(f32[1024,512]{1,0:T(8,128)S(1)} %shard_map.77), channel_id=1, source_target_pairs={{0,64},{64,0},{1,65},{65,1},{2,66},{66,2},{3,67},{67,3},{4,68},{68... | collective-permute-start | bytes 6291464 | tf_op jit(solution)/shard_map/ppermute | solution.py:178
  107.0 10.2 %collective-permute-start.19 = (bf16[1024,256]{1,0:T(8,128)(2,1)S(1)}, bf16[1024,256]{1,0:T(8,128)(2,1)S(1)}, u32[]{:S(2)}, u32[]{:S(2)}) collective-permute-start(bf16[1024,256]{1,0:T(8,128)(2,1)S(1)} %collective-permute-done.17.refs_5_), channel_id=1, source_target_pairs={{0,4},{4,8},{8,12},{12,16},{16,20},{20,24},{24,28},{28,32},{32,36}... | collective-permute-start | bytes 1572872 | tf_op jit(solution)/shard_map/stream_0_step_8/ppermute | solution.py:164

commit v5 on v4

--- a/solution.py
+++ b/solution.py
@@ -14,6 +14,7 @@
 VMEM = pl.BlockSpec(memory_space=pltpu.VMEM)
 PARAMS = pltpu.CompilerParams(vmem_limit_bytes=40 * 1024 * 1024)
 SWAP = [(0, 1), (1, 0)]
+STEP, CODES, CODE_ROWS = 12, 10, 16
 
 
 def below(axis, size):
@@ -88,14 +89,29 @@
         total = jnp.dot(a_all[rows, :], b, preferred_element_type=jnp.float32)
         for i in range(added):
             total = total + extra[i, rows, :]
-        out_ref[rows, :] = total
-
-
-def layers_kernel(in_hbm, out_ref, parts, sem):
-    copy = pltpu.make_async_copy(in_hbm, parts, sem)
-    copy.start()
-    copy.wait()
-    out_ref[...] = (parts[0] + parts[1]) + (parts[2] + parts[3])
+        if len(out_ref.shape) == 2:
+            out_ref[rows, :] = total
+        else:
+            encode(total, out_ref.at[tile])
+
+
+def encode(total, out_ref):
+    top = jnp.max(jnp.abs(total), keepdims=True)
+    scale, code = jnp.ones_like(top), jnp.zeros_like(top)
+    for c in range(1, CODES + 1):
+        small = top < 2.0 ** (14 - STEP * c)
+        scale = jnp.where(small, 2.0 ** (STEP * c), scale)
+        code = jnp.where(small, float(c), code)
+    out_ref[:BS, :] = total * scale
+    out_ref[BS:, :] = jnp.broadcast_to(code, (CODE_ROWS, total.shape[1]))
+
+
+def decoded(parts):
+    code = parts[:, BS:, :1].astype(jnp.float32).max(axis=1, keepdims=True)
+    scale = jnp.ones_like(code)
+    for c in range(1, CODES + 1):
+        scale = jnp.where(code > c - 0.5, 2.0 ** (-STEP * c), scale)
+    return parts[:, :BS].astype(jnp.float32) * scale
 
 
 def after(value, earlier):
@@ -125,11 +141,13 @@
     last = cols // 2
     held = [[own], [lax.ppermute(own, "core", SWAP)]]
 
-    def product(steps, arrays, adds=()):
+    def product(steps, arrays, adds=(), coded=False):
         n = len(steps)
         return pl.pallas_call(
             functools.partial(product_kernel, steps, cols, len(adds)),
-            out_shape=jax.ShapeDtypeStruct((ROWS, width), jnp.float32),
+            out_shape=jax.ShapeDtypeStruct((ROWS // BS, BS + CODE_ROWS, width), jnp.float32)
+            if coded
+            else jax.ShapeDtypeStruct((ROWS, width), jnp.float32),
             in_specs=[HBM] * (5 + len(arrays) + len(adds)),
             out_specs=VMEM,
             scratch_shapes=[
@@ -149,21 +167,21 @@
     ]
     far_away = [(i, (i + 2) % chips) for i in range(chips)]
     b_all = [None] * 5
-    b_other = others = None
+    b_other = None
+    turned = []
     for step in range(1, last + 1):
         for j in range(2):
             if (step, j) == (last, 1):
                 continue
             sent = held[j][-1]
-            if step == last:
-                shards = held[1][1 : last - 1]
-                shards[-1] = after(shards[-1], sent)
-                others = product(range(1, last - 1), shards)
-                sent = after(sent, others)
+            if j == 1 and step > 4:
+                sent = after(sent, turned[step - 5])
             with jax.named_scope(f"stream_{j}_step_{step}"):
                 held[j].append(lax.ppermute(sent, ("core", "col"), ring))
+            if j == 1 and step > 1:
+                turned.append(lax.ppermute(held[1][step - 1], "core", SWAP))
             if (step, j) == (1, 1):
-                b_other = lax.ppermute(after(b_eff, own), "core", SWAP)
+                b_other = lax.ppermute(after(b_eff, sent), "core", SWAP)
             if (step, j) == (2, 1):
                 b_all[0] = jnp.concatenate([b_eff, after(b_other, sent)])
                 b_all[1] = lax.ppermute(b_all[0], ("y", "core"), near_by)
@@ -171,24 +189,17 @@
                 b_all[3] = lax.ppermute(after(b_eff, sent), "y", far_away)
             if (step, j) == (5, 1):
                 b_all[2] = lax.ppermute(after(b_all[1], sent), "core", SWAP)
-            if (step, j) == (6, 1):
+            if (step, j) == (6, 0):
                 b_all[4] = lax.ppermute(after(b_all[3], sent), "core", SWAP)
-
-    others = product((last - 1,), held[1][last - 1 :], (others,))
-    others = lax.ppermute(others, "core", SWAP)
-    mine = product(range(last - 1), held[0][: last - 1])
-    mine = product((last - 1,), held[0][last - 1 : last], (mine,))
-    parts = product((last,), held[0][last:], (mine, others))
-    parts = parts.reshape(-1, BS, width)
-    parts = lax.all_to_all(parts, "layer", 0, 0)
-    return pl.pallas_call(
-        layers_kernel,
-        out_shape=jax.ShapeDtypeStruct((BS, width), jnp.float32),
-        in_specs=[HBM],
-        out_specs=VMEM,
-        scratch_shapes=[pltpu.VMEM(parts.shape, jnp.float32), pltpu.SemaphoreType.DMA],
-        compiler_params=PARAMS,
-    )(parts)
+    turned.append(lax.ppermute(held[1][last - 1], "core", SWAP))
+
+    shards = held[0] + turned[::-1]
+    near = product(range(last - 1), shards[: last - 1])
+    across = product(range(last + 2, cols), shards[last + 2 :])
+    steps = range(last - 1, last + 2)
+    parts = product(steps, [shards[s] for s in steps], (near, across), True)
+    parts = parts.astype(jnp.float16)
+    return decoded(lax.all_to_all(parts, "layer", 0, 0)).sum(axis=0)
 
 
 def solution(mesh):

time: 149 us -> 139 us (0.933)
  blocking collectives: 27.8 us -> 17 us
  starting transfers between devices: 90.5 us -> 98 us
  waiting for transfers between devices: 16.1 us -> 9.6 us
  Pallas kernels: 11 us -> 9.33 us
  other arithmetic: 0 us -> 1.52 us
    all_to_all x1, blocking collectives: 27.8 us -> 17 us  [on_device(): return decoded(lax.all_to_all(parts, 'layer', 0, 0)).sum(axis=0)]
    ppermute x2 -> x8, starting transfers between devices: 6.81 us -> 17.2 us  [the longest x6 13.3 us: on_device(): turned.append(lax.ppermute(held[1][step - 1], 'core', SWAP))]
    ppermute x15, waiting for transfers between devices: 16.1 us -> 8.34 us  [on_device(): held[j].append(lax.ppermute(sent, ('core', 'col'), ring))]
    ppermute x15, starting transfers between devices: 59.3 us -> 57.8 us  [on_device(): held[j].append(lax.ppermute(sent, ('core', 'col'), ring))]
    pallas_call x5 -> x3, Pallas kernels: 7.51 us -> 6.94 us  [product(): pl.pallas_call(functools.partial(product_kernel, steps, cols, len(adds)),...]
  transfers between devices with their start and end apart: 22 -> 28, of which waited for: 6 -> 7; matrix products, arithmetic and copies ran while one was open for 1% -> 1% of each run, Pallas kernels for 4% -> 4%
where the time goes in v5:
time: 139 us; the launch traced here: 137 us
  starting transfers between devices  98 us (71%)
  blocking collectives  17 us (12%)
  waiting for transfers between devices  9.6 us (7%)
  Pallas kernels  9.33 us (7%)
  other arithmetic  1.52 us (1%)
    ppermute x15, starting transfers between devices, on_device(): held[j].append(lax.ppermute(sent, ('core', 'col'), ring))  57.8 us
    all_to_all x1, blocking collectives, on_device(): return decoded(lax.all_to_all(parts, 'layer', 0, 0)).sum(axis=0)  17 us
    ppermute x6, starting transfers between devices, on_device(): turned.append(lax.ppermute(held[1][step - 1], 'core', SWAP))  13.3 us
    ppermute x1, starting transfers between devices, on_device(): held = [[own], [lax.ppermute(own, 'core', SWAP)]]  8.92 us
    ppermute x15, waiting for transfers between devices, on_device(): held[j].append(lax.ppermute(sent, ('core', 'col'), ring))  8.34 us
    pallas_call x3, Pallas kernels, product(): pl.pallas_call(functools.partial(product_kernel, steps, cols, len(adds)),...  6.94 us
    ppermute x1, starting transfers between devices, on_device(): b_all[1] = lax.ppermute(b_all[0], ('y', 'core'), near_by)  4.64 us
    ppermute x1, starting transfers between devices, on_device(): b_all[3] = lax.ppermute(after(b_eff, sent), 'y', far_away)  4.19 us
  transfers between devices with their start and end apart: 28, of which 7 were waited for; matrix products, arithmetic and copies ran while one was open for 1% of the time, Pallas kernels for 4%

profile of v5, /device:TPU:1, one launch (start us, length us, event | category | flops | bytes accessed | tf_op | source)
XLA Modules:
  0.0 137.1 jit_solution(1496644836973001054)
XLA Ops:
  0.0 2.4 %shard_map.73 = (bf16[1024,256]{1,0:T(8,128)(2,1)}, bf16[512,512]{1,0:T(8,128)(2,1)}) custom-call(s32[4]{0:T(128)} %bitcast.1, s32[1,2,2]{2,1,0:T(2,128)} %refs_1_.1, s32[4]{0:T(128)} %refs_2_.1, s32[1,16]{1,0:T(1,128)} %refs_3_.1, s32[2]{0:T(128)} %refs_4_.1, bf16[1,1024,256]{2,1,0:T(8,128)(2,1)} %refs_5_.1, bf16[1,512,512]{2,1,0:T(8,128)(2,1)} %refs_6_.1), custom_call_target="tpu_custom_call" | custom-call | tf_op jit(solution)/shard_map/pallas_call | solution.py:128
  2.4 0.0 copy-start
  2.4 8.9 %collective-permute-start = (bf16[1024,256]{1,0:T(8,128)(2,1)}, bf16[1024,256]{1,0:T(8,128)(2,1)S(1)}, u32[]{:S(2)}, u32[]{:S(2)}) collective-permute-start(bf16[1024,256]{1,0:T(8,128)(2,1)} %get-tuple-element.16.refs_5_), channel_id=1, source_target_pairs={{0,64},{64,0},{1,65},{65,1},{2,66},{66,2},{3,67},{67,3},{4,68},{68... | collective-permute-start | bytes 1572872 | tf_op jit(solution)/shard_map/ppermute | solution.py:142
  11.3 5.7 %collective-permute-start.10 = (bf16[1024,256]{1,0:T(8,128)(2,1)}, bf16[1024,256]{1,0:T(8,128)(2,1)S(1)}, u32[]{:S(2)}, u32[]{:S(2)}) collective-permute-start(bf16[1024,256]{1,0:T(8,128)(2,1)} %get-tuple-element.16.refs_5_), channel_id=1, source_target_pairs={{0,4},{4,8},{8,12},{12,16},{16,20},{20,24},{24,28},{28,32},{32,36}... | collective-permute-start | bytes 1572872 | tf_op jit(solution)/shard_map/stream_0_step_1/ppermute | solution.py:180
  17.1 0.0 collective-permute-done
  17.1 2.6 %collective-permute-start.2 = (bf16[1024,256]{1,0:T(8,128)(2,1)S(1)}, bf16[1024,256]{1,0:T(8,128)(2,1)S(1)}, u32[]{:S(2)}, u32[]{:S(2)}) collective-permute-start(bf16[1024,256]{1,0:T(8,128)(2,1)S(1)} %collective-permute-done), channel_id=1, source_target_pairs={{0,4},{4,8},{8,12},{12,16},{16,20},{20,24},{24,28},{28,32},{32,36}... | collective-permute-start | bytes 1572872 | tf_op jit(solution)/shard_map/stream_1_step_1/ppermute | solution.py:180
  19.8 3.8 %collective-permute-done.10.refs_6_ = bf16[1024,256]{1,0:T(8,128)(2,1)S(1)} collective-permute-done((bf16[1024,256]{1,0:T(8,128)(2,1)}, bf16[1024,256]{1,0:T(8,128)(2,1)S(1)}, u32[]{:S(2)}, u32[]{:S(2)}) %collective-permute-start.10) | collective-permute-done | bytes 524320 | tf_op jit(solution)/shard_map/stream_0_step_1/ppermute | solution.py:180
  23.5 4.9 %collective-permute-start.11 = (bf16[1024,256]{1,0:T(8,128)(2,1)S(1)}, bf16[1024,256]{1,0:T(8,128)(2,1)S(1)}, u32[]{:S(2)}, u32[]{:S(2)}) collective-permute-start(bf16[1024,256]{1,0:T(8,128)(2,1)S(1)} %collective-permute-done.10.refs_6_), channel_id=1, source_target_pairs={{0,4},{4,8},{8,12},{12,16},{16,20},{20,24},{24,28},{28,32},{32,36}... | collective-permute-start | bytes 1572872 | tf_op jit(solution)/shard_map/stream_0_step_2/ppermute | solution.py:180
  28.4 0.6 collective-permute-done.2
  29.0 5.0 %collective-permute-start.4 = (bf16[1024,256]{1,0:T(8,128)(2,1)S(1)}, bf16[1024,256]{1,0:T(8,128)(2,1)S(1)}, u32[]{:S(2)}, u32[]{:S(2)}) collective-permute-start(bf16[1024,256]{1,0:T(8,128)(2,1)S(1)} %collective-permute-done.2), channel_id=1, source_target_pairs={{0,4},{4,8},{8,12},{12,16},{16,20},{20,24},{24,28},{28,32},{32,36}... | collective-permute-start | bytes 1572872 | tf_op jit(solution)/shard_map/stream_1_step_2/ppermute | solution.py:180
  34.1 1.9 %collective-permute-start.1 = (bf16[512,512]{1,0:T(8,128)(2,1)}, bf16[512,512]{1,0:T(8,128)(2,1)S(1)}, u32[]{:S(2)}, u32[]{:S(2)}) collective-permute-start(bf16[512,512]{1,0:T(8,128)(2,1)} %get-tuple-element.21), channel_id=1, source_target_pairs={{0,64},{64,0},{1,65},{65,1},{2,66},{66,2},{3,67},{67,3},{4,68},{68... | collective-permute-start | bytes 1572872 | tf_op jit(solution)/shard_map/ppermute | solution.py:184
  36.0 0.0 collective-permute-done.11.refs_7_
  36.0 3.7 %collective-permute-start.12 = (bf16[1024,256]{1,0:T(8,128)(2,1)S(1)}, bf16[1024,256]{1,0:T(8,128)(2,1)S(1)}, u32[]{:S(2)}, u32[]{:S(2)}) collective-permute-start(bf16[1024,256]{1,0:T(8,128)(2,1)S(1)} %collective-permute-done.11.refs_7_), channel_id=1, source_target_pairs={{0,4},{4,8},{8,12},{12,16},{16,20},{20,24},{24,28},{28,32},{32,36}... | collective-permute-start | bytes 1572872 | tf_op jit(solution)/shard_map/stream_0_step_3/ppermute | solution.py:180
  39.7 0.6 collective-permute-done.4
  40.3 5.0 %collective-permute-start.5 = (bf16[1024,256]{1,0:T(8,128)(2,1)S(1)}, bf16[1024,256]{1,0:T(8,128)(2,1)S(1)}, u32[]{:S(2)}, u32[]{:S(2)}) collective-permute-start(bf16[1024,256]{1,0:T(8,128)(2,1)S(1)} %collective-permute-done.4), channel_id=1, source_target_pairs={{0,4},{4,8},{8,12},{12,16},{16,20},{20,24},{24,28},{28,32},{32,36}... | collective-permute-start | bytes 1572872 | tf_op jit(solution)/shard_map/stream_1_step_3/ppermute | solution.py:180
  45.3 1.1 constant_dynamic-update-slice_fusion.1
  46.4 0.0 collective-permute-done.1
  46.4 4.6 %collective-permute-start.3 = (bf16[1024,512]{1,0:T(8,128)(2,1)S(1)}, bf16[1024,512]{1,0:T(8,128)(2,1)S(1)}, u32[]{:S(2)}, u32[]{:S(2)}) collective-permute-start(bf16[1024,512]{1,0:T(8,128)(2,1)S(1)} %constant_dynamic-update-slice_fusion.refs_0_), channel_id=1, source_target_pairs={{0,128},{64,448},{128,256},{192,64},{256,384},{320,192},{384,0},{4... | collective-permute-start | bytes 3145736 | tf_op jit(solution)/shard_map/ppermute | solution.py:187
  51.1 0.0 collective-permute-done.12.refs_8_
  51.1 1.9 %collective-permute-start.13 = (bf16[1024,256]{1,0:T(8,128)(2,1)S(1)}, bf16[1024,256]{1,0:T(8,128)(2,1)S(1)}, u32[]{:S(2)}, u32[]{:S(2)}) collective-permute-start(bf16[1024,256]{1,0:T(8,128)(2,1)S(1)} %collective-permute-done.12.refs_8_), channel_id=1, source_target_pairs={{0,4},{4,8},{8,12},{12,16},{16,20},{20,24},{24,28},{28,32},{32,36}... | collective-permute-start | bytes 1572872 | tf_op jit(solution)/shard_map/stream_0_step_4/ppermute | solution.py:180
  53.0 1.9 %collective-permute-start.7 = (bf16[1024,256]{1,0:T(8,128)(2,1)S(1)}, bf16[1024,256]{1,0:T(8,128)(2,1)S(1)}, u32[]{:S(2)}, u32[]{:S(2)}) collective-permute-start(bf16[1024,256]{1,0:T(8,128)(2,1)S(1)} %collective-permute-done.2), channel_id=1, source_target_pairs={{0,64},{64,0},{1,65},{65,1},{2,66},{66,2},{3,67},{67,3},{4,68},{68... | collective-permute-start | bytes 1572872 | tf_op jit(solution)/shard_map/ppermute | solution.py:182
  54.9 0.0 collective-permute-done.5
  55.0 3.0 %collective-permute-start.6 = (bf16[1024,256]{1,0:T(8,128)(2,1)S(1)}, bf16[1024,256]{1,0:T(8,128)(2,1)S(1)}, u32[]{:S(2)}, u32[]{:S(2)}) collective-permute-start(bf16[1024,256]{1,0:T(8,128)(2,1)S(1)} %collective-permute-done.5), channel_id=1, source_target_pairs={{0,4},{4,8},{8,12},{12,16},{16,20},{20,24},{24,28},{28,32},{32,36}... | collective-permute-start | bytes 1572872 | tf_op jit(solution)/shard_map/stream_1_step_4/ppermute | solution.py:180
  58.0 3.0 %collective-permute-start.20 = (bf16[1024,256]{1,0:T(8,128)(2,1)S(1)}, bf16[1024,256]{1,0:T(8,128)(2,1)S(1)}, u32[]{:S(2)}, u32[]{:S(2)}) collective-permute-start(bf16[1024,256]{1,0:T(8,128)(2,1)S(1)} %collective-permute-done.4), channel_id=1, source_target_pairs={{0,64},{64,0},{1,65},{65,1},{2,66},{66,2},{3,67},{67,3},{4,68},{68... | collective-permute-start | bytes 1572872 | tf_op jit(solution)/shard_map/ppermute | solution.py:182
  61.0 0.3 collective-permute-done.13.refs_9_
  61.3 3.1 %collective-permute-start.14 = (bf16[1024,256]{1,0:T(8,128)(2,1)S(1)}, bf16[1024,256]{1,0:T(8,128)(2,1)S(1)}, u32[]{:S(2)}, u32[]{:S(2)}) collective-permute-start(bf16[1024,256]{1,0:T(8,128)(2,1)S(1)} %collective-permute-done.13.refs_9_), channel_id=1, source_target_pairs={{0,4},{4,8},{8,12},{12,16},{16,20},{20,24},{24,28},{28,32},{32,36}... | collective-permute-start | bytes 1572872 | tf_op jit(solution)/shard_map/stream_0_step_5/ppermute | solution.py:180
  64.4 0.0 collective-permute-done.7.refs_10_
  64.4 2.5 %collective-permute-done.6 = bf16[1024,256]{1,0:T(8,128)(2,1)S(1)} collective-permute-done((bf16[1024,256]{1,0:T(8,128)(2,1)S(1)}, bf16[1024,256]{1,0:T(8,128)(2,1)S(1)}, u32[]{:S(2)}, u32[]{:S(2)}) %collective-permute-start.6) | collective-permute-done | bytes 524320 | tf_op jit(solution)/shard_map/stream_1_step_4/ppermute | solution.py:180
  66.9 2.8 %collective-permute-start.19 = (bf16[1024,256]{1,0:T(8,128)(2,1)S(1)}, bf16[1024,256]{1,0:T(8,128)(2,1)S(1)}, u32[]{:S(2)}, u32[]{:S(2)}) collective-permute-start(bf16[1024,256]{1,0:T(8,128)(2,1)S(1)} %collective-permute-done.6), channel_id=1, source_target_pairs={{0,4},{4,8},{8,12},{12,16},{16,20},{20,24},{24,28},{28,32},{32,36}... | collective-permute-start | bytes 1572872 | tf_op jit(solution)/shard_map/stream_1_step_5/ppermute | solution.py:180
  69.8 4.2 %collective-permute-start.9 = (bf16[512,512]{1,0:T(8,128)(2,1)S(1)}, bf16[512,512]{1,0:T(8,128)(2,1)S(1)}, u32[]{:S(2)}, u32[]{:S(2)}) collective-permute-start(bf16[512,512]{1,0:T(8,128)(2,1)S(1)} %copy-done.1), channel_id=1, source_target_pairs={{0,256},{128,384},{256,0},{384,128},{1,257},{129,385},{257,1},{385... | collective-permute-start | bytes 1572872 | tf_op jit(solution)/shard_map/ppermute | solution.py:189
  74.0 0.0 collective-permute-done.3.refs_1_
  74.0 2.2 %collective-permute-start.8 = (bf16[1024,512]{1,0:T(8,128)(2,1)S(1)}, bf16[1024,512]{1,0:T(8,128)(2,1)S(1)}, u32[]{:S(2)}, u32[]{:S(2)}) collective-permute-start(bf16[1024,512]{1,0:T(8,128)(2,1)S(1)} %collective-permute-done.3.refs_1_), channel_id=1, source_target_pairs={{0,64},{64,0},{1,65},{65,1},{2,66},{66,2},{3,67},{67,3},{4,68},{68... | collective-permute-start | bytes 3145736 | tf_op jit(solution)/shard_map/ppermute | solution.py:191
  76.2 0.0 collective-permute-done.20.refs_9_
  76.2 2.2 %collective-permute-start.22 = (bf16[1024,256]{1,0:T(8,128)(2,1)S(1)}, bf16[1024,256]{1,0:T(8,128)(2,1)S(1)}, u32[]{:S(2)}, u32[]{:S(2)}) collective-permute-start(bf16[1024,256]{1,0:T(8,128)(2,1)S(1)} %collective-permute-done.5), channel_id=1, source_target_pairs={{0,64},{64,0},{1,65},{65,1},{2,66},{66,2},{3,67},{67,3},{4,68},{68... | collective-permute-start | bytes 1572872 | tf_op jit(solution)/shard_map/ppermute | solution.py:182
  78.3 0.0 collective-permute-done.14.refs_10_
  78.3 4.6 %collective-permute-start.16 = (bf16[1024,256]{1,0:T(8,128)(2,1)S(1)}, bf16[1024,256]{1,0:T(8,128)(2,1)S(1)}, u32[]{:S(2)}, u32[]{:S(2)}) collective-permute-start(bf16[1024,256]{1,0:T(8,128)(2,1)S(1)} %collective-permute-done.14.refs_10_), channel_id=1, source_target_pairs={{0,4},{4,8},{8,12},{12,16},{16,20},{20,24},{24,28},{28,32},{32,36}... | collective-permute-start | bytes 1572872 | tf_op jit(solution)/shard_map/stream_0_step_6/ppermute | solution.py:180
  83.0 0.0 collective-permute-done.19
  83.0 2.0 %collective-permute-start.21 = (bf16[1024,256]{1,0:T(8,128)(2,1)S(1)}, bf16[1024,256]{1,0:T(8,128)(2,1)S(1)}, u32[]{:S(2)}, u32[]{:S(2)}) collective-permute-start(bf16[1024,256]{1,0:T(8,128)(2,1)S(1)} %collective-permute-done.19), channel_id=1, source_target_pairs={{0,4},{4,8},{8,12},{12,16},{16,20},{20,24},{24,28},{28,32},{32,36}... | collective-permute-start | bytes 1572872 | tf_op jit(solution)/shard_map/stream_1_step_6/ppermute | solution.py:180
  85.0 1.2 collective-permute-done.9.refs_3_
  86.3 3.1 %collective-permute-start.15 = (bf16[512,512]{1,0:T(8,128)(2,1)S(1)}, bf16[512,512]{1,0:T(8,128)(2,1)S(1)}, u32[]{:S(2)}, u32[]{:S(2)}) collective-permute-start(bf16[512,512]{1,0:T(8,128)(2,1)S(1)} %collective-permute-done.9.refs_3_), channel_id=1, source_target_pairs={{0,64},{64,0},{1,65},{65,1},{2,66},{66,2},{3,67},{67,3},{4,68},{68... | collective-permute-start | bytes 1572872 | tf_op jit(solution)/shard_map/ppermute | solution.py:193
  89.4 0.0 collective-permute-done.16.refs_11_
  89.4 4.7 %collective-permute-start.17 = (bf16[1024,256]{1,0:T(8,128)(2,1)S(1)}, bf16[1024,256]{1,0:T(8,128)(2,1)S(1)}, u32[]{:S(2)}, u32[]{:S(2)}) collective-permute-start(bf16[1024,256]{1,0:T(8,128)(2,1)S(1)} %collective-permute-done.16.refs_11_), channel_id=1, source_target_pairs={{0,4},{4,8},{8,12},{12,16},{16,20},{20,24},{24,28},{28,32},{32,36}... | collective-permute-start | bytes 1572872 | tf_op jit(solution)/shard_map/stream_0_step_7/ppermute | solution.py:180
  94.1 0.0 collective-permute-done.22.refs_8_
  94.1 0.6 collective-permute-done.21
  94.7 5.0 %collective-permute-start.23 = (bf16[1024,256]{1,0:T(8,128)(2,1)S(1)}, bf16[1024,256]{1,0:T(8,128)(2,1)S(1)}, u32[]{:S(2)}, u32[]{:S(2)}) collective-permute-start(bf16[1024,256]{1,0:T(8,128)(2,1)S(1)} %collective-permute-done.21), channel_id=1, source_target_pairs={{0,4},{4,8},{8,12},{12,16},{16,20},{20,24},{24,28},{28,32},{32,36}... | collective-permute-start | bytes 1572872 | tf_op jit(solution)/shard_map/stream_1_step_7/ppermute | solution.py:180
  99.7 1.9 %collective-permute-start.27 = (bf16[1024,256]{1,0:T(8,128)(2,1)S(1)}, bf16[1024,256]{1,0:T(8,128)(2,1)S(1)}, u32[]{:S(2)}, u32[]{:S(2)}) collective-permute-start(bf16[1024,256]{1,0:T(8,128)(2,1)S(1)} %collective-permute-done.6), channel_id=1, source_target_pairs={{0,64},{64,0},{1,65},{65,1},{2,66},{66,2},{3,67},{67,3},{4,68},{68... | collective-permute-start | bytes 1572872 | tf_op jit(solution)/shard_map/ppermute | solution.py:182
  101.6 0.0 collective-permute-done.15.refs_4_
  101.7 2.4 %collective-permute-start.26 = (bf16[1024,256]{1,0:T(8,128)(2,1)S(1)}, bf16[1024,256]{1,0:T(8,128)(2,1)S(1)}, u32[]{:S(2)}, u32[]{:S(2)}) collective-permute-start(bf16[1024,256]{1,0:T(8,128)(2,1)S(1)} %collective-permute-done.19), channel_id=1, source_target_pairs={{0,64},{64,0},{1,65},{65,1},{2,66},{66,2},{3,67},{67,3},{4,68},{68... | collective-permute-start | bytes 1572872 | tf_op jit(solution)/shard_map/ppermute | solution.py:182
  104.1 0.0 collective-permute-done.8.refs_2_
  104.1 1.9 %collective-permute-start.25 = (bf16[1024,256]{1,0:T(8,128)(2,1)S(1)}, bf16[1024,256]{1,0:T(8,128)(2,1)S(1)}, u32[]{:S(2)}, u32[]{:S(2)}) collective-permute-start(bf16[1024,256]{1,0:T(8,128)(2,1)S(1)} %collective-permute-done.21), channel_id=1, source_target_pairs={{0,64},{64,0},{1,65},{65,1},{2,66},{66,2},{3,67},{67,3},{4,68},{68... | collective-permute-start | bytes 1572872 | tf_op jit(solution)/shard_map/ppermute | solution.py:182
  106.0 0.0 collective-permute-done.17.refs_5_
  106.0 3.6 %collective-permute-start.18 = (bf16[1024,256]{1,0:T(8,128)(2,1)S(1)}, bf16[1024,256]{1,0:T(8,128)(2,1)S(1)}, u32[]{:S(2)}, u32[]{:S(2)}) collective-permute-start(bf16[1024,256]{1,0:T(8,128)(2,1)S(1)} %collective-permute-done.17.refs_5_), channel_id=1, source_target_pairs={{0,4},{4,8},{8,12},{12,16},{16,20},{20,24},{24,28},{28,32},{32,36}... | collective-permute-start | bytes 1572872 | tf_op jit(solution)/shard_map/stream_0_step_8/ppermute | solution.py:180
  109.6 0.0 collective-permute-done.23
  109.6 1.9 %collective-permute-start.24 = (bf16[1024,256]{1,0:T(8,128)(2,1)S(1)}, bf16[1024,256]{1,0:T(8,128)(2,1)S(1)}, u32[]{:S(2)}, u32[]{:S(2)}) collective-permute-start(bf16[1024,256]{1,0:T(8,128)(2,1)S(1)} %collective-permute-done.23), channel_id=1, source_target_pairs={{0,64},{64,0},{1,65},{65,1},{2,66},{66,2},{3,67},{67,3},{4,68},{68... | collective-permute-start | bytes 1572872 | tf_op jit(solution)/shard_map/ppermute | solution.py:194
  111.5 2.7 %shard_map.74.refs_8_ = f32[1024,512]{1,0:T(8,128)S(1)} custom-call(bf16[1024,512]{1,0:T(8,128)(2,1)S(1)} %constant_dynamic-update-slice_fusion.refs_0_, bf16[1024,512]{1,0:T(8,128)(2,1)S(1)} %collective-permute-done.3.refs_1_, bf16[1024,512]{1,0:T(8,128)(2,1)S(1)} %collective-permute-done.8.refs_2_, bf16[512,512]{1,0:T(8,128)(2,1)S(1)} %collective-permute-done.9.refs_3_, ...), custom_call_target="tpu_custom_call" | custom-call | flops 1879048192 | bytes 2097152 | tf_op jit(solution)/shard_map/pallas_call | solution.py:146
  114.2 0.0 collective-permute-done.27.refs_7_
  114.2 0.0 collective-permute-done.26.refs_6_
  114.2 2.4 %shard_map.75.refs_9_ = f32[1024,512]{1,0:T(8,128)S(1)} custom-call(bf16[1024,512]{1,0:T(8,128)(2,1)S(1)} %constant_dynamic-update-slice_fusion.refs_0_, bf16[1024,512]{1,0:T(8,128)(2,1)S(1)} %collective-permute-done.3.refs_1_, bf16[1024,512]{1,0:T(8,128)(2,1)S(1)} %collective-permute-done.8.refs_2_, bf16[512,512]{1,0:T(8,128)(2,1)S(1)} %collective-permute-done.9.refs_3_, ...), custom_call_target="tpu_custom_call" | custom-call | flops 1610612736 | bytes 2097152 | tf_op jit(solution)/shard_map/pallas_call | solution.py:146
  116.6 0.0 collective-permute-done.18.refs_6_
  116.6 1.9 %shard_map.76 = f32[4,272,512]{2,1,0:T(8,128)S(1)} custom-call(bf16[1024,512]{1,0:T(8,128)(2,1)S(1)} %constant_dynamic-update-slice_fusion.refs_0_, bf16[1024,512]{1,0:T(8,128)(2,1)S(1)} %collective-permute-done.3.refs_1_, bf16[1024,512]{1,0:T(8,128)(2,1)S(1)} %collective-permute-done.8.refs_2_, bf16[512,512]{1,0:T(8,128)(2,1)S(1)} %collective-permute-done.9.refs_3_, ...), custom_call_target="tpu_custom_call" | custom-call | flops 805306368 | bytes 2097152 | tf_op jit(solution)/shard_map/pallas_call | solution.py:146
  118.5 0.3 convert_element_type.9
  118.8 17.0 %all_to_all.5 = f16[4,272,512]{2,1,0:T(8,128)(2,1)S(1)} all-to-all(f16[4,272,512]{2,1,0:T(8,128)(2,1)S(1)} %convert_element_type.9), channel_id=1, replica_groups=mesh['y'=4,'core'=2,'col'=16,'layer'=4] {'layer'}, dimensions={0} | all-to-all | bytes 2228224 | tf_op jit(solution)/shard_map/all_to_all | solution.py:202
  135.8 0.1 convert_reduce_fusion
  136.0 1.1 multiply_reduce_fusion
  (7 shorter events, 0.1 us)
Async XLA Ops:
  2.4 67.4 %copy-start.1 = (bf16[512,512]{1,0:T(8,128)(2,1)S(1)}, bf16[512,512]{1,0:T(8,128)(2,1)}, u32[]{:S(2)}) copy-start(bf16[512,512]{1,0:T(8,128)(2,1)} %get-tuple-element.21) | copy-start | bytes 1572868
  2.4 109.1 %copy-start = (bf16[1024,256]{1,0:T(8,128)(2,1)S(1)}, bf16[1024,256]{1,0:T(8,128)(2,1)}, u32[]{:S(2)}) copy-start(bf16[1024,256]{1,0:T(8,128)(2,1)} %get-tuple-element.16.refs_5_) | copy-start | bytes 1572868
  2.4 14.7 %collective-permute-start = (bf16[1024,256]{1,0:T(8,128)(2,1)}, bf16[1024,256]{1,0:T(8,128)(2,1)S(1)}, u32[]{:S(2)}, u32[]{:S(2)}) collective-permute-start(bf16[1024,256]{1,0:T(8,128)(2,1)} %get-tuple-element.16.refs_5_), channel_id=1, source_target_pairs={{0,64},{64,0},{1,65},{65,1},{2,66},{66,2},{3,67},{67,3},{4,68},{68... | collective-permute-start | bytes 1572872 | tf_op jit(solution)/shard_map/ppermute | solution.py:142
  11.3 12.2 %collective-permute-start.10 = (bf16[1024,256]{1,0:T(8,128)(2,1)}, bf16[1024,256]{1,0:T(8,128)(2,1)S(1)}, u32[]{:S(2)}, u32[]{:S(2)}) collective-permute-start(bf16[1024,256]{1,0:T(8,128)(2,1)} %get-tuple-element.16.refs_5_), channel_id=1, source_target_pairs={{0,4},{4,8},{8,12},{12,16},{16,20},{20,24},{24,28},{28,32},{32,36}... | collective-permute-start | bytes 1572872 | tf_op jit(solution)/shard_map/stream_0_step_1/ppermute | solution.py:180
  17.1 11.9 %collective-permute-start.2 = (bf16[1024,256]{1,0:T(8,128)(2,1)S(1)}, bf16[1024,256]{1,0:T(8,128)(2,1)S(1)}, u32[]{:S(2)}, u32[]{:S(2)}) collective-permute-start(bf16[1024,256]{1,0:T(8,128)(2,1)S(1)} %collective-permute-done), channel_id=1, source_target_pairs={{0,4},{4,8},{8,12},{12,16},{16,20},{20,24},{24,28},{28,32},{32,36}... | collective-permute-start | bytes 1572872 | tf_op jit(solution)/shard_map/stream_1_step_1/ppermute | solution.py:180
  23.5 12.5 %collective-permute-start.11 = (bf16[1024,256]{1,0:T(8,128)(2,1)S(1)}, bf16[1024,256]{1,0:T(8,128)(2,1)S(1)}, u32[]{:S(2)}, u32[]{:S(2)}) collective-permute-start(bf16[1024,256]{1,0:T(8,128)(2,1)S(1)} %collective-permute-done.10.refs_6_), channel_id=1, source_target_pairs={{0,4},{4,8},{8,12},{12,16},{16,20},{20,24},{24,28},{28,32},{32,36}... | collective-permute-start | bytes 1572872 | tf_op jit(solution)/shard_map/stream_0_step_2/ppermute | solution.py:180
  29.0 11.2 %collective-permute-start.4 = (bf16[1024,256]{1,0:T(8,128)(2,1)S(1)}, bf16[1024,256]{1,0:T(8,128)(2,1)S(1)}, u32[]{:S(2)}, u32[]{:S(2)}) collective-permute-start(bf16[1024,256]{1,0:T(8,128)(2,1)S(1)} %collective-permute-done.2), channel_id=1, source_target_pairs={{0,4},{4,8},{8,12},{12,16},{16,20},{20,24},{24,28},{28,32},{32,36}... | collective-permute-start | bytes 1572872 | tf_op jit(solution)/shard_map/stream_1_step_2/ppermute | solution.py:180
  34.1 12.3 %collective-permute-start.1 = (bf16[512,512]{1,0:T(8,128)(2,1)}, bf16[512,512]{1,0:T(8,128)(2,1)S(1)}, u32[]{:S(2)}, u32[]{:S(2)}) collective-permute-start(bf16[512,512]{1,0:T(8,128)(2,1)} %get-tuple-element.21), channel_id=1, source_target_pairs={{0,64},{64,0},{1,65},{65,1},{2,66},{66,2},{3,67},{67,3},{4,68},{68... | collective-permute-start | bytes 1572872 | tf_op jit(solution)/shard_map/ppermute | solution.py:184
  36.0 15.1 %collective-permute-start.12 = (bf16[1024,256]{1,0:T(8,128)(2,1)S(1)}, bf16[1024,256]{1,0:T(8,128)(2,1)S(1)}, u32[]{:S(2)}, u32[]{:S(2)}) collective-permute-start(bf16[1024,256]{1,0:T(8,128)(2,1)S(1)} %collective-permute-done.11.refs_7_), channel_id=1, source_target_pairs={{0,4},{4,8},{8,12},{12,16},{16,20},{20,24},{24,28},{28,32},{32,36}... | collective-permute-start | bytes 1572872 | tf_op jit(solution)/shard_map/stream_0_step_3/ppermute | solution.py:180
  40.3 14.7 %collective-permute-start.5 = (bf16[1024,256]{1,0:T(8,128)(2,1)S(1)}, bf16[1024,256]{1,0:T(8,128)(2,1)S(1)}, u32[]{:S(2)}, u32[]{:S(2)}) collective-permute-start(bf16[1024,256]{1,0:T(8,128)(2,1)S(1)} %collective-permute-done.4), channel_id=1, source_target_pairs={{0,4},{4,8},{8,12},{12,16},{16,20},{20,24},{24,28},{28,32},{32,36}... | collective-permute-start | bytes 1572872 | tf_op jit(solution)/shard_map/stream_1_step_3/ppermute | solution.py:180
  46.4 27.5 %collective-permute-start.3 = (bf16[1024,512]{1,0:T(8,128)(2,1)S(1)}, bf16[1024,512]{1,0:T(8,128)(2,1)S(1)}, u32[]{:S(2)}, u32[]{:S(2)}) collective-permute-start(bf16[1024,512]{1,0:T(8,128)(2,1)S(1)} %constant_dynamic-update-slice_fusion.refs_0_), channel_id=1, source_target_pairs={{0,128},{64,448},{128,256},{192,64},{256,384},{320,192},{384,0},{4... | collective-permute-start | bytes 3145736 | tf_op jit(solution)/shard_map/ppermute | solution.py:187
  51.1 10.2 %collective-permute-start.13 = (bf16[1024,256]{1,0:T(8,128)(2,1)S(1)}, bf16[1024,256]{1,0:T(8,128)(2,1)S(1)}, u32[]{:S(2)}, u32[]{:S(2)}) collective-permute-start(bf16[1024,256]{1,0:T(8,128)(2,1)S(1)} %collective-permute-done.12.refs_8_), channel_id=1, source_target_pairs={{0,4},{4,8},{8,12},{12,16},{16,20},{20,24},{24,28},{28,32},{32,36}... | collective-permute-start | bytes 1572872 | tf_op jit(solution)/shard_map/stream_0_step_4/ppermute | solution.py:180
  53.0 11.4 %collective-permute-start.7 = (bf16[1024,256]{1,0:T(8,128)(2,1)S(1)}, bf16[1024,256]{1,0:T(8,128)(2,1)S(1)}, u32[]{:S(2)}, u32[]{:S(2)}) collective-permute-start(bf16[1024,256]{1,0:T(8,128)(2,1)S(1)} %collective-permute-done.2), channel_id=1, source_target_pairs={{0,64},{64,0},{1,65},{65,1},{2,66},{66,2},{3,67},{67,3},{4,68},{68... | collective-permute-start | bytes 1572872 | tf_op jit(solution)/shard_map/ppermute | solution.py:182
  55.0 12.0 %collective-permute-start.6 = (bf16[1024,256]{1,0:T(8,128)(2,1)S(1)}, bf16[1024,256]{1,0:T(8,128)(2,1)S(1)}, u32[]{:S(2)}, u32[]{:S(2)}) collective-permute-start(bf16[1024,256]{1,0:T(8,128)(2,1)S(1)} %collective-permute-done.5), channel_id=1, source_target_pairs={{0,4},{4,8},{8,12},{12,16},{16,20},{20,24},{24,28},{28,32},{32,36}... | collective-permute-start | bytes 1572872 | tf_op jit(solution)/shard_map/stream_1_step_4/ppermute | solution.py:180
  58.0 18.2 %collective-permute-start.20 = (bf16[1024,256]{1,0:T(8,128)(2,1)S(1)}, bf16[1024,256]{1,0:T(8,128)(2,1)S(1)}, u32[]{:S(2)}, u32[]{:S(2)}) collective-permute-start(bf16[1024,256]{1,0:T(8,128)(2,1)S(1)} %collective-permute-done.4), channel_id=1, source_target_pairs={{0,64},{64,0},{1,65},{65,1},{2,66},{66,2},{3,67},{67,3},{4,68},{68... | collective-permute-start | bytes 1572872 | tf_op jit(solution)/shard_map/ppermute | solution.py:182
  61.3 17.0 %collective-permute-start.14 = (bf16[1024,256]{1,0:T(8,128)(2,1)S(1)}, bf16[1024,256]{1,0:T(8,128)(2,1)S(1)}, u32[]{:S(2)}, u32[]{:S(2)}) collective-permute-start(bf16[1024,256]{1,0:T(8,128)(2,1)S(1)} %collective-permute-done.13.refs_9_), channel_id=1, source_target_pairs={{0,4},{4,8},{8,12},{12,16},{16,20},{20,24},{24,28},{28,32},{32,36}... | collective-permute-start | bytes 1572872 | tf_op jit(solution)/shard_map/stream_0_step_5/ppermute | solution.py:180
  66.9 16.0 %collective-permute-start.19 = (bf16[1024,256]{1,0:T(8,128)(2,1)S(1)}, bf16[1024,256]{1,0:T(8,128)(2,1)S(1)}, u32[]{:S(2)}, u32[]{:S(2)}) collective-permute-start(bf16[1024,256]{1,0:T(8,128)(2,1)S(1)} %collective-permute-done.6), channel_id=1, source_target_pairs={{0,4},{4,8},{8,12},{12,16},{16,20},{20,24},{24,28},{28,32},{32,36}... | collective-permute-start | bytes 1572872 | tf_op jit(solution)/shard_map/stream_1_step_5/ppermute | solution.py:180
  69.8 16.5 %collective-permute-start.9 = (bf16[512,512]{1,0:T(8,128)(2,1)S(1)}, bf16[512,512]{1,0:T(8,128)(2,1)S(1)}, u32[]{:S(2)}, u32[]{:S(2)}) collective-permute-start(bf16[512,512]{1,0:T(8,128)(2,1)S(1)} %copy-done.1), channel_id=1, source_target_pairs={{0,256},{128,384},{256,0},{384,128},{1,257},{129,385},{257,1},{385... | collective-permute-start | bytes 1572872 | tf_op jit(solution)/shard_map/ppermute | solution.py:189
  74.0 30.1 %collective-permute-start.8 = (bf16[1024,512]{1,0:T(8,128)(2,1)S(1)}, bf16[1024,512]{1,0:T(8,128)(2,1)S(1)}, u32[]{:S(2)}, u32[]{:S(2)}) collective-permute-start(bf16[1024,512]{1,0:T(8,128)(2,1)S(1)} %collective-permute-done.3.refs_1_), channel_id=1, source_target_pairs={{0,64},{64,0},{1,65},{65,1},{2,66},{66,2},{3,67},{67,3},{4,68},{68... | collective-permute-start | bytes 3145736 | tf_op jit(solution)/shard_map/ppermute | solution.py:191
  76.2 17.9 %collective-permute-start.22 = (bf16[1024,256]{1,0:T(8,128)(2,1)S(1)}, bf16[1024,256]{1,0:T(8,128)(2,1)S(1)}, u32[]{:S(2)}, u32[]{:S(2)}) collective-permute-start(bf16[1024,256]{1,0:T(8,128)(2,1)S(1)} %collective-permute-done.5), channel_id=1, source_target_pairs={{0,64},{64,0},{1,65},{65,1},{2,66},{66,2},{3,67},{67,3},{4,68},{68... | collective-permute-start | bytes 1572872 | tf_op jit(solution)/shard_map/ppermute | solution.py:182
  78.3 11.1 %collective-permute-start.16 = (bf16[1024,256]{1,0:T(8,128)(2,1)S(1)}, bf16[1024,256]{1,0:T(8,128)(2,1)S(1)}, u32[]{:S(2)}, u32[]{:S(2)}) collective-permute-start(bf16[1024,256]{1,0:T(8,128)(2,1)S(1)} %collective-permute-done.14.refs_10_), channel_id=1, source_target_pairs={{0,4},{4,8},{8,12},{12,16},{16,20},{20,24},{24,28},{28,32},{32,36}... | collective-permute-start | bytes 1572872 | tf_op jit(solution)/shard_map/stream_0_step_6/ppermute | solution.py:180
  83.0 11.7 %collective-permute-start.21 = (bf16[1024,256]{1,0:T(8,128)(2,1)S(1)}, bf16[1024,256]{1,0:T(8,128)(2,1)S(1)}, u32[]{:S(2)}, u32[]{:S(2)}) collective-permute-start(bf16[1024,256]{1,0:T(8,128)(2,1)S(1)} %collective-permute-done.19), channel_id=1, source_target_pairs={{0,4},{4,8},{8,12},{12,16},{16,20},{20,24},{24,28},{28,32},{32,36}... | collective-permute-start | bytes 1572872 | tf_op jit(solution)/shard_map/stream_1_step_6/ppermute | solution.py:180
  86.3 15.4 %collective-permute-start.15 = (bf16[512,512]{1,0:T(8,128)(2,1)S(1)}, bf16[512,512]{1,0:T(8,128)(2,1)S(1)}, u32[]{:S(2)}, u32[]{:S(2)}) collective-permute-start(bf16[512,512]{1,0:T(8,128)(2,1)S(1)} %collective-permute-done.9.refs_3_), channel_id=1, source_target_pairs={{0,64},{64,0},{1,65},{65,1},{2,66},{66,2},{3,67},{67,3},{4,68},{68... | collective-permute-start | bytes 1572872 | tf_op jit(solution)/shard_map/ppermute | solution.py:193
  89.4 16.6 %collective-permute-start.17 = (bf16[1024,256]{1,0:T(8,128)(2,1)S(1)}, bf16[1024,256]{1,0:T(8,128)(2,1)S(1)}, u32[]{:S(2)}, u32[]{:S(2)}) collective-permute-start(bf16[1024,256]{1,0:T(8,128)(2,1)S(1)} %collective-permute-done.16.refs_11_), channel_id=1, source_target_pairs={{0,4},{4,8},{8,12},{12,16},{16,20},{20,24},{24,28},{28,32},{32,36}... | collective-permute-start | bytes 1572872 | tf_op jit(solution)/shard_map/stream_0_step_7/ppermute | solution.py:180
  94.7 14.9 %collective-permute-start.23 = (bf16[1024,256]{1,0:T(8,128)(2,1)S(1)}, bf16[1024,256]{1,0:T(8,128)(2,1)S(1)}, u32[]{:S(2)}, u32[]{:S(2)}) collective-permute-start(bf16[1024,256]{1,0:T(8,128)(2,1)S(1)} %collective-permute-done.21), channel_id=1, source_target_pairs={{0,4},{4,8},{8,12},{12,16},{16,20},{20,24},{24,28},{28,32},{32,36}... | collective-permute-start | bytes 1572872 | tf_op jit(solution)/shard_map/stream_1_step_7/ppermute | solution.py:180
  99.7 14.5 %collective-permute-start.27 = (bf16[1024,256]{1,0:T(8,128)(2,1)S(1)}, bf16[1024,256]{1,0:T(8,128)(2,1)S(1)}, u32[]{:S(2)}, u32[]{:S(2)}) collective-permute-start(bf16[1024,256]{1,0:T(8,128)(2,1)S(1)} %collective-permute-done.6), channel_id=1, source_target_pairs={{0,64},{64,0},{1,65},{65,1},{2,66},{66,2},{3,67},{67,3},{4,68},{68... | collective-permute-start | bytes 1572872 | tf_op jit(solution)/shard_map/ppermute | solution.py:182
  101.7 12.6 %collective-permute-start.26 = (bf16[1024,256]{1,0:T(8,128)(2,1)S(1)}, bf16[1024,256]{1,0:T(8,128)(2,1)S(1)}, u32[]{:S(2)}, u32[]{:S(2)}) collective-permute-start(bf16[1024,256]{1,0:T(8,128)(2,1)S(1)} %collective-permute-done.19), channel_id=1, source_target_pairs={{0,64},{64,0},{1,65},{65,1},{2,66},{66,2},{3,67},{67,3},{4,68},{68... | collective-permute-start | bytes 1572872 | tf_op jit(solution)/shard_map/ppermute | solution.py:182
  104.1 10.1 %collective-permute-start.25 = (bf16[1024,256]{1,0:T(8,128)(2,1)S(1)}, bf16[1024,256]{1,0:T(8,128)(2,1)S(1)}, u32[]{:S(2)}, u32[]{:S(2)}) collective-permute-start(bf16[1024,256]{1,0:T(8,128)(2,1)S(1)} %collective-permute-done.21), channel_id=1, source_target_pairs={{0,64},{64,0},{1,65},{65,1},{2,66},{66,2},{3,67},{67,3},{4,68},{68... | collective-permute-start | bytes 1572872 | tf_op jit(solution)/shard_map/ppermute | solution.py:182
  106.0 10.6 %collective-permute-start.18 = (bf16[1024,256]{1,0:T(8,128)(2,1)S(1)}, bf16[1024,256]{1,0:T(8,128)(2,1)S(1)}, u32[]{:S(2)}, u32[]{:S(2)}) collective-permute-start(bf16[1024,256]{1,0:T(8,128)(2,1)S(1)} %collective-permute-done.17.refs_5_), channel_id=1, source_target_pairs={{0,4},{4,8},{8,12},{12,16},{16,20},{20,24},{24,28},{28,32},{32,36}... | collective-permute-start | bytes 1572872 | tf_op jit(solution)/shard_map/stream_0_step_8/ppermute | solution.py:180
  109.6 7.0 %collective-permute-start.24 = (bf16[1024,256]{1,0:T(8,128)(2,1)S(1)}, bf16[1024,256]{1,0:T(8,128)(2,1)S(1)}, u32[]{:S(2)}, u32[]{:S(2)}) collective-permute-start(bf16[1024,256]{1,0:T(8,128)(2,1)S(1)} %collective-permute-done.23), channel_id=1, source_target_pairs={{0,64},{64,0},{1,65},{65,1},{2,66},{66,2},{3,67},{67,3},{4,68},{68... | collective-permute-start | bytes 1572872 | tf_op jit(solution)/shard_map/ppermute | solution.py:194

commit v6 on v5

--- a/solution.py
+++ b/solution.py
@@ -26,32 +26,54 @@
     return kept.astype(jnp.bfloat16)
 
 
-def mask_kernel(*refs):
-    count = 7
-    a_out, b_out = refs[count : count + 2]
-    slots, sems = refs[count + 2 : -1], refs[-1]
-    copies = [pltpu.make_async_copy(refs[i], slots[i], sems.at[i]) for i in range(count)]
+def fetched(refs):
+    sems, refs = refs[-1], refs[:-1]
+    count = len(refs) // 2
+    copies = [pltpu.make_async_copy(refs[i], refs[count + 1 + i], sems.at[i]) for i in range(count)]
     for copy in copies:
         copy.start()
     for copy in copies:
         copy.wait()
-    mask_a, mask_b, rows, inner, cols, a, b = slots
+    return refs[count], refs[count + 1 :]
+
+
+def mask_a_kernel(*refs):
+    out_ref, (mask, rows, inner, a) = fetched(refs)
     columns = inner[0, lax.axis_index("col")]
     for i in range(ROWS // BS):
         place = slice(i * BS, (i + 1) * BS)
-        a_out[place, :] = masked(a[0, place, :], rows[i] * mask_a[i], columns)
-    first = (lax.axis_index("y") * CORES + lax.axis_index("core")) * mask_b.shape[1]
-    for k in range(mask_b.shape[1]):
-        for n in range(mask_b.shape[2]):
+        out_ref[place, :] = masked(a[0, place, :], rows[i] * mask[i], columns)
+
+
+def mask_b_kernel(*refs):
+    out_ref, (mask, inner, cols, b) = fetched(refs)
+    first = (lax.axis_index("y") * CORES + lax.axis_index("core")) * mask.shape[1]
+    for k in range(mask.shape[1]):
+        for n in range(mask.shape[2]):
             place = (slice(k * BS, (k + 1) * BS), slice(n * BS, (n + 1) * BS))
-            size = inner[0, first + k] * mask_b[0, k, n]
-            b_out[place] = masked(b[(0,) + place], size, cols[n])
+            size = inner[0, first + k] * mask[0, k, n]
+            out_ref[place] = masked(b[(0,) + place], size, cols[n])
+
+
+def mask_call(kernel, shape, *args):
+    spaces = [pltpu.SMEM] * (len(args) - 1) + [pltpu.VMEM]
+    return pl.pallas_call(
+        kernel,
+        out_shape=jax.ShapeDtypeStruct(shape, jnp.bfloat16),
+        in_specs=[pl.BlockSpec(memory_space=pltpu.HBM)] * len(args),
+        out_specs=VMEM,
+        scratch_shapes=[s(x.shape, x.dtype) for s, x in zip(spaces, args)]
+        + [pltpu.SemaphoreType.DMA((len(args),))],
+        compiler_params=pltpu.CompilerParams(vmem_limit_bytes=60 * 1024 * 1024),
+    )(*args)
 
 
 def product_kernel(steps, blocks, added, *refs):
-    b_refs, refs = refs[:5], refs[5:]
+    b_refs, refs = refs[:4], refs[4:]
     a_refs, refs = refs[: len(steps)], refs[len(steps) :]
-    adds, (out_ref, a_all, b_all, extra, sems) = refs[:added], refs[added:]
+    adds, refs = refs[:added], refs[added:]
+    outs, (a_all, b_all, extra, sems) = refs[:-4], refs[-4:]
+    out_ref, own_ref = outs[0], outs[-1]
     z, y, core = lax.axis_index("col"), lax.axis_index("y"), lax.axis_index("core")
     way = 2 * core - 1
     first, count = steps[0], len(steps)
@@ -61,7 +83,7 @@
         (0, 0, y, mine), (0, 1, y, theirs),
         (1, 0, y + way, mine), (1, 1, y + way, theirs),
         (2, 0, y - way, theirs), (2, 1, y - way, mine),
-        (3, 0, y + 2, mine), (4, 0, y + 2, theirs),
+        (3, 0, y + 2, mine), (3, 1, y + 2, theirs),
     )
     for i, at, chip, owner in parts:
         for half in range(2):
@@ -89,10 +111,14 @@
         total = jnp.dot(a_all[rows, :], b, preferred_element_type=jnp.float32)
         for i in range(added):
             total = total + extra[i, rows, :]
-        if len(out_ref.shape) == 2:
+        if len(outs) == 1:
             out_ref[rows, :] = total
         else:
             encode(total, out_ref.at[tile])
+
+            @pl.when(lax.axis_index("layer") == tile)
+            def _(total=total):
+                own_ref[...] = total
 
 
 def encode(total, out_ref):
@@ -106,11 +132,12 @@
     out_ref[BS:, :] = jnp.broadcast_to(code, (CODE_ROWS, total.shape[1]))
 
 
-def decoded(parts):
+def decoded(parts, own):
     code = parts[:, BS:, :1].astype(jnp.float32).max(axis=1, keepdims=True)
     scale = jnp.ones_like(code)
     for c in range(1, CODES + 1):
         scale = jnp.where(code > c - 0.5, 2.0 ** (-STEP * c), scale)
+    scale = jnp.where(jnp.arange(parts.shape[0])[:, None, None] == own, 0.0, scale)
     return parts[:, :BS].astype(jnp.float32) * scale
 
 
@@ -124,20 +151,9 @@
     ring = [
         (c * cols + i, c * cols + (i + (1, -1)[c]) % cols) for c in range(CORES) for i in range(cols)
     ]
-    args = (mask_a.reshape(-1), mask_b, row_sizes, inner_sizes, col_sizes, a_panel, b_panel)
-    own, b_eff = pl.pallas_call(
-        mask_kernel,
-        out_shape=tuple(
-            jax.ShapeDtypeStruct(p.shape[1:], jnp.bfloat16) for p in (a_panel, b_panel)
-        ),
-        in_specs=[pl.BlockSpec(memory_space=pltpu.HBM)] * len(args),
-        out_specs=(VMEM, VMEM),
-        scratch_shapes=[pltpu.SMEM(x.shape, x.dtype) for x in args[:5]]
-        + [pltpu.VMEM(x.shape, x.dtype) for x in args[5:]]
-        + [pltpu.SemaphoreType.DMA((len(args),))],
-        compiler_params=pltpu.CompilerParams(vmem_limit_bytes=60 * 1024 * 1024),
-    )(*args)
-
+    own = mask_call(
+        mask_a_kernel, a_panel.shape[1:], mask_a.reshape(-1), row_sizes, inner_sizes, a_panel
+    )
     last = cols // 2
     held = [[own], [lax.ppermute(own, "core", SWAP)]]
 
@@ -145,11 +161,14 @@
         n = len(steps)
         return pl.pallas_call(
             functools.partial(product_kernel, steps, cols, len(adds)),
-            out_shape=jax.ShapeDtypeStruct((ROWS // BS, BS + CODE_ROWS, width), jnp.float32)
+            out_shape=(
+                jax.ShapeDtypeStruct((ROWS // BS, BS + CODE_ROWS, width), jnp.float32),
+                jax.ShapeDtypeStruct((BS, width), jnp.float32),
+            )
             if coded
             else jax.ShapeDtypeStruct((ROWS, width), jnp.float32),
-            in_specs=[HBM] * (5 + len(arrays) + len(adds)),
-            out_specs=VMEM,
+            in_specs=[HBM] * (4 + len(arrays) + len(adds)),
+            out_specs=(VMEM, VMEM) if coded else VMEM,
             scratch_shapes=[
                 pltpu.VMEM((ROWS, n * BS), jnp.bfloat16),
                 pltpu.VMEM((n, BS, width), jnp.bfloat16),
@@ -165,41 +184,46 @@
     near_by = [
         (i * CORES + c, (i + (1, -1)[c]) % chips * CORES + c) for i in range(chips) for c in range(CORES)
     ]
-    far_away = [(i, (i + 2) % chips) for i in range(chips)]
-    b_all = [None] * 5
-    b_other = None
+    b_eff = b_other = None
+    b_all = [None] * 4
     turned = []
     for step in range(1, last + 1):
         for j in range(2):
             if (step, j) == (last, 1):
                 continue
             sent = held[j][-1]
-            if j == 1 and step > 4:
-                sent = after(sent, turned[step - 5])
             with jax.named_scope(f"stream_{j}_step_{step}"):
                 held[j].append(lax.ppermute(sent, ("core", "col"), ring))
+            if (step, j) == (1, 0):
+                sizes_k = after(inner_sizes, held[0][1])
+                b_eff = mask_call(
+                    mask_b_kernel, b_panel.shape[1:], mask_b, sizes_k, col_sizes, b_panel
+                )
+            if (step, j) == (1, 1):
+                with jax.named_scope("b_swap"):
+                    b_other = lax.ppermute(b_eff, "core", SWAP)
+            if (step, j) == (2, 1):
+                b_all[0] = jnp.concatenate([b_eff, after(b_other, sent)])
+                with jax.named_scope("b_near"):
+                    b_all[1] = lax.ppermute(b_all[0], ("y", "core"), near_by)
+            if (step, j) == (3, 1):
+                with jax.named_scope("b_far"):
+                    b_all[3] = lax.ppermute(after(b_all[1], sent), ("y", "core"), near_by)
+            if (step, j) == (5, 1):
+                with jax.named_scope("b_turn"):
+                    b_all[2] = lax.ppermute(after(b_all[1], sent), "core", SWAP)
             if j == 1 and step > 1:
                 turned.append(lax.ppermute(held[1][step - 1], "core", SWAP))
-            if (step, j) == (1, 1):
-                b_other = lax.ppermute(after(b_eff, sent), "core", SWAP)
-            if (step, j) == (2, 1):
-                b_all[0] = jnp.concatenate([b_eff, after(b_other, sent)])
-                b_all[1] = lax.ppermute(b_all[0], ("y", "core"), near_by)
-            if (step, j) == (3, 1):
-                b_all[3] = lax.ppermute(after(b_eff, sent), "y", far_away)
-            if (step, j) == (5, 1):
-                b_all[2] = lax.ppermute(after(b_all[1], sent), "core", SWAP)
-            if (step, j) == (6, 0):
-                b_all[4] = lax.ppermute(after(b_all[3], sent), "core", SWAP)
     turned.append(lax.ppermute(held[1][last - 1], "core", SWAP))
 
     shards = held[0] + turned[::-1]
     near = product(range(last - 1), shards[: last - 1])
-    across = product(range(last + 2, cols), shards[last + 2 :])
-    steps = range(last - 1, last + 2)
-    parts = product(steps, [shards[s] for s in steps], (near, across), True)
+    across = product(range(last + 3, cols), shards[last + 3 :])
+    steps = range(last - 1, last + 3)
+    parts, mine = product(steps, [shards[s] for s in steps], (near, across), True)
     parts = parts.astype(jnp.float16)
-    return decoded(lax.all_to_all(parts, "layer", 0, 0)).sum(axis=0)
+    parts = decoded(lax.all_to_all(parts, "layer", 0, 0), lax.axis_index("layer"))
+    return mine + parts.sum(axis=0)
 
 
 def solution(mesh):

time: 139 us -> 142 us (1.022)
  blocking collectives: 17 us -> 0 us
  waiting for transfers between devices: 9.6 us -> 23.6 us
  starting transfers between devices: 98 us -> 101 us
  Pallas kernels: 9.33 us -> 12 us
  other arithmetic: 1.52 us -> 3.73 us
    all_to_all x1 -> x0, blocking collectives: 17 us -> none  [on_device(): return decoded(lax.all_to_all(parts, 'layer', 0, 0)).sum(axis=0)]
    all_to_all x0 -> x1, waiting for transfers between devices: none -> 14.7 us  [on_device(): lax.all_to_all(parts, 'layer', 0, 0)]
    all_to_all x0 -> x1, starting transfers between devices: none -> 4.01 us  [on_device(): lax.all_to_all(parts, 'layer', 0, 0)]
    ppermute x3 -> x2, starting transfers between devices: 9.25 us -> 6.56 us  [the longest x1 4.64 us: on_device(): b_all[3] = lax.ppermute(after(b_all[1], sent), ('y', 'core'), near_by)]
    pallas_call x1 -> x2, Pallas kernels: 2.39 us -> 4.06 us  [mask_call(): pl.pallas_call(kernel, out_shape=jax.ShapeDtypeStruct(shape, jnp.bfloat16...]
    ppermute x1, starting transfers between devices: 1.92 us -> 3.51 us  [on_device(): turned.append(lax.ppermute(held[1][last - 1], 'core', SWAP))]
  transfers between devices with their start and end apart: 28 -> 28, of which waited for: 7 -> 7; matrix products, arithmetic and copies ran while one was open for 1% -> 1% of each run, Pallas kernels for 4% -> 5%
where the time goes in v6:
time: 142 us; the launch traced here: 141 us
  starting transfers between devices  101 us (71%)
  waiting for transfers between devices  23.6 us (17%)
  Pallas kernels  12 us (8%)
  other arithmetic  3.73 us (3%)
    ppermute x15, starting transfers between devices, on_device(): held[j].append(lax.ppermute(sent, ('core', 'col'), ring))  57.9 us
    all_to_all x1, waiting for transfers between devices, on_device(): lax.all_to_all(parts, 'layer', 0, 0)  14.7 us
    ppermute x6, starting transfers between devices, on_device(): turned.append(lax.ppermute(held[1][step - 1], 'core', SWAP))  13.4 us
    ppermute x15, waiting for transfers between devices, on_device(): held[j].append(lax.ppermute(sent, ('core', 'col'), ring))  8.81 us
    ppermute x1, starting transfers between devices, on_device(): held = [[own], [lax.ppermute(own, 'core', SWAP)]]  8.79 us
    pallas_call x3, Pallas kernels, product(): pl.pallas_call(functools.partial(product_kernel, steps, cols, len(adds)),...  7.97 us
    ppermute x1, starting transfers between devices, on_device(): b_all[1] = lax.ppermute(b_all[0], ('y', 'core'), near_by)  4.77 us
    ppermute x1, starting transfers between devices, on_device(): b_all[3] = lax.ppermute(after(b_all[1], sent), ('y', 'core'), near_by)  4.64 us
  transfers between devices with their start and end apart: 28, of which 7 were waited for; matrix products, arithmetic and copies ran while one was open for 1% of the time, Pallas kernels for 5%

profile of v6, /device:TPU:1, one launch (start us, length us, event | category | flops | bytes accessed | tf_op | source)
XLA Modules:
  0.0 140.6 jit_solution(15788847934843496741)
XLA Ops:
  0.0 2.0 %shard_map.73.refs_4_ = bf16[1024,256]{1,0:T(8,128)(2,1)} custom-call(s32[4]{0:T(128)} %bitcast.1, s32[4]{0:T(128)} %refs_1_.1, s32[1,16]{1,0:T(1,128)} %refs_1_.2, bf16[1,1024,256]{2,1,0:T(8,128)(2,1)} %refs_3_.2), custom_call_target="tpu_custom_call" | custom-call | tf_op jit(solution)/shard_map/pallas_call | solution.py:60
  2.0 8.8 %collective-permute-start.2 = (bf16[1024,256]{1,0:T(8,128)(2,1)}, bf16[1024,256]{1,0:T(8,128)(2,1)S(1)}, u32[]{:S(2)}, u32[]{:S(2)}) collective-permute-start(bf16[1024,256]{1,0:T(8,128)(2,1)} %shard_map.73.refs_4_), channel_id=1, source_target_pairs={{0,64},{64,0},{1,65},{65,1},{2,66},{66,2},{3,67},{67,3},{4,68},{68... | collective-permute-start | bytes 1572872 | tf_op jit(solution)/shard_map/ppermute | solution.py:158
  10.8 5.7 %collective-permute-start = (bf16[1024,256]{1,0:T(8,128)(2,1)}, bf16[1024,256]{1,0:T(8,128)(2,1)S(1)}, u32[]{:S(2)}, u32[]{:S(2)}) collective-permute-start(bf16[1024,256]{1,0:T(8,128)(2,1)} %shard_map.73.refs_4_), channel_id=1, source_target_pairs={{0,4},{4,8},{8,12},{12,16},{16,20},{20,24},{24,28},{28,32},{32,36}... | collective-permute-start | bytes 1572872 | tf_op jit(solution)/shard_map/stream_0_step_1/ppermute | solution.py:196
  16.6 0.0 collective-permute-done.2
  16.6 2.6 %collective-permute-start.3 = (bf16[1024,256]{1,0:T(8,128)(2,1)S(1)}, bf16[1024,256]{1,0:T(8,128)(2,1)S(1)}, u32[]{:S(2)}, u32[]{:S(2)}) collective-permute-start(bf16[1024,256]{1,0:T(8,128)(2,1)S(1)} %collective-permute-done.2), channel_id=1, source_target_pairs={{0,4},{4,8},{8,12},{12,16},{16,20},{20,24},{24,28},{28,32},{32,36}... | collective-permute-start | bytes 1572872 | tf_op jit(solution)/shard_map/stream_1_step_1/ppermute | solution.py:196
  19.2 3.8 %collective-permute-done.refs_5_ = bf16[1024,256]{1,0:T(8,128)(2,1)S(1)} collective-permute-done((bf16[1024,256]{1,0:T(8,128)(2,1)}, bf16[1024,256]{1,0:T(8,128)(2,1)S(1)}, u32[]{:S(2)}, u32[]{:S(2)}) %collective-permute-start) | collective-permute-done | bytes 524320 | tf_op jit(solution)/shard_map/stream_0_step_1/ppermute | solution.py:196
  23.0 4.9 %collective-permute-start.10 = (bf16[1024,256]{1,0:T(8,128)(2,1)S(1)}, bf16[1024,256]{1,0:T(8,128)(2,1)S(1)}, u32[]{:S(2)}, u32[]{:S(2)}) collective-permute-start(bf16[1024,256]{1,0:T(8,128)(2,1)S(1)} %collective-permute-done.refs_5_), channel_id=1, source_target_pairs={{0,4},{4,8},{8,12},{12,16},{16,20},{20,24},{24,28},{28,32},{32,36}... | collective-permute-start | bytes 1572872 | tf_op jit(solution)/shard_map/stream_0_step_2/ppermute | solution.py:196
  27.9 0.6 collective-permute-done.3
  28.5 5.0 %collective-permute-start.5 = (bf16[1024,256]{1,0:T(8,128)(2,1)S(1)}, bf16[1024,256]{1,0:T(8,128)(2,1)S(1)}, u32[]{:S(2)}, u32[]{:S(2)}) collective-permute-start(bf16[1024,256]{1,0:T(8,128)(2,1)S(1)} %collective-permute-done.3), channel_id=1, source_target_pairs={{0,4},{4,8},{8,12},{12,16},{16,20},{20,24},{24,28},{28,32},{32,36}... | collective-permute-start | bytes 1572872 | tf_op jit(solution)/shard_map/stream_1_step_2/ppermute | solution.py:196
  33.5 2.0 %shard_map.74 = bf16[512,512]{1,0:T(8,128)(2,1)} custom-call(s32[1,2,2]{2,1,0:T(2,128)} %refs_0_.1, s32[1,16]{1,0:T(1,128)} %refs_1_.2, s32[2]{0:T(128)} %refs_2_.3, bf16[1,512,512]{2,1,0:T(8,128)(2,1)} %refs_3_.3), custom_call_target="tpu_custom_call" | custom-call | tf_op jit(solution)/shard_map/pallas_call | solution.py:60
  35.6 1.9 %collective-permute-start.1 = (bf16[512,512]{1,0:T(8,128)(2,1)}, bf16[512,512]{1,0:T(8,128)(2,1)S(1)}, u32[]{:S(2)}, u32[]{:S(2)}) collective-permute-start(bf16[512,512]{1,0:T(8,128)(2,1)} %shard_map.74), channel_id=1, source_target_pairs={{0,64},{64,0},{1,65},{65,1},{2,66},{66,2},{3,67},{67,3},{4,68},{68... | collective-permute-start | bytes 1572872 | tf_op jit(solution)/shard_map/b_swap/ppermute | solution.py:204
  37.5 0.0 collective-permute-done.10.refs_6_
  37.5 3.1 %collective-permute-start.11 = (bf16[1024,256]{1,0:T(8,128)(2,1)S(1)}, bf16[1024,256]{1,0:T(8,128)(2,1)S(1)}, u32[]{:S(2)}, u32[]{:S(2)}) collective-permute-start(bf16[1024,256]{1,0:T(8,128)(2,1)S(1)} %collective-permute-done.10.refs_6_), channel_id=1, source_target_pairs={{0,4},{4,8},{8,12},{12,16},{16,20},{20,24},{24,28},{28,32},{32,36}... | collective-permute-start | bytes 1572872 | tf_op jit(solution)/shard_map/stream_0_step_3/ppermute | solution.py:196
  40.6 0.0 collective-permute-done.5
  40.6 4.2 %collective-permute-start.6 = (bf16[1024,256]{1,0:T(8,128)(2,1)S(1)}, bf16[1024,256]{1,0:T(8,128)(2,1)S(1)}, u32[]{:S(2)}, u32[]{:S(2)}) collective-permute-start(bf16[1024,256]{1,0:T(8,128)(2,1)S(1)} %collective-permute-done.5), channel_id=1, source_target_pairs={{0,4},{4,8},{8,12},{12,16},{16,20},{20,24},{24,28},{28,32},{32,36}... | collective-permute-start | bytes 1572872 | tf_op jit(solution)/shard_map/stream_1_step_3/ppermute | solution.py:196
  44.8 0.0 collective-permute-done.1
  44.8 1.1 pad_maximum_fusion.refs_0_
  45.9 4.8 %collective-permute-start.4 = (bf16[1024,512]{1,0:T(8,128)(2,1)S(1)}, bf16[1024,512]{1,0:T(8,128)(2,1)S(1)}, u32[]{:S(2)}, u32[]{:S(2)}) collective-permute-start(bf16[1024,512]{1,0:T(8,128)(2,1)S(1)} %pad_maximum_fusion.refs_0_), channel_id=1, source_target_pairs={{0,128},{64,448},{128,256},{192,64},{256,384},{320,192},{384,0},{4... | collective-permute-start | bytes 3145736 | tf_op jit(solution)/shard_map/b_near/ppermute | solution.py:208
  50.7 0.0 collective-permute-done.11.refs_7_
  50.7 1.9 %collective-permute-start.12 = (bf16[1024,256]{1,0:T(8,128)(2,1)S(1)}, bf16[1024,256]{1,0:T(8,128)(2,1)S(1)}, u32[]{:S(2)}, u32[]{:S(2)}) collective-permute-start(bf16[1024,256]{1,0:T(8,128)(2,1)S(1)} %collective-permute-done.11.refs_7_), channel_id=1, source_target_pairs={{0,4},{4,8},{8,12},{12,16},{16,20},{20,24},{24,28},{28,32},{32,36}... | collective-permute-start | bytes 1572872 | tf_op jit(solution)/shard_map/stream_0_step_4/ppermute | solution.py:196
  52.6 0.7 collective-permute-done.6
  53.4 4.3 %collective-permute-start.7 = (bf16[1024,256]{1,0:T(8,128)(2,1)S(1)}, bf16[1024,256]{1,0:T(8,128)(2,1)S(1)}, u32[]{:S(2)}, u32[]{:S(2)}) collective-permute-start(bf16[1024,256]{1,0:T(8,128)(2,1)S(1)} %collective-permute-done.6), channel_id=1, source_target_pairs={{0,4},{4,8},{8,12},{12,16},{16,20},{20,24},{24,28},{28,32},{32,36}... | collective-permute-start | bytes 1572872 | tf_op jit(solution)/shard_map/stream_1_step_4/ppermute | solution.py:196
  57.6 2.1 %collective-permute-start.26 = (bf16[1024,256]{1,0:T(8,128)(2,1)}, bf16[1024,256]{1,0:T(8,128)(2,1)S(1)}, u32[]{:S(2)}, u32[]{:S(2)}) collective-permute-start(bf16[1024,256]{1,0:T(8,128)(2,1)} %copy-done.1), channel_id=1, source_target_pairs={{0,64},{64,0},{1,65},{65,1},{2,66},{66,2},{3,67},{67,3},{4,68},{68... | collective-permute-start | bytes 1572872 | tf_op jit(solution)/shard_map/ppermute | solution.py:216
  59.8 1.2 collective-permute-done.12.refs_8_
  60.9 3.7 %collective-permute-start.13 = (bf16[1024,256]{1,0:T(8,128)(2,1)S(1)}, bf16[1024,256]{1,0:T(8,128)(2,1)S(1)}, u32[]{:S(2)}, u32[]{:S(2)}) collective-permute-start(bf16[1024,256]{1,0:T(8,128)(2,1)S(1)} %collective-permute-done.12.refs_8_), channel_id=1, source_target_pairs={{0,4},{4,8},{8,12},{12,16},{16,20},{20,24},{24,28},{28,32},{32,36}... | collective-permute-start | bytes 1572872 | tf_op jit(solution)/shard_map/stream_0_step_5/ppermute | solution.py:196
  64.6 1.9 %collective-permute-done.7 = bf16[1024,256]{1,0:T(8,128)(2,1)S(1)} collective-permute-done((bf16[1024,256]{1,0:T(8,128)(2,1)S(1)}, bf16[1024,256]{1,0:T(8,128)(2,1)S(1)}, u32[]{:S(2)}, u32[]{:S(2)}) %collective-permute-start.7) | collective-permute-done | bytes 524320 | tf_op jit(solution)/shard_map/stream_1_step_4/ppermute | solution.py:196
  66.6 2.8 %collective-permute-start.17 = (bf16[1024,256]{1,0:T(8,128)(2,1)S(1)}, bf16[1024,256]{1,0:T(8,128)(2,1)S(1)}, u32[]{:S(2)}, u32[]{:S(2)}) collective-permute-start(bf16[1024,256]{1,0:T(8,128)(2,1)S(1)} %collective-permute-done.7), channel_id=1, source_target_pairs={{0,4},{4,8},{8,12},{12,16},{16,20},{20,24},{24,28},{28,32},{32,36}... | collective-permute-start | bytes 1572872 | tf_op jit(solution)/shard_map/stream_1_step_5/ppermute | solution.py:196
  69.4 2.6 %collective-permute-start.25 = (bf16[1024,256]{1,0:T(8,128)(2,1)S(1)}, bf16[1024,256]{1,0:T(8,128)(2,1)S(1)}, u32[]{:S(2)}, u32[]{:S(2)}) collective-permute-start(bf16[1024,256]{1,0:T(8,128)(2,1)S(1)} %collective-permute-done.5), channel_id=1, source_target_pairs={{0,64},{64,0},{1,65},{65,1},{2,66},{66,2},{3,67},{67,3},{4,68},{68... | collective-permute-start | bytes 1572872 | tf_op jit(solution)/shard_map/ppermute | solution.py:216
  72.0 0.0 collective-permute-done.4.refs_1_
  72.0 4.6 %collective-permute-start.9 = (bf16[1024,512]{1,0:T(8,128)(2,1)S(1)}, bf16[1024,512]{1,0:T(8,128)(2,1)S(1)}, u32[]{:S(2)}, u32[]{:S(2)}) collective-permute-start(bf16[1024,512]{1,0:T(8,128)(2,1)S(1)} %collective-permute-done.4.refs_1_), channel_id=1, source_target_pairs={{0,128},{64,448},{128,256},{192,64},{256,384},{320,192},{384,0},{4... | collective-permute-start | bytes 3145736 | tf_op jit(solution)/shard_map/b_far/ppermute | solution.py:211
  76.7 0.0 collective-permute-done.26.refs_8_
  76.7 1.9 %collective-permute-start.24 = (bf16[1024,256]{1,0:T(8,128)(2,1)S(1)}, bf16[1024,256]{1,0:T(8,128)(2,1)S(1)}, u32[]{:S(2)}, u32[]{:S(2)}) collective-permute-start(bf16[1024,256]{1,0:T(8,128)(2,1)S(1)} %collective-permute-done.6), channel_id=1, source_target_pairs={{0,64},{64,0},{1,65},{65,1},{2,66},{66,2},{3,67},{67,3},{4,68},{68... | collective-permute-start | bytes 1572872 | tf_op jit(solution)/shard_map/ppermute | solution.py:216
  78.6 0.0 collective-permute-done.13.refs_9_
  78.6 4.9 %collective-permute-start.14 = (bf16[1024,256]{1,0:T(8,128)(2,1)S(1)}, bf16[1024,256]{1,0:T(8,128)(2,1)S(1)}, u32[]{:S(2)}, u32[]{:S(2)}) collective-permute-start(bf16[1024,256]{1,0:T(8,128)(2,1)S(1)} %collective-permute-done.13.refs_9_), channel_id=1, source_target_pairs={{0,4},{4,8},{8,12},{12,16},{16,20},{20,24},{24,28},{28,32},{32,36}... | collective-permute-start | bytes 1572872 | tf_op jit(solution)/shard_map/stream_0_step_6/ppermute | solution.py:196
  83.5 0.0 collective-permute-done.17
  83.5 1.9 %collective-permute-start.18 = (bf16[1024,256]{1,0:T(8,128)(2,1)S(1)}, bf16[1024,256]{1,0:T(8,128)(2,1)S(1)}, u32[]{:S(2)}, u32[]{:S(2)}) collective-permute-start(bf16[1024,256]{1,0:T(8,128)(2,1)S(1)} %collective-permute-done.17), channel_id=1, source_target_pairs={{0,4},{4,8},{8,12},{12,16},{16,20},{20,24},{24,28},{28,32},{32,36}... | collective-permute-start | bytes 1572872 | tf_op jit(solution)/shard_map/stream_1_step_6/ppermute | solution.py:196
  85.4 0.0 collective-permute-done.25.refs_7_
  85.5 1.9 %collective-permute-start.8 = (bf16[1024,512]{1,0:T(8,128)(2,1)S(1)}, bf16[1024,512]{1,0:T(8,128)(2,1)S(1)}, u32[]{:S(2)}, u32[]{:S(2)}) collective-permute-start(bf16[1024,512]{1,0:T(8,128)(2,1)S(1)} %collective-permute-done.4.refs_1_), channel_id=1, source_target_pairs={{0,64},{64,0},{1,65},{65,1},{2,66},{66,2},{3,67},{67,3},{4,68},{68... | collective-permute-start | bytes 3145736 | tf_op jit(solution)/shard_map/b_turn/ppermute | solution.py:214
  87.4 0.0 collective-permute-done.24.refs_6_
  87.4 2.4 %collective-permute-start.23 = (bf16[1024,256]{1,0:T(8,128)(2,1)S(1)}, bf16[1024,256]{1,0:T(8,128)(2,1)S(1)}, u32[]{:S(2)}, u32[]{:S(2)}) collective-permute-start(bf16[1024,256]{1,0:T(8,128)(2,1)S(1)} %collective-permute-done.7), channel_id=1, source_target_pairs={{0,64},{64,0},{1,65},{65,1},{2,66},{66,2},{3,67},{67,3},{4,68},{68... | collective-permute-start | bytes 1572872 | tf_op jit(solution)/shard_map/ppermute | solution.py:216
  89.8 0.0 collective-permute-done.14.refs_10_
  89.8 4.8 %collective-permute-start.15 = (bf16[1024,256]{1,0:T(8,128)(2,1)S(1)}, bf16[1024,256]{1,0:T(8,128)(2,1)S(1)}, u32[]{:S(2)}, u32[]{:S(2)}) collective-permute-start(bf16[1024,256]{1,0:T(8,128)(2,1)S(1)} %collective-permute-done.14.refs_10_), channel_id=1, source_target_pairs={{0,4},{4,8},{8,12},{12,16},{16,20},{20,24},{24,28},{28,32},{32,36}... | collective-permute-start | bytes 1572872 | tf_op jit(solution)/shard_map/stream_0_step_7/ppermute | solution.py:196
  94.6 0.6 collective-permute-done.18
  95.2 5.0 %collective-permute-start.19 = (bf16[1024,256]{1,0:T(8,128)(2,1)S(1)}, bf16[1024,256]{1,0:T(8,128)(2,1)S(1)}, u32[]{:S(2)}, u32[]{:S(2)}) collective-permute-start(bf16[1024,256]{1,0:T(8,128)(2,1)S(1)} %collective-permute-done.18), channel_id=1, source_target_pairs={{0,4},{4,8},{8,12},{12,16},{16,20},{20,24},{24,28},{28,32},{32,36}... | collective-permute-start | bytes 1572872 | tf_op jit(solution)/shard_map/stream_1_step_7/ppermute | solution.py:196
  100.2 0.0 collective-permute-done.9.refs_3_
  100.3 1.9 %collective-permute-start.22 = (bf16[1024,256]{1,0:T(8,128)(2,1)S(1)}, bf16[1024,256]{1,0:T(8,128)(2,1)S(1)}, u32[]{:S(2)}, u32[]{:S(2)}) collective-permute-start(bf16[1024,256]{1,0:T(8,128)(2,1)S(1)} %collective-permute-done.17), channel_id=1, source_target_pairs={{0,64},{64,0},{1,65},{65,1},{2,66},{66,2},{3,67},{67,3},{4,68},{68... | collective-permute-start | bytes 1572872 | tf_op jit(solution)/shard_map/ppermute | solution.py:216
  102.2 0.0 collective-permute-done.23.refs_5_
  102.2 2.4 %collective-permute-start.21 = (bf16[1024,256]{1,0:T(8,128)(2,1)S(1)}, bf16[1024,256]{1,0:T(8,128)(2,1)S(1)}, u32[]{:S(2)}, u32[]{:S(2)}) collective-permute-start(bf16[1024,256]{1,0:T(8,128)(2,1)S(1)} %collective-permute-done.18), channel_id=1, source_target_pairs={{0,64},{64,0},{1,65},{65,1},{2,66},{66,2},{3,67},{67,3},{4,68},{68... | collective-permute-start | bytes 1572872 | tf_op jit(solution)/shard_map/ppermute | solution.py:216
  104.6 0.0 collective-permute-done.15.refs_4_
  104.6 3.1 %collective-permute-start.16 = (bf16[1024,256]{1,0:T(8,128)(2,1)S(1)}, bf16[1024,256]{1,0:T(8,128)(2,1)S(1)}, u32[]{:S(2)}, u32[]{:S(2)}) collective-permute-start(bf16[1024,256]{1,0:T(8,128)(2,1)S(1)} %collective-permute-done.15.refs_4_), channel_id=1, source_target_pairs={{0,4},{4,8},{8,12},{12,16},{16,20},{20,24},{24,28},{28,32},{32,36}... | collective-permute-start | bytes 1572872 | tf_op jit(solution)/shard_map/stream_0_step_8/ppermute | solution.py:196
  107.7 0.0 collective-permute-done.19
  107.7 3.5 %collective-permute-start.20 = (bf16[1024,256]{1,0:T(8,128)(2,1)S(1)}, bf16[1024,256]{1,0:T(8,128)(2,1)S(1)}, u32[]{:S(2)}, u32[]{:S(2)}) collective-permute-start(bf16[1024,256]{1,0:T(8,128)(2,1)S(1)} %collective-permute-done.19), channel_id=1, source_target_pairs={{0,64},{64,0},{1,65},{65,1},{2,66},{66,2},{3,67},{67,3},{4,68},{68... | collective-permute-start | bytes 1572872 | tf_op jit(solution)/shard_map/ppermute | solution.py:217
  111.2 0.0 collective-permute-done.8.refs_2_
  111.2 0.0 collective-permute-done.22.refs_4_
  111.2 2.0 %shard_map.76.refs_9_ = f32[1024,512]{1,0:T(8,128)S(1)} custom-call(bf16[1024,512]{1,0:T(8,128)(2,1)S(1)} %pad_maximum_fusion.refs_0_, bf16[1024,512]{1,0:T(8,128)(2,1)S(1)} %collective-permute-done.4.refs_1_, bf16[1024,512]{1,0:T(8,128)(2,1)S(1)} %collective-permute-done.8.refs_2_, bf16[1024,512]{1,0:T(8,128)(2,1)S(1)} %collective-permute-done.9.refs_3_, ...), custom_call_target="tpu_custom_call" | custom-call | flops 1342177280 | bytes 2097152 | tf_op jit(solution)/shard_map/pallas_call | solution.py:162
  113.3 2.7 %shard_map.75.refs_8_ = f32[1024,512]{1,0:T(8,128)S(1)} custom-call(bf16[1024,512]{1,0:T(8,128)(2,1)S(1)} %pad_maximum_fusion.refs_0_, bf16[1024,512]{1,0:T(8,128)(2,1)S(1)} %collective-permute-done.4.refs_1_, bf16[1024,512]{1,0:T(8,128)(2,1)S(1)} %collective-permute-done.8.refs_2_, bf16[1024,512]{1,0:T(8,128)(2,1)S(1)} %collective-permute-done.9.refs_3_, ...), custom_call_target="tpu_custom_call" | custom-call | flops 1879048192 | bytes 2097152 | tf_op jit(solution)/shard_map/pallas_call | solution.py:162
  115.9 0.0 collective-permute-done.21.refs_7_
  116.0 3.3 %shard_map.77 = (f32[4,272,512]{2,1,0:T(8,128)S(1)}, f32[256,512]{1,0:T(8,128)S(1)}) custom-call(bf16[1024,512]{1,0:T(8,128)(2,1)S(1)} %pad_maximum_fusion.refs_0_, bf16[1024,512]{1,0:T(8,128)(2,1)S(1)} %collective-permute-done.4.refs_1_, bf16[1024,512]{1,0:T(8,128)(2,1)S(1)} %collective-permute-done.8.refs_2_, ...), custom_call_target="tpu_custom_call" | custom-call | flops 1073741824 | bytes 2097152 | tf_op jit(solution)/shard_map/pallas_call | solution.py:162
  119.3 1.3 convert_element_type.9
  120.6 4.0 %all-to-all-start = ((f16[4,272,512]{2,1,0:T(8,128)(2,1)}), f16[4,272,512]{2,1,0:T(8,128)(2,1)S(1)}, u32[]{:S(2)}, u32[]{:S(2)}) async-start(f16[4,272,512]{2,1,0:T(8,128)(2,1)} %convert_element_type.9), calls=%async_computation | async-start | bytes 2228224 | tf_op jit(solution)/shard_map/all_to_all | solution.py:225
  124.6 14.7 %all-to-all-done = f16[4,272,512]{2,1,0:T(8,128)(2,1)S(1)} async-done(((f16[4,272,512]{2,1,0:T(8,128)(2,1)}), f16[4,272,512]{2,1,0:T(8,128)(2,1)S(1)}, u32[]{:S(2)}, u32[]{:S(2)}) %all-to-all-start) | async-done | bytes 1114144 | tf_op jit(solution)/shard_map/all_to_all | solution.py:225
  139.3 0.1 convert_reduce_fusion
  139.4 0.3 multiply_reduce_fusion
  139.8 0.9 add.3
  (7 shorter events, 0.0 us)
Async XLA Ops:
  2.0 14.6 %collective-permute-start.2 = (bf16[1024,256]{1,0:T(8,128)(2,1)}, bf16[1024,256]{1,0:T(8,128)(2,1)S(1)}, u32[]{:S(2)}, u32[]{:S(2)}) collective-permute-start(bf16[1024,256]{1,0:T(8,128)(2,1)} %shard_map.73.refs_4_), channel_id=1, source_target_pairs={{0,64},{64,0},{1,65},{65,1},{2,66},{66,2},{3,67},{67,3},{4,68},{68... | collective-permute-start | bytes 1572872 | tf_op jit(solution)/shard_map/ppermute | solution.py:158
  10.8 12.2 %collective-permute-start = (bf16[1024,256]{1,0:T(8,128)(2,1)}, bf16[1024,256]{1,0:T(8,128)(2,1)S(1)}, u32[]{:S(2)}, u32[]{:S(2)}) collective-permute-start(bf16[1024,256]{1,0:T(8,128)(2,1)} %shard_map.73.refs_4_), channel_id=1, source_target_pairs={{0,4},{4,8},{8,12},{12,16},{16,20},{20,24},{24,28},{28,32},{32,36}... | collective-permute-start | bytes 1572872 | tf_op jit(solution)/shard_map/stream_0_step_1/ppermute | solution.py:196
  16.6 11.9 %collective-permute-start.3 = (bf16[1024,256]{1,0:T(8,128)(2,1)S(1)}, bf16[1024,256]{1,0:T(8,128)(2,1)S(1)}, u32[]{:S(2)}, u32[]{:S(2)}) collective-permute-start(bf16[1024,256]{1,0:T(8,128)(2,1)S(1)} %collective-permute-done.2), channel_id=1, source_target_pairs={{0,4},{4,8},{8,12},{12,16},{16,20},{20,24},{24,28},{28,32},{32,36}... | collective-permute-start | bytes 1572872 | tf_op jit(solution)/shard_map/stream_1_step_1/ppermute | solution.py:196
  23.0 14.5 %collective-permute-start.10 = (bf16[1024,256]{1,0:T(8,128)(2,1)S(1)}, bf16[1024,256]{1,0:T(8,128)(2,1)S(1)}, u32[]{:S(2)}, u32[]{:S(2)}) collective-permute-start(bf16[1024,256]{1,0:T(8,128)(2,1)S(1)} %collective-permute-done.refs_5_), channel_id=1, source_target_pairs={{0,4},{4,8},{8,12},{12,16},{16,20},{20,24},{24,28},{28,32},{32,36}... | collective-permute-start | bytes 1572872 | tf_op jit(solution)/shard_map/stream_0_step_2/ppermute | solution.py:196
  28.5 16.3 %copy-start.1 = (bf16[1024,256]{1,0:T(8,128)(2,1)}, bf16[1024,256]{1,0:T(8,128)(2,1)S(1)}, u32[]{:S(2)}) copy-start(bf16[1024,256]{1,0:T(8,128)(2,1)S(1)} %collective-permute-done.3) | copy-start | bytes 1572868
  28.5 12.1 %collective-permute-start.5 = (bf16[1024,256]{1,0:T(8,128)(2,1)S(1)}, bf16[1024,256]{1,0:T(8,128)(2,1)S(1)}, u32[]{:S(2)}, u32[]{:S(2)}) collective-permute-start(bf16[1024,256]{1,0:T(8,128)(2,1)S(1)} %collective-permute-done.3), channel_id=1, source_target_pairs={{0,4},{4,8},{8,12},{12,16},{16,20},{20,24},{24,28},{28,32},{32,36}... | collective-permute-start | bytes 1572872 | tf_op jit(solution)/shard_map/stream_1_step_2/ppermute | solution.py:196
  35.6 9.2 %collective-permute-start.1 = (bf16[512,512]{1,0:T(8,128)(2,1)}, bf16[512,512]{1,0:T(8,128)(2,1)S(1)}, u32[]{:S(2)}, u32[]{:S(2)}) collective-permute-start(bf16[512,512]{1,0:T(8,128)(2,1)} %shard_map.74), channel_id=1, source_target_pairs={{0,64},{64,0},{1,65},{65,1},{2,66},{66,2},{3,67},{67,3},{4,68},{68... | collective-permute-start | bytes 1572872 | tf_op jit(solution)/shard_map/b_swap/ppermute | solution.py:204
  37.5 13.2 %collective-permute-start.11 = (bf16[1024,256]{1,0:T(8,128)(2,1)S(1)}, bf16[1024,256]{1,0:T(8,128)(2,1)S(1)}, u32[]{:S(2)}, u32[]{:S(2)}) collective-permute-start(bf16[1024,256]{1,0:T(8,128)(2,1)S(1)} %collective-permute-done.10.refs_6_), channel_id=1, source_target_pairs={{0,4},{4,8},{8,12},{12,16},{16,20},{20,24},{24,28},{28,32},{32,36}... | collective-permute-start | bytes 1572872 | tf_op jit(solution)/shard_map/stream_0_step_3/ppermute | solution.py:196
  40.6 12.7 %collective-permute-start.6 = (bf16[1024,256]{1,0:T(8,128)(2,1)S(1)}, bf16[1024,256]{1,0:T(8,128)(2,1)S(1)}, u32[]{:S(2)}, u32[]{:S(2)}) collective-permute-start(bf16[1024,256]{1,0:T(8,128)(2,1)S(1)} %collective-permute-done.5), channel_id=1, source_target_pairs={{0,4},{4,8},{8,12},{12,16},{16,20},{20,24},{24,28},{28,32},{32,36}... | collective-permute-start | bytes 1572872 | tf_op jit(solution)/shard_map/stream_1_step_3/ppermute | solution.py:196
  45.9 67.3 %copy-start = (bf16[1024,256]{1,0:T(8,128)(2,1)S(1)}, bf16[1024,256]{1,0:T(8,128)(2,1)}, u32[]{:S(2)}) copy-start(bf16[1024,256]{1,0:T(8,128)(2,1)} %shard_map.73.refs_4_) | copy-start | bytes 1572868
  45.9 26.1 %collective-permute-start.4 = (bf16[1024,512]{1,0:T(8,128)(2,1)S(1)}, bf16[1024,512]{1,0:T(8,128)(2,1)S(1)}, u32[]{:S(2)}, u32[]{:S(2)}) collective-permute-start(bf16[1024,512]{1,0:T(8,128)(2,1)S(1)} %pad_maximum_fusion.refs_0_), channel_id=1, source_target_pairs={{0,128},{64,448},{128,256},{192,64},{256,384},{320,192},{384,0},{4... | collective-permute-start | bytes 3145736 | tf_op jit(solution)/shard_map/b_near/ppermute | solution.py:208
  50.7 10.2 %collective-permute-start.12 = (bf16[1024,256]{1,0:T(8,128)(2,1)S(1)}, bf16[1024,256]{1,0:T(8,128)(2,1)S(1)}, u32[]{:S(2)}, u32[]{:S(2)}) collective-permute-start(bf16[1024,256]{1,0:T(8,128)(2,1)S(1)} %collective-permute-done.11.refs_7_), channel_id=1, source_target_pairs={{0,4},{4,8},{8,12},{12,16},{16,20},{20,24},{24,28},{28,32},{32,36}... | collective-permute-start | bytes 1572872 | tf_op jit(solution)/shard_map/stream_0_step_4/ppermute | solution.py:196
  53.4 13.2 %collective-permute-start.7 = (bf16[1024,256]{1,0:T(8,128)(2,1)S(1)}, bf16[1024,256]{1,0:T(8,128)(2,1)S(1)}, u32[]{:S(2)}, u32[]{:S(2)}) collective-permute-start(bf16[1024,256]{1,0:T(8,128)(2,1)S(1)} %collective-permute-done.6), channel_id=1, source_target_pairs={{0,4},{4,8},{8,12},{12,16},{16,20},{20,24},{24,28},{28,32},{32,36}... | collective-permute-start | bytes 1572872 | tf_op jit(solution)/shard_map/stream_1_step_4/ppermute | solution.py:196
  57.6 19.1 %collective-permute-start.26 = (bf16[1024,256]{1,0:T(8,128)(2,1)}, bf16[1024,256]{1,0:T(8,128)(2,1)S(1)}, u32[]{:S(2)}, u32[]{:S(2)}) collective-permute-start(bf16[1024,256]{1,0:T(8,128)(2,1)} %copy-done.1), channel_id=1, source_target_pairs={{0,64},{64,0},{1,65},{65,1},{2,66},{66,2},{3,67},{67,3},{4,68},{68... | collective-permute-start | bytes 1572872 | tf_op jit(solution)/shard_map/ppermute | solution.py:216
  60.9 17.7 %collective-permute-start.13 = (bf16[1024,256]{1,0:T(8,128)(2,1)S(1)}, bf16[1024,256]{1,0:T(8,128)(2,1)S(1)}, u32[]{:S(2)}, u32[]{:S(2)}) collective-permute-start(bf16[1024,256]{1,0:T(8,128)(2,1)S(1)} %collective-permute-done.12.refs_8_), channel_id=1, source_target_pairs={{0,4},{4,8},{8,12},{12,16},{16,20},{20,24},{24,28},{28,32},{32,36}... | collective-permute-start | bytes 1572872 | tf_op jit(solution)/shard_map/stream_0_step_5/ppermute | solution.py:196
  66.6 16.9 %collective-permute-start.17 = (bf16[1024,256]{1,0:T(8,128)(2,1)S(1)}, bf16[1024,256]{1,0:T(8,128)(2,1)S(1)}, u32[]{:S(2)}, u32[]{:S(2)}) collective-permute-start(bf16[1024,256]{1,0:T(8,128)(2,1)S(1)} %collective-permute-done.7), channel_id=1, source_target_pairs={{0,4},{4,8},{8,12},{12,16},{16,20},{20,24},{24,28},{28,32},{32,36}... | collective-permute-start | bytes 1572872 | tf_op jit(solution)/shard_map/stream_1_step_5/ppermute | solution.py:196
  69.4 16.1 %collective-permute-start.25 = (bf16[1024,256]{1,0:T(8,128)(2,1)S(1)}, bf16[1024,256]{1,0:T(8,128)(2,1)S(1)}, u32[]{:S(2)}, u32[]{:S(2)}) collective-permute-start(bf16[1024,256]{1,0:T(8,128)(2,1)S(1)} %collective-permute-done.5), channel_id=1, source_target_pairs={{0,64},{64,0},{1,65},{65,1},{2,66},{66,2},{3,67},{67,3},{4,68},{68... | collective-permute-start | bytes 1572872 | tf_op jit(solution)/shard_map/ppermute | solution.py:216
  72.0 28.2 %collective-permute-start.9 = (bf16[1024,512]{1,0:T(8,128)(2,1)S(1)}, bf16[1024,512]{1,0:T(8,128)(2,1)S(1)}, u32[]{:S(2)}, u32[]{:S(2)}) collective-permute-start(bf16[1024,512]{1,0:T(8,128)(2,1)S(1)} %collective-permute-done.4.refs_1_), channel_id=1, source_target_pairs={{0,128},{64,448},{128,256},{192,64},{256,384},{320,192},{384,0},{4... | collective-permute-start | bytes 3145736 | tf_op jit(solution)/shard_map/b_far/ppermute | solution.py:211
  76.7 10.7 %collective-permute-start.24 = (bf16[1024,256]{1,0:T(8,128)(2,1)S(1)}, bf16[1024,256]{1,0:T(8,128)(2,1)S(1)}, u32[]{:S(2)}, u32[]{:S(2)}) collective-permute-start(bf16[1024,256]{1,0:T(8,128)(2,1)S(1)} %collective-permute-done.6), channel_id=1, source_target_pairs={{0,64},{64,0},{1,65},{65,1},{2,66},{66,2},{3,67},{67,3},{4,68},{68... | collective-permute-start | bytes 1572872 | tf_op jit(solution)/shard_map/ppermute | solution.py:216
  78.6 11.2 %collective-permute-start.14 = (bf16[1024,256]{1,0:T(8,128)(2,1)S(1)}, bf16[1024,256]{1,0:T(8,128)(2,1)S(1)}, u32[]{:S(2)}, u32[]{:S(2)}) collective-permute-start(bf16[1024,256]{1,0:T(8,128)(2,1)S(1)} %collective-permute-done.13.refs_9_), channel_id=1, source_target_pairs={{0,4},{4,8},{8,12},{12,16},{16,20},{20,24},{24,28},{28,32},{32,36}... | collective-permute-start | bytes 1572872 | tf_op jit(solution)/shard_map/stream_0_step_6/ppermute | solution.py:196
  83.5 11.7 %collective-permute-start.18 = (bf16[1024,256]{1,0:T(8,128)(2,1)S(1)}, bf16[1024,256]{1,0:T(8,128)(2,1)S(1)}, u32[]{:S(2)}, u32[]{:S(2)}) collective-permute-start(bf16[1024,256]{1,0:T(8,128)(2,1)S(1)} %collective-permute-done.17), channel_id=1, source_target_pairs={{0,4},{4,8},{8,12},{12,16},{16,20},{20,24},{24,28},{28,32},{32,36}... | collective-permute-start | bytes 1572872 | tf_op jit(solution)/shard_map/stream_1_step_6/ppermute | solution.py:196
  85.5 25.8 %collective-permute-start.8 = (bf16[1024,512]{1,0:T(8,128)(2,1)S(1)}, bf16[1024,512]{1,0:T(8,128)(2,1)S(1)}, u32[]{:S(2)}, u32[]{:S(2)}) collective-permute-start(bf16[1024,512]{1,0:T(8,128)(2,1)S(1)} %collective-permute-done.4.refs_1_), channel_id=1, source_target_pairs={{0,64},{64,0},{1,65},{65,1},{2,66},{66,2},{3,67},{67,3},{4,68},{68... | collective-permute-start | bytes 3145736 | tf_op jit(solution)/shard_map/b_turn/ppermute | solution.py:214
  87.4 14.8 %collective-permute-start.23 = (bf16[1024,256]{1,0:T(8,128)(2,1)S(1)}, bf16[1024,256]{1,0:T(8,128)(2,1)S(1)}, u32[]{:S(2)}, u32[]{:S(2)}) collective-permute-start(bf16[1024,256]{1,0:T(8,128)(2,1)S(1)} %collective-permute-done.7), channel_id=1, source_target_pairs={{0,64},{64,0},{1,65},{65,1},{2,66},{66,2},{3,67},{67,3},{4,68},{68... | collective-permute-start | bytes 1572872 | tf_op jit(solution)/shard_map/ppermute | solution.py:216
  89.8 14.8 %collective-permute-start.15 = (bf16[1024,256]{1,0:T(8,128)(2,1)S(1)}, bf16[1024,256]{1,0:T(8,128)(2,1)S(1)}, u32[]{:S(2)}, u32[]{:S(2)}) collective-permute-start(bf16[1024,256]{1,0:T(8,128)(2,1)S(1)} %collective-permute-done.14.refs_10_), channel_id=1, source_target_pairs={{0,4},{4,8},{8,12},{12,16},{16,20},{20,24},{24,28},{28,32},{32,36}... | collective-permute-start | bytes 1572872 | tf_op jit(solution)/shard_map/stream_0_step_7/ppermute | solution.py:196
  95.2 12.5 %collective-permute-start.19 = (bf16[1024,256]{1,0:T(8,128)(2,1)S(1)}, bf16[1024,256]{1,0:T(8,128)(2,1)S(1)}, u32[]{:S(2)}, u32[]{:S(2)}) collective-permute-start(bf16[1024,256]{1,0:T(8,128)(2,1)S(1)} %collective-permute-done.18), channel_id=1, source_target_pairs={{0,4},{4,8},{8,12},{12,16},{16,20},{20,24},{24,28},{28,32},{32,36}... | collective-permute-start | bytes 1572872 | tf_op jit(solution)/shard_map/stream_1_step_7/ppermute | solution.py:196
  100.3 11.0 %collective-permute-start.22 = (bf16[1024,256]{1,0:T(8,128)(2,1)S(1)}, bf16[1024,256]{1,0:T(8,128)(2,1)S(1)}, u32[]{:S(2)}, u32[]{:S(2)}) collective-permute-start(bf16[1024,256]{1,0:T(8,128)(2,1)S(1)} %collective-permute-done.17), channel_id=1, source_target_pairs={{0,64},{64,0},{1,65},{65,1},{2,66},{66,2},{3,67},{67,3},{4,68},{68... | collective-permute-start | bytes 1572872 | tf_op jit(solution)/shard_map/ppermute | solution.py:216
  102.2 13.7 %collective-permute-start.21 = (bf16[1024,256]{1,0:T(8,128)(2,1)S(1)}, bf16[1024,256]{1,0:T(8,128)(2,1)S(1)}, u32[]{:S(2)}, u32[]{:S(2)}) collective-permute-start(bf16[1024,256]{1,0:T(8,128)(2,1)S(1)} %collective-permute-done.18), channel_id=1, source_target_pairs={{0,64},{64,0},{1,65},{65,1},{2,66},{66,2},{3,67},{67,3},{4,68},{68... | collective-permute-start | bytes 1572872 | tf_op jit(solution)/shard_map/ppermute | solution.py:216
  104.6 11.3 %collective-permute-start.16 = (bf16[1024,256]{1,0:T(8,128)(2,1)S(1)}, bf16[1024,256]{1,0:T(8,128)(2,1)S(1)}, u32[]{:S(2)}, u32[]{:S(2)}) collective-permute-start(bf16[1024,256]{1,0:T(8,128)(2,1)S(1)} %collective-permute-done.15.refs_4_), channel_id=1, source_target_pairs={{0,4},{4,8},{8,12},{12,16},{16,20},{20,24},{24,28},{28,32},{32,36}... | collective-permute-start | bytes 1572872 | tf_op jit(solution)/shard_map/stream_0_step_8/ppermute | solution.py:196
  107.7 8.3 %collective-permute-start.20 = (bf16[1024,256]{1,0:T(8,128)(2,1)S(1)}, bf16[1024,256]{1,0:T(8,128)(2,1)S(1)}, u32[]{:S(2)}, u32[]{:S(2)}) collective-permute-start(bf16[1024,256]{1,0:T(8,128)(2,1)S(1)} %collective-permute-done.19), channel_id=1, source_target_pairs={{0,64},{64,0},{1,65},{65,1},{2,66},{66,2},{3,67},{67,3},{4,68},{68... | collective-permute-start | bytes 1572872 | tf_op jit(solution)/shard_map/ppermute | solution.py:217
  120.6 18.7 %all-to-all-start = ((f16[4,272,512]{2,1,0:T(8,128)(2,1)}), f16[4,272,512]{2,1,0:T(8,128)(2,1)S(1)}, u32[]{:S(2)}, u32[]{:S(2)}) async-start(f16[4,272,512]{2,1,0:T(8,128)(2,1)} %convert_element_type.9), calls=%async_computation | async-start | bytes 2228224 | tf_op jit(solution)/shard_map/all_to_all | solution.py:225

commit v7 on v6

--- a/solution.py
+++ b/solution.py
@@ -71,9 +71,7 @@
 def product_kernel(steps, blocks, added, *refs):
     b_refs, refs = refs[:4], refs[4:]
     a_refs, refs = refs[: len(steps)], refs[len(steps) :]
-    adds, refs = refs[:added], refs[added:]
-    outs, (a_all, b_all, extra, sems) = refs[:-4], refs[-4:]
-    out_ref, own_ref = outs[0], outs[-1]
+    adds, (out_ref, a_all, b_all, extra, sems) = refs[:added], refs[added:]
     z, y, core = lax.axis_index("col"), lax.axis_index("y"), lax.axis_index("core")
     way = 2 * core - 1
     first, count = steps[0], len(steps)
@@ -111,14 +109,10 @@
         total = jnp.dot(a_all[rows, :], b, preferred_element_type=jnp.float32)
         for i in range(added):
             total = total + extra[i, rows, :]
-        if len(outs) == 1:
+        if len(out_ref.shape) == 2:
             out_ref[rows, :] = total
         else:
             encode(total, out_ref.at[tile])
-
-            @pl.when(lax.axis_index("layer") == tile)
-            def _(total=total):
-                own_ref[...] = total
 
 
 def encode(total, out_ref):
@@ -132,12 +126,11 @@
     out_ref[BS:, :] = jnp.broadcast_to(code, (CODE_ROWS, total.shape[1]))
 
 
-def decoded(parts, own):
+def decoded(parts):
     code = parts[:, BS:, :1].astype(jnp.float32).max(axis=1, keepdims=True)
     scale = jnp.ones_like(code)
     for c in range(1, CODES + 1):
         scale = jnp.where(code > c - 0.5, 2.0 ** (-STEP * c), scale)
-    scale = jnp.where(jnp.arange(parts.shape[0])[:, None, None] == own, 0.0, scale)
     return parts[:, :BS].astype(jnp.float32) * scale
 
 
@@ -154,6 +147,7 @@
     own = mask_call(
         mask_a_kernel, a_panel.shape[1:], mask_a.reshape(-1), row_sizes, inner_sizes, a_panel
     )
+
     last = cols // 2
     held = [[own], [lax.ppermute(own, "core", SWAP)]]
 
@@ -161,14 +155,11 @@
         n = len(steps)
         return pl.pallas_call(
             functools.partial(product_kernel, steps, cols, len(adds)),
-            out_shape=(
-                jax.ShapeDtypeStruct((ROWS // BS, BS + CODE_ROWS, width), jnp.float32),
-                jax.ShapeDtypeStruct((BS, width), jnp.float32),
-            )
+            out_shape=jax.ShapeDtypeStruct((ROWS // BS, BS + CODE_ROWS, width), jnp.float32)
             if coded
             else jax.ShapeDtypeStruct((ROWS, width), jnp.float32),
             in_specs=[HBM] * (4 + len(arrays) + len(adds)),
-            out_specs=(VMEM, VMEM) if coded else VMEM,
+            out_specs=VMEM,
             scratch_shapes=[
                 pltpu.VMEM((ROWS, n * BS), jnp.bfloat16),
                 pltpu.VMEM((n, BS, width), jnp.bfloat16),
@@ -184,7 +175,7 @@
     near_by = [
         (i * CORES + c, (i + (1, -1)[c]) % chips * CORES + c) for i in range(chips) for c in range(CORES)
     ]
-    b_eff = b_other = None
+    b_eff = b_turned = None
     b_all = [None] * 4
     turned = []
     for step in range(1, last + 1):
@@ -192,38 +183,41 @@
             if (step, j) == (last, 1):
                 continue
             sent = held[j][-1]
+            if (step, j) == (6, 0):
+                sent = after(sent, b_all[2])
+            if j == 1 and step > 3:
+                sent = after(sent, turned[step - 4])
             with jax.named_scope(f"stream_{j}_step_{step}"):
                 held[j].append(lax.ppermute(sent, ("core", "col"), ring))
             if (step, j) == (1, 0):
-                sizes_k = after(inner_sizes, held[0][1])
+                sizes_k = after(inner_sizes, held[1][0])
                 b_eff = mask_call(
                     mask_b_kernel, b_panel.shape[1:], mask_b, sizes_k, col_sizes, b_panel
                 )
             if (step, j) == (1, 1):
                 with jax.named_scope("b_swap"):
-                    b_other = lax.ppermute(b_eff, "core", SWAP)
+                    b_turned = lax.ppermute(b_eff, "core", SWAP)
             if (step, j) == (2, 1):
-                b_all[0] = jnp.concatenate([b_eff, after(b_other, sent)])
+                b_all[0] = jnp.concatenate([b_eff, b_turned])
                 with jax.named_scope("b_near"):
                     b_all[1] = lax.ppermute(b_all[0], ("y", "core"), near_by)
             if (step, j) == (3, 1):
                 with jax.named_scope("b_far"):
-                    b_all[3] = lax.ppermute(after(b_all[1], sent), ("y", "core"), near_by)
-            if (step, j) == (5, 1):
+                    b_all[3] = lax.ppermute(b_all[1], ("y", "core"), near_by)
+            if (step, j) == (4, 0):
                 with jax.named_scope("b_turn"):
                     b_all[2] = lax.ppermute(after(b_all[1], sent), "core", SWAP)
             if j == 1 and step > 1:
-                turned.append(lax.ppermute(held[1][step - 1], "core", SWAP))
+                turned.append(lax.ppermute(after(held[1][step - 1], sent), "core", SWAP))
     turned.append(lax.ppermute(held[1][last - 1], "core", SWAP))
 
     shards = held[0] + turned[::-1]
     near = product(range(last - 1), shards[: last - 1])
-    across = product(range(last + 3, cols), shards[last + 3 :])
-    steps = range(last - 1, last + 3)
-    parts, mine = product(steps, [shards[s] for s in steps], (near, across), True)
+    across = product(range(last + 2, cols), shards[last + 2 :])
+    steps = range(last - 1, last + 2)
+    parts = product(steps, [shards[s] for s in steps], (near, across), True)
     parts = parts.astype(jnp.float16)
-    parts = decoded(lax.all_to_all(parts, "layer", 0, 0), lax.axis_index("layer"))
-    return mine + parts.sum(axis=0)
+    return decoded(lax.all_to_all(parts, "layer", 0, 0)).sum(axis=0)
 
 
 def solution(mesh):

time: 142 us -> 138 us (0.972)
  blocking collectives: 0 us -> 19.2 us
  waiting for transfers between devices: 23.6 us -> 7.44 us
  starting transfers between devices: 101 us -> 96.1 us
    all_to_all x0 -> x1, blocking collectives: none -> 19.2 us  [on_device(): return decoded(lax.all_to_all(parts, 'layer', 0, 0)).sum(axis=0)]
    all_to_all x1 -> x0, waiting for transfers between devices: 14.7 us -> none  [on_device(): lax.all_to_all(parts, 'layer', 0, 0)]
    all_to_all x1 -> x0, starting transfers between devices: 4.01 us -> none  [on_device(): lax.all_to_all(parts, 'layer', 0, 0)]
    ppermute x15, starting transfers between devices: 57.9 us -> 56 us  [on_device(): held[j].append(lax.ppermute(sent, ('core', 'col'), ring))]
  transfers between devices with their start and end apart: 28 -> 27, of which waited for: 7 -> 7; matrix products, arithmetic and copies ran while one was open for 1% -> 1% of each run, Pallas kernels for 5% -> 5%
where the time goes in v7:
time: 138 us; the launch traced here: 137 us
  starting transfers between devices  96.1 us (70%)
  blocking collectives  19.2 us (14%)
  Pallas kernels  11 us (8%)
  waiting for transfers between devices  7.44 us (5%)
  other arithmetic  2.63 us (2%)
    ppermute x15, starting transfers between devices, on_device(): held[j].append(lax.ppermute(sent, ('core', 'col'), ring))  56 us
    all_to_all x1, blocking collectives, on_device(): return decoded(lax.all_to_all(parts, 'layer', 0, 0)).sum(axis=0)  19.2 us
    ppermute x6, starting transfers between devices, on_device(): turned.append(lax.ppermute(after(held[1][step - 1], sent), 'core', SWAP))  15.2 us
    ppermute x1, starting transfers between devices, on_device(): held = [[own], [lax.ppermute(own, 'core', SWAP)]]  8.92 us
    ppermute x15, waiting for transfers between devices, on_device(): held[j].append(lax.ppermute(sent, ('core', 'col'), ring))  7.41 us
    pallas_call x3, Pallas kernels, product(): pl.pallas_call(functools.partial(product_kernel, steps, cols, len(adds)),...  6.94 us
    ppermute x1, starting transfers between devices, on_device(): b_all[1] = lax.ppermute(b_all[0], ('y', 'core'), near_by)  4.64 us
    pallas_call x2, Pallas kernels, mask_call(): pl.pallas_call(kernel, out_shape=jax.ShapeDtypeStruct(shape, jnp.bfloat16...  4.07 us
  transfers between devices with their start and end apart: 27, of which 7 were waited for; matrix products, arithmetic and copies ran while one was open for 1% of the time, Pallas kernels for 5%

profile of v7, /device:TPU:1, one launch (start us, length us, event | category | flops | bytes accessed | tf_op | source)
XLA Modules:
  0.0 136.8 jit_solution(13092768081942690239)
XLA Ops:
  0.0 2.0 %shard_map.73.refs_4_ = bf16[1024,256]{1,0:T(8,128)(2,1)} custom-call(s32[4]{0:T(128)} %bitcast.1, s32[4]{0:T(128)} %refs_1_.1, s32[1,16]{1,0:T(1,128)} %refs_1_.2, bf16[1,1024,256]{2,1,0:T(8,128)(2,1)} %refs_3_.2), custom_call_target="tpu_custom_call" | custom-call | tf_op jit(solution)/shard_map/pallas_call | solution.py:60
  2.1 8.9 %collective-permute-start = (bf16[1024,256]{1,0:T(8,128)(2,1)}, bf16[1024,256]{1,0:T(8,128)(2,1)S(1)}, u32[]{:S(2)}, u32[]{:S(2)}) collective-permute-start(bf16[1024,256]{1,0:T(8,128)(2,1)} %shard_map.73.refs_4_), channel_id=1, source_target_pairs={{0,64},{64,0},{1,65},{65,1},{2,66},{66,2},{3,67},{67,3},{4,68},{68... | collective-permute-start | bytes 1572872 | tf_op jit(solution)/shard_map/ppermute | solution.py:152
  11.0 5.7 %collective-permute-start.3 = (bf16[1024,256]{1,0:T(8,128)(2,1)}, bf16[1024,256]{1,0:T(8,128)(2,1)S(1)}, u32[]{:S(2)}, u32[]{:S(2)}) collective-permute-start(bf16[1024,256]{1,0:T(8,128)(2,1)} %shard_map.73.refs_4_), channel_id=1, source_target_pairs={{0,4},{4,8},{8,12},{12,16},{16,20},{20,24},{24,28},{28,32},{32,36}... | collective-permute-start | bytes 1572872 | tf_op jit(solution)/shard_map/stream_0_step_1/ppermute | solution.py:191
  16.7 0.0 collective-permute-done
  16.8 2.6 %collective-permute-start.13 = (bf16[1024,256]{1,0:T(8,128)(2,1)S(1)}, bf16[1024,256]{1,0:T(8,128)(2,1)S(1)}, u32[]{:S(2)}, u32[]{:S(2)}) collective-permute-start(bf16[1024,256]{1,0:T(8,128)(2,1)S(1)} %collective-permute-done), channel_id=1, source_target_pairs={{0,4},{4,8},{8,12},{12,16},{16,20},{20,24},{24,28},{28,32},{32,36}... | collective-permute-start | bytes 1572872 | tf_op jit(solution)/shard_map/stream_1_step_1/ppermute | solution.py:191
  19.4 2.0 %shard_map.74 = bf16[512,512]{1,0:T(8,128)(2,1)} custom-call(s32[1,2,2]{2,1,0:T(2,128)} %refs_0_.1, s32[1,16]{1,0:T(1,128)} %refs_1_.2, s32[2]{0:T(128)} %refs_2_.3, bf16[1,512,512]{2,1,0:T(8,128)(2,1)} %refs_3_.3), custom_call_target="tpu_custom_call" | custom-call | tf_op jit(solution)/shard_map/pallas_call | solution.py:60
  21.4 1.9 %collective-permute-start.1 = (bf16[512,512]{1,0:T(8,128)(2,1)}, bf16[512,512]{1,0:T(8,128)(2,1)S(1)}, u32[]{:S(2)}, u32[]{:S(2)}) collective-permute-start(bf16[512,512]{1,0:T(8,128)(2,1)} %shard_map.74), channel_id=1, source_target_pairs={{0,64},{64,0},{1,65},{65,1},{2,66},{66,2},{3,67},{67,3},{4,68},{68... | collective-permute-start | bytes 1572872 | tf_op jit(solution)/shard_map/b_swap/ppermute | solution.py:199
  23.4 0.0 collective-permute-done.3.refs_5_
  23.4 4.7 %collective-permute-start.4 = (bf16[1024,256]{1,0:T(8,128)(2,1)S(1)}, bf16[1024,256]{1,0:T(8,128)(2,1)S(1)}, u32[]{:S(2)}, u32[]{:S(2)}) collective-permute-start(bf16[1024,256]{1,0:T(8,128)(2,1)S(1)} %collective-permute-done.3.refs_5_), channel_id=1, source_target_pairs={{0,4},{4,8},{8,12},{12,16},{16,20},{20,24},{24,28},{28,32},{32,36}... | collective-permute-start | bytes 1572872 | tf_op jit(solution)/shard_map/stream_0_step_2/ppermute | solution.py:191
  28.1 0.6 collective-permute-done.13
  28.7 5.0 %collective-permute-start.14 = (bf16[1024,256]{1,0:T(8,128)(2,1)S(1)}, bf16[1024,256]{1,0:T(8,128)(2,1)S(1)}, u32[]{:S(2)}, u32[]{:S(2)}) collective-permute-start(bf16[1024,256]{1,0:T(8,128)(2,1)S(1)} %collective-permute-done.13), channel_id=1, source_target_pairs={{0,4},{4,8},{8,12},{12,16},{16,20},{20,24},{24,28},{28,32},{32,36}... | collective-permute-start | bytes 1572872 | tf_op jit(solution)/shard_map/stream_1_step_2/ppermute | solution.py:191
  33.7 0.0 collective-permute-done.1
  33.7 1.1 pad_maximum_fusion.refs_0_
  34.8 4.6 %collective-permute-start.2 = (bf16[1024,512]{1,0:T(8,128)(2,1)S(1)}, bf16[1024,512]{1,0:T(8,128)(2,1)S(1)}, u32[]{:S(2)}, u32[]{:S(2)}) collective-permute-start(bf16[1024,512]{1,0:T(8,128)(2,1)S(1)} %pad_maximum_fusion.refs_0_), channel_id=1, source_target_pairs={{0,128},{64,448},{128,256},{192,64},{256,384},{320,192},{384,0},{4... | collective-permute-start | bytes 3145736 | tf_op jit(solution)/shard_map/b_near/ppermute | solution.py:203
  39.5 0.0 collective-permute-done.4.refs_6_
  39.5 1.9 %collective-permute-start.5 = (bf16[1024,256]{1,0:T(8,128)(2,1)S(1)}, bf16[1024,256]{1,0:T(8,128)(2,1)S(1)}, u32[]{:S(2)}, u32[]{:S(2)}) collective-permute-start(bf16[1024,256]{1,0:T(8,128)(2,1)S(1)} %collective-permute-done.4.refs_6_), channel_id=1, source_target_pairs={{0,4},{4,8},{8,12},{12,16},{16,20},{20,24},{24,28},{28,32},{32,36}... | collective-permute-start | bytes 1572872 | tf_op jit(solution)/shard_map/stream_0_step_3/ppermute | solution.py:191
  41.4 1.9 %collective-permute-start.16 = (bf16[1024,256]{1,0:T(8,128)(2,1)S(1)}, bf16[1024,256]{1,0:T(8,128)(2,1)S(1)}, u32[]{:S(2)}, u32[]{:S(2)}) collective-permute-start(bf16[1024,256]{1,0:T(8,128)(2,1)S(1)} %collective-permute-done.13), channel_id=1, source_target_pairs={{0,64},{64,0},{1,65},{65,1},{2,66},{66,2},{3,67},{67,3},{4,68},{68... | collective-permute-start | bytes 1572872 | tf_op jit(solution)/shard_map/ppermute | solution.py:211
  43.3 0.0 collective-permute-done.14
  43.3 2.4 %collective-permute-start.15 = (bf16[1024,256]{1,0:T(8,128)(2,1)S(1)}, bf16[1024,256]{1,0:T(8,128)(2,1)S(1)}, u32[]{:S(2)}, u32[]{:S(2)}) collective-permute-start(bf16[1024,256]{1,0:T(8,128)(2,1)S(1)} %collective-permute-done.14), channel_id=1, source_target_pairs={{0,4},{4,8},{8,12},{12,16},{16,20},{20,24},{24,28},{28,32},{32,36}... | collective-permute-start | bytes 1572872 | tf_op jit(solution)/shard_map/stream_1_step_3/ppermute | solution.py:191
  45.8 3.6 %collective-permute-start.18 = (bf16[1024,256]{1,0:T(8,128)(2,1)S(1)}, bf16[1024,256]{1,0:T(8,128)(2,1)S(1)}, u32[]{:S(2)}, u32[]{:S(2)}) collective-permute-start(bf16[1024,256]{1,0:T(8,128)(2,1)S(1)} %collective-permute-done.14), channel_id=1, source_target_pairs={{0,64},{64,0},{1,65},{65,1},{2,66},{66,2},{3,67},{67,3},{4,68},{68... | collective-permute-start | bytes 1572872 | tf_op jit(solution)/shard_map/ppermute | solution.py:211
  49.4 0.3 collective-permute-done.5.refs_7_
  49.7 3.1 %collective-permute-start.8 = (bf16[1024,256]{1,0:T(8,128)(2,1)S(1)}, bf16[1024,256]{1,0:T(8,128)(2,1)S(1)}, u32[]{:S(2)}, u32[]{:S(2)}) collective-permute-start(bf16[1024,256]{1,0:T(8,128)(2,1)S(1)} %collective-permute-done.5.refs_7_), channel_id=1, source_target_pairs={{0,4},{4,8},{8,12},{12,16},{16,20},{20,24},{24,28},{28,32},{32,36}... | collective-permute-start | bytes 1572872 | tf_op jit(solution)/shard_map/stream_0_step_4/ppermute | solution.py:191
  52.8 0.0 collective-permute-done.16.refs_9_
  52.8 2.5 %collective-permute-done.15 = bf16[1024,256]{1,0:T(8,128)(2,1)S(1)} collective-permute-done((bf16[1024,256]{1,0:T(8,128)(2,1)S(1)}, bf16[1024,256]{1,0:T(8,128)(2,1)S(1)}, u32[]{:S(2)}, u32[]{:S(2)}) %collective-permute-start.15) | collective-permute-done | bytes 524320 | tf_op jit(solution)/shard_map/stream_1_step_3/ppermute | solution.py:191
  55.3 0.0 collective-permute-done.2.refs_1_
  55.3 2.7 %collective-permute-start.6 = (bf16[1024,512]{1,0:T(8,128)(2,1)S(1)}, bf16[1024,512]{1,0:T(8,128)(2,1)S(1)}, u32[]{:S(2)}, u32[]{:S(2)}) collective-permute-start(bf16[1024,512]{1,0:T(8,128)(2,1)S(1)} %collective-permute-done.2.refs_1_), channel_id=1, source_target_pairs={{0,64},{64,0},{1,65},{65,1},{2,66},{66,2},{3,67},{67,3},{4,68},{68... | collective-permute-start | bytes 3145736 | tf_op jit(solution)/shard_map/b_turn/ppermute | solution.py:209
  58.0 2.0 %collective-permute-start.17 = (bf16[1024,256]{1,0:T(8,128)(2,1)S(1)}, bf16[1024,256]{1,0:T(8,128)(2,1)S(1)}, u32[]{:S(2)}, u32[]{:S(2)}) collective-permute-start(bf16[1024,256]{1,0:T(8,128)(2,1)S(1)} %collective-permute-done.15), channel_id=1, source_target_pairs={{0,4},{4,8},{8,12},{12,16},{16,20},{20,24},{24,28},{28,32},{32,36}... | collective-permute-start | bytes 1572872 | tf_op jit(solution)/shard_map/stream_1_step_4/ppermute | solution.py:191
  60.1 0.9 collective-permute-done.8.refs_8_
  60.9 3.0 %collective-permute-start.9 = (bf16[1024,256]{1,0:T(8,128)(2,1)S(1)}, bf16[1024,256]{1,0:T(8,128)(2,1)S(1)}, u32[]{:S(2)}, u32[]{:S(2)}) collective-permute-start(bf16[1024,256]{1,0:T(8,128)(2,1)S(1)} %collective-permute-done.8.refs_8_), channel_id=1, source_target_pairs={{0,4},{4,8},{8,12},{12,16},{16,20},{20,24},{24,28},{28,32},{32,36}... | collective-permute-start | bytes 1572872 | tf_op jit(solution)/shard_map/stream_0_step_5/ppermute | solution.py:191
  64.0 2.1 %collective-permute-start.20 = (bf16[1024,256]{1,0:T(8,128)(2,1)S(1)}, bf16[1024,256]{1,0:T(8,128)(2,1)S(1)}, u32[]{:S(2)}, u32[]{:S(2)}) collective-permute-start(bf16[1024,256]{1,0:T(8,128)(2,1)S(1)} %collective-permute-done.15), channel_id=1, source_target_pairs={{0,64},{64,0},{1,65},{65,1},{2,66},{66,2},{3,67},{67,3},{4,68},{68... | collective-permute-start | bytes 1572872 | tf_op jit(solution)/shard_map/ppermute | solution.py:211
  66.1 0.0 collective-permute-done.18.refs_8_
  66.1 2.2 %collective-permute-done.17 = bf16[1024,256]{1,0:T(8,128)(2,1)S(1)} collective-permute-done((bf16[1024,256]{1,0:T(8,128)(2,1)S(1)}, bf16[1024,256]{1,0:T(8,128)(2,1)S(1)}, u32[]{:S(2)}, u32[]{:S(2)}) %collective-permute-start.17) | collective-permute-done | bytes 524320 | tf_op jit(solution)/shard_map/stream_1_step_4/ppermute | solution.py:191
  68.3 2.9 %collective-permute-start.19 = (bf16[1024,256]{1,0:T(8,128)(2,1)S(1)}, bf16[1024,256]{1,0:T(8,128)(2,1)S(1)}, u32[]{:S(2)}, u32[]{:S(2)}) collective-permute-start(bf16[1024,256]{1,0:T(8,128)(2,1)S(1)} %collective-permute-done.17), channel_id=1, source_target_pairs={{0,4},{4,8},{8,12},{12,16},{16,20},{20,24},{24,28},{28,32},{32,36}... | collective-permute-start | bytes 1572872 | tf_op jit(solution)/shard_map/stream_1_step_5/ppermute | solution.py:191
  71.2 3.0 %collective-permute-start.22 = (bf16[1024,256]{1,0:T(8,128)(2,1)S(1)}, bf16[1024,256]{1,0:T(8,128)(2,1)S(1)}, u32[]{:S(2)}, u32[]{:S(2)}) collective-permute-start(bf16[1024,256]{1,0:T(8,128)(2,1)S(1)} %collective-permute-done.17), channel_id=1, source_target_pairs={{0,64},{64,0},{1,65},{65,1},{2,66},{66,2},{3,67},{67,3},{4,68},{68... | collective-permute-start | bytes 1572872 | tf_op jit(solution)/shard_map/ppermute | solution.py:211
  74.2 0.0 collective-permute-done.9.refs_9_
  74.2 0.0 collective-permute-done.6.refs_2_
  74.2 4.9 %collective-permute-start.10 = (bf16[1024,256]{1,0:T(8,128)(2,1)S(1)}, bf16[1024,256]{1,0:T(8,128)(2,1)S(1)}, u32[]{:S(2)}, u32[]{:S(2)}) collective-permute-start(bf16[1024,256]{1,0:T(8,128)(2,1)S(1)} %collective-permute-done.9.refs_9_), channel_id=1, source_target_pairs={{0,4},{4,8},{8,12},{12,16},{16,20},{20,24},{24,28},{28,32},{32,36}... | collective-permute-start | bytes 1572872 | tf_op jit(solution)/shard_map/stream_0_step_6/ppermute | solution.py:191
  79.1 0.0 collective-permute-done.20.refs_7_
  79.1 0.4 collective-permute-done.19
  79.5 2.9 %collective-permute-start.21 = (bf16[1024,256]{1,0:T(8,128)(2,1)S(1)}, bf16[1024,256]{1,0:T(8,128)(2,1)S(1)}, u32[]{:S(2)}, u32[]{:S(2)}) collective-permute-start(bf16[1024,256]{1,0:T(8,128)(2,1)S(1)} %collective-permute-done.19), channel_id=1, source_target_pairs={{0,4},{4,8},{8,12},{12,16},{16,20},{20,24},{24,28},{28,32},{32,36}... | collective-permute-start | bytes 1572872 | tf_op jit(solution)/shard_map/stream_1_step_6/ppermute | solution.py:191
  82.4 3.2 %collective-permute-start.7 = (bf16[1024,512]{1,0:T(8,128)(2,1)S(1)}, bf16[1024,512]{1,0:T(8,128)(2,1)S(1)}, u32[]{:S(2)}, u32[]{:S(2)}) collective-permute-start(bf16[1024,512]{1,0:T(8,128)(2,1)S(1)} %collective-permute-done.2.refs_1_), channel_id=1, source_target_pairs={{0,128},{64,448},{128,256},{192,64},{256,384},{320,192},{384,0},{4... | collective-permute-start | bytes 3145736 | tf_op jit(solution)/shard_map/b_far/ppermute | solution.py:206
  85.7 0.0 collective-permute-done.10.refs_10_
  85.7 4.5 %collective-permute-start.11 = (bf16[1024,256]{1,0:T(8,128)(2,1)S(1)}, bf16[1024,256]{1,0:T(8,128)(2,1)S(1)}, u32[]{:S(2)}, u32[]{:S(2)}) collective-permute-start(bf16[1024,256]{1,0:T(8,128)(2,1)S(1)} %collective-permute-done.10.refs_10_), channel_id=1, source_target_pairs={{0,4},{4,8},{8,12},{12,16},{16,20},{20,24},{24,28},{28,32},{32,36}... | collective-permute-start | bytes 1572872 | tf_op jit(solution)/shard_map/stream_0_step_7/ppermute | solution.py:191
  90.2 0.0 collective-permute-done.22.refs_6_
  90.2 0.6 collective-permute-done.21
  90.8 5.3 %collective-permute-start.23 = (bf16[1024,256]{1,0:T(8,128)(2,1)S(1)}, bf16[1024,256]{1,0:T(8,128)(2,1)S(1)}, u32[]{:S(2)}, u32[]{:S(2)}) collective-permute-start(bf16[1024,256]{1,0:T(8,128)(2,1)S(1)} %collective-permute-done.21), channel_id=1, source_target_pairs={{0,4},{4,8},{8,12},{12,16},{16,20},{20,24},{24,28},{28,32},{32,36}... | collective-permute-start | bytes 1572872 | tf_op jit(solution)/shard_map/stream_1_step_7/ppermute | solution.py:191
  96.1 2.6 %collective-permute-start.26 = (bf16[1024,256]{1,0:T(8,128)(2,1)S(1)}, bf16[1024,256]{1,0:T(8,128)(2,1)S(1)}, u32[]{:S(2)}, u32[]{:S(2)}) collective-permute-start(bf16[1024,256]{1,0:T(8,128)(2,1)S(1)} %collective-permute-done.19), channel_id=1, source_target_pairs={{0,64},{64,0},{1,65},{65,1},{2,66},{66,2},{3,67},{67,3},{4,68},{68... | collective-permute-start | bytes 1572872 | tf_op jit(solution)/shard_map/ppermute | solution.py:211
  98.7 1.9 %collective-permute-start.25 = (bf16[1024,256]{1,0:T(8,128)(2,1)S(1)}, bf16[1024,256]{1,0:T(8,128)(2,1)S(1)}, u32[]{:S(2)}, u32[]{:S(2)}) collective-permute-start(bf16[1024,256]{1,0:T(8,128)(2,1)S(1)} %collective-permute-done.21), channel_id=1, source_target_pairs={{0,64},{64,0},{1,65},{65,1},{2,66},{66,2},{3,67},{67,3},{4,68},{68... | collective-permute-start | bytes 1572872 | tf_op jit(solution)/shard_map/ppermute | solution.py:211
  100.6 0.0 collective-permute-done.11.refs_4_
  100.7 4.9 %collective-permute-start.12 = (bf16[1024,256]{1,0:T(8,128)(2,1)S(1)}, bf16[1024,256]{1,0:T(8,128)(2,1)S(1)}, u32[]{:S(2)}, u32[]{:S(2)}) collective-permute-start(bf16[1024,256]{1,0:T(8,128)(2,1)S(1)} %collective-permute-done.11.refs_4_), channel_id=1, source_target_pairs={{0,4},{4,8},{8,12},{12,16},{16,20},{20,24},{24,28},{28,32},{32,36}... | collective-permute-start | bytes 1572872 | tf_op jit(solution)/shard_map/stream_0_step_8/ppermute | solution.py:191
  105.5 0.0 collective-permute-done.23
  105.5 3.5 %collective-permute-start.24 = (bf16[1024,256]{1,0:T(8,128)(2,1)S(1)}, bf16[1024,256]{1,0:T(8,128)(2,1)S(1)}, u32[]{:S(2)}, u32[]{:S(2)}) collective-permute-start(bf16[1024,256]{1,0:T(8,128)(2,1)S(1)} %collective-permute-done.23), channel_id=1, source_target_pairs={{0,64},{64,0},{1,65},{65,1},{2,66},{66,2},{3,67},{67,3},{4,68},{68... | collective-permute-start | bytes 1572872 | tf_op jit(solution)/shard_map/ppermute | solution.py:212
  109.1 0.0 collective-permute-done.7.refs_3_
  109.1 2.7 %shard_map.75.refs_7_ = f32[1024,512]{1,0:T(8,128)S(1)} custom-call(bf16[1024,512]{1,0:T(8,128)(2,1)S(1)} %pad_maximum_fusion.refs_0_, bf16[1024,512]{1,0:T(8,128)(2,1)S(1)} %collective-permute-done.2.refs_1_, bf16[1024,512]{1,0:T(8,128)(2,1)S(1)} %collective-permute-done.6.refs_2_, bf16[1024,512]{1,0:T(8,128)(2,1)S(1)} %collective-permute-done.7.refs_3_, ...), custom_call_target="tpu_custom_call" | custom-call | flops 1879048192 | bytes 2097152 | tf_op jit(solution)/shard_map/pallas_call | solution.py:156
  111.8 0.0 collective-permute-done.26.refs_5_
  111.8 0.0 collective-permute-done.25.refs_4_
  111.8 2.4 %shard_map.76.refs_8_ = f32[1024,512]{1,0:T(8,128)S(1)} custom-call(bf16[1024,512]{1,0:T(8,128)(2,1)S(1)} %pad_maximum_fusion.refs_0_, bf16[1024,512]{1,0:T(8,128)(2,1)S(1)} %collective-permute-done.2.refs_1_, bf16[1024,512]{1,0:T(8,128)(2,1)S(1)} %collective-permute-done.6.refs_2_, bf16[1024,512]{1,0:T(8,128)(2,1)S(1)} %collective-permute-done.7.refs_3_, ...), custom_call_target="tpu_custom_call" | custom-call | flops 1610612736 | bytes 2097152 | tf_op jit(solution)/shard_map/pallas_call | solution.py:156
  114.1 0.0 collective-permute-done.12.refs_5_
  114.2 0.0 collective-permute-done.24.refs_6_
  114.2 1.9 %shard_map.77 = f32[4,272,512]{2,1,0:T(8,128)S(1)} custom-call(bf16[1024,512]{1,0:T(8,128)(2,1)S(1)} %pad_maximum_fusion.refs_0_, bf16[1024,512]{1,0:T(8,128)(2,1)S(1)} %collective-permute-done.2.refs_1_, bf16[1024,512]{1,0:T(8,128)(2,1)S(1)} %collective-permute-done.6.refs_2_, bf16[1024,512]{1,0:T(8,128)(2,1)S(1)} %collective-permute-done.7.refs_3_, ...), custom_call_target="tpu_custom_call" | custom-call | flops 805306368 | bytes 2097152 | tf_op jit(solution)/shard_map/pallas_call | solution.py:156
  116.1 0.3 convert_element_type.9
  116.4 19.2 %all_to_all.5 = f16[4,272,512]{2,1,0:T(8,128)(2,1)S(1)} all-to-all(f16[4,272,512]{2,1,0:T(8,128)(2,1)S(1)} %convert_element_type.9), channel_id=1, replica_groups=mesh['y'=4,'core'=2,'col'=16,'layer'=4] {'layer'}, dimensions={0} | all-to-all | bytes 2228224 | tf_op jit(solution)/shard_map/all_to_all | solution.py:220
  135.5 0.1 convert_reduce_fusion
  135.6 1.1 multiply_reduce_fusion
  (3 shorter events, 0.0 us)
Async XLA Ops:
  2.0 107.0 %copy-start = (bf16[1024,256]{1,0:T(8,128)(2,1)S(1)}, bf16[1024,256]{1,0:T(8,128)(2,1)}, u32[]{:S(2)}) copy-start(bf16[1024,256]{1,0:T(8,128)(2,1)} %shard_map.73.refs_4_) | copy-start | bytes 1572868
  2.1 14.7 %collective-permute-start = (bf16[1024,256]{1,0:T(8,128)(2,1)}, bf16[1024,256]{1,0:T(8,128)(2,1)S(1)}, u32[]{:S(2)}, u32[]{:S(2)}) collective-permute-start(bf16[1024,256]{1,0:T(8,128)(2,1)} %shard_map.73.refs_4_), channel_id=1, source_target_pairs={{0,64},{64,0},{1,65},{65,1},{2,66},{66,2},{3,67},{67,3},{4,68},{68... | collective-permute-start | bytes 1572872 | tf_op jit(solution)/shard_map/ppermute | solution.py:152
  11.0 12.4 %collective-permute-start.3 = (bf16[1024,256]{1,0:T(8,128)(2,1)}, bf16[1024,256]{1,0:T(8,128)(2,1)S(1)}, u32[]{:S(2)}, u32[]{:S(2)}) collective-permute-start(bf16[1024,256]{1,0:T(8,128)(2,1)} %shard_map.73.refs_4_), channel_id=1, source_target_pairs={{0,4},{4,8},{8,12},{12,16},{16,20},{20,24},{24,28},{28,32},{32,36}... | collective-permute-start | bytes 1572872 | tf_op jit(solution)/shard_map/stream_0_step_1/ppermute | solution.py:191
  16.8 11.9 %collective-permute-start.13 = (bf16[1024,256]{1,0:T(8,128)(2,1)S(1)}, bf16[1024,256]{1,0:T(8,128)(2,1)S(1)}, u32[]{:S(2)}, u32[]{:S(2)}) collective-permute-start(bf16[1024,256]{1,0:T(8,128)(2,1)S(1)} %collective-permute-done), channel_id=1, source_target_pairs={{0,4},{4,8},{8,12},{12,16},{16,20},{20,24},{24,28},{28,32},{32,36}... | collective-permute-start | bytes 1572872 | tf_op jit(solution)/shard_map/stream_1_step_1/ppermute | solution.py:191
  21.4 12.3 %collective-permute-start.1 = (bf16[512,512]{1,0:T(8,128)(2,1)}, bf16[512,512]{1,0:T(8,128)(2,1)S(1)}, u32[]{:S(2)}, u32[]{:S(2)}) collective-permute-start(bf16[512,512]{1,0:T(8,128)(2,1)} %shard_map.74), channel_id=1, source_target_pairs={{0,64},{64,0},{1,65},{65,1},{2,66},{66,2},{3,67},{67,3},{4,68},{68... | collective-permute-start | bytes 1572872 | tf_op jit(solution)/shard_map/b_swap/ppermute | solution.py:199
  23.4 16.1 %collective-permute-start.4 = (bf16[1024,256]{1,0:T(8,128)(2,1)S(1)}, bf16[1024,256]{1,0:T(8,128)(2,1)S(1)}, u32[]{:S(2)}, u32[]{:S(2)}) collective-permute-start(bf16[1024,256]{1,0:T(8,128)(2,1)S(1)} %collective-permute-done.3.refs_5_), channel_id=1, source_target_pairs={{0,4},{4,8},{8,12},{12,16},{16,20},{20,24},{24,28},{28,32},{32,36}... | collective-permute-start | bytes 1572872 | tf_op jit(solution)/shard_map/stream_0_step_2/ppermute | solution.py:191
  28.7 14.7 %collective-permute-start.14 = (bf16[1024,256]{1,0:T(8,128)(2,1)S(1)}, bf16[1024,256]{1,0:T(8,128)(2,1)S(1)}, u32[]{:S(2)}, u32[]{:S(2)}) collective-permute-start(bf16[1024,256]{1,0:T(8,128)(2,1)S(1)} %collective-permute-done.13), channel_id=1, source_target_pairs={{0,4},{4,8},{8,12},{12,16},{16,20},{20,24},{24,28},{28,32},{32,36}... | collective-permute-start | bytes 1572872 | tf_op jit(solution)/shard_map/stream_1_step_2/ppermute | solution.py:191
  34.8 20.5 %collective-permute-start.2 = (bf16[1024,512]{1,0:T(8,128)(2,1)S(1)}, bf16[1024,512]{1,0:T(8,128)(2,1)S(1)}, u32[]{:S(2)}, u32[]{:S(2)}) collective-permute-start(bf16[1024,512]{1,0:T(8,128)(2,1)S(1)} %pad_maximum_fusion.refs_0_), channel_id=1, source_target_pairs={{0,128},{64,448},{128,256},{192,64},{256,384},{320,192},{384,0},{4... | collective-permute-start | bytes 3145736 | tf_op jit(solution)/shard_map/b_near/ppermute | solution.py:203
  39.5 10.2 %collective-permute-start.5 = (bf16[1024,256]{1,0:T(8,128)(2,1)S(1)}, bf16[1024,256]{1,0:T(8,128)(2,1)S(1)}, u32[]{:S(2)}, u32[]{:S(2)}) collective-permute-start(bf16[1024,256]{1,0:T(8,128)(2,1)S(1)} %collective-permute-done.4.refs_6_), channel_id=1, source_target_pairs={{0,4},{4,8},{8,12},{12,16},{16,20},{20,24},{24,28},{28,32},{32,36}... | collective-permute-start | bytes 1572872 | tf_op jit(solution)/shard_map/stream_0_step_3/ppermute | solution.py:191
  41.4 11.4 %collective-permute-start.16 = (bf16[1024,256]{1,0:T(8,128)(2,1)S(1)}, bf16[1024,256]{1,0:T(8,128)(2,1)S(1)}, u32[]{:S(2)}, u32[]{:S(2)}) collective-permute-start(bf16[1024,256]{1,0:T(8,128)(2,1)S(1)} %collective-permute-done.13), channel_id=1, source_target_pairs={{0,64},{64,0},{1,65},{65,1},{2,66},{66,2},{3,67},{67,3},{4,68},{68... | collective-permute-start | bytes 1572872 | tf_op jit(solution)/shard_map/ppermute | solution.py:211
  43.3 12.0 %collective-permute-start.15 = (bf16[1024,256]{1,0:T(8,128)(2,1)S(1)}, bf16[1024,256]{1,0:T(8,128)(2,1)S(1)}, u32[]{:S(2)}, u32[]{:S(2)}) collective-permute-start(bf16[1024,256]{1,0:T(8,128)(2,1)S(1)} %collective-permute-done.14), channel_id=1, source_target_pairs={{0,4},{4,8},{8,12},{12,16},{16,20},{20,24},{24,28},{28,32},{32,36}... | collective-permute-start | bytes 1572872 | tf_op jit(solution)/shard_map/stream_1_step_3/ppermute | solution.py:191
  45.8 20.3 %collective-permute-start.18 = (bf16[1024,256]{1,0:T(8,128)(2,1)S(1)}, bf16[1024,256]{1,0:T(8,128)(2,1)S(1)}, u32[]{:S(2)}, u32[]{:S(2)}) collective-permute-start(bf16[1024,256]{1,0:T(8,128)(2,1)S(1)} %collective-permute-done.14), channel_id=1, source_target_pairs={{0,64},{64,0},{1,65},{65,1},{2,66},{66,2},{3,67},{67,3},{4,68},{68... | collective-permute-start | bytes 1572872 | tf_op jit(solution)/shard_map/ppermute | solution.py:211
  49.7 11.2 %collective-permute-start.8 = (bf16[1024,256]{1,0:T(8,128)(2,1)S(1)}, bf16[1024,256]{1,0:T(8,128)(2,1)S(1)}, u32[]{:S(2)}, u32[]{:S(2)}) collective-permute-start(bf16[1024,256]{1,0:T(8,128)(2,1)S(1)} %collective-permute-done.5.refs_7_), channel_id=1, source_target_pairs={{0,4},{4,8},{8,12},{12,16},{16,20},{20,24},{24,28},{28,32},{32,36}... | collective-permute-start | bytes 1572872 | tf_op jit(solution)/shard_map/stream_0_step_4/ppermute | solution.py:191
  55.3 18.9 %collective-permute-start.6 = (bf16[1024,512]{1,0:T(8,128)(2,1)S(1)}, bf16[1024,512]{1,0:T(8,128)(2,1)S(1)}, u32[]{:S(2)}, u32[]{:S(2)}) collective-permute-start(bf16[1024,512]{1,0:T(8,128)(2,1)S(1)} %collective-permute-done.2.refs_1_), channel_id=1, source_target_pairs={{0,64},{64,0},{1,65},{65,1},{2,66},{66,2},{3,67},{67,3},{4,68},{68... | collective-permute-start | bytes 3145736 | tf_op jit(solution)/shard_map/b_turn/ppermute | solution.py:209
  58.0 10.2 %collective-permute-start.17 = (bf16[1024,256]{1,0:T(8,128)(2,1)S(1)}, bf16[1024,256]{1,0:T(8,128)(2,1)S(1)}, u32[]{:S(2)}, u32[]{:S(2)}) collective-permute-start(bf16[1024,256]{1,0:T(8,128)(2,1)S(1)} %collective-permute-done.15), channel_id=1, source_target_pairs={{0,4},{4,8},{8,12},{12,16},{16,20},{20,24},{24,28},{28,32},{32,36}... | collective-permute-start | bytes 1572872 | tf_op jit(solution)/shard_map/stream_1_step_4/ppermute | solution.py:191
  60.9 13.2 %collective-permute-start.9 = (bf16[1024,256]{1,0:T(8,128)(2,1)S(1)}, bf16[1024,256]{1,0:T(8,128)(2,1)S(1)}, u32[]{:S(2)}, u32[]{:S(2)}) collective-permute-start(bf16[1024,256]{1,0:T(8,128)(2,1)S(1)} %collective-permute-done.8.refs_8_), channel_id=1, source_target_pairs={{0,4},{4,8},{8,12},{12,16},{16,20},{20,24},{24,28},{28,32},{32,36}... | collective-permute-start | bytes 1572872 | tf_op jit(solution)/shard_map/stream_0_step_5/ppermute | solution.py:191
  64.0 15.1 %collective-permute-start.20 = (bf16[1024,256]{1,0:T(8,128)(2,1)S(1)}, bf16[1024,256]{1,0:T(8,128)(2,1)S(1)}, u32[]{:S(2)}, u32[]{:S(2)}) collective-permute-start(bf16[1024,256]{1,0:T(8,128)(2,1)S(1)} %collective-permute-done.15), channel_id=1, source_target_pairs={{0,64},{64,0},{1,65},{65,1},{2,66},{66,2},{3,67},{67,3},{4,68},{68... | collective-permute-start | bytes 1572872 | tf_op jit(solution)/shard_map/ppermute | solution.py:211
  68.3 11.2 %collective-permute-start.19 = (bf16[1024,256]{1,0:T(8,128)(2,1)S(1)}, bf16[1024,256]{1,0:T(8,128)(2,1)S(1)}, u32[]{:S(2)}, u32[]{:S(2)}) collective-permute-start(bf16[1024,256]{1,0:T(8,128)(2,1)S(1)} %collective-permute-done.17), channel_id=1, source_target_pairs={{0,4},{4,8},{8,12},{12,16},{16,20},{20,24},{24,28},{28,32},{32,36}... | collective-permute-start | bytes 1572872 | tf_op jit(solution)/shard_map/stream_1_step_5/ppermute | solution.py:191
  71.2 19.0 %collective-permute-start.22 = (bf16[1024,256]{1,0:T(8,128)(2,1)S(1)}, bf16[1024,256]{1,0:T(8,128)(2,1)S(1)}, u32[]{:S(2)}, u32[]{:S(2)}) collective-permute-start(bf16[1024,256]{1,0:T(8,128)(2,1)S(1)} %collective-permute-done.17), channel_id=1, source_target_pairs={{0,64},{64,0},{1,65},{65,1},{2,66},{66,2},{3,67},{67,3},{4,68},{68... | collective-permute-start | bytes 1572872 | tf_op jit(solution)/shard_map/ppermute | solution.py:211
  74.2 11.5 %collective-permute-start.10 = (bf16[1024,256]{1,0:T(8,128)(2,1)S(1)}, bf16[1024,256]{1,0:T(8,128)(2,1)S(1)}, u32[]{:S(2)}, u32[]{:S(2)}) collective-permute-start(bf16[1024,256]{1,0:T(8,128)(2,1)S(1)} %collective-permute-done.9.refs_9_), channel_id=1, source_target_pairs={{0,4},{4,8},{8,12},{12,16},{16,20},{20,24},{24,28},{28,32},{32,36}... | collective-permute-start | bytes 1572872 | tf_op jit(solution)/shard_map/stream_0_step_6/ppermute | solution.py:191
  79.5 11.3 %collective-permute-start.21 = (bf16[1024,256]{1,0:T(8,128)(2,1)S(1)}, bf16[1024,256]{1,0:T(8,128)(2,1)S(1)}, u32[]{:S(2)}, u32[]{:S(2)}) collective-permute-start(bf16[1024,256]{1,0:T(8,128)(2,1)S(1)} %collective-permute-done.19), channel_id=1, source_target_pairs={{0,4},{4,8},{8,12},{12,16},{16,20},{20,24},{24,28},{28,32},{32,36}... | collective-permute-start | bytes 1572872 | tf_op jit(solution)/shard_map/stream_1_step_6/ppermute | solution.py:191
  82.4 26.6 %collective-permute-start.7 = (bf16[1024,512]{1,0:T(8,128)(2,1)S(1)}, bf16[1024,512]{1,0:T(8,128)(2,1)S(1)}, u32[]{:S(2)}, u32[]{:S(2)}) collective-permute-start(bf16[1024,512]{1,0:T(8,128)(2,1)S(1)} %collective-permute-done.2.refs_1_), channel_id=1, source_target_pairs={{0,128},{64,448},{128,256},{192,64},{256,384},{320,192},{384,0},{4... | collective-permute-start | bytes 3145736 | tf_op jit(solution)/shard_map/b_far/ppermute | solution.py:206
  85.7 14.9 %collective-permute-start.11 = (bf16[1024,256]{1,0:T(8,128)(2,1)S(1)}, bf16[1024,256]{1,0:T(8,128)(2,1)S(1)}, u32[]{:S(2)}, u32[]{:S(2)}) collective-permute-start(bf16[1024,256]{1,0:T(8,128)(2,1)S(1)} %collective-permute-done.10.refs_10_), channel_id=1, source_target_pairs={{0,4},{4,8},{8,12},{12,16},{16,20},{20,24},{24,28},{28,32},{32,36}... | collective-permute-start | bytes 1572872 | tf_op jit(solution)/shard_map/stream_0_step_7/ppermute | solution.py:191
  90.8 14.7 %collective-permute-start.23 = (bf16[1024,256]{1,0:T(8,128)(2,1)S(1)}, bf16[1024,256]{1,0:T(8,128)(2,1)S(1)}, u32[]{:S(2)}, u32[]{:S(2)}) collective-permute-start(bf16[1024,256]{1,0:T(8,128)(2,1)S(1)} %collective-permute-done.21), channel_id=1, source_target_pairs={{0,4},{4,8},{8,12},{12,16},{16,20},{20,24},{24,28},{28,32},{32,36}... | collective-permute-start | bytes 1572872 | tf_op jit(solution)/shard_map/stream_1_step_7/ppermute | solution.py:191
  96.1 15.7 %collective-permute-start.26 = (bf16[1024,256]{1,0:T(8,128)(2,1)S(1)}, bf16[1024,256]{1,0:T(8,128)(2,1)S(1)}, u32[]{:S(2)}, u32[]{:S(2)}) collective-permute-start(bf16[1024,256]{1,0:T(8,128)(2,1)S(1)} %collective-permute-done.19), channel_id=1, source_target_pairs={{0,64},{64,0},{1,65},{65,1},{2,66},{66,2},{3,67},{67,3},{4,68},{68... | collective-permute-start | bytes 1572872 | tf_op jit(solution)/shard_map/ppermute | solution.py:211
  98.7 13.0 %collective-permute-start.25 = (bf16[1024,256]{1,0:T(8,128)(2,1)S(1)}, bf16[1024,256]{1,0:T(8,128)(2,1)S(1)}, u32[]{:S(2)}, u32[]{:S(2)}) collective-permute-start(bf16[1024,256]{1,0:T(8,128)(2,1)S(1)} %collective-permute-done.21), channel_id=1, source_target_pairs={{0,64},{64,0},{1,65},{65,1},{2,66},{66,2},{3,67},{67,3},{4,68},{68... | collective-permute-start | bytes 1572872 | tf_op jit(solution)/shard_map/ppermute | solution.py:211
  100.7 13.5 %collective-permute-start.12 = (bf16[1024,256]{1,0:T(8,128)(2,1)S(1)}, bf16[1024,256]{1,0:T(8,128)(2,1)S(1)}, u32[]{:S(2)}, u32[]{:S(2)}) collective-permute-start(bf16[1024,256]{1,0:T(8,128)(2,1)S(1)} %collective-permute-done.11.refs_4_), channel_id=1, source_target_pairs={{0,4},{4,8},{8,12},{12,16},{16,20},{20,24},{24,28},{28,32},{32,36}... | collective-permute-start | bytes 1572872 | tf_op jit(solution)/shard_map/stream_0_step_8/ppermute | solution.py:191
  105.5 8.6 %collective-permute-start.24 = (bf16[1024,256]{1,0:T(8,128)(2,1)S(1)}, bf16[1024,256]{1,0:T(8,128)(2,1)S(1)}, u32[]{:S(2)}, u32[]{:S(2)}) collective-permute-start(bf16[1024,256]{1,0:T(8,128)(2,1)S(1)} %collective-permute-done.23), channel_id=1, source_target_pairs={{0,64},{64,0},{1,65},{65,1},{2,66},{66,2},{3,67},{67,3},{4,68},{68... | collective-permute-start | bytes 1572872 | tf_op jit(solution)/shard_map/ppermute | solution.py:212

commit v8 on v7

--- a/solution.py
+++ b/solution.py
@@ -183,8 +183,8 @@
             if (step, j) == (last, 1):
                 continue
             sent = held[j][-1]
-            if (step, j) == (6, 0):
-                sent = after(sent, b_all[2])
+            if (step, j) == (5, 0):
+                sent = after(sent, b_all[1])
             if j == 1 and step > 3:
                 sent = after(sent, turned[step - 4])
             with jax.named_scope(f"stream_{j}_step_{step}"):
@@ -204,11 +204,11 @@
             if (step, j) == (3, 1):
                 with jax.named_scope("b_far"):
                     b_all[3] = lax.ppermute(b_all[1], ("y", "core"), near_by)
-            if (step, j) == (4, 0):
+            if (step, j) == (4, 1):
                 with jax.named_scope("b_turn"):
                     b_all[2] = lax.ppermute(after(b_all[1], sent), "core", SWAP)
             if j == 1 and step > 1:
-                turned.append(lax.ppermute(after(held[1][step - 1], sent), "core", SWAP))
+                turned.append(lax.ppermute(held[1][step - 1], "core", SWAP))
     turned.append(lax.ppermute(held[1][last - 1], "core", SWAP))
 
     shards = held[0] + turned[::-1]

time: 138 us -> 136 us (0.986)
  starting transfers between devices: 96.1 us -> 92.7 us
  waiting for transfers between devices: 7.44 us -> 8.92 us
    ppermute x6, starting transfers between devices: 15.2 us -> 12.7 us  [on_device(): turned.append(lax.ppermute(held[1][step - 1], 'core', SWAP))]
    ppermute x15, waiting for transfers between devices: 7.41 us -> 8.89 us  [on_device(): held[j].append(lax.ppermute(sent, ('core', 'col'), ring))]
  transfers between devices with their start and end apart: 27 -> 27, of which waited for: 7 -> 6; matrix products, arithmetic and copies ran while one was open for 1% -> 1% of each run, Pallas kernels for 5% -> 5%
where the time goes in v8:
time: 136 us; the launch traced here: 135 us
  starting transfers between devices  92.7 us (68%)
  blocking collectives  19.1 us (14%)
  Pallas kernels  11 us (8%)
  waiting for transfers between devices  8.92 us (7%)
  other arithmetic  2.63 us (2%)
    ppermute x15, starting transfers between devices, on_device(): held[j].append(lax.ppermute(sent, ('core', 'col'), ring))  54.9 us
    all_to_all x1, blocking collectives, on_device(): return decoded(lax.all_to_all(parts, 'layer', 0, 0)).sum(axis=0)  19.1 us
    ppermute x6, starting transfers between devices, on_device(): turned.append(lax.ppermute(held[1][step - 1], 'core', SWAP))  12.7 us
    ppermute x1, starting transfers between devices, on_device(): held = [[own], [lax.ppermute(own, 'core', SWAP)]]  8.92 us
    ppermute x15, waiting for transfers between devices, on_device(): held[j].append(lax.ppermute(sent, ('core', 'col'), ring))  8.89 us
    pallas_call x3, Pallas kernels, product(): pl.pallas_call(functools.partial(product_kernel, steps, cols, len(adds)),...  6.93 us
    ppermute x1, starting transfers between devices, on_device(): b_all[1] = lax.ppermute(b_all[0], ('y', 'core'), near_by)  4.64 us
    ppermute x1, starting transfers between devices, on_device(): b_all[3] = lax.ppermute(b_all[1], ('y', 'core'), near_by)  4.1 us
  transfers between devices with their start and end apart: 27, of which 6 were waited for; matrix products, arithmetic and copies ran while one was open for 1% of the time, Pallas kernels for 5%

profile of v8, /device:TPU:1, one launch (start us, length us, event | category | flops | bytes accessed | tf_op | source)
XLA Modules:
  0.0 134.7 jit_solution(8925320671802677412)
XLA Ops:
  0.0 2.0 %shard_map.73.refs_4_ = bf16[1024,256]{1,0:T(8,128)(2,1)} custom-call(s32[4]{0:T(128)} %bitcast.1, s32[4]{0:T(128)} %refs_1_.1, s32[1,16]{1,0:T(1,128)} %refs_1_.2, bf16[1,1024,256]{2,1,0:T(8,128)(2,1)} %refs_3_.2), custom_call_target="tpu_custom_call" | custom-call | tf_op jit(solution)/shard_map/pallas_call | solution.py:60
  2.1 8.9 %collective-permute-start = (bf16[1024,256]{1,0:T(8,128)(2,1)}, bf16[1024,256]{1,0:T(8,128)(2,1)S(1)}, u32[]{:S(2)}, u32[]{:S(2)}) collective-permute-start(bf16[1024,256]{1,0:T(8,128)(2,1)} %shard_map.73.refs_4_), channel_id=1, source_target_pairs={{0,64},{64,0},{1,65},{65,1},{2,66},{66,2},{3,67},{67,3},{4,68},{68... | collective-permute-start | bytes 1572872 | tf_op jit(solution)/shard_map/ppermute | solution.py:152
  11.0 5.7 %collective-permute-start.9 = (bf16[1024,256]{1,0:T(8,128)(2,1)}, bf16[1024,256]{1,0:T(8,128)(2,1)S(1)}, u32[]{:S(2)}, u32[]{:S(2)}) collective-permute-start(bf16[1024,256]{1,0:T(8,128)(2,1)} %shard_map.73.refs_4_), channel_id=1, source_target_pairs={{0,4},{4,8},{8,12},{12,16},{16,20},{20,24},{24,28},{28,32},{32,36}... | collective-permute-start | bytes 1572872 | tf_op jit(solution)/shard_map/stream_0_step_1/ppermute | solution.py:191
  16.7 0.0 collective-permute-done
  16.8 2.6 %collective-permute-start.3 = (bf16[1024,256]{1,0:T(8,128)(2,1)S(1)}, bf16[1024,256]{1,0:T(8,128)(2,1)S(1)}, u32[]{:S(2)}, u32[]{:S(2)}) collective-permute-start(bf16[1024,256]{1,0:T(8,128)(2,1)S(1)} %collective-permute-done), channel_id=1, source_target_pairs={{0,4},{4,8},{8,12},{12,16},{16,20},{20,24},{24,28},{28,32},{32,36}... | collective-permute-start | bytes 1572872 | tf_op jit(solution)/shard_map/stream_1_step_1/ppermute | solution.py:191
  19.4 2.0 %shard_map.74 = bf16[512,512]{1,0:T(8,128)(2,1)} custom-call(s32[1,2,2]{2,1,0:T(2,128)} %refs_0_.1, s32[1,16]{1,0:T(1,128)} %refs_1_.2, s32[2]{0:T(128)} %refs_2_.3, bf16[1,512,512]{2,1,0:T(8,128)(2,1)} %refs_3_.3), custom_call_target="tpu_custom_call" | custom-call | tf_op jit(solution)/shard_map/pallas_call | solution.py:60
  21.4 1.9 %collective-permute-start.1 = (bf16[512,512]{1,0:T(8,128)(2,1)}, bf16[512,512]{1,0:T(8,128)(2,1)S(1)}, u32[]{:S(2)}, u32[]{:S(2)}) collective-permute-start(bf16[512,512]{1,0:T(8,128)(2,1)} %shard_map.74), channel_id=1, source_target_pairs={{0,64},{64,0},{1,65},{65,1},{2,66},{66,2},{3,67},{67,3},{4,68},{68... | collective-permute-start | bytes 1572872 | tf_op jit(solution)/shard_map/b_swap/ppermute | solution.py:199
  23.4 0.0 collective-permute-done.9.refs_5_
  23.4 4.7 %collective-permute-start.10 = (bf16[1024,256]{1,0:T(8,128)(2,1)S(1)}, bf16[1024,256]{1,0:T(8,128)(2,1)S(1)}, u32[]{:S(2)}, u32[]{:S(2)}) collective-permute-start(bf16[1024,256]{1,0:T(8,128)(2,1)S(1)} %collective-permute-done.9.refs_5_), channel_id=1, source_target_pairs={{0,4},{4,8},{8,12},{12,16},{16,20},{20,24},{24,28},{28,32},{32,36}... | collective-permute-start | bytes 1572872 | tf_op jit(solution)/shard_map/stream_0_step_2/ppermute | solution.py:191
  28.1 0.6 collective-permute-done.3
  28.7 5.0 %collective-permute-start.4 = (bf16[1024,256]{1,0:T(8,128)(2,1)S(1)}, bf16[1024,256]{1,0:T(8,128)(2,1)S(1)}, u32[]{:S(2)}, u32[]{:S(2)}) collective-permute-start(bf16[1024,256]{1,0:T(8,128)(2,1)S(1)} %collective-permute-done.3), channel_id=1, source_target_pairs={{0,4},{4,8},{8,12},{12,16},{16,20},{20,24},{24,28},{28,32},{32,36}... | collective-permute-start | bytes 1572872 | tf_op jit(solution)/shard_map/stream_1_step_2/ppermute | solution.py:191
  33.7 0.0 collective-permute-done.1
  33.7 1.1 pad_maximum_fusion.refs_0_
  34.8 4.6 %collective-permute-start.2 = (bf16[1024,512]{1,0:T(8,128)(2,1)S(1)}, bf16[1024,512]{1,0:T(8,128)(2,1)S(1)}, u32[]{:S(2)}, u32[]{:S(2)}) collective-permute-start(bf16[1024,512]{1,0:T(8,128)(2,1)S(1)} %pad_maximum_fusion.refs_0_), channel_id=1, source_target_pairs={{0,128},{64,448},{128,256},{192,64},{256,384},{320,192},{384,0},{4... | collective-permute-start | bytes 3145736 | tf_op jit(solution)/shard_map/b_near/ppermute | solution.py:203
  39.5 0.0 collective-permute-done.10.refs_6_
  39.5 1.9 %collective-permute-start.11 = (bf16[1024,256]{1,0:T(8,128)(2,1)S(1)}, bf16[1024,256]{1,0:T(8,128)(2,1)S(1)}, u32[]{:S(2)}, u32[]{:S(2)}) collective-permute-start(bf16[1024,256]{1,0:T(8,128)(2,1)S(1)} %collective-permute-done.10.refs_6_), channel_id=1, source_target_pairs={{0,4},{4,8},{8,12},{12,16},{16,20},{20,24},{24,28},{28,32},{32,36}... | collective-permute-start | bytes 1572872 | tf_op jit(solution)/shard_map/stream_0_step_3/ppermute | solution.py:191
  41.4 1.9 %collective-permute-start.6 = (bf16[1024,256]{1,0:T(8,128)(2,1)S(1)}, bf16[1024,256]{1,0:T(8,128)(2,1)S(1)}, u32[]{:S(2)}, u32[]{:S(2)}) collective-permute-start(bf16[1024,256]{1,0:T(8,128)(2,1)S(1)} %collective-permute-done.3), channel_id=1, source_target_pairs={{0,64},{64,0},{1,65},{65,1},{2,66},{66,2},{3,67},{67,3},{4,68},{68... | collective-permute-start | bytes 1572872 | tf_op jit(solution)/shard_map/ppermute | solution.py:211
  43.3 0.0 collective-permute-done.4
  43.3 2.4 %collective-permute-start.5 = (bf16[1024,256]{1,0:T(8,128)(2,1)S(1)}, bf16[1024,256]{1,0:T(8,128)(2,1)S(1)}, u32[]{:S(2)}, u32[]{:S(2)}) collective-permute-start(bf16[1024,256]{1,0:T(8,128)(2,1)S(1)} %collective-permute-done.4), channel_id=1, source_target_pairs={{0,4},{4,8},{8,12},{12,16},{16,20},{20,24},{24,28},{28,32},{32,36}... | collective-permute-start | bytes 1572872 | tf_op jit(solution)/shard_map/stream_1_step_3/ppermute | solution.py:191
  45.8 3.9 %collective-permute-done.11.refs_7_ = bf16[1024,256]{1,0:T(8,128)(2,1)S(1)} collective-permute-done((bf16[1024,256]{1,0:T(8,128)(2,1)S(1)}, bf16[1024,256]{1,0:T(8,128)(2,1)S(1)}, u32[]{:S(2)}, u32[]{:S(2)}) %collective-permute-start.11) | collective-permute-done | bytes 524320 | tf_op jit(solution)/shard_map/stream_0_step_3/ppermute | solution.py:191
  49.7 3.1 %collective-permute-start.12 = (bf16[1024,256]{1,0:T(8,128)(2,1)S(1)}, bf16[1024,256]{1,0:T(8,128)(2,1)S(1)}, u32[]{:S(2)}, u32[]{:S(2)}) collective-permute-start(bf16[1024,256]{1,0:T(8,128)(2,1)S(1)} %collective-permute-done.11.refs_7_), channel_id=1, source_target_pairs={{0,4},{4,8},{8,12},{12,16},{16,20},{20,24},{24,28},{28,32},{32,36}... | collective-permute-start | bytes 1572872 | tf_op jit(solution)/shard_map/stream_0_step_4/ppermute | solution.py:191
  52.8 1.9 %collective-permute-start.18 = (bf16[1024,256]{1,0:T(8,128)(2,1)S(1)}, bf16[1024,256]{1,0:T(8,128)(2,1)S(1)}, u32[]{:S(2)}, u32[]{:S(2)}) collective-permute-start(bf16[1024,256]{1,0:T(8,128)(2,1)S(1)} %collective-permute-done.4), channel_id=1, source_target_pairs={{0,64},{64,0},{1,65},{65,1},{2,66},{66,2},{3,67},{67,3},{4,68},{68... | collective-permute-start | bytes 1572872 | tf_op jit(solution)/shard_map/ppermute | solution.py:211
  54.8 0.0 collective-permute-done.6.refs_9_
  54.8 0.6 collective-permute-done.5
  55.3 2.8 %collective-permute-start.17 = (bf16[1024,256]{1,0:T(8,128)(2,1)S(1)}, bf16[1024,256]{1,0:T(8,128)(2,1)S(1)}, u32[]{:S(2)}, u32[]{:S(2)}) collective-permute-start(bf16[1024,256]{1,0:T(8,128)(2,1)S(1)} %collective-permute-done.5), channel_id=1, source_target_pairs={{0,4},{4,8},{8,12},{12,16},{16,20},{20,24},{24,28},{28,32},{32,36}... | collective-permute-start | bytes 1572872 | tf_op jit(solution)/shard_map/stream_1_step_4/ppermute | solution.py:191
  58.2 0.0 collective-permute-done.2.refs_1_
  58.2 2.8 %collective-permute-done.12.refs_8_ = bf16[1024,256]{1,0:T(8,128)(2,1)S(1)} collective-permute-done((bf16[1024,256]{1,0:T(8,128)(2,1)S(1)}, bf16[1024,256]{1,0:T(8,128)(2,1)S(1)}, u32[]{:S(2)}, u32[]{:S(2)}) %collective-permute-start.12) | collective-permute-done | bytes 524320 | tf_op jit(solution)/shard_map/stream_0_step_4/ppermute | solution.py:191
  60.9 3.0 %collective-permute-start.13 = (bf16[1024,256]{1,0:T(8,128)(2,1)S(1)}, bf16[1024,256]{1,0:T(8,128)(2,1)S(1)}, u32[]{:S(2)}, u32[]{:S(2)}) collective-permute-start(bf16[1024,256]{1,0:T(8,128)(2,1)S(1)} %collective-permute-done.12.refs_8_), channel_id=1, source_target_pairs={{0,4},{4,8},{8,12},{12,16},{16,20},{20,24},{24,28},{28,32},{32,36}... | collective-permute-start | bytes 1572872 | tf_op jit(solution)/shard_map/stream_0_step_5/ppermute | solution.py:191
  64.0 2.1 %collective-permute-start.20 = (bf16[1024,256]{1,0:T(8,128)(2,1)S(1)}, bf16[1024,256]{1,0:T(8,128)(2,1)S(1)}, u32[]{:S(2)}, u32[]{:S(2)}) collective-permute-start(bf16[1024,256]{1,0:T(8,128)(2,1)S(1)} %collective-permute-done.5), channel_id=1, source_target_pairs={{0,64},{64,0},{1,65},{65,1},{2,66},{66,2},{3,67},{67,3},{4,68},{68... | collective-permute-start | bytes 1572872 | tf_op jit(solution)/shard_map/ppermute | solution.py:211
  66.1 0.0 collective-permute-done.18.refs_8_
  66.1 0.4 collective-permute-done.17
  66.6 3.9 %collective-permute-start.19 = (bf16[1024,256]{1,0:T(8,128)(2,1)S(1)}, bf16[1024,256]{1,0:T(8,128)(2,1)S(1)}, u32[]{:S(2)}, u32[]{:S(2)}) collective-permute-start(bf16[1024,256]{1,0:T(8,128)(2,1)S(1)} %collective-permute-done.17), channel_id=1, source_target_pairs={{0,4},{4,8},{8,12},{12,16},{16,20},{20,24},{24,28},{28,32},{32,36}... | collective-permute-start | bytes 1572872 | tf_op jit(solution)/shard_map/stream_1_step_5/ppermute | solution.py:191
  70.5 1.9 %collective-permute-start.7 = (bf16[1024,512]{1,0:T(8,128)(2,1)S(1)}, bf16[1024,512]{1,0:T(8,128)(2,1)S(1)}, u32[]{:S(2)}, u32[]{:S(2)}) collective-permute-start(bf16[1024,512]{1,0:T(8,128)(2,1)S(1)} %collective-permute-done.2.refs_1_), channel_id=1, source_target_pairs={{0,64},{64,0},{1,65},{65,1},{2,66},{66,2},{3,67},{67,3},{4,68},{68... | collective-permute-start | bytes 3145736 | tf_op jit(solution)/shard_map/b_turn/ppermute | solution.py:209
  72.4 2.4 %collective-permute-start.22 = (bf16[1024,256]{1,0:T(8,128)(2,1)S(1)}, bf16[1024,256]{1,0:T(8,128)(2,1)S(1)}, u32[]{:S(2)}, u32[]{:S(2)}) collective-permute-start(bf16[1024,256]{1,0:T(8,128)(2,1)S(1)} %collective-permute-done.17), channel_id=1, source_target_pairs={{0,64},{64,0},{1,65},{65,1},{2,66},{66,2},{3,67},{67,3},{4,68},{68... | collective-permute-start | bytes 1572872 | tf_op jit(solution)/shard_map/ppermute | solution.py:211
  74.8 0.0 collective-permute-done.13.refs_9_
  74.8 4.2 %collective-permute-start.14 = (bf16[1024,256]{1,0:T(8,128)(2,1)S(1)}, bf16[1024,256]{1,0:T(8,128)(2,1)S(1)}, u32[]{:S(2)}, u32[]{:S(2)}) collective-permute-start(bf16[1024,256]{1,0:T(8,128)(2,1)S(1)} %collective-permute-done.13.refs_9_), channel_id=1, source_target_pairs={{0,4},{4,8},{8,12},{12,16},{16,20},{20,24},{24,28},{28,32},{32,36}... | collective-permute-start | bytes 1572872 | tf_op jit(solution)/shard_map/stream_0_step_6/ppermute | solution.py:191
  79.0 0.0 collective-permute-done.20.refs_7_
  79.0 0.0 collective-permute-done.19
  79.1 2.5 %collective-permute-start.21 = (bf16[1024,256]{1,0:T(8,128)(2,1)S(1)}, bf16[1024,256]{1,0:T(8,128)(2,1)S(1)}, u32[]{:S(2)}, u32[]{:S(2)}) collective-permute-start(bf16[1024,256]{1,0:T(8,128)(2,1)S(1)} %collective-permute-done.19), channel_id=1, source_target_pairs={{0,4},{4,8},{8,12},{12,16},{16,20},{20,24},{24,28},{28,32},{32,36}... | collective-permute-start | bytes 1572872 | tf_op jit(solution)/shard_map/stream_1_step_6/ppermute | solution.py:191
  81.6 4.1 %collective-permute-start.8 = (bf16[1024,512]{1,0:T(8,128)(2,1)S(1)}, bf16[1024,512]{1,0:T(8,128)(2,1)S(1)}, u32[]{:S(2)}, u32[]{:S(2)}) collective-permute-start(bf16[1024,512]{1,0:T(8,128)(2,1)S(1)} %collective-permute-done.2.refs_1_), channel_id=1, source_target_pairs={{0,128},{64,448},{128,256},{192,64},{256,384},{320,192},{384,0},{4... | collective-permute-start | bytes 3145736 | tf_op jit(solution)/shard_map/b_far/ppermute | solution.py:206
  85.7 0.0 collective-permute-done.14.refs_10_
  85.7 4.4 %collective-permute-start.15 = (bf16[1024,256]{1,0:T(8,128)(2,1)S(1)}, bf16[1024,256]{1,0:T(8,128)(2,1)S(1)}, u32[]{:S(2)}, u32[]{:S(2)}) collective-permute-start(bf16[1024,256]{1,0:T(8,128)(2,1)S(1)} %collective-permute-done.14.refs_10_), channel_id=1, source_target_pairs={{0,4},{4,8},{8,12},{12,16},{16,20},{20,24},{24,28},{28,32},{32,36}... | collective-permute-start | bytes 1572872 | tf_op jit(solution)/shard_map/stream_0_step_7/ppermute | solution.py:191
  90.2 0.0 collective-permute-done.22.refs_6_
  90.2 0.6 collective-permute-done.21
  90.8 5.3 %collective-permute-start.23 = (bf16[1024,256]{1,0:T(8,128)(2,1)S(1)}, bf16[1024,256]{1,0:T(8,128)(2,1)S(1)}, u32[]{:S(2)}, u32[]{:S(2)}) collective-permute-start(bf16[1024,256]{1,0:T(8,128)(2,1)S(1)} %collective-permute-done.21), channel_id=1, source_target_pairs={{0,4},{4,8},{8,12},{12,16},{16,20},{20,24},{24,28},{28,32},{32,36}... | collective-permute-start | bytes 1572872 | tf_op jit(solution)/shard_map/stream_1_step_7/ppermute | solution.py:191
  96.1 1.9 %collective-permute-start.26 = (bf16[1024,256]{1,0:T(8,128)(2,1)S(1)}, bf16[1024,256]{1,0:T(8,128)(2,1)S(1)}, u32[]{:S(2)}, u32[]{:S(2)}) collective-permute-start(bf16[1024,256]{1,0:T(8,128)(2,1)S(1)} %collective-permute-done.19), channel_id=1, source_target_pairs={{0,64},{64,0},{1,65},{65,1},{2,66},{66,2},{3,67},{67,3},{4,68},{68... | collective-permute-start | bytes 1572872 | tf_op jit(solution)/shard_map/ppermute | solution.py:211
  98.0 0.0 collective-permute-done.7.refs_2_
  98.0 2.4 %collective-permute-start.25 = (bf16[1024,256]{1,0:T(8,128)(2,1)S(1)}, bf16[1024,256]{1,0:T(8,128)(2,1)S(1)}, u32[]{:S(2)}, u32[]{:S(2)}) collective-permute-start(bf16[1024,256]{1,0:T(8,128)(2,1)S(1)} %collective-permute-done.21), channel_id=1, source_target_pairs={{0,64},{64,0},{1,65},{65,1},{2,66},{66,2},{3,67},{67,3},{4,68},{68... | collective-permute-start | bytes 1572872 | tf_op jit(solution)/shard_map/ppermute | solution.py:211
  100.4 0.0 collective-permute-done.15.refs_4_
  100.4 3.1 %collective-permute-start.16 = (bf16[1024,256]{1,0:T(8,128)(2,1)S(1)}, bf16[1024,256]{1,0:T(8,128)(2,1)S(1)}, u32[]{:S(2)}, u32[]{:S(2)}) collective-permute-start(bf16[1024,256]{1,0:T(8,128)(2,1)S(1)} %collective-permute-done.15.refs_4_), channel_id=1, source_target_pairs={{0,4},{4,8},{8,12},{12,16},{16,20},{20,24},{24,28},{28,32},{32,36}... | collective-permute-start | bytes 1572872 | tf_op jit(solution)/shard_map/stream_0_step_8/ppermute | solution.py:191
  103.6 0.0 collective-permute-done.23
  103.6 3.5 %collective-permute-start.24 = (bf16[1024,256]{1,0:T(8,128)(2,1)S(1)}, bf16[1024,256]{1,0:T(8,128)(2,1)S(1)}, u32[]{:S(2)}, u32[]{:S(2)}) collective-permute-start(bf16[1024,256]{1,0:T(8,128)(2,1)S(1)} %collective-permute-done.23), channel_id=1, source_target_pairs={{0,64},{64,0},{1,65},{65,1},{2,66},{66,2},{3,67},{67,3},{4,68},{68... | collective-permute-start | bytes 1572872 | tf_op jit(solution)/shard_map/ppermute | solution.py:212
  107.1 0.0 collective-permute-done.8.refs_3_
  107.2 2.7 %shard_map.75.refs_7_ = f32[1024,512]{1,0:T(8,128)S(1)} custom-call(bf16[1024,512]{1,0:T(8,128)(2,1)S(1)} %pad_maximum_fusion.refs_0_, bf16[1024,512]{1,0:T(8,128)(2,1)S(1)} %collective-permute-done.2.refs_1_, bf16[1024,512]{1,0:T(8,128)(2,1)S(1)} %collective-permute-done.7.refs_2_, bf16[1024,512]{1,0:T(8,128)(2,1)S(1)} %collective-permute-done.8.refs_3_, ...), custom_call_target="tpu_custom_call" | custom-call | flops 1879048192 | bytes 2097152 | tf_op jit(solution)/shard_map/pallas_call | solution.py:156
  109.8 0.0 collective-permute-done.26.refs_5_
  109.8 0.0 collective-permute-done.25.refs_4_
  109.8 2.4 %shard_map.76.refs_8_ = f32[1024,512]{1,0:T(8,128)S(1)} custom-call(bf16[1024,512]{1,0:T(8,128)(2,1)S(1)} %pad_maximum_fusion.refs_0_, bf16[1024,512]{1,0:T(8,128)(2,1)S(1)} %collective-permute-done.2.refs_1_, bf16[1024,512]{1,0:T(8,128)(2,1)S(1)} %collective-permute-done.7.refs_2_, bf16[1024,512]{1,0:T(8,128)(2,1)S(1)} %collective-permute-done.8.refs_3_, ...), custom_call_target="tpu_custom_call" | custom-call | flops 1610612736 | bytes 2097152 | tf_op jit(solution)/shard_map/pallas_call | solution.py:156
  112.2 0.0 collective-permute-done.16.refs_5_
  112.2 0.0 collective-permute-done.24.refs_6_
  112.2 1.9 %shard_map.77 = f32[4,272,512]{2,1,0:T(8,128)S(1)} custom-call(bf16[1024,512]{1,0:T(8,128)(2,1)S(1)} %pad_maximum_fusion.refs_0_, bf16[1024,512]{1,0:T(8,128)(2,1)S(1)} %collective-permute-done.2.refs_1_, bf16[1024,512]{1,0:T(8,128)(2,1)S(1)} %collective-permute-done.7.refs_2_, bf16[1024,512]{1,0:T(8,128)(2,1)S(1)} %collective-permute-done.8.refs_3_, ...), custom_call_target="tpu_custom_call" | custom-call | flops 805306368 | bytes 2097152 | tf_op jit(solution)/shard_map/pallas_call | solution.py:156
  114.2 0.3 convert_element_type.9
  114.4 19.1 %all_to_all.5 = f16[4,272,512]{2,1,0:T(8,128)(2,1)S(1)} all-to-all(f16[4,272,512]{2,1,0:T(8,128)(2,1)S(1)} %convert_element_type.9), channel_id=1, replica_groups=mesh['y'=4,'core'=2,'col'=16,'layer'=4] {'layer'}, dimensions={0} | all-to-all | bytes 2228224 | tf_op jit(solution)/shard_map/all_to_all | solution.py:220
  133.5 0.1 convert_reduce_fusion
  133.6 1.1 multiply_reduce_fusion
  (3 shorter events, 0.0 us)
Async XLA Ops:
  2.0 105.1 %copy-start = (bf16[1024,256]{1,0:T(8,128)(2,1)S(1)}, bf16[1024,256]{1,0:T(8,128)(2,1)}, u32[]{:S(2)}) copy-start(bf16[1024,256]{1,0:T(8,128)(2,1)} %shard_map.73.refs_4_) | copy-start | bytes 1572868
  2.1 14.7 %collective-permute-start = (bf16[1024,256]{1,0:T(8,128)(2,1)}, bf16[1024,256]{1,0:T(8,128)(2,1)S(1)}, u32[]{:S(2)}, u32[]{:S(2)}) collective-permute-start(bf16[1024,256]{1,0:T(8,128)(2,1)} %shard_map.73.refs_4_), channel_id=1, source_target_pairs={{0,64},{64,0},{1,65},{65,1},{2,66},{66,2},{3,67},{67,3},{4,68},{68... | collective-permute-start | bytes 1572872 | tf_op jit(solution)/shard_map/ppermute | solution.py:152
  11.0 12.4 %collective-permute-start.9 = (bf16[1024,256]{1,0:T(8,128)(2,1)}, bf16[1024,256]{1,0:T(8,128)(2,1)S(1)}, u32[]{:S(2)}, u32[]{:S(2)}) collective-permute-start(bf16[1024,256]{1,0:T(8,128)(2,1)} %shard_map.73.refs_4_), channel_id=1, source_target_pairs={{0,4},{4,8},{8,12},{12,16},{16,20},{20,24},{24,28},{28,32},{32,36}... | collective-permute-start | bytes 1572872 | tf_op jit(solution)/shard_map/stream_0_step_1/ppermute | solution.py:191
  16.8 11.9 %collective-permute-start.3 = (bf16[1024,256]{1,0:T(8,128)(2,1)S(1)}, bf16[1024,256]{1,0:T(8,128)(2,1)S(1)}, u32[]{:S(2)}, u32[]{:S(2)}) collective-permute-start(bf16[1024,256]{1,0:T(8,128)(2,1)S(1)} %collective-permute-done), channel_id=1, source_target_pairs={{0,4},{4,8},{8,12},{12,16},{16,20},{20,24},{24,28},{28,32},{32,36}... | collective-permute-start | bytes 1572872 | tf_op jit(solution)/shard_map/stream_1_step_1/ppermute | solution.py:191
  21.4 12.3 %collective-permute-start.1 = (bf16[512,512]{1,0:T(8,128)(2,1)}, bf16[512,512]{1,0:T(8,128)(2,1)S(1)}, u32[]{:S(2)}, u32[]{:S(2)}) collective-permute-start(bf16[512,512]{1,0:T(8,128)(2,1)} %shard_map.74), channel_id=1, source_target_pairs={{0,64},{64,0},{1,65},{65,1},{2,66},{66,2},{3,67},{67,3},{4,68},{68... | collective-permute-start | bytes 1572872 | tf_op jit(solution)/shard_map/b_swap/ppermute | solution.py:199
  23.4 16.1 %collective-permute-start.10 = (bf16[1024,256]{1,0:T(8,128)(2,1)S(1)}, bf16[1024,256]{1,0:T(8,128)(2,1)S(1)}, u32[]{:S(2)}, u32[]{:S(2)}) collective-permute-start(bf16[1024,256]{1,0:T(8,128)(2,1)S(1)} %collective-permute-done.9.refs_5_), channel_id=1, source_target_pairs={{0,4},{4,8},{8,12},{12,16},{16,20},{20,24},{24,28},{28,32},{32,36}... | collective-permute-start | bytes 1572872 | tf_op jit(solution)/shard_map/stream_0_step_2/ppermute | solution.py:191
  28.7 14.7 %collective-permute-start.4 = (bf16[1024,256]{1,0:T(8,128)(2,1)S(1)}, bf16[1024,256]{1,0:T(8,128)(2,1)S(1)}, u32[]{:S(2)}, u32[]{:S(2)}) collective-permute-start(bf16[1024,256]{1,0:T(8,128)(2,1)S(1)} %collective-permute-done.3), channel_id=1, source_target_pairs={{0,4},{4,8},{8,12},{12,16},{16,20},{20,24},{24,28},{28,32},{32,36}... | collective-permute-start | bytes 1572872 | tf_op jit(solution)/shard_map/stream_1_step_2/ppermute | solution.py:191
  34.8 23.3 %collective-permute-start.2 = (bf16[1024,512]{1,0:T(8,128)(2,1)S(1)}, bf16[1024,512]{1,0:T(8,128)(2,1)S(1)}, u32[]{:S(2)}, u32[]{:S(2)}) collective-permute-start(bf16[1024,512]{1,0:T(8,128)(2,1)S(1)} %pad_maximum_fusion.refs_0_), channel_id=1, source_target_pairs={{0,128},{64,448},{128,256},{192,64},{256,384},{320,192},{384,0},{4... | collective-permute-start | bytes 3145736 | tf_op jit(solution)/shard_map/b_near/ppermute | solution.py:203
  39.5 10.2 %collective-permute-start.11 = (bf16[1024,256]{1,0:T(8,128)(2,1)S(1)}, bf16[1024,256]{1,0:T(8,128)(2,1)S(1)}, u32[]{:S(2)}, u32[]{:S(2)}) collective-permute-start(bf16[1024,256]{1,0:T(8,128)(2,1)S(1)} %collective-permute-done.10.refs_6_), channel_id=1, source_target_pairs={{0,4},{4,8},{8,12},{12,16},{16,20},{20,24},{24,28},{28,32},{32,36}... | collective-permute-start | bytes 1572872 | tf_op jit(solution)/shard_map/stream_0_step_3/ppermute | solution.py:191
  41.4 13.4 %collective-permute-start.6 = (bf16[1024,256]{1,0:T(8,128)(2,1)S(1)}, bf16[1024,256]{1,0:T(8,128)(2,1)S(1)}, u32[]{:S(2)}, u32[]{:S(2)}) collective-permute-start(bf16[1024,256]{1,0:T(8,128)(2,1)S(1)} %collective-permute-done.3), channel_id=1, source_target_pairs={{0,64},{64,0},{1,65},{65,1},{2,66},{66,2},{3,67},{67,3},{4,68},{68... | collective-permute-start | bytes 1572872 | tf_op jit(solution)/shard_map/ppermute | solution.py:211
  43.3 12.0 %collective-permute-start.5 = (bf16[1024,256]{1,0:T(8,128)(2,1)S(1)}, bf16[1024,256]{1,0:T(8,128)(2,1)S(1)}, u32[]{:S(2)}, u32[]{:S(2)}) collective-permute-start(bf16[1024,256]{1,0:T(8,128)(2,1)S(1)} %collective-permute-done.4), channel_id=1, source_target_pairs={{0,4},{4,8},{8,12},{12,16},{16,20},{20,24},{24,28},{28,32},{32,36}... | collective-permute-start | bytes 1572872 | tf_op jit(solution)/shard_map/stream_1_step_3/ppermute | solution.py:191
  49.7 11.2 %collective-permute-start.12 = (bf16[1024,256]{1,0:T(8,128)(2,1)S(1)}, bf16[1024,256]{1,0:T(8,128)(2,1)S(1)}, u32[]{:S(2)}, u32[]{:S(2)}) collective-permute-start(bf16[1024,256]{1,0:T(8,128)(2,1)S(1)} %collective-permute-done.11.refs_7_), channel_id=1, source_target_pairs={{0,4},{4,8},{8,12},{12,16},{16,20},{20,24},{24,28},{28,32},{32,36}... | collective-permute-start | bytes 1572872 | tf_op jit(solution)/shard_map/stream_0_step_4/ppermute | solution.py:191
  52.8 13.3 %collective-permute-start.18 = (bf16[1024,256]{1,0:T(8,128)(2,1)S(1)}, bf16[1024,256]{1,0:T(8,128)(2,1)S(1)}, u32[]{:S(2)}, u32[]{:S(2)}) collective-permute-start(bf16[1024,256]{1,0:T(8,128)(2,1)S(1)} %collective-permute-done.4), channel_id=1, source_target_pairs={{0,64},{64,0},{1,65},{65,1},{2,66},{66,2},{3,67},{67,3},{4,68},{68... | collective-permute-start | bytes 1572872 | tf_op jit(solution)/shard_map/ppermute | solution.py:211
  55.3 11.2 %collective-permute-start.17 = (bf16[1024,256]{1,0:T(8,128)(2,1)S(1)}, bf16[1024,256]{1,0:T(8,128)(2,1)S(1)}, u32[]{:S(2)}, u32[]{:S(2)}) collective-permute-start(bf16[1024,256]{1,0:T(8,128)(2,1)S(1)} %collective-permute-done.5), channel_id=1, source_target_pairs={{0,4},{4,8},{8,12},{12,16},{16,20},{20,24},{24,28},{28,32},{32,36}... | collective-permute-start | bytes 1572872 | tf_op jit(solution)/shard_map/stream_1_step_4/ppermute | solution.py:191
  60.9 13.9 %collective-permute-start.13 = (bf16[1024,256]{1,0:T(8,128)(2,1)S(1)}, bf16[1024,256]{1,0:T(8,128)(2,1)S(1)}, u32[]{:S(2)}, u32[]{:S(2)}) collective-permute-start(bf16[1024,256]{1,0:T(8,128)(2,1)S(1)} %collective-permute-done.12.refs_8_), channel_id=1, source_target_pairs={{0,4},{4,8},{8,12},{12,16},{16,20},{20,24},{24,28},{28,32},{32,36}... | collective-permute-start | bytes 1572872 | tf_op jit(solution)/shard_map/stream_0_step_5/ppermute | solution.py:191
  64.0 15.1 %collective-permute-start.20 = (bf16[1024,256]{1,0:T(8,128)(2,1)S(1)}, bf16[1024,256]{1,0:T(8,128)(2,1)S(1)}, u32[]{:S(2)}, u32[]{:S(2)}) collective-permute-start(bf16[1024,256]{1,0:T(8,128)(2,1)S(1)} %collective-permute-done.5), channel_id=1, source_target_pairs={{0,64},{64,0},{1,65},{65,1},{2,66},{66,2},{3,67},{67,3},{4,68},{68... | collective-permute-start | bytes 1572872 | tf_op jit(solution)/shard_map/ppermute | solution.py:211
  66.6 12.5 %collective-permute-start.19 = (bf16[1024,256]{1,0:T(8,128)(2,1)S(1)}, bf16[1024,256]{1,0:T(8,128)(2,1)S(1)}, u32[]{:S(2)}, u32[]{:S(2)}) collective-permute-start(bf16[1024,256]{1,0:T(8,128)(2,1)S(1)} %collective-permute-done.17), channel_id=1, source_target_pairs={{0,4},{4,8},{8,12},{12,16},{16,20},{20,24},{24,28},{28,32},{32,36}... | collective-permute-start | bytes 1572872 | tf_op jit(solution)/shard_map/stream_1_step_5/ppermute | solution.py:191
  70.5 27.5 %collective-permute-start.7 = (bf16[1024,512]{1,0:T(8,128)(2,1)S(1)}, bf16[1024,512]{1,0:T(8,128)(2,1)S(1)}, u32[]{:S(2)}, u32[]{:S(2)}) collective-permute-start(bf16[1024,512]{1,0:T(8,128)(2,1)S(1)} %collective-permute-done.2.refs_1_), channel_id=1, source_target_pairs={{0,64},{64,0},{1,65},{65,1},{2,66},{66,2},{3,67},{67,3},{4,68},{68... | collective-permute-start | bytes 3145736 | tf_op jit(solution)/shard_map/b_turn/ppermute | solution.py:209
  72.4 17.8 %collective-permute-start.22 = (bf16[1024,256]{1,0:T(8,128)(2,1)S(1)}, bf16[1024,256]{1,0:T(8,128)(2,1)S(1)}, u32[]{:S(2)}, u32[]{:S(2)}) collective-permute-start(bf16[1024,256]{1,0:T(8,128)(2,1)S(1)} %collective-permute-done.17), channel_id=1, source_target_pairs={{0,64},{64,0},{1,65},{65,1},{2,66},{66,2},{3,67},{67,3},{4,68},{68... | collective-permute-start | bytes 1572872 | tf_op jit(solution)/shard_map/ppermute | solution.py:211
  74.8 10.9 %collective-permute-start.14 = (bf16[1024,256]{1,0:T(8,128)(2,1)S(1)}, bf16[1024,256]{1,0:T(8,128)(2,1)S(1)}, u32[]{:S(2)}, u32[]{:S(2)}) collective-permute-start(bf16[1024,256]{1,0:T(8,128)(2,1)S(1)} %collective-permute-done.13.refs_9_), channel_id=1, source_target_pairs={{0,4},{4,8},{8,12},{12,16},{16,20},{20,24},{24,28},{28,32},{32,36}... | collective-permute-start | bytes 1572872 | tf_op jit(solution)/shard_map/stream_0_step_6/ppermute | solution.py:191
  79.1 11.7 %collective-permute-start.21 = (bf16[1024,256]{1,0:T(8,128)(2,1)S(1)}, bf16[1024,256]{1,0:T(8,128)(2,1)S(1)}, u32[]{:S(2)}, u32[]{:S(2)}) collective-permute-start(bf16[1024,256]{1,0:T(8,128)(2,1)S(1)} %collective-permute-done.19), channel_id=1, source_target_pairs={{0,4},{4,8},{8,12},{12,16},{16,20},{20,24},{24,28},{28,32},{32,36}... | collective-permute-start | bytes 1572872 | tf_op jit(solution)/shard_map/stream_1_step_6/ppermute | solution.py:191
  81.6 25.5 %collective-permute-start.8 = (bf16[1024,512]{1,0:T(8,128)(2,1)S(1)}, bf16[1024,512]{1,0:T(8,128)(2,1)S(1)}, u32[]{:S(2)}, u32[]{:S(2)}) collective-permute-start(bf16[1024,512]{1,0:T(8,128)(2,1)S(1)} %collective-permute-done.2.refs_1_), channel_id=1, source_target_pairs={{0,128},{64,448},{128,256},{192,64},{256,384},{320,192},{384,0},{4... | collective-permute-start | bytes 3145736 | tf_op jit(solution)/shard_map/b_far/ppermute | solution.py:206
  85.7 14.7 %collective-permute-start.15 = (bf16[1024,256]{1,0:T(8,128)(2,1)S(1)}, bf16[1024,256]{1,0:T(8,128)(2,1)S(1)}, u32[]{:S(2)}, u32[]{:S(2)}) collective-permute-start(bf16[1024,256]{1,0:T(8,128)(2,1)S(1)} %collective-permute-done.14.refs_10_), channel_id=1, source_target_pairs={{0,4},{4,8},{8,12},{12,16},{16,20},{20,24},{24,28},{28,32},{32,36}... | collective-permute-start | bytes 1572872 | tf_op jit(solution)/shard_map/stream_0_step_7/ppermute | solution.py:191
  90.8 12.8 %collective-permute-start.23 = (bf16[1024,256]{1,0:T(8,128)(2,1)S(1)}, bf16[1024,256]{1,0:T(8,128)(2,1)S(1)}, u32[]{:S(2)}, u32[]{:S(2)}) collective-permute-start(bf16[1024,256]{1,0:T(8,128)(2,1)S(1)} %collective-permute-done.21), channel_id=1, source_target_pairs={{0,4},{4,8},{8,12},{12,16},{16,20},{20,24},{24,28},{28,32},{32,36}... | collective-permute-start | bytes 1572872 | tf_op jit(solution)/shard_map/stream_1_step_7/ppermute | solution.py:191
  96.1 13.7 %collective-permute-start.26 = (bf16[1024,256]{1,0:T(8,128)(2,1)S(1)}, bf16[1024,256]{1,0:T(8,128)(2,1)S(1)}, u32[]{:S(2)}, u32[]{:S(2)}) collective-permute-start(bf16[1024,256]{1,0:T(8,128)(2,1)S(1)} %collective-permute-done.19), channel_id=1, source_target_pairs={{0,64},{64,0},{1,65},{65,1},{2,66},{66,2},{3,67},{67,3},{4,68},{68... | collective-permute-start | bytes 1572872 | tf_op jit(solution)/shard_map/ppermute | solution.py:211
  98.0 11.8 %collective-permute-start.25 = (bf16[1024,256]{1,0:T(8,128)(2,1)S(1)}, bf16[1024,256]{1,0:T(8,128)(2,1)S(1)}, u32[]{:S(2)}, u32[]{:S(2)}) collective-permute-start(bf16[1024,256]{1,0:T(8,128)(2,1)S(1)} %collective-permute-done.21), channel_id=1, source_target_pairs={{0,64},{64,0},{1,65},{65,1},{2,66},{66,2},{3,67},{67,3},{4,68},{68... | collective-permute-start | bytes 1572872 | tf_op jit(solution)/shard_map/ppermute | solution.py:211
  100.4 11.8 %collective-permute-start.16 = (bf16[1024,256]{1,0:T(8,128)(2,1)S(1)}, bf16[1024,256]{1,0:T(8,128)(2,1)S(1)}, u32[]{:S(2)}, u32[]{:S(2)}) collective-permute-start(bf16[1024,256]{1,0:T(8,128)(2,1)S(1)} %collective-permute-done.15.refs_4_), channel_id=1, source_target_pairs={{0,4},{4,8},{8,12},{12,16},{16,20},{20,24},{24,28},{28,32},{32,36}... | collective-permute-start | bytes 1572872 | tf_op jit(solution)/shard_map/stream_0_step_8/ppermute | solution.py:191
  103.6 8.6 %collective-permute-start.24 = (bf16[1024,256]{1,0:T(8,128)(2,1)S(1)}, bf16[1024,256]{1,0:T(8,128)(2,1)S(1)}, u32[]{:S(2)}, u32[]{:S(2)}) collective-permute-start(bf16[1024,256]{1,0:T(8,128)(2,1)S(1)} %collective-permute-done.23), channel_id=1, source_target_pairs={{0,64},{64,0},{1,65},{65,1},{2,66},{66,2},{3,67},{67,3},{4,68},{68... | collective-permute-start | bytes 1572872 | tf_op jit(solution)/shard_map/ppermute | solution.py:212

commit v9 on v8

--- a/solution.py
+++ b/solution.py
@@ -112,7 +112,8 @@
         if len(out_ref.shape) == 2:
             out_ref[rows, :] = total
         else:
-            encode(total, out_ref.at[tile])
+            owners = out_ref.shape[0]
+            encode(total, out_ref.at[lax.rem(tile - lax.axis_index("layer") + owners, owners)])
 
 
 def encode(total, out_ref):
@@ -216,8 +217,13 @@
     across = product(range(last + 2, cols), shards[last + 2 :])
     steps = range(last - 1, last + 2)
     parts = product(steps, [shards[s] for s in steps], (near, across), True)
-    parts = parts.astype(jnp.float16)
-    return decoded(lax.all_to_all(parts, "layer", 0, 0)).sum(axis=0)
+    layers = sizes["layer"]
+    total = decoded(parts[:1])[0]
+    for d in (2, 1, 3):
+        pairs = [(i, (i + d) % layers) for i in range(layers)]
+        part = lax.ppermute(parts[d : d + 1].astype(jnp.float16), "layer", pairs)
+        total = total + decoded(part)[0]
+    return total
 
 
 def solution(mesh):

time: 136 us -> 159 us (1.17)
  between operations: 0.45 us -> 26.5 us
  blocking collectives: 19.1 us -> 0 us
  starting transfers between devices: 92.7 us -> 104 us
  other arithmetic: 2.63 us -> 7.15 us
    all_to_all x1 -> x0, blocking collectives: 19.1 us -> none  [on_device(): return decoded(lax.all_to_all(parts, 'layer', 0, 0)).sum(axis=0)]
    ppermute x0 -> x3, starting transfers between devices: none -> 11.2 us  [on_device(): part = lax.ppermute(parts[d:d + 1].astype(jnp.float16), 'layer', pairs)]
    reduce_max x1 -> x4, other arithmetic: 0.12 us -> 3.78 us  [decoded(): code = parts[:, BS:, :1].astype(jnp.float32).max(axis=1, keepdims=True)]
    add x0 -> x1, other arithmetic: none -> 2 us  [on_device(): total = total + decoded(part)[0]]
  transfers between devices with their start and end apart: 27 -> 30, of which waited for: 6 -> 6; matrix products, arithmetic and copies ran while one was open for 1% -> 2% of each run, Pallas kernels for 5% -> 4%
where the time goes in v9:
time: 159 us; the launch traced here: 158 us
  starting transfers between devices  104 us (65%)
  between operations  26.5 us (17%)
  Pallas kernels  11 us (7%)
  waiting for transfers between devices  8.93 us (6%)
  other arithmetic  7.15 us (4%)
    ppermute x15, starting transfers between devices, on_device(): held[j].append(lax.ppermute(sent, ('core', 'col'), ring))  54.9 us
    ppermute x6, starting transfers between devices, on_device(): turned.append(lax.ppermute(held[1][step - 1], 'core', SWAP))  12.7 us
    ppermute x3, starting transfers between devices, on_device(): part = lax.ppermute(parts[d:d + 1].astype(jnp.float16), 'layer', pairs)  11.2 us
    ppermute x1, starting transfers between devices, on_device(): held = [[own], [lax.ppermute(own, 'core', SWAP)]]  8.92 us
    ppermute x15, waiting for transfers between devices, on_device(): held[j].append(lax.ppermute(sent, ('core', 'col'), ring))  8.89 us
    pallas_call x3, Pallas kernels, product(): pl.pallas_call(functools.partial(product_kernel, steps, cols, len(adds)),...  6.92 us
    ppermute x1, starting transfers between devices, on_device(): b_all[1] = lax.ppermute(b_all[0], ('y', 'core'), near_by)  4.64 us
    ppermute x1, starting transfers between devices, on_device(): b_all[3] = lax.ppermute(b_all[1], ('y', 'core'), near_by)  4.1 us
  transfers between devices with their start and end apart: 30, of which 6 were waited for; matrix products, arithmetic and copies ran while one was open for 2% of the time, Pallas kernels for 4%

profile of v9, /device:TPU:1, one launch (start us, length us, event | category | flops | bytes accessed | tf_op | source)
XLA Modules:
  0.0 157.6 jit_solution(14168816189384218377)
XLA Ops:
  0.0 2.0 %shard_map.73.refs_4_ = bf16[1024,256]{1,0:T(8,128)(2,1)} custom-call(s32[4]{0:T(128)} %bitcast.3, s32[4]{0:T(128)} %refs_1_.1, s32[1,16]{1,0:T(1,128)} %refs_1_.2, bf16[1,1024,256]{2,1,0:T(8,128)(2,1)} %refs_3_.2), custom_call_target="tpu_custom_call" | custom-call | tf_op jit(solution)/shard_map/pallas_call | solution.py:60
  2.0 8.9 %collective-permute-start = (bf16[1024,256]{1,0:T(8,128)(2,1)}, bf16[1024,256]{1,0:T(8,128)(2,1)S(1)}, u32[]{:S(2)}, u32[]{:S(2)}) collective-permute-start(bf16[1024,256]{1,0:T(8,128)(2,1)} %shard_map.73.refs_4_), channel_id=1, source_target_pairs={{0,64},{64,0},{1,65},{65,1},{2,66},{66,2},{3,67},{67,3},{4,68},{68... | collective-permute-start | bytes 1572872 | tf_op jit(solution)/shard_map/ppermute | solution.py:153
  11.0 5.7 %collective-permute-start.9 = (bf16[1024,256]{1,0:T(8,128)(2,1)}, bf16[1024,256]{1,0:T(8,128)(2,1)S(1)}, u32[]{:S(2)}, u32[]{:S(2)}) collective-permute-start(bf16[1024,256]{1,0:T(8,128)(2,1)} %shard_map.73.refs_4_), channel_id=1, source_target_pairs={{0,4},{4,8},{8,12},{12,16},{16,20},{20,24},{24,28},{28,32},{32,36}... | collective-permute-start | bytes 1572872 | tf_op jit(solution)/shard_map/stream_0_step_1/ppermute | solution.py:192
  16.7 0.0 collective-permute-done
  16.7 2.6 %collective-permute-start.3 = (bf16[1024,256]{1,0:T(8,128)(2,1)S(1)}, bf16[1024,256]{1,0:T(8,128)(2,1)S(1)}, u32[]{:S(2)}, u32[]{:S(2)}) collective-permute-start(bf16[1024,256]{1,0:T(8,128)(2,1)S(1)} %collective-permute-done), channel_id=1, source_target_pairs={{0,4},{4,8},{8,12},{12,16},{16,20},{20,24},{24,28},{28,32},{32,36}... | collective-permute-start | bytes 1572872 | tf_op jit(solution)/shard_map/stream_1_step_1/ppermute | solution.py:192
  19.4 2.0 %shard_map.74 = bf16[512,512]{1,0:T(8,128)(2,1)} custom-call(s32[1,2,2]{2,1,0:T(2,128)} %refs_0_.1, s32[1,16]{1,0:T(1,128)} %refs_1_.2, s32[2]{0:T(128)} %refs_2_.3, bf16[1,512,512]{2,1,0:T(8,128)(2,1)} %refs_3_.3), custom_call_target="tpu_custom_call" | custom-call | tf_op jit(solution)/shard_map/pallas_call | solution.py:60
  21.4 1.9 %collective-permute-start.1 = (bf16[512,512]{1,0:T(8,128)(2,1)}, bf16[512,512]{1,0:T(8,128)(2,1)S(1)}, u32[]{:S(2)}, u32[]{:S(2)}) collective-permute-start(bf16[512,512]{1,0:T(8,128)(2,1)} %shard_map.74), channel_id=1, source_target_pairs={{0,64},{64,0},{1,65},{65,1},{2,66},{66,2},{3,67},{67,3},{4,68},{68... | collective-permute-start | bytes 1572872 | tf_op jit(solution)/shard_map/b_swap/ppermute | solution.py:200
  23.3 0.0 collective-permute-done.9.refs_5_
  23.4 4.7 %collective-permute-start.10 = (bf16[1024,256]{1,0:T(8,128)(2,1)S(1)}, bf16[1024,256]{1,0:T(8,128)(2,1)S(1)}, u32[]{:S(2)}, u32[]{:S(2)}) collective-permute-start(bf16[1024,256]{1,0:T(8,128)(2,1)S(1)} %collective-permute-done.9.refs_5_), channel_id=1, source_target_pairs={{0,4},{4,8},{8,12},{12,16},{16,20},{20,24},{24,28},{28,32},{32,36}... | collective-permute-start | bytes 1572872 | tf_op jit(solution)/shard_map/stream_0_step_2/ppermute | solution.py:192
  28.1 0.6 collective-permute-done.3
  28.7 5.0 %collective-permute-start.4 = (bf16[1024,256]{1,0:T(8,128)(2,1)S(1)}, bf16[1024,256]{1,0:T(8,128)(2,1)S(1)}, u32[]{:S(2)}, u32[]{:S(2)}) collective-permute-start(bf16[1024,256]{1,0:T(8,128)(2,1)S(1)} %collective-permute-done.3), channel_id=1, source_target_pairs={{0,4},{4,8},{8,12},{12,16},{16,20},{20,24},{24,28},{28,32},{32,36}... | collective-permute-start | bytes 1572872 | tf_op jit(solution)/shard_map/stream_1_step_2/ppermute | solution.py:192
  33.7 0.0 collective-permute-done.1
  33.7 1.1 pad_maximum_fusion.refs_0_
  34.8 4.6 %collective-permute-start.2 = (bf16[1024,512]{1,0:T(8,128)(2,1)S(1)}, bf16[1024,512]{1,0:T(8,128)(2,1)S(1)}, u32[]{:S(2)}, u32[]{:S(2)}) collective-permute-start(bf16[1024,512]{1,0:T(8,128)(2,1)S(1)} %pad_maximum_fusion.refs_0_), channel_id=1, source_target_pairs={{0,128},{64,448},{128,256},{192,64},{256,384},{320,192},{384,0},{4... | collective-permute-start | bytes 3145736 | tf_op jit(solution)/shard_map/b_near/ppermute | solution.py:204
  39.5 0.0 collective-permute-done.10.refs_6_
  39.5 1.9 %collective-permute-start.11 = (bf16[1024,256]{1,0:T(8,128)(2,1)S(1)}, bf16[1024,256]{1,0:T(8,128)(2,1)S(1)}, u32[]{:S(2)}, u32[]{:S(2)}) collective-permute-start(bf16[1024,256]{1,0:T(8,128)(2,1)S(1)} %collective-permute-done.10.refs_6_), channel_id=1, source_target_pairs={{0,4},{4,8},{8,12},{12,16},{16,20},{20,24},{24,28},{28,32},{32,36}... | collective-permute-start | bytes 1572872 | tf_op jit(solution)/shard_map/stream_0_step_3/ppermute | solution.py:192
  41.4 1.9 %collective-permute-start.6 = (bf16[1024,256]{1,0:T(8,128)(2,1)S(1)}, bf16[1024,256]{1,0:T(8,128)(2,1)S(1)}, u32[]{:S(2)}, u32[]{:S(2)}) collective-permute-start(bf16[1024,256]{1,0:T(8,128)(2,1)S(1)} %collective-permute-done.3), channel_id=1, source_target_pairs={{0,64},{64,0},{1,65},{65,1},{2,66},{66,2},{3,67},{67,3},{4,68},{68... | collective-permute-start | bytes 1572872 | tf_op jit(solution)/shard_map/ppermute | solution.py:212
  43.3 0.0 collective-permute-done.4
  43.3 2.4 %collective-permute-start.5 = (bf16[1024,256]{1,0:T(8,128)(2,1)S(1)}, bf16[1024,256]{1,0:T(8,128)(2,1)S(1)}, u32[]{:S(2)}, u32[]{:S(2)}) collective-permute-start(bf16[1024,256]{1,0:T(8,128)(2,1)S(1)} %collective-permute-done.4), channel_id=1, source_target_pairs={{0,4},{4,8},{8,12},{12,16},{16,20},{20,24},{24,28},{28,32},{32,36}... | collective-permute-start | bytes 1572872 | tf_op jit(solution)/shard_map/stream_1_step_3/ppermute | solution.py:192
  45.8 3.9 %collective-permute-done.11.refs_7_ = bf16[1024,256]{1,0:T(8,128)(2,1)S(1)} collective-permute-done((bf16[1024,256]{1,0:T(8,128)(2,1)S(1)}, bf16[1024,256]{1,0:T(8,128)(2,1)S(1)}, u32[]{:S(2)}, u32[]{:S(2)}) %collective-permute-start.11) | collective-permute-done | bytes 524320 | tf_op jit(solution)/shard_map/stream_0_step_3/ppermute | solution.py:192
  49.7 3.1 %collective-permute-start.12 = (bf16[1024,256]{1,0:T(8,128)(2,1)S(1)}, bf16[1024,256]{1,0:T(8,128)(2,1)S(1)}, u32[]{:S(2)}, u32[]{:S(2)}) collective-permute-start(bf16[1024,256]{1,0:T(8,128)(2,1)S(1)} %collective-permute-done.11.refs_7_), channel_id=1, source_target_pairs={{0,4},{4,8},{8,12},{12,16},{16,20},{20,24},{24,28},{28,32},{32,36}... | collective-permute-start | bytes 1572872 | tf_op jit(solution)/shard_map/stream_0_step_4/ppermute | solution.py:192
  52.8 1.9 %collective-permute-start.18 = (bf16[1024,256]{1,0:T(8,128)(2,1)S(1)}, bf16[1024,256]{1,0:T(8,128)(2,1)S(1)}, u32[]{:S(2)}, u32[]{:S(2)}) collective-permute-start(bf16[1024,256]{1,0:T(8,128)(2,1)S(1)} %collective-permute-done.4), channel_id=1, source_target_pairs={{0,64},{64,0},{1,65},{65,1},{2,66},{66,2},{3,67},{67,3},{4,68},{68... | collective-permute-start | bytes 1572872 | tf_op jit(solution)/shard_map/ppermute | solution.py:212
  54.8 0.6 collective-permute-done.5
  55.3 2.8 %collective-permute-start.17 = (bf16[1024,256]{1,0:T(8,128)(2,1)S(1)}, bf16[1024,256]{1,0:T(8,128)(2,1)S(1)}, u32[]{:S(2)}, u32[]{:S(2)}) collective-permute-start(bf16[1024,256]{1,0:T(8,128)(2,1)S(1)} %collective-permute-done.5), channel_id=1, source_target_pairs={{0,4},{4,8},{8,12},{12,16},{16,20},{20,24},{24,28},{28,32},{32,36}... | collective-permute-start | bytes 1572872 | tf_op jit(solution)/shard_map/stream_1_step_4/ppermute | solution.py:192
  58.1 2.8 %collective-permute-done.12.refs_8_ = bf16[1024,256]{1,0:T(8,128)(2,1)S(1)} collective-permute-done((bf16[1024,256]{1,0:T(8,128)(2,1)S(1)}, bf16[1024,256]{1,0:T(8,128)(2,1)S(1)}, u32[]{:S(2)}, u32[]{:S(2)}) %collective-permute-start.12) | collective-permute-done | bytes 524320 | tf_op jit(solution)/shard_map/stream_0_step_4/ppermute | solution.py:192
  60.9 3.0 %collective-permute-start.13 = (bf16[1024,256]{1,0:T(8,128)(2,1)S(1)}, bf16[1024,256]{1,0:T(8,128)(2,1)S(1)}, u32[]{:S(2)}, u32[]{:S(2)}) collective-permute-start(bf16[1024,256]{1,0:T(8,128)(2,1)S(1)} %collective-permute-done.12.refs_8_), channel_id=1, source_target_pairs={{0,4},{4,8},{8,12},{12,16},{16,20},{20,24},{24,28},{28,32},{32,36}... | collective-permute-start | bytes 1572872 | tf_op jit(solution)/shard_map/stream_0_step_5/ppermute | solution.py:192
  63.9 2.1 %collective-permute-start.20 = (bf16[1024,256]{1,0:T(8,128)(2,1)S(1)}, bf16[1024,256]{1,0:T(8,128)(2,1)S(1)}, u32[]{:S(2)}, u32[]{:S(2)}) collective-permute-start(bf16[1024,256]{1,0:T(8,128)(2,1)S(1)} %collective-permute-done.5), channel_id=1, source_target_pairs={{0,64},{64,0},{1,65},{65,1},{2,66},{66,2},{3,67},{67,3},{4,68},{68... | collective-permute-start | bytes 1572872 | tf_op jit(solution)/shard_map/ppermute | solution.py:212
  66.1 0.0 collective-permute-done.18.refs_8_
  66.1 0.4 collective-permute-done.17
  66.5 3.9 %collective-permute-start.19 = (bf16[1024,256]{1,0:T(8,128)(2,1)S(1)}, bf16[1024,256]{1,0:T(8,128)(2,1)S(1)}, u32[]{:S(2)}, u32[]{:S(2)}) collective-permute-start(bf16[1024,256]{1,0:T(8,128)(2,1)S(1)} %collective-permute-done.17), channel_id=1, source_target_pairs={{0,4},{4,8},{8,12},{12,16},{16,20},{20,24},{24,28},{28,32},{32,36}... | collective-permute-start | bytes 1572872 | tf_op jit(solution)/shard_map/stream_1_step_5/ppermute | solution.py:192
  70.4 1.9 %collective-permute-start.7 = (bf16[1024,512]{1,0:T(8,128)(2,1)S(1)}, bf16[1024,512]{1,0:T(8,128)(2,1)S(1)}, u32[]{:S(2)}, u32[]{:S(2)}) collective-permute-start(bf16[1024,512]{1,0:T(8,128)(2,1)S(1)} %collective-permute-done.2.refs_1_), channel_id=1, source_target_pairs={{0,64},{64,0},{1,65},{65,1},{2,66},{66,2},{3,67},{67,3},{4,68},{68... | collective-permute-start | bytes 3145736 | tf_op jit(solution)/shard_map/b_turn/ppermute | solution.py:210
  72.4 2.4 %collective-permute-start.22 = (bf16[1024,256]{1,0:T(8,128)(2,1)S(1)}, bf16[1024,256]{1,0:T(8,128)(2,1)S(1)}, u32[]{:S(2)}, u32[]{:S(2)}) collective-permute-start(bf16[1024,256]{1,0:T(8,128)(2,1)S(1)} %collective-permute-done.17), channel_id=1, source_target_pairs={{0,64},{64,0},{1,65},{65,1},{2,66},{66,2},{3,67},{67,3},{4,68},{68... | collective-permute-start | bytes 1572872 | tf_op jit(solution)/shard_map/ppermute | solution.py:212
  74.8 4.2 %collective-permute-start.14 = (bf16[1024,256]{1,0:T(8,128)(2,1)S(1)}, bf16[1024,256]{1,0:T(8,128)(2,1)S(1)}, u32[]{:S(2)}, u32[]{:S(2)}) collective-permute-start(bf16[1024,256]{1,0:T(8,128)(2,1)S(1)} %collective-permute-done.13.refs_9_), channel_id=1, source_target_pairs={{0,4},{4,8},{8,12},{12,16},{16,20},{20,24},{24,28},{28,32},{32,36}... | collective-permute-start | bytes 1572872 | tf_op jit(solution)/shard_map/stream_0_step_6/ppermute | solution.py:192
  79.0 0.0 collective-permute-done.19
  79.0 2.5 %collective-permute-start.21 = (bf16[1024,256]{1,0:T(8,128)(2,1)S(1)}, bf16[1024,256]{1,0:T(8,128)(2,1)S(1)}, u32[]{:S(2)}, u32[]{:S(2)}) collective-permute-start(bf16[1024,256]{1,0:T(8,128)(2,1)S(1)} %collective-permute-done.19), channel_id=1, source_target_pairs={{0,4},{4,8},{8,12},{12,16},{16,20},{20,24},{24,28},{28,32},{32,36}... | collective-permute-start | bytes 1572872 | tf_op jit(solution)/shard_map/stream_1_step_6/ppermute | solution.py:192
  81.6 4.1 %collective-permute-start.8 = (bf16[1024,512]{1,0:T(8,128)(2,1)S(1)}, bf16[1024,512]{1,0:T(8,128)(2,1)S(1)}, u32[]{:S(2)}, u32[]{:S(2)}) collective-permute-start(bf16[1024,512]{1,0:T(8,128)(2,1)S(1)} %collective-permute-done.2.refs_1_), channel_id=1, source_target_pairs={{0,128},{64,448},{128,256},{192,64},{256,384},{320,192},{384,0},{4... | collective-permute-start | bytes 3145736 | tf_op jit(solution)/shard_map/b_far/ppermute | solution.py:207
  85.7 0.0 collective-permute-done.14.refs_10_
  85.7 4.4 %collective-permute-start.15 = (bf16[1024,256]{1,0:T(8,128)(2,1)S(1)}, bf16[1024,256]{1,0:T(8,128)(2,1)S(1)}, u32[]{:S(2)}, u32[]{:S(2)}) collective-permute-start(bf16[1024,256]{1,0:T(8,128)(2,1)S(1)} %collective-permute-done.14.refs_10_), channel_id=1, source_target_pairs={{0,4},{4,8},{8,12},{12,16},{16,20},{20,24},{24,28},{28,32},{32,36}... | collective-permute-start | bytes 1572872 | tf_op jit(solution)/shard_map/stream_0_step_7/ppermute | solution.py:192
  90.2 0.6 collective-permute-done.21
  90.7 5.3 %collective-permute-start.23 = (bf16[1024,256]{1,0:T(8,128)(2,1)S(1)}, bf16[1024,256]{1,0:T(8,128)(2,1)S(1)}, u32[]{:S(2)}, u32[]{:S(2)}) collective-permute-start(bf16[1024,256]{1,0:T(8,128)(2,1)S(1)} %collective-permute-done.21), channel_id=1, source_target_pairs={{0,4},{4,8},{8,12},{12,16},{16,20},{20,24},{24,28},{28,32},{32,36}... | collective-permute-start | bytes 1572872 | tf_op jit(solution)/shard_map/stream_1_step_7/ppermute | solution.py:192
  96.1 1.9 %collective-permute-start.26 = (bf16[1024,256]{1,0:T(8,128)(2,1)S(1)}, bf16[1024,256]{1,0:T(8,128)(2,1)S(1)}, u32[]{:S(2)}, u32[]{:S(2)}) collective-permute-start(bf16[1024,256]{1,0:T(8,128)(2,1)S(1)} %collective-permute-done.19), channel_id=1, source_target_pairs={{0,64},{64,0},{1,65},{65,1},{2,66},{66,2},{3,67},{67,3},{4,68},{68... | collective-permute-start | bytes 1572872 | tf_op jit(solution)/shard_map/ppermute | solution.py:212
  98.0 0.0 collective-permute-done.7.refs_2_
  98.0 2.4 %collective-permute-start.25 = (bf16[1024,256]{1,0:T(8,128)(2,1)S(1)}, bf16[1024,256]{1,0:T(8,128)(2,1)S(1)}, u32[]{:S(2)}, u32[]{:S(2)}) collective-permute-start(bf16[1024,256]{1,0:T(8,128)(2,1)S(1)} %collective-permute-done.21), channel_id=1, source_target_pairs={{0,64},{64,0},{1,65},{65,1},{2,66},{66,2},{3,67},{67,3},{4,68},{68... | collective-permute-start | bytes 1572872 | tf_op jit(solution)/shard_map/ppermute | solution.py:212
  100.4 0.0 collective-permute-done.15.refs_4_
  100.4 3.1 %collective-permute-start.16 = (bf16[1024,256]{1,0:T(8,128)(2,1)S(1)}, bf16[1024,256]{1,0:T(8,128)(2,1)S(1)}, u32[]{:S(2)}, u32[]{:S(2)}) collective-permute-start(bf16[1024,256]{1,0:T(8,128)(2,1)S(1)} %collective-permute-done.15.refs_4_), channel_id=1, source_target_pairs={{0,4},{4,8},{8,12},{12,16},{16,20},{20,24},{24,28},{28,32},{32,36}... | collective-permute-start | bytes 1572872 | tf_op jit(solution)/shard_map/stream_0_step_8/ppermute | solution.py:192
  103.6 0.0 collective-permute-done.23
  103.6 3.5 %collective-permute-start.24 = (bf16[1024,256]{1,0:T(8,128)(2,1)S(1)}, bf16[1024,256]{1,0:T(8,128)(2,1)S(1)}, u32[]{:S(2)}, u32[]{:S(2)}) collective-permute-start(bf16[1024,256]{1,0:T(8,128)(2,1)S(1)} %collective-permute-done.23), channel_id=1, source_target_pairs={{0,64},{64,0},{1,65},{65,1},{2,66},{66,2},{3,67},{67,3},{4,68},{68... | collective-permute-start | bytes 1572872 | tf_op jit(solution)/shard_map/ppermute | solution.py:213
  107.1 2.7 %shard_map.75.refs_7_ = f32[1024,512]{1,0:T(8,128)S(1)} custom-call(bf16[1024,512]{1,0:T(8,128)(2,1)S(1)} %pad_maximum_fusion.refs_0_, bf16[1024,512]{1,0:T(8,128)(2,1)S(1)} %collective-permute-done.2.refs_1_, bf16[1024,512]{1,0:T(8,128)(2,1)S(1)} %collective-permute-done.7.refs_2_, bf16[1024,512]{1,0:T(8,128)(2,1)S(1)} %collective-permute-done.8.refs_3_, ...), custom_call_target="tpu_custom_call" | custom-call | flops 1879048192 | bytes 2097152 | tf_op jit(solution)/shard_map/pallas_call | solution.py:157
  109.8 0.0 collective-permute-done.25.refs_4_
  109.8 2.4 %shard_map.76.refs_8_ = f32[1024,512]{1,0:T(8,128)S(1)} custom-call(bf16[1024,512]{1,0:T(8,128)(2,1)S(1)} %pad_maximum_fusion.refs_0_, bf16[1024,512]{1,0:T(8,128)(2,1)S(1)} %collective-permute-done.2.refs_1_, bf16[1024,512]{1,0:T(8,128)(2,1)S(1)} %collective-permute-done.7.refs_2_, bf16[1024,512]{1,0:T(8,128)(2,1)S(1)} %collective-permute-done.8.refs_3_, ...), custom_call_target="tpu_custom_call" | custom-call | flops 1610612736 | bytes 2097152 | tf_op jit(solution)/shard_map/pallas_call | solution.py:157
  112.2 0.0 collective-permute-done.16.refs_5_
  112.2 1.9 %shard_map.77 = f32[4,272,512]{2,1,0:T(8,128)S(1)} custom-call(bf16[1024,512]{1,0:T(8,128)(2,1)S(1)} %pad_maximum_fusion.refs_0_, bf16[1024,512]{1,0:T(8,128)(2,1)S(1)} %collective-permute-done.2.refs_1_, bf16[1024,512]{1,0:T(8,128)(2,1)S(1)} %collective-permute-done.7.refs_2_, bf16[1024,512]{1,0:T(8,128)(2,1)S(1)} %collective-permute-done.8.refs_3_, ...), custom_call_target="tpu_custom_call" | custom-call | flops 805306368 | bytes 2097152 | tf_op jit(solution)/shard_map/pallas_call | solution.py:157
  114.1 0.3 convert.5
  114.4 0.2 fusion.4
  114.6 4.7 %collective-permute-start.27 = (f16[1,272,512]{2,1,0:T(8,128)(2,1)S(1)}, f16[1,272,512]{2,1,0:T(8,128)(2,1)S(1)}, u32[]{:S(2)}, u32[]{:S(2)}) collective-permute-start(f16[1,272,512]{2,1,0:T(8,128)(2,1)S(1)} %get-tuple-element.19), channel_id=1, source_target_pairs={{0,2},{1,3},{2,0},{3,1},{4,6},{5,7},{6,4},{7,5},{8,10},{9,11},{10,... | collective-permute-start | bytes 835592 | tf_op jit(solution)/shard_map/ppermute | solution.py:224
  119.2 2.2 %collective-permute-start.28 = (f16[1,272,512]{2,1,0:T(8,128)(2,1)S(1)}, f16[1,272,512]{2,1,0:T(8,128)(2,1)}, u32[]{:S(2)}, u32[]{:S(2)}) collective-permute-start(f16[1,272,512]{2,1,0:T(8,128)(2,1)S(1)} %get-tuple-element.21), channel_id=1, source_target_pairs={{0,1},{1,2},{2,3},{3,0},{4,5},{5,6},{6,7},{7,4},{8,9},{9,10},{10,1... | collective-permute-start | bytes 835592 | tf_op jit(solution)/shard_map/ppermute | solution.py:224
  121.5 4.3 %collective-permute-start.29 = (f16[1,272,512]{2,1,0:T(8,128)(2,1)S(1)}, f16[1,272,512]{2,1,0:T(8,128)(2,1)}, u32[]{:S(2)}, u32[]{:S(2)}) collective-permute-start(f16[1,272,512]{2,1,0:T(8,128)(2,1)S(1)} %get-tuple-element.20), channel_id=1, source_target_pairs={{0,3},{1,0},{2,1},{3,2},{4,7},{5,4},{6,5},{7,6},{8,11},{9,8},{10,9... | collective-permute-start | bytes 835592 | tf_op jit(solution)/shard_map/ppermute | solution.py:224
  125.7 0.6 slice_reduce_fusion
  132.9 0.6 convert_reduce_fusion.2
  139.9 0.0 collective-permute-done.28
  139.9 1.3 convert_reduce_fusion.1
  147.7 0.0 collective-permute-done.29
  147.7 1.3 convert_reduce_fusion
  155.6 2.0 %fusion.3 = f32[256,512]{1,0:T(8,128)} fusion(f32[4,272,512]{2,1,0:T(8,128)S(1)} %shard_map.77, f16[1,272,512]{2,1,0:T(8,128)(2,1)} %collective-permute-done.29, f16[1,272,512]{2,1,0:T(8,128)(2,1)} %collective-permute-done.28, f16[1,272,512]{2,1,0:T(8,128)(2,1)S(1)} %collective-permute-done.27, f32[]{:T(128)S(6)} %select_n.212, f32[]{:T(128)S(6)} %select_n.211, ...), kind=kLoop, calls=%fused_computation.5 | loop fusion | flops 1310720 | bytes 1835024 | tf_op jit(solution)/shard_map/add | solution.py:225
  (11 shorter events, 0.0 us)
Async XLA Ops:
  2.0 105.1 %copy-start = (bf16[1024,256]{1,0:T(8,128)(2,1)S(1)}, bf16[1024,256]{1,0:T(8,128)(2,1)}, u32[]{:S(2)}) copy-start(bf16[1024,256]{1,0:T(8,128)(2,1)} %shard_map.73.refs_4_) | copy-start | bytes 1572868
  2.0 14.7 %collective-permute-start = (bf16[1024,256]{1,0:T(8,128)(2,1)}, bf16[1024,256]{1,0:T(8,128)(2,1)S(1)}, u32[]{:S(2)}, u32[]{:S(2)}) collective-permute-start(bf16[1024,256]{1,0:T(8,128)(2,1)} %shard_map.73.refs_4_), channel_id=1, source_target_pairs={{0,64},{64,0},{1,65},{65,1},{2,66},{66,2},{3,67},{67,3},{4,68},{68... | collective-permute-start | bytes 1572872 | tf_op jit(solution)/shard_map/ppermute | solution.py:153
  11.0 12.4 %collective-permute-start.9 = (bf16[1024,256]{1,0:T(8,128)(2,1)}, bf16[1024,256]{1,0:T(8,128)(2,1)S(1)}, u32[]{:S(2)}, u32[]{:S(2)}) collective-permute-start(bf16[1024,256]{1,0:T(8,128)(2,1)} %shard_map.73.refs_4_), channel_id=1, source_target_pairs={{0,4},{4,8},{8,12},{12,16},{16,20},{20,24},{24,28},{28,32},{32,36}... | collective-permute-start | bytes 1572872 | tf_op jit(solution)/shard_map/stream_0_step_1/ppermute | solution.py:192
  16.7 11.9 %collective-permute-start.3 = (bf16[1024,256]{1,0:T(8,128)(2,1)S(1)}, bf16[1024,256]{1,0:T(8,128)(2,1)S(1)}, u32[]{:S(2)}, u32[]{:S(2)}) collective-permute-start(bf16[1024,256]{1,0:T(8,128)(2,1)S(1)} %collective-permute-done), channel_id=1, source_target_pairs={{0,4},{4,8},{8,12},{12,16},{16,20},{20,24},{24,28},{28,32},{32,36}... | collective-permute-start | bytes 1572872 | tf_op jit(solution)/shard_map/stream_1_step_1/ppermute | solution.py:192
  21.4 12.3 %collective-permute-start.1 = (bf16[512,512]{1,0:T(8,128)(2,1)}, bf16[512,512]{1,0:T(8,128)(2,1)S(1)}, u32[]{:S(2)}, u32[]{:S(2)}) collective-permute-start(bf16[512,512]{1,0:T(8,128)(2,1)} %shard_map.74), channel_id=1, source_target_pairs={{0,64},{64,0},{1,65},{65,1},{2,66},{66,2},{3,67},{67,3},{4,68},{68... | collective-permute-start | bytes 1572872 | tf_op jit(solution)/shard_map/b_swap/ppermute | solution.py:200
  23.4 16.1 %collective-permute-start.10 = (bf16[1024,256]{1,0:T(8,128)(2,1)S(1)}, bf16[1024,256]{1,0:T(8,128)(2,1)S(1)}, u32[]{:S(2)}, u32[]{:S(2)}) collective-permute-start(bf16[1024,256]{1,0:T(8,128)(2,1)S(1)} %collective-permute-done.9.refs_5_), channel_id=1, source_target_pairs={{0,4},{4,8},{8,12},{12,16},{16,20},{20,24},{24,28},{28,32},{32,36}... | collective-permute-start | bytes 1572872 | tf_op jit(solution)/shard_map/stream_0_step_2/ppermute | solution.py:192
  28.7 14.7 %collective-permute-start.4 = (bf16[1024,256]{1,0:T(8,128)(2,1)S(1)}, bf16[1024,256]{1,0:T(8,128)(2,1)S(1)}, u32[]{:S(2)}, u32[]{:S(2)}) collective-permute-start(bf16[1024,256]{1,0:T(8,128)(2,1)S(1)} %collective-permute-done.3), channel_id=1, source_target_pairs={{0,4},{4,8},{8,12},{12,16},{16,20},{20,24},{24,28},{28,32},{32,36}... | collective-permute-start | bytes 1572872 | tf_op jit(solution)/shard_map/stream_1_step_2/ppermute | solution.py:192
  34.8 23.3 %collective-permute-start.2 = (bf16[1024,512]{1,0:T(8,128)(2,1)S(1)}, bf16[1024,512]{1,0:T(8,128)(2,1)S(1)}, u32[]{:S(2)}, u32[]{:S(2)}) collective-permute-start(bf16[1024,512]{1,0:T(8,128)(2,1)S(1)} %pad_maximum_fusion.refs_0_), channel_id=1, source_target_pairs={{0,128},{64,448},{128,256},{192,64},{256,384},{320,192},{384,0},{4... | collective-permute-start | bytes 3145736 | tf_op jit(solution)/shard_map/b_near/ppermute | solution.py:204
  39.5 10.2 %collective-permute-start.11 = (bf16[1024,256]{1,0:T(8,128)(2,1)S(1)}, bf16[1024,256]{1,0:T(8,128)(2,1)S(1)}, u32[]{:S(2)}, u32[]{:S(2)}) collective-permute-start(bf16[1024,256]{1,0:T(8,128)(2,1)S(1)} %collective-permute-done.10.refs_6_), channel_id=1, source_target_pairs={{0,4},{4,8},{8,12},{12,16},{16,20},{20,24},{24,28},{28,32},{32,36}... | collective-permute-start | bytes 1572872 | tf_op jit(solution)/shard_map/stream_0_step_3/ppermute | solution.py:192
  41.4 13.4 %collective-permute-start.6 = (bf16[1024,256]{1,0:T(8,128)(2,1)S(1)}, bf16[1024,256]{1,0:T(8,128)(2,1)S(1)}, u32[]{:S(2)}, u32[]{:S(2)}) collective-permute-start(bf16[1024,256]{1,0:T(8,128)(2,1)S(1)} %collective-permute-done.3), channel_id=1, source_target_pairs={{0,64},{64,0},{1,65},{65,1},{2,66},{66,2},{3,67},{67,3},{4,68},{68... | collective-permute-start | bytes 1572872 | tf_op jit(solution)/shard_map/ppermute | solution.py:212
  43.3 12.0 %collective-permute-start.5 = (bf16[1024,256]{1,0:T(8,128)(2,1)S(1)}, bf16[1024,256]{1,0:T(8,128)(2,1)S(1)}, u32[]{:S(2)}, u32[]{:S(2)}) collective-permute-start(bf16[1024,256]{1,0:T(8,128)(2,1)S(1)} %collective-permute-done.4), channel_id=1, source_target_pairs={{0,4},{4,8},{8,12},{12,16},{16,20},{20,24},{24,28},{28,32},{32,36}... | collective-permute-start | bytes 1572872 | tf_op jit(solution)/shard_map/stream_1_step_3/ppermute | solution.py:192
  49.7 11.2 %collective-permute-start.12 = (bf16[1024,256]{1,0:T(8,128)(2,1)S(1)}, bf16[1024,256]{1,0:T(8,128)(2,1)S(1)}, u32[]{:S(2)}, u32[]{:S(2)}) collective-permute-start(bf16[1024,256]{1,0:T(8,128)(2,1)S(1)} %collective-permute-done.11.refs_7_), channel_id=1, source_target_pairs={{0,4},{4,8},{8,12},{12,16},{16,20},{20,24},{24,28},{28,32},{32,36}... | collective-permute-start | bytes 1572872 | tf_op jit(solution)/shard_map/stream_0_step_4/ppermute | solution.py:192
  52.8 13.3 %collective-permute-start.18 = (bf16[1024,256]{1,0:T(8,128)(2,1)S(1)}, bf16[1024,256]{1,0:T(8,128)(2,1)S(1)}, u32[]{:S(2)}, u32[]{:S(2)}) collective-permute-start(bf16[1024,256]{1,0:T(8,128)(2,1)S(1)} %collective-permute-done.4), channel_id=1, source_target_pairs={{0,64},{64,0},{1,65},{65,1},{2,66},{66,2},{3,67},{67,3},{4,68},{68... | collective-permute-start | bytes 1572872 | tf_op jit(solution)/shard_map/ppermute | solution.py:212
  55.3 11.2 %collective-permute-start.17 = (bf16[1024,256]{1,0:T(8,128)(2,1)S(1)}, bf16[1024,256]{1,0:T(8,128)(2,1)S(1)}, u32[]{:S(2)}, u32[]{:S(2)}) collective-permute-start(bf16[1024,256]{1,0:T(8,128)(2,1)S(1)} %collective-permute-done.5), channel_id=1, source_target_pairs={{0,4},{4,8},{8,12},{12,16},{16,20},{20,24},{24,28},{28,32},{32,36}... | collective-permute-start | bytes 1572872 | tf_op jit(solution)/shard_map/stream_1_step_4/ppermute | solution.py:192
  60.9 13.9 %collective-permute-start.13 = (bf16[1024,256]{1,0:T(8,128)(2,1)S(1)}, bf16[1024,256]{1,0:T(8,128)(2,1)S(1)}, u32[]{:S(2)}, u32[]{:S(2)}) collective-permute-start(bf16[1024,256]{1,0:T(8,128)(2,1)S(1)} %collective-permute-done.12.refs_8_), channel_id=1, source_target_pairs={{0,4},{4,8},{8,12},{12,16},{16,20},{20,24},{24,28},{28,32},{32,36}... | collective-permute-start | bytes 1572872 | tf_op jit(solution)/shard_map/stream_0_step_5/ppermute | solution.py:192
  63.9 15.1 %collective-permute-start.20 = (bf16[1024,256]{1,0:T(8,128)(2,1)S(1)}, bf16[1024,256]{1,0:T(8,128)(2,1)S(1)}, u32[]{:S(2)}, u32[]{:S(2)}) collective-permute-start(bf16[1024,256]{1,0:T(8,128)(2,1)S(1)} %collective-permute-done.5), channel_id=1, source_target_pairs={{0,64},{64,0},{1,65},{65,1},{2,66},{66,2},{3,67},{67,3},{4,68},{68... | collective-permute-start | bytes 1572872 | tf_op jit(solution)/shard_map/ppermute | solution.py:212
  66.5 12.5 %collective-permute-start.19 = (bf16[1024,256]{1,0:T(8,128)(2,1)S(1)}, bf16[1024,256]{1,0:T(8,128)(2,1)S(1)}, u32[]{:S(2)}, u32[]{:S(2)}) collective-permute-start(bf16[1024,256]{1,0:T(8,128)(2,1)S(1)} %collective-permute-done.17), channel_id=1, source_target_pairs={{0,4},{4,8},{8,12},{12,16},{16,20},{20,24},{24,28},{28,32},{32,36}... | collective-permute-start | bytes 1572872 | tf_op jit(solution)/shard_map/stream_1_step_5/ppermute | solution.py:192
  70.4 27.5 %collective-permute-start.7 = (bf16[1024,512]{1,0:T(8,128)(2,1)S(1)}, bf16[1024,512]{1,0:T(8,128)(2,1)S(1)}, u32[]{:S(2)}, u32[]{:S(2)}) collective-permute-start(bf16[1024,512]{1,0:T(8,128)(2,1)S(1)} %collective-permute-done.2.refs_1_), channel_id=1, source_target_pairs={{0,64},{64,0},{1,65},{65,1},{2,66},{66,2},{3,67},{67,3},{4,68},{68... | collective-permute-start | bytes 3145736 | tf_op jit(solution)/shard_map/b_turn/ppermute | solution.py:210
  72.4 17.8 %collective-permute-start.22 = (bf16[1024,256]{1,0:T(8,128)(2,1)S(1)}, bf16[1024,256]{1,0:T(8,128)(2,1)S(1)}, u32[]{:S(2)}, u32[]{:S(2)}) collective-permute-start(bf16[1024,256]{1,0:T(8,128)(2,1)S(1)} %collective-permute-done.17), channel_id=1, source_target_pairs={{0,64},{64,0},{1,65},{65,1},{2,66},{66,2},{3,67},{67,3},{4,68},{68... | collective-permute-start | bytes 1572872 | tf_op jit(solution)/shard_map/ppermute | solution.py:212
  74.8 10.9 %collective-permute-start.14 = (bf16[1024,256]{1,0:T(8,128)(2,1)S(1)}, bf16[1024,256]{1,0:T(8,128)(2,1)S(1)}, u32[]{:S(2)}, u32[]{:S(2)}) collective-permute-start(bf16[1024,256]{1,0:T(8,128)(2,1)S(1)} %collective-permute-done.13.refs_9_), channel_id=1, source_target_pairs={{0,4},{4,8},{8,12},{12,16},{16,20},{20,24},{24,28},{28,32},{32,36}... | collective-permute-start | bytes 1572872 | tf_op jit(solution)/shard_map/stream_0_step_6/ppermute | solution.py:192
  79.0 11.7 %collective-permute-start.21 = (bf16[1024,256]{1,0:T(8,128)(2,1)S(1)}, bf16[1024,256]{1,0:T(8,128)(2,1)S(1)}, u32[]{:S(2)}, u32[]{:S(2)}) collective-permute-start(bf16[1024,256]{1,0:T(8,128)(2,1)S(1)} %collective-permute-done.19), channel_id=1, source_target_pairs={{0,4},{4,8},{8,12},{12,16},{16,20},{20,24},{24,28},{28,32},{32,36}... | collective-permute-start | bytes 1572872 | tf_op jit(solution)/shard_map/stream_1_step_6/ppermute | solution.py:192
  81.6 25.5 %collective-permute-start.8 = (bf16[1024,512]{1,0:T(8,128)(2,1)S(1)}, bf16[1024,512]{1,0:T(8,128)(2,1)S(1)}, u32[]{:S(2)}, u32[]{:S(2)}) collective-permute-start(bf16[1024,512]{1,0:T(8,128)(2,1)S(1)} %collective-permute-done.2.refs_1_), channel_id=1, source_target_pairs={{0,128},{64,448},{128,256},{192,64},{256,384},{320,192},{384,0},{4... | collective-permute-start | bytes 3145736 | tf_op jit(solution)/shard_map/b_far/ppermute | solution.py:207
  85.7 14.7 %collective-permute-start.15 = (bf16[1024,256]{1,0:T(8,128)(2,1)S(1)}, bf16[1024,256]{1,0:T(8,128)(2,1)S(1)}, u32[]{:S(2)}, u32[]{:S(2)}) collective-permute-start(bf16[1024,256]{1,0:T(8,128)(2,1)S(1)} %collective-permute-done.14.refs_10_), channel_id=1, source_target_pairs={{0,4},{4,8},{8,12},{12,16},{16,20},{20,24},{24,28},{28,32},{32,36}... | collective-permute-start | bytes 1572872 | tf_op jit(solution)/shard_map/stream_0_step_7/ppermute | solution.py:192
  90.7 12.8 %collective-permute-start.23 = (bf16[1024,256]{1,0:T(8,128)(2,1)S(1)}, bf16[1024,256]{1,0:T(8,128)(2,1)S(1)}, u32[]{:S(2)}, u32[]{:S(2)}) collective-permute-start(bf16[1024,256]{1,0:T(8,128)(2,1)S(1)} %collective-permute-done.21), channel_id=1, source_target_pairs={{0,4},{4,8},{8,12},{12,16},{16,20},{20,24},{24,28},{28,32},{32,36}... | collective-permute-start | bytes 1572872 | tf_op jit(solution)/shard_map/stream_1_step_7/ppermute | solution.py:192
  96.1 13.7 %collective-permute-start.26 = (bf16[1024,256]{1,0:T(8,128)(2,1)S(1)}, bf16[1024,256]{1,0:T(8,128)(2,1)S(1)}, u32[]{:S(2)}, u32[]{:S(2)}) collective-permute-start(bf16[1024,256]{1,0:T(8,128)(2,1)S(1)} %collective-permute-done.19), channel_id=1, source_target_pairs={{0,64},{64,0},{1,65},{65,1},{2,66},{66,2},{3,67},{67,3},{4,68},{68... | collective-permute-start | bytes 1572872 | tf_op jit(solution)/shard_map/ppermute | solution.py:212
  98.0 11.8 %collective-permute-start.25 = (bf16[1024,256]{1,0:T(8,128)(2,1)S(1)}, bf16[1024,256]{1,0:T(8,128)(2,1)S(1)}, u32[]{:S(2)}, u32[]{:S(2)}) collective-permute-start(bf16[1024,256]{1,0:T(8,128)(2,1)S(1)} %collective-permute-done.21), channel_id=1, source_target_pairs={{0,64},{64,0},{1,65},{65,1},{2,66},{66,2},{3,67},{67,3},{4,68},{68... | collective-permute-start | bytes 1572872 | tf_op jit(solution)/shard_map/ppermute | solution.py:212
  100.4 11.8 %collective-permute-start.16 = (bf16[1024,256]{1,0:T(8,128)(2,1)S(1)}, bf16[1024,256]{1,0:T(8,128)(2,1)S(1)}, u32[]{:S(2)}, u32[]{:S(2)}) collective-permute-start(bf16[1024,256]{1,0:T(8,128)(2,1)S(1)} %collective-permute-done.15.refs_4_), channel_id=1, source_target_pairs={{0,4},{4,8},{8,12},{12,16},{16,20},{20,24},{24,28},{28,32},{32,36}... | collective-permute-start | bytes 1572872 | tf_op jit(solution)/shard_map/stream_0_step_8/ppermute | solution.py:192
  103.6 8.6 %collective-permute-start.24 = (bf16[1024,256]{1,0:T(8,128)(2,1)S(1)}, bf16[1024,256]{1,0:T(8,128)(2,1)S(1)}, u32[]{:S(2)}, u32[]{:S(2)}) collective-permute-start(bf16[1024,256]{1,0:T(8,128)(2,1)S(1)} %collective-permute-done.23), channel_id=1, source_target_pairs={{0,64},{64,0},{1,65},{65,1},{2,66},{66,2},{3,67},{67,3},{4,68},{68... | collective-permute-start | bytes 1572872 | tf_op jit(solution)/shard_map/ppermute | solution.py:213
  114.6 18.3 %collective-permute-start.27 = (f16[1,272,512]{2,1,0:T(8,128)(2,1)S(1)}, f16[1,272,512]{2,1,0:T(8,128)(2,1)S(1)}, u32[]{:S(2)}, u32[]{:S(2)}) collective-permute-start(f16[1,272,512]{2,1,0:T(8,128)(2,1)S(1)} %get-tuple-element.19), channel_id=1, source_target_pairs={{0,2},{1,3},{2,0},{3,1},{4,6},{5,7},{6,4},{7,5},{8,10},{9,11},{10,... | collective-permute-start | bytes 835592 | tf_op jit(solution)/shard_map/ppermute | solution.py:224
  119.2 20.7 %collective-permute-start.28 = (f16[1,272,512]{2,1,0:T(8,128)(2,1)S(1)}, f16[1,272,512]{2,1,0:T(8,128)(2,1)}, u32[]{:S(2)}, u32[]{:S(2)}) collective-permute-start(f16[1,272,512]{2,1,0:T(8,128)(2,1)S(1)} %get-tuple-element.21), channel_id=1, source_target_pairs={{0,1},{1,2},{2,3},{3,0},{4,5},{5,6},{6,7},{7,4},{8,9},{9,10},{10,1... | collective-permute-start | bytes 835592 | tf_op jit(solution)/shard_map/ppermute | solution.py:224
  121.5 26.2 %collective-permute-start.29 = (f16[1,272,512]{2,1,0:T(8,128)(2,1)S(1)}, f16[1,272,512]{2,1,0:T(8,128)(2,1)}, u32[]{:S(2)}, u32[]{:S(2)}) collective-permute-start(f16[1,272,512]{2,1,0:T(8,128)(2,1)S(1)} %get-tuple-element.20), channel_id=1, source_target_pairs={{0,3},{1,0},{2,1},{3,2},{4,7},{5,4},{6,5},{7,6},{8,11},{9,8},{10,9... | collective-permute-start | bytes 835592 | tf_op jit(solution)/shard_map/ppermute | solution.py:224
